TPU v7x, 32 devices: a whole 2x2x4 slice. The times are simulated.
32 devices in a mesh: dp: 4 (over z), mp: 8 (over y, x, core).
Axes of the slice: x: 2, y: 2, z: 4, core: 2. Of those that a mesh axis runs over, the one named last changes fastest.
Arguments:
- tokens: bfloat16 [2, 1024, 4, 2048], P(None, 'mp', 'dp'), may hold values from -6 to 6
- lengths: int32 [2, 4], P(None, 'dp'), may hold values from 256 to 1024, as said below
- norm_gain: float32 [2048], replicated, may hold values from 0.1 to 1.9
- in_proj: bfloat16 [2048, 3, 2048], P(None, None, 'mp'), may hold values from -0.125 to 0.125
- short_taps: float32 [3, 3, 2048], P(None, None, 'mp'), may hold values from -3 to 3
- conv_skip: float32 [2048], P('mp'), may hold values from 0.5 to 1.5
- filter_residue: float32 [2048, 16], P('mp'), may hold values from -0.4 to 0.4
- filter_rate: float32 [2048, 16], P('mp'), may hold values from 0.002 to 0.05
- filter_freq: float32 [2048, 16], P('mp'), may hold values from 0 to 1
- out_proj: bfloat16 [2048, 2048], P('mp'), may hold values from -0.125 to 0.125
- mlp_gain: float32 [2048], replicated, may hold values from 0.1 to 1.9
- gate_proj: bfloat16 [2048, 5632], P(None, 'mp'), may hold values from -0.125 to 0.125
- up_proj: bfloat16 [2048, 5632], P(None, 'mp'), may hold values from -0.125 to 0.125
- down_proj: bfloat16 [5632, 2048], P('mp'), may hold values from -0.078125 to 0.078125
- cotangent: bfloat16 [2, 1024, 4, 2048], P(None, 'mp', 'dp'), may hold values from -6 to 6
Outputs:
- layer_out: bfloat16 [2, 1024, 4, 2048], P(None, 'mp', 'dp')
- grad_tokens: float32 [2, 1024, 4, 2048], P(None, 'mp', 'dp')
- grad_norm_gain: float32 [2048], replicated
- grad_in_proj: float32 [2048, 3, 2048], P(None, None, 'mp')
- grad_short_taps: float32 [3, 3, 2048], P(None, None, 'mp')
- grad_conv_skip: float32 [2048], P('mp')
- grad_filter_residue: float32 [2048, 16], P('mp')
- grad_filter_rate: float32 [2048, 16], P('mp')
- grad_filter_freq: float32 [2048, 16], P('mp')
- grad_out_proj: float32 [2048, 2048], P('mp')
- grad_mlp_gain: float32 [2048], replicated
- grad_gate_proj: float32 [2048, 5632], P(None, 'mp')
- grad_up_proj: float32 [2048, 5632], P(None, 'mp')
- grad_down_proj: float32 [5632, 2048], P('mp')
Inputs may be any that keep to these rules, and one draw needn't show every extreme that they name: `lengths`: each sequence holds one document from its first position, at least a quarter of 1024 long; among the sequences of all micro-batches held by one index of dp, one (drawn) is exactly 1024 long.
All inputs are finite; a program needn't handle non-finite values.
Results may differ from a plain program's by a relative error of at most 0.017.
Values may be sent and summed in bfloat16 or wider, within the bound.
No kernel may reach another device: no remote copies, remote signals or barrier semaphores. Data moves between devices by JAX's collectives and lax.ppermute only.
A program may use at most 768 MiB of HBM per device.

v0:
```python
from functools import partial

import jax
import jax.numpy as jnp
from jax import lax
from jax.sharding import PartitionSpec as P

epsilon = 1e-06


def modal_filter(residue, rate, freq, length):
    positions = jnp.arange(length).astype(jnp.float32)

    def add_pole(running, pole):
        res_col, rate_col, freq_col = pole
        shaped = (
            res_col[:, None]
            * jnp.exp(-rate_col[:, None] * positions[None, :])
            * jnp.cos(freq_col[:, None] * positions[None, :])
        )
        return (running + shaped, None)

    start_val = jnp.zeros((residue.shape[0], length), jnp.float32)
    total, unused = lax.scan(add_pole, start_val, (residue.T, rate.T, freq.T))
    return total


def norm_forward(rows_in, gain_vec):
    scale_rows = lax.rsqrt(jnp.mean(rows_in * rows_in, axis=-1, keepdims=True) + epsilon)
    return rows_in * scale_rows * gain_vec


def contract_rows(left, right):
    return lax.dot_general(
        left, right, (((0,), (0,)), ((), ())), preferred_element_type=jnp.float32
    )


def contract_cols(left, right):
    return lax.dot_general(
        left, right, (((1,), (1,)), ((), ())), preferred_element_type=jnp.float32
    )


def lag_table(filt_pad, offset, block_len):
    chans = filt_pad.shape[0]
    segment = filt_pad[:, offset * block_len : offset * block_len + 2 * block_len]
    reverse = segment[:, ::-1]
    tiled = jnp.broadcast_to(reverse[:, None, :], (chans, block_len, 2 * block_len)).reshape(
        chans, 2 * block_len * block_len
    )
    window = tiled[:, block_len - 1 : block_len - 1 + block_len * (2 * block_len - 1)]
    return window.reshape(chans, block_len, 2 * block_len - 1)[:, :, :block_len]


def lag_fold(grad_table, block_len):
    chans = grad_table.shape[0]
    wide = jnp.pad(grad_table, ((0, 0), (0, 0), (0, block_len - 1)))
    flat_rows = wide.reshape(chans, block_len * (2 * block_len - 1))
    placed = jnp.pad(flat_rows, ((0, 0), (block_len - 1, 1)))
    summed_rev = jnp.sum(placed.reshape(chans, block_len, 2 * block_len), axis=1)
    return summed_rev[:, ::-1]


def local(
    tokens,
    lengths,
    norm_gain,
    in_proj,
    short_taps,
    conv_skip,
    filter_residue,
    filter_rate,
    filter_freq,
    out_proj,
    mlp_gain,
    gate_proj,
    up_proj,
    down_proj,
    cotangent,
):
    micro_count, local_len, seq_count, model_width = tokens.shape
    channels = in_proj.shape[2]
    hidden_units = gate_proj.shape[1]
    length = local_len * lax.axis_size("mp")
    nblocks = max(1, length // 128)
    block_len = length // nblocks
    local_rows = local_len * seq_count
    in_flat = in_proj.reshape(model_width, 3 * channels)
    mlp_both = jnp.concatenate([gate_proj, up_proj], axis=1)
    filt_vals, filter_pull = jax.vjp(
        partial(modal_filter, length=length), filter_residue, filter_rate, filter_freq
    )
    filt_low = filt_vals.astype(jnp.bfloat16)
    filt_pad = jnp.concatenate([jnp.zeros((channels, block_len), jnp.bfloat16), filt_low], axis=1)
    lag_tables = [lag_table(filt_pad, offset, block_len) for offset in range(nblocks)]
    positions = lax.axis_index("mp") * local_len + jnp.arange(local_len)
    grad_in = jnp.zeros((model_width, 3 * channels), jnp.float32)
    grad_taps = jnp.zeros(short_taps.shape, jnp.float32)
    grad_skip = jnp.zeros(conv_skip.shape, jnp.float32)
    grad_tables = [
        jnp.zeros((channels, block_len, block_len), jnp.float32) for offset in range(nblocks)
    ]
    grad_out = jnp.zeros(out_proj.shape, jnp.float32)
    grad_both = jnp.zeros((model_width, 2 * hidden_units), jnp.float32)
    grad_down = jnp.zeros(down_proj.shape, jnp.float32)
    grad_gain_one = jnp.zeros(norm_gain.shape, jnp.float32)
    grad_gain_two = jnp.zeros(mlp_gain.shape, jnp.float32)
    out_list = []
    grad_list = []
    for micro_idx in range(micro_count):
        valid_rows = (positions[:, None] < lengths[micro_idx][None, :]).astype(jnp.float32)
        tokens_local = tokens[micro_idx].reshape(local_rows, model_width)
        rows_in = tokens_local.astype(jnp.float32)
        normed_low = norm_forward(rows_in, norm_gain).astype(jnp.bfloat16)
        projected = jnp.dot(
            lax.all_gather(normed_low, "mp", axis=0, tiled=True),
            in_flat,
            preferred_element_type=jnp.float32,
        )
        proj_grid = projected.reshape(length, seq_count, 3, channels)
        padded_proj = jnp.pad(proj_grid, ((2, 0), (0, 0), (0, 0), (0, 0)))
        shorted = (
            short_taps[0] * padded_proj[2:]
            + short_taps[1] * padded_proj[1:-1]
            + short_taps[2] * padded_proj[:-2]
        )
        query_part = shorted[:, :, 0]
        key_part = shorted[:, :, 1]
        value_part = shorted[:, :, 2]
        mixed_low = (key_part * value_part).astype(jnp.bfloat16)
        mixed_exact = mixed_low.astype(jnp.float32)
        mixed_blocks = mixed_low.reshape(nblocks, block_len, seq_count, channels)
        conv_total = jnp.zeros((nblocks, block_len, seq_count, channels), jnp.float32)
        for offset in range(nblocks):
            term = jnp.einsum(
                "cab,nbsc->nasc",
                lag_tables[offset],
                mixed_blocks[: nblocks - offset],
                preferred_element_type=jnp.float32,
            )
            conv_total = conv_total.at[offset:].add(term)
        response = conv_total.reshape(length, seq_count, channels) + conv_skip * mixed_exact
        gated_low = (
            (query_part * response).astype(jnp.bfloat16).reshape(length * seq_count, channels)
        )
        branch = lax.psum_scatter(
            jnp.dot(gated_low, out_proj, preferred_element_type=jnp.float32),
            "mp",
            scatter_dimension=0,
            tiled=True,
        )
        second = rows_in + branch
        mlp_normed = norm_forward(second, mlp_gain).astype(jnp.bfloat16)
        both_out = jnp.dot(
            lax.all_gather(mlp_normed, "mp", axis=0, tiled=True),
            mlp_both,
            preferred_element_type=jnp.float32,
        )
        gate_vals = both_out[:, :hidden_units]
        up_vals = both_out[:, hidden_units:]
        sigmas = jax.nn.sigmoid(gate_vals)
        silu_vals = gate_vals * sigmas
        hidden_low = (silu_vals * up_vals).astype(jnp.bfloat16)
        mlp_out = lax.psum_scatter(
            jnp.dot(hidden_low, down_proj, preferred_element_type=jnp.float32).astype(jnp.bfloat16),
            "mp",
            scatter_dimension=0,
            tiled=True,
        ).astype(jnp.float32)
        final_rows = second + mlp_out
        out_list.append(
            (final_rows * valid_rows)
            .astype(jnp.bfloat16)
            .reshape(local_len, seq_count, model_width)
        )
        grad_final = (
            cotangent[micro_idx].reshape(local_rows, model_width).astype(jnp.float32) * valid_rows
        )
        grad_final_all = lax.all_gather(grad_final.astype(jnp.bfloat16), "mp", axis=0, tiled=True)
        grad_hidden = contract_cols(grad_final_all, down_proj)
        grad_down = grad_down + contract_rows(hidden_low, grad_final_all)
        grad_gate = grad_hidden * up_vals * sigmas * (1.0 + gate_vals * (1.0 - sigmas))
        grad_up = grad_hidden * silu_vals
        grad_both_low = jnp.concatenate([grad_gate, grad_up], axis=1).astype(jnp.bfloat16)
        grad_both = grad_both + contract_rows(
            lax.all_gather(mlp_normed, "mp", axis=0, tiled=True), grad_both_low
        )
        grad_mlp_normed = lax.psum_scatter(
            contract_cols(grad_both_low, mlp_both), "mp", scatter_dimension=0, tiled=True
        )
        unused, norm_pull_two = jax.vjp(norm_forward, second, mlp_gain)
        grad_second_norm, gain_two_term = norm_pull_two(grad_mlp_normed)
        grad_gain_two = grad_gain_two + gain_two_term
        grad_second = grad_final + grad_second_norm
        grad_branch_all = lax.all_gather(grad_second.astype(jnp.bfloat16), "mp", axis=0, tiled=True)
        grad_gated = contract_cols(grad_branch_all, out_proj).reshape(length, seq_count, channels)
        grad_out = grad_out + contract_rows(gated_low, grad_branch_all)
        grad_query = grad_gated * response
        grad_response = grad_gated * query_part
        grad_skip = grad_skip + jnp.sum(grad_response * mixed_exact, axis=(0, 1))
        grad_conv_blocks = grad_response.astype(jnp.bfloat16).reshape(
            nblocks, block_len, seq_count, channels
        )
        grad_mixed_blocks = jnp.zeros((nblocks, block_len, seq_count, channels), jnp.float32)
        for offset in range(nblocks):
            back_term = jnp.einsum(
                "cab,nasc->nbsc",
                lag_tables[offset],
                grad_conv_blocks[offset:],
                preferred_element_type=jnp.float32,
            )
            grad_mixed_blocks = grad_mixed_blocks.at[: nblocks - offset].add(back_term)
            grad_tables[offset] = grad_tables[offset] + jnp.einsum(
                "nasc,nbsc->cab",
                grad_conv_blocks[offset:],
                mixed_blocks[: nblocks - offset],
                preferred_element_type=jnp.float32,
            )
        grad_mixed = (
            grad_mixed_blocks.reshape(length, seq_count, channels) + conv_skip * grad_response
        )
        grad_key = grad_mixed * value_part
        grad_value = grad_mixed * key_part
        grad_shorted = jnp.stack([grad_query, grad_key, grad_value], axis=2)
        grad_taps = grad_taps + jnp.stack(
            [
                jnp.sum(grad_shorted * padded_proj[2:], axis=(0, 1)),
                jnp.sum(grad_shorted * padded_proj[1:-1], axis=(0, 1)),
                jnp.sum(grad_shorted * padded_proj[:-2], axis=(0, 1)),
            ],
            axis=0,
        )
        later_pad = jnp.pad(grad_shorted, ((0, 2), (0, 0), (0, 0), (0, 0)))
        grad_proj = (
            short_taps[0] * later_pad[:-2]
            + short_taps[1] * later_pad[1:-1]
            + short_taps[2] * later_pad[2:]
        )
        grad_proj_low = grad_proj.reshape(length * seq_count, 3 * channels).astype(jnp.bfloat16)
        grad_in = grad_in + contract_rows(
            lax.all_gather(normed_low, "mp", axis=0, tiled=True), grad_proj_low
        )
        grad_normed = lax.psum_scatter(
            contract_cols(grad_proj_low, in_flat), "mp", scatter_dimension=0, tiled=True
        )
        unused, norm_pull_one = jax.vjp(norm_forward, rows_in, norm_gain)
        grad_rows_norm, gain_one_term = norm_pull_one(grad_normed)
        grad_gain_one = grad_gain_one + gain_one_term
        grad_list.append((grad_second + grad_rows_norm).reshape(local_len, seq_count, model_width))
    grad_filt_pad = jnp.zeros((channels, length + block_len), jnp.float32)
    for offset in range(nblocks):
        lag_grad = lag_fold(grad_tables[offset], block_len)
        grad_filt_pad = grad_filt_pad + jnp.pad(
            lag_grad,
            ((0, 0), (offset * block_len, length + block_len - offset * block_len - 2 * block_len)),
        )
    grad_filt = grad_filt_pad[:, block_len:]
    grad_residue, grad_rate, grad_freq = filter_pull(grad_filt)
    summed = (
        lax.psum(grad_in.astype(jnp.bfloat16), "dp").astype(jnp.float32),
        lax.psum(grad_taps.astype(jnp.bfloat16), "dp").astype(jnp.float32),
        lax.psum(grad_skip.astype(jnp.bfloat16), "dp").astype(jnp.float32),
        lax.psum(grad_residue.astype(jnp.bfloat16), "dp").astype(jnp.float32),
        lax.psum(grad_rate.astype(jnp.bfloat16), "dp").astype(jnp.float32),
        lax.psum(grad_freq.astype(jnp.bfloat16), "dp").astype(jnp.float32),
        lax.psum(grad_out.astype(jnp.bfloat16), "dp").astype(jnp.float32),
        lax.psum(grad_both.astype(jnp.bfloat16), "dp").astype(jnp.float32),
        lax.psum(grad_down.astype(jnp.bfloat16), "dp").astype(jnp.float32),
    )
    gains = lax.psum((grad_gain_one, grad_gain_two), ("dp", "mp"))
    layer_out = jnp.stack(out_list, axis=0)
    grad_tokens = jnp.stack(grad_list, axis=0)
    return (
        layer_out,
        grad_tokens,
        gains[0],
        summed[0].reshape(model_width, 3, channels),
        summed[1],
        summed[2],
        summed[3],
        summed[4],
        summed[5],
        summed[6],
        gains[1],
        summed[7][:, :hidden_units],
        summed[7][:, hidden_units:],
        summed[8],
    )


def solution(mesh):
    return jax.shard_map(
        local,
        mesh=mesh,
        in_specs=(
            P(None, "mp", "dp", None),
            P(None, "dp"),
            P(),
            P(None, None, "mp"),
            P(None, None, "mp"),
            P("mp"),
            P("mp", None),
            P("mp", None),
            P("mp", None),
            P("mp", None),
            P(),
            P(None, "mp"),
            P(None, "mp"),
            P("mp", None),
            P(None, "mp", "dp", None),
        ),
        out_specs=(
            P(None, "mp", "dp", None),
            P(None, "mp", "dp", None),
            P(),
            P(None, None, "mp"),
            P(None, None, "mp"),
            P("mp"),
            P("mp", None),
            P("mp", None),
            P("mp", None),
            P("mp", None),
            P(),
            P(None, "mp"),
            P(None, "mp"),
            P("mp", None),
        ),
        check_vma=False,
    )
```

profile of v0, /device:TPU:0, one launch (start us, length us, event | category | flops | bytes accessed | tf_op | source)
XLA Modules:
  0.0 3605.0 jit_solution(6585775059911183929)
XLA Ops:
  13.3 193.6 %while.81 = (s32[]{:T(128)}, f32[256,1024]{1,0:T(8,128)}, f32[16,256,1024]{2,1,0:T(8,128)}, f32[16,256,1]{1,2,0:T(1,128)S(1)}, f32[16,256,1024]{2,1,0:T(8,128)},...) while((s32[]{:T(128)}, f32[256,1024]{1,0:T(8,128)}, ...), condition=%wide.region_2.3_spmd.clone.clone, body=%wide.region_1.2_spmd.clone.clone.sunk | while | flops 2360579 | bytes 6317203 | solution.py:24
  216.7 41.7 %copy.188 = bf16[32,8,128,256]{3,1,2,0:T(8,128)(2,1)S(1)} copy(bf16[32,8,128,256]{3,2,1,0:T(8,128)(2,1)S(1)} %bitcast.606) | data formatting | bytes 33554432
  267.0 56.7 %reshape.2319 = bf16[256,128,255]{2,1,0:T(8,128)(2,1)} reshape(bf16[256,32640]{1,0:T(8,128)(2,1)} %slice.1394) | data formatting | bytes 33423360 | tf_op jit(solution)/shard_map/reshape | solution.py:53
  325.5 41.7 %copy.189 = bf16[32,8,128,256]{3,1,2,0:T(8,128)(2,1)S(1)} copy(bf16[32,8,128,256]{3,2,1,0:T(8,128)(2,1)S(1)} %bitcast.607) | data formatting | bytes 33554432
  375.8 56.7 %reshape.2322 = bf16[256,128,255]{2,1,0:T(8,128)(2,1)} reshape(bf16[256,32640]{1,0:T(8,128)(2,1)} %slice.1399) | data formatting | bytes 33423360 | tf_op jit(solution)/shard_map/reshape | solution.py:53
  434.2 41.7 %copy.190 = bf16[32,8,128,256]{3,1,2,0:T(8,128)(2,1)S(1)} copy(bf16[32,8,128,256]{3,2,1,0:T(8,128)(2,1)S(1)} %bitcast.608) | data formatting | bytes 33554432
  484.5 56.9 %reshape.2325 = bf16[256,128,255]{2,1,0:T(8,128)(2,1)} reshape(bf16[256,32640]{1,0:T(8,128)(2,1)} %slice.1404) | data formatting | bytes 33423360 | tf_op jit(solution)/shard_map/reshape | solution.py:53
  543.1 41.7 %copy.191 = bf16[32,8,128,256]{3,1,2,0:T(8,128)(2,1)S(1)} copy(bf16[32,8,128,256]{3,2,1,0:T(8,128)(2,1)S(1)} %bitcast.609) | data formatting | bytes 33554432
  593.4 56.7 %reshape.2329 = bf16[256,128,255]{2,1,0:T(8,128)(2,1)} reshape(bf16[256,32640]{1,0:T(8,128)(2,1)} %slice.1409) | data formatting | bytes 33423360 | tf_op jit(solution)/shard_map/reshape | solution.py:53
  651.8 41.7 %copy.192 = bf16[32,8,128,256]{3,1,2,0:T(8,128)(2,1)S(1)} copy(bf16[32,8,128,256]{3,2,1,0:T(8,128)(2,1)S(1)} %bitcast.610) | data formatting | bytes 33554432
  702.1 56.7 %reshape.2333 = bf16[256,128,255]{2,1,0:T(8,128)(2,1)} reshape(bf16[256,32640]{1,0:T(8,128)(2,1)} %slice.1414) | data formatting | bytes 33423360 | tf_op jit(solution)/shard_map/reshape | solution.py:53
  760.5 41.7 %copy.193 = bf16[32,8,128,256]{3,1,2,0:T(8,128)(2,1)S(1)} copy(bf16[32,8,128,256]{3,2,1,0:T(8,128)(2,1)S(1)} %bitcast.611) | data formatting | bytes 33554432
  810.9 56.9 %reshape.2337 = bf16[256,128,255]{2,1,0:T(8,128)(2,1)} reshape(bf16[256,32640]{1,0:T(8,128)(2,1)} %slice.1419) | data formatting | bytes 33423360 | tf_op jit(solution)/shard_map/reshape | solution.py:53
  869.5 41.7 %copy.194 = bf16[32,8,128,256]{3,1,2,0:T(8,128)(2,1)S(1)} copy(bf16[32,8,128,256]{3,2,1,0:T(8,128)(2,1)S(1)} %bitcast.612) | data formatting | bytes 33554432
  919.9 56.7 %reshape.2341 = bf16[256,128,255]{2,1,0:T(8,128)(2,1)} reshape(bf16[256,32640]{1,0:T(8,128)(2,1)} %slice.1424) | data formatting | bytes 33423360 | tf_op jit(solution)/shard_map/reshape | solution.py:53
  978.3 41.7 %copy.195 = bf16[32,8,128,256]{3,1,2,0:T(8,128)(2,1)S(1)} copy(bf16[32,8,128,256]{3,2,1,0:T(8,128)(2,1)S(1)} %bitcast.613) | data formatting | bytes 33554432
  1028.7 57.1 %reshape.2345 = bf16[256,128,255]{2,1,0:T(8,128)(2,1)} reshape(bf16[256,32640]{1,0:T(8,128)(2,1)} %slice.1429) | data formatting | bytes 33423360 | tf_op jit(solution)/shard_map/reshape | solution.py:53
  1388.2 67.9 %reduce-scatter.9.cloned.1.call-done = f32[128,2048]{1,0:T(8,128)} async-done(((f32[1024,2048]{1,0:T(8,128)}), f32[128,2048]{1,0:T(8,128)}) %reduce-scatter.9.cloned.1.call-update) | async-done | bytes 1048592 | tf_op jit(solution)/shard_map/reduce_scatter | solution.py:147
  1456.1 75.0 %reduce-scatter.13.cloned.1.call-done = f32[128,2048]{1,0:T(8,128)} async-done(((f32[1024,2048]{1,0:T(8,128)}), f32[128,2048]{1,0:T(8,128)}) %reduce-scatter.13.cloned.1.call-update) | async-done | bytes 1048592 | tf_op jit(solution)/shard_map/reduce_scatter | solution.py:147
  1546.6 26.5 all-gather.11.cloned.1.call-done
  1584.8 27.3 all-gather.17.cloned.1.call-done
  1634.1 71.3 %reduce-scatter.17.cloned.1.call-done = f32[128,2048]{1,0:T(8,128)} async-done(((f32[1024,2048]{1,0:T(8,128)}), f32[128,2048]{1,0:T(8,128)}) %reduce-scatter.17.cloned.1.call-update) | async-done | bytes 1048592 | tf_op jit(solution)/shard_map/reduce_scatter | solution.py:189
  1710.3 35.6 all-gather.15.cloned.1.call-done
  1757.6 27.0 all-gather.21.cloned.1.call-done
  1819.6 58.3 %reduce-scatter.21.cloned.1.call-done = f32[128,2048]{1,0:T(8,128)} async-done(((f32[1024,2048]{1,0:T(8,128)}), f32[128,2048]{1,0:T(8,128)}) %reduce-scatter.21.cloned.1.call-update) | async-done | bytes 1048592 | tf_op jit(solution)/shard_map/reduce_scatter | solution.py:189
  1879.7 53.5 %reduce-scatter.11.cloned.1.call-done = bf16[128,2048]{1,0:T(8,128)(2,1)} async-done(((bf16[1024,2048]{1,0:T(8,128)(2,1)}), bf16[128,2048]{1,0:T(8,128)(2,1)}) %reduce-scatter.11.cloned.1.call-update) | async-done | bytes 524304 | tf_op jit(solution)/shard_map/reduce_scatter | solution.py:165
  1933.2 55.5 %reduce-scatter.15.cloned.1.call-done = bf16[128,2048]{1,0:T(8,128)(2,1)} async-done(((bf16[1024,2048]{1,0:T(8,128)(2,1)}), bf16[128,2048]{1,0:T(8,128)(2,1)}) %reduce-scatter.15.cloned.1.call-update) | async-done | bytes 524304 | tf_op jit(solution)/shard_map/reduce_scatter | solution.py:165
  2014.4 16.3 all-gather.19.cloned.1.call-done
  2040.8 29.0 all-gather.23.cloned.1.call-done
  2449.8 19.0 pad.169
  2468.7 33.9 reshape.2389
  2502.6 15.2 pad.170
  2517.9 14.6 copy.196
  2532.5 18.7 pad.172
  2551.2 33.4 reshape.2391
  2584.6 15.2 pad.173
  2599.8 14.7 copy.197
  2614.5 18.7 pad.190
  2633.3 33.4 reshape.2403
  2666.7 15.2 pad.191
  2681.9 14.8 copy.203
  2696.7 18.7 pad.187
  2715.4 33.5 reshape.2401
  2748.9 15.2 pad.188
  2764.1 14.6 copy.202
  2778.7 18.7 pad.184
  2797.3 33.5 reshape.2399
  2830.8 15.4 pad.185
  2846.2 14.6 copy.201
  2860.8 18.7 pad.181
  2879.5 33.4 reshape.2397
  2912.9 15.2 pad.182
  2960.3 18.7 pad.178
  2979.1 33.5 reshape.2395
  3012.5 15.2 pad.179
  3027.7 15.2 copy.199
  3162.3 18.7 pad.175
  3181.0 33.5 reshape.2393
  3214.5 15.7 pad.176
  3230.2 14.6 copy.198
  3257.5 58.5 %while.80 = (s32[]{:T(128)}, bf16[16,256]{1,0:T(8,128)(2,1)S(1)}, bf16[16,256]{1,0:T(8,128)(2,1)S(1)}, bf16[16,256]{1,0:T(8,128)(2,1)S(1)}, f32[16,256,1024]{2,1...) while((s32[]{:T(128)}, bf16[16,256]{1,0:T(8,128)(2,1)S(1)}, ...), condition=%wide.region_44.45_spmd.clone.clone, body=%wide.region_40.44_spmd.clone.clone.sunk | while | flops 3146243 | bytes 5265573 | solution.py:24
  3316.1 25.0 all-reduce.30
  3353.0 43.4 %all-reduce.29 = (f32[2048]{0:T(1024)}, f32[2048]{0:T(1024)}) all-reduce(f32[2048]{0:T(1024)S(1)} %add.641, f32[2048]{0:T(1024)S(1)} %copy-done.103), channel_id=1, replica_groups=mesh['dp'=4,'mp'=8] {'dp','mp'}, use_global_device_ids=true, to_apply=%region_20.21 | all-reduce | flops 4096 | bytes 32768 | tf_op jit(solution)/shard_map/psum | solution.py:271
  3396.4 171.1 %all-reduce.34.cloned.1.call-done = (bf16[2048,1408]{1,0:T(8,128)(2,1)}, bf16[2048,3,256]{2,0,1:T(8,128)(2,1)}, bf16[256,2048]{1,0:T(8,128)(2,1)}, bf16[704,2048]{1,0:T(8,128)(2,1)}) async-done(((bf16[2048,1408]{1,0:T(8,128)(2,1)}, bf16[2048,3,256]{2,0,1:T(8,128)(2,1)}, bf16[256,2048]{1,0:T(8,128)(2,1)}, bf16[704,2048]{1,0:T(8,128)(2,1)}), (bf16[2048,1408]{1,0:T(8,128)(2,1)}, ...) | async-done | bytes 12845072 | tf_op jit(solution)/shard_map/psum | solution.py:268
  (819 shorter events, 1374.0 us)
Async XLA Ops:
  7.2 1604.9 %copy-start = (bf16[704,2048]{1,0:T(8,128)(2,1)S(1)}, bf16[704,2048]{1,0:T(8,128)(2,1)}, u32[]{:S(2)}) copy-start(bf16[704,2048]{1,0:T(8,128)(2,1)} %param.104) | copy-start | bytes 8650756
  7.2 1078.7 %all-gather.9.cloned.1.call-start = ((), (), s32[]{:S(2)}) async-start(), calls=%async_computation.8 | async-start | bytes 4718592 | tf_op jit(solution)/shard_map/all_gather | solution.py:117
  12.4 1085.4 %all-gather.13.cloned.1.call-start = ((), (), s32[]{:S(2)}) async-start(), calls=%async_computation.12 | async-start | bytes 4718592 | tf_op jit(solution)/shard_map/all_gather | solution.py:117
  13.2 1442.9 %reduce-scatter.9.cloned.1.call-start = ((), (), s32[]{:S(2)}) async-start(), calls=%async_computation.9 | async-start | bytes 9437184 | tf_op jit(solution)/shard_map/reduce_scatter | solution.py:147
  693.5 65.3 %copy-start.86 = (bf16[256,256]{1,0:T(8,128)(2,1)S(1)}, bf16[256,256]{1,0:T(8,128)(2,1)}, u32[]{:S(2)}) copy-start(bf16[256,256]{1,0:T(8,128)(2,1)} %get-tuple-element.1061) | copy-start | bytes 393220
  802.3 65.5 %copy-start.85 = (bf16[256,256]{1,0:T(8,128)(2,1)S(1)}, bf16[256,256]{1,0:T(8,128)(2,1)}, u32[]{:S(2)}) copy-start(bf16[256,256]{1,0:T(8,128)(2,1)} %get-tuple-element.1060) | copy-start | bytes 393220
  911.2 65.4 %copy-start.84 = (bf16[256,256]{1,0:T(8,128)(2,1)S(1)}, bf16[256,256]{1,0:T(8,128)(2,1)}, u32[]{:S(2)}) copy-start(bf16[256,256]{1,0:T(8,128)(2,1)} %get-tuple-element.1059) | copy-start | bytes 393220
  1028.7 57.2 %copy-start.108 = (f32[3,3,256]{2,1,0:T(4,128)S(1)}, f32[3,3,256]{2,1,0:T(4,128)}, u32[]{:S(2)}) copy-start(f32[3,3,256]{2,1,0:T(4,128)} %param.95) | copy-start | bytes 27652
  1085.9 24.0 copy-start.95
  1085.9 24.0 copy-start.97
  1085.9 24.0 copy-start.99
  1143.3 86.2 %copy-start.72 = (bf16[2,128,256]{1,0,2:T(2,128)(2,1)}, bf16[2,128,256]{1,0,2:T(2,128)(2,1)S(1)}, u32[]{:S(2)}) copy-start(bf16[2,128,256]{1,0,2:T(2,128)(2,1)S(1)} %copy.183) | copy-start | bytes 393220
  1266.0 17.0 copy-start.22
  1293.4 16.9 copy-start.26
  1311.4 21.4 copy-start.58
  1314.4 33.6 copy-start.74
  1356.5 15.0 copy-start.101
  1382.1 149.0 %reduce-scatter.13.cloned.1.call-start = ((), (), s32[]{:S(2)}) async-start(), calls=%async_computation.13 | async-start | bytes 9437184 | tf_op jit(solution)/shard_map/reduce_scatter | solution.py:147
  1388.1 147.1 %copy-start.93 = (f32[2048]{0:T(1024)S(1)}, f32[2048]{0:T(1024)}, u32[]{:S(2)}) copy-start(f32[2048]{0:T(1024)} %param.101) | copy-start | bytes 24580
  1388.1 148.3 %copy-start.119 = (s32[2,1]{0,1:T(1,128)S(1)}, s32[2,1]{0,1:T(1,128)}, u32[]{:S(2)}) copy-start(s32[2,1]{0,1:T(1,128)} %param.92) | copy-start | bytes 28
  1388.1 184.9 %all-gather.11.cloned.1.call-start = ((), (), s32[]{:S(2)}) async-start(), calls=%async_computation.10 | async-start | bytes 4718592 | tf_op jit(solution)/shard_map/all_gather | solution.py:156
  1536.2 75.9 %all-gather.17.cloned.1.call-start = ((), (), s32[]{:S(2)}) async-start(), calls=%async_computation.16 | async-start | bytes 4718592 | tf_op jit(solution)/shard_map/all_gather | solution.py:180
  1540.8 164.7 %reduce-scatter.17.cloned.1.call-start = ((), (), s32[]{:S(2)}) async-start(), calls=%async_computation.17 | async-start | bytes 9437184 | tf_op jit(solution)/shard_map/reduce_scatter | solution.py:189
  1634.0 111.9 %all-gather.15.cloned.1.call-start = ((), (), s32[]{:S(2)}) async-start(), calls=%async_computation.14 | async-start | bytes 4718592 | tf_op jit(solution)/shard_map/all_gather | solution.py:156
  1709.0 75.7 %all-gather.21.cloned.1.call-start = ((), (), s32[]{:S(2)}) async-start(), calls=%async_computation.20 | async-start | bytes 4718592 | tf_op jit(solution)/shard_map/all_gather | solution.py:180
  1709.8 168.2 %reduce-scatter.21.cloned.1.call-start = ((), (), s32[]{:S(2)}) async-start(), calls=%async_computation.21 | async-start | bytes 9437184 | tf_op jit(solution)/shard_map/reduce_scatter | solution.py:189
  1806.5 126.7 %reduce-scatter.11.cloned.1.call-start = ((), (), s32[]{:S(2)}) async-start(), calls=%async_computation.11 | async-start | bytes 4718592 | tf_op jit(solution)/shard_map/reduce_scatter | solution.py:165
  1812.9 175.8 %reduce-scatter.15.cloned.1.call-start = ((), (), s32[]{:S(2)}) async-start(), calls=%async_computation.15 | async-start | bytes 4718592 | tf_op jit(solution)/shard_map/reduce_scatter | solution.py:165
  1819.3 169.4 %copy-start.12 = (f32[128,2048]{1,0:T(8,128)S(1)}, f32[128,2048]{1,0:T(8,128)}, u32[]{:S(2)}) copy-start(f32[128,2048]{1,0:T(8,128)} %copy-done.11) | copy-start | bytes 3145732
  1819.3 169.4 %copy-start.13 = (f32[128,2048]{1,0:T(8,128)S(1)}, f32[128,2048]{1,0:T(8,128)}, u32[]{:S(2)}) copy-start(f32[128,2048]{1,0:T(8,128)} %get-tuple-element.1050) | copy-start | bytes 3145732
  1819.4 211.3 %all-gather.19.cloned.1.call-start = ((), (), s32[]{:S(2)}) async-start(), calls=%async_computation.18 | async-start | bytes 4718592 | tf_op jit(solution)/shard_map/all_gather | solution.py:196
  1879.7 114.7 %copy-start.88 = (f32[256,128]{0,1:T(8,128)S(1)}, f32[256,128]{0,1:T(8,128)}, u32[]{:S(2)}) copy-start(f32[256,128]{0,1:T(8,128)} %get-tuple-element.1057) | copy-start | bytes 393220
  1879.7 115.5 %copy-start.87 = (f32[256,128]{0,1:T(8,128)S(1)}, f32[256,128]{0,1:T(8,128)}, u32[]{:S(2)}) copy-start(f32[256,128]{0,1:T(8,128)} %get-tuple-element.1053) | copy-start | bytes 393220
  1993.8 76.0 %all-gather.23.cloned.1.call-start = ((), (), s32[]{:S(2)}) async-start(), calls=%async_computation.22 | async-start | bytes 4718592 | tf_op jit(solution)/shard_map/all_gather | solution.py:196
  1994.4 1349.6 %reduce-scatter.19.cloned.1.call-start = ((), (), s32[]{:S(2)}) async-start(), calls=%async_computation.19 | async-start | bytes 9437184 | tf_op jit(solution)/shard_map/reduce_scatter | solution.py:244
  2004.5 26.2 copy-start.10
  2004.5 26.2 copy-start.45
  2128.3 17.4 copy-start.60
  2130.6 26.3 copy-start.76
  2216.9 18.1 copy-start.62
  2218.1 16.9 copy-start.55
  2219.3 28.7 copy-start.77
  2291.5 1052.5 %reduce-scatter.23.cloned.1.call-start = ((), (), s32[]{:S(2)}) async-start(), calls=%async_computation.23 | async-start | bytes 9437184 | tf_op jit(solution)/shard_map/reduce_scatter | solution.py:244
  2364.5 26.2 slice-start.16
  2364.5 26.2 slice-start.17
  2420.5 1146.9 %all-reduce.34.cloned.1.call-start = ((), (), s32[]{:S(2)}) async-start(), calls=%async_computation.24 | async-start | bytes 25690112 | tf_op jit(solution)/shard_map/psum | solution.py:268
  3027.7 15.2 copy-start.50
  3048.8 28.4 slice-start
  3048.8 28.4 slice-start.1
  3048.8 28.4 slice-start.2
  3048.8 28.4 slice-start.3
  3062.8 14.9 slice-start.6
  3062.9 16.0 slice-start.7
  3083.0 28.4 slice-start.8
  3083.0 28.4 slice-start.9
  3083.0 28.4 slice-start.10
  3083.0 28.4 slice-start.11
  3097.1 16.0 slice-start.15
  3257.5 86.6 %copy-start.8 = (bf16[2,128,1,2048]{3,1,2,0:T(8,128)(2,1)S(1)}, bf16[2,128,1,2048]{3,1,2,0:T(8,128)(2,1)}, u32[]{:S(2)}) copy-start(bf16[2,128,1,2048]{3,1,2,0:T(8,128)(2,1)} %param.91) | copy-start | bytes 3145732
  3257.5 86.6 %copy-start.94 = (f32[2048]{0:T(1024)S(1)}, f32[2048]{0:T(1024)}, u32[]{:S(2)}) copy-start(f32[2048]{0:T(1024)} %param.93) | copy-start | bytes 24580
  3257.5 86.6 %copy-start.110 = (f32[128]{0:T(128)S(1)}, f32[128]{0:T(128)}, u32[]{:S(2)}) copy-start(f32[128]{0:T(128)} %copy-done.109) | copy-start | bytes 1540
  3257.5 86.6 %copy-start.112 = (f32[128]{0:T(128)S(1)}, f32[128]{0:T(128)}, u32[]{:S(2)}) copy-start(f32[128]{0:T(128)} %copy-done.111) | copy-start | bytes 1540
  3257.5 88.8 %copy-start.116 = (f32[128]{0:T(128)S(1)}, f32[128]{0:T(128)}, u32[]{:S(2)}) copy-start(f32[128]{0:T(128)} %copy-done.115) | copy-start | bytes 1540
  3257.5 88.8 %copy-start.118 = (f32[128]{0:T(128)S(1)}, f32[128]{0:T(128)}, u32[]{:S(2)}) copy-start(f32[128]{0:T(128)} %copy-done.117) | copy-start | bytes 1540
  (108 other events, 853.7 us)
Sparse Core Ops, SparseCore 0:
  12.5 39.4 all-gather.8
  54.5 36.7 all-gather.12
  1382.2 73.8 reduce-scatter.8
  1459.8 71.2 reduce-scatter.12
  1536.3 36.6 all-gather.10
  1575.4 36.7 all-gather.16
  1634.2 71.2 reduce-scatter.16
  1709.1 36.6 all-gather.14
  1747.9 36.7 all-gather.20
  1806.6 71.2 reduce-scatter.20
  1881.9 51.3 reduce-scatter.10
  1937.4 51.3 reduce-scatter.14
  1993.9 36.7 all-gather.18
  2033.0 36.7 all-gather.22
  2291.6 71.2 reduce-scatter.18
  2420.6 71.2 reduce-scatter.22
  3129.1 438.3 all-reduce.33
where the time goes:
time: 3630 us; the launch traced here: 3610 us
  local copies, waits for them, and re-layouts  1850 us (51%)
  waiting for transfers between devices  717 us (20%)
  matrix products  550 us (15%)
  other arithmetic  406 us (11%)
  blocking collectives  68.4 us (2%)
    unnamed x331, local copies, waits for them, and re-layouts  494 us
    reshape x8, local copies, waits for them, and re-layouts, lag_table(): return window.reshape(chans, block_len, 2 * block_len - 1)[:, :, :block_len]  455 us
    reshape x8, local copies, waits for them, and re-layouts, lag_fold(): flat_rows = wide.reshape(chans, block_len * (2 * block_len - 1))  268 us
    psum x1, waiting for transfers between devices, local(): lax.psum(grad_both.astype(jnp.bfloat16), 'dp').astype(jnp.float32)  171 us
    pad x8, local copies, waits for them, and re-layouts, lag_fold(): wide = jnp.pad(grad_table, ((0, 0), (0, 0), (0, block_len - 1)))  150 us
    reduce_scatter x2, waiting for transfers between devices, local(): lax.psum_scatter(jnp.dot(gated_low, out_proj, preferred_element_type=jnp....  143 us
    dot_general x16, matrix products, local(): jnp.einsum('cab,nbsc->nasc', lag_tables[offset], mixed_blocks[:nblocks -...  139 us
    dot_general x14, matrix products, local(): jnp.einsum('nasc,nbsc->cab', grad_conv_blocks[offset:], mixed_blocks[:nbl...  130 us
  transfers between devices with their start and end apart: 17, of which 13 were waited for; matrix products, arithmetic and copies ran while one was open for 61% of the time, Pallas kernels for 0%

commit v1 on v0

v1 whole, which is shorter than its diff:
```python
from functools import partial

import jax
import jax.numpy as jnp
import numpy as np
from jax import lax
from jax.experimental import pallas as pl
from jax.experimental.pallas import tpu as pltpu
from jax.sharding import PartitionSpec as P

epsilon = 1e-06
bf16 = jnp.bfloat16
f32 = jnp.float32
STEP = 32
VMEM_LIMIT = 52 * 1024 * 1024


def dft_matrix(length):
    freqs = np.arange(length)[:, None]
    times = np.arange(length)[None, :]
    angle = np.pi * (((2 * freqs + 1) * times) % (4 * length)) / (2 * length)
    return np.concatenate([np.cos(angle), -np.sin(angle)], axis=0)


def dot32(left, right):
    return jnp.dot(left, right, preferred_element_type=f32)


def contract_rows(left, right):
    return lax.dot_general(left, right, (((0,), (0,)), ((), ())), preferred_element_type=f32)


def contract_cols(left, right):
    return lax.dot_general(left, right, (((1,), (1,)), ((), ())), preferred_element_type=f32)


def row_scale(rows_in):
    return lax.rsqrt(jnp.mean(rows_in * rows_in, axis=-1, keepdims=True) + epsilon)


def norm_back(grad_y, rows_in, scale, gain):
    weighted = gain * grad_y
    inner = jnp.mean(weighted * rows_in, axis=-1, keepdims=True)
    return scale * weighted - rows_in * (scale * scale * scale) * inner


def filter_kernel(hre_ref, him_ref, lre_ref, lim_ref, res_ref, dft_ref, spec_ref, filt_ref):
    blocks, poles, chans = hre_ref.shape
    step = lre_ref.shape[1]
    residue = res_ref[...]

    def fill(block, carry):
        pre = residue * hre_ref[block]
        pim = residue * him_ref[block]
        total = jnp.zeros((step, chans), f32)
        for pole in range(poles):
            total = total + (
                pre[pole : pole + 1] * lre_ref[pole] - pim[pole : pole + 1] * lim_ref[pole]
            )
        filt_ref[pl.ds(pl.multiple_of(block * step, step), step), :] = total.astype(bf16)
        return carry

    lax.fori_loop(0, blocks, fill, 0)
    spec_ref[...] = dot32(dft_ref[...], filt_ref[...])


def pole_kernel(grad_ref, hre_ref, him_ref, lre_ref, lim_ref, sum_ref, vre_ref, vim_ref, turned):
    blocks, poles, chans = hre_ref.shape
    step = lre_ref.shape[1]
    for late in range(step):
        turned[late] = grad_ref[pl.ds(late, blocks, stride=step), :]
    starts = step * lax.broadcasted_iota(jnp.int32, (blocks, chans), 0).astype(f32)

    for pole in range(poles):
        lre, lim = lre_ref[pole], lim_ref[pole]
        part = turned[step - 1]
        sre = part * lre[step - 1 : step]
        sim = part * lim[step - 1 : step]
        tre, tim = sre, sim
        for late in range(step - 2, -1, -1):
            part = turned[late]
            sre = sre + part * lre[late : late + 1]
            sim = sim + part * lim[late : late + 1]
            if late:
                tre = tre + sre
                tim = tim + sim
        hre = hre_ref[:, pole, :]
        him = him_ref[:, pole, :]
        wre = starts * sre + tre
        wim = starts * sim + tim
        sum_ref[pole : pole + 1, :] = jnp.sum(hre * sre - him * sim, axis=0, keepdims=True)
        vre_ref[pole : pole + 1, :] = jnp.sum(hre * wre - him * wim, axis=0, keepdims=True)
        vim_ref[pole : pole + 1, :] = jnp.sum(hre * wim + him * wre, axis=0, keepdims=True)


def load_padded(me, parts, pad):
    blocks, _, rows, _ = parts[0].shape
    for index, part in enumerate(parts):
        pad[index, 0:8, :] = jnp.zeros((8, pad.shape[2]), f32)
        for block in range(blocks):
            pad[index, 8 + block * rows : 8 + (block + 1) * rows, :] = part[me ^ block, 0].astype(f32)


def short_rows(pad, taps, index, start, count):
    total = taps[index : index + 1] * pad[index, 8 + start : 8 + start + count, :]
    for back in (1, 2):
        tap = taps[3 * back + index : 3 * back + index + 1]
        total = total + tap * pad[index, 8 + start - back : 8 + start - back + count, :]
    return total


def mixer_kernel(
    me_ref, q_ref, k_ref, v_ref, taps_ref, skip_ref, filt_ref, dft_ref, inv_ref,
    gated_ref, resp_ref, spec_ref, pad, mixed, product, conv,
):
    me = me_ref[0]
    blocks, _, rows, chans = q_ref.shape
    length = blocks * rows
    load_padded(me, (q_ref, k_ref, v_ref), pad)
    taps = taps_ref[...]
    skip = skip_ref[...]
    for block in range(blocks):
        start = block * rows
        key = short_rows(pad, taps, 1, start, rows)
        value = short_rows(pad, taps, 2, start, rows)
        mixed[start : start + rows, :] = (key * value).astype(bf16)
    spec_ref[0] = dot32(dft_ref[...], mixed[...])
    for block in range(blocks):
        re = slice(block * rows, (block + 1) * rows)
        im = slice(length + block * rows, length + (block + 1) * rows)
        mre, mim = spec_ref[0, re, :], spec_ref[0, im, :]
        hre, him = filt_ref[re, :], filt_ref[im, :]
        product[re, :] = (mre * hre - mim * him).astype(bf16)
        product[im, :] = (mre * him + mim * hre).astype(bf16)
    conv[...] = dot32(inv_ref[...], product[...])
    for block in range(blocks):
        start = block * rows
        response = conv[start : start + rows, :] + skip * mixed[start : start + rows, :].astype(f32)
        resp_ref[0, start : start + rows, :] = response
        query = short_rows(pad, taps, 0, start, rows)
        gated_ref[me ^ block, 0] = (query * response).astype(bf16)


def mixer_back_kernel(
    me_ref, gg_ref, q_ref, k_ref, v_ref, resp_ref, spec_ref, taps_ref, skip_ref, filt_ref, dft_ref, inv_ref,
    gproj_ref, gtaps_ref, gskip_ref, gfilt_ref, pad, late, response_grad, grad_conv, spectrum, product, lags, conv,
):
    me = me_ref[0]
    sequence = pl.program_id(0)
    blocks, _, rows, chans = q_ref.shape
    length = blocks * rows
    load_padded(me, (q_ref, k_ref, v_ref), pad)
    taps = taps_ref[...]
    skip = skip_ref[...]

    @pl.when(sequence == 0)
    def _():
        gtaps_ref[...] = jnp.zeros_like(gtaps_ref)
        gskip_ref[...] = jnp.zeros_like(gskip_ref)
        lags[...] = jnp.zeros_like(lags)

    late[:, length : length + 8, :] = jnp.zeros((3, 8, chans), f32)
    skip_sum = jnp.zeros((1, chans), f32)
    for block in range(blocks):
        start = block * rows
        at = slice(start, start + rows)
        incoming = gg_ref[me ^ block, 0].astype(f32)
        query = short_rows(pad, taps, 0, start, rows)
        key = short_rows(pad, taps, 1, start, rows)
        value = short_rows(pad, taps, 2, start, rows)
        mixed = (key * value).astype(bf16).astype(f32)
        grad = incoming * query
        response_grad[at, :] = grad
        grad_conv[at, :] = grad.astype(bf16)
        late[0, at, :] = incoming * resp_ref[0, at, :]
        skip_sum = skip_sum + jnp.sum(grad * mixed, axis=0, keepdims=True)
    gskip_ref[...] += skip_sum

    spectrum[...] = dot32(dft_ref[...], grad_conv[...])
    for block in range(blocks):
        re = slice(block * rows, (block + 1) * rows)
        im = slice(length + block * rows, length + (block + 1) * rows)
        gre, gim = spectrum[re, :], spectrum[im, :]
        hre, him = filt_ref[re, :], filt_ref[im, :]
        mre, mim = spec_ref[0, re, :], spec_ref[0, im, :]
        product[re, :] = (gre * hre + gim * him).astype(bf16)
        product[im, :] = (gim * hre - gre * him).astype(bf16)
        lags[re, :] += gre * mre + gim * mim
        lags[im, :] += gim * mre - gre * mim
    conv[...] = dot32(inv_ref[...], product[...])

    for block in range(blocks):
        start = block * rows
        at = slice(start, start + rows)
        key = short_rows(pad, taps, 1, start, rows)
        value = short_rows(pad, taps, 2, start, rows)
        grad_mixed = conv[at, :] + skip * response_grad[at, :]
        late[1, at, :] = grad_mixed * value
        late[2, at, :] = grad_mixed * key

    sums = [jnp.zeros((1, chans), f32) for _ in range(9)]
    for block in range(blocks):
        start = block * rows
        for index in range(3):
            grad = late[index, start : start + rows, :]
            total = taps[index : index + 1] * grad
            for back in (1, 2):
                tap = taps[3 * back + index : 3 * back + index + 1]
                total = total + tap * late[index, start + back : start + back + rows, :]
            gproj_ref[me ^ block, 0, :, index * chans : (index + 1) * chans] = total.astype(bf16)
            for back in range(3):
                shifted = pad[index, 8 + start - back : 8 + start - back + rows, :]
                sums[3 * back + index] = sums[3 * back + index] + jnp.sum(
                    grad * shifted, axis=0, keepdims=True
                )
    for index in range(9):
        gtaps_ref[index : index + 1, :] += sums[index]

    @pl.when(sequence == pl.num_programs(0) - 1)
    def _():
        product[...] = lags[...].astype(bf16)
        gfilt_ref[...] = dot32(inv_ref[...], product[...])


def whole(shape):
    return pl.BlockSpec(shape, lambda *_: (0,) * len(shape), pipeline_mode=pl.Buffered(1))


def params():
    return pltpu.CompilerParams(vmem_limit_bytes=VMEM_LIMIT)


def make_filter(tables, residue_t, dft):
    hre, him, lre, lim = tables
    chans = residue_t.shape[1]
    length = dft.shape[1]
    operands = (hre, him, lre, lim, residue_t, dft)
    return pl.pallas_call(
        filter_kernel,
        grid=(1,),
        in_specs=[whole(op.shape) for op in operands],
        out_specs=whole((2 * length, chans)),
        out_shape=jax.ShapeDtypeStruct((2 * length, chans), f32),
        scratch_shapes=[pltpu.VMEM((length, chans), bf16)],
        compiler_params=params(),
        name="modal_filter",
    )(*operands)


def pole_gradients(grad_filt, tables):
    hre, him, lre, lim = tables
    blocks, poles, chans = hre.shape
    step = lre.shape[1]
    lanes = min(chans, 128)

    def lane_block(*lead):
        return pl.BlockSpec(lead + (lanes,), lambda c: (0,) * len(lead) + (c,))

    operands = (grad_filt, hre, him, lre, lim)
    return pl.pallas_call(
        pole_kernel,
        grid=(chans // lanes,),
        in_specs=[lane_block(*op.shape[:-1]) for op in operands],
        out_specs=[lane_block(poles)] * 3,
        out_shape=[jax.ShapeDtypeStruct((poles, chans), f32)] * 3,
        scratch_shapes=[pltpu.VMEM((step, blocks, lanes), f32)],
        compiler_params=params(),
        name="pole_gradients",
    )(*operands)


def mixer(me, proj, taps9, skip, filt_spec, dft, inverse):
    blocks, seqs, rows, triple = proj.shape
    chans = triple // 3
    length = blocks * rows

    def part(index):
        return pl.BlockSpec((blocks, 1, rows, chans), lambda s, m: (0, s, 0, index))

    return pl.pallas_call(
        mixer_kernel,
        grid_spec=pltpu.PrefetchScalarGridSpec(
            num_scalar_prefetch=1,
            grid=(seqs,),
            in_specs=[part(0), part(1), part(2), whole(taps9.shape), whole(skip.shape),
                      whole(filt_spec.shape), whole(dft.shape), whole(inverse.shape)],
            out_specs=[
                pl.BlockSpec((blocks, 1, rows, chans), lambda s, m: (0, s, 0, 0)),
                pl.BlockSpec((1, length, chans), lambda s, m: (s, 0, 0)),
                pl.BlockSpec((1, 2 * length, chans), lambda s, m: (s, 0, 0)),
            ],
            scratch_shapes=[
                pltpu.VMEM((3, length + 8, chans), f32),
                pltpu.VMEM((length, chans), bf16),
                pltpu.VMEM((2 * length, chans), bf16),
                pltpu.VMEM((length, chans), f32),
            ],
        ),
        out_shape=[
            jax.ShapeDtypeStruct((blocks, seqs, rows, chans), bf16),
            jax.ShapeDtypeStruct((seqs, length, chans), f32),
            jax.ShapeDtypeStruct((seqs, 2 * length, chans), f32),
        ],
        compiler_params=params(),
        name="mixer_forward",
    )(me, proj, proj, proj, taps9, skip, filt_spec, dft, inverse)


def mixer_back(me, grad_gated, proj, response, spec, taps9, skip, filt_spec, dft, inverse):
    blocks, seqs, rows, triple = proj.shape
    chans = triple // 3
    length = blocks * rows

    def part(index):
        return pl.BlockSpec((blocks, 1, rows, chans), lambda s, m: (0, s, 0, index))

    return pl.pallas_call(
        mixer_back_kernel,
        grid_spec=pltpu.PrefetchScalarGridSpec(
            num_scalar_prefetch=1,
            grid=(seqs,),
            in_specs=[part(0), part(0), part(1), part(2),
                      pl.BlockSpec((1, length, chans), lambda s, m: (s, 0, 0)),
                      pl.BlockSpec((1, 2 * length, chans), lambda s, m: (s, 0, 0)),
                      whole(taps9.shape), whole(skip.shape),
                      whole(filt_spec.shape), whole(dft.shape), whole(inverse.shape)],
            out_specs=[
                pl.BlockSpec((blocks, 1, rows, triple), lambda s, m: (0, s, 0, 0)),
                whole(taps9.shape),
                whole(skip.shape),
                whole((length, chans)),
            ],
            scratch_shapes=[
                pltpu.VMEM((3, length + 8, chans), f32),
                pltpu.VMEM((3, length + 8, chans), f32),
                pltpu.VMEM((length, chans), f32),
                pltpu.VMEM((length, chans), bf16),
                pltpu.VMEM((2 * length, chans), f32),
                pltpu.VMEM((2 * length, chans), bf16),
                pltpu.VMEM((2 * length, chans), f32),
                pltpu.VMEM((length, chans), f32),
            ],
        ),
        out_shape=[
            jax.ShapeDtypeStruct((blocks, seqs, rows, triple), bf16),
            jax.ShapeDtypeStruct(taps9.shape, f32),
            jax.ShapeDtypeStruct(skip.shape, f32),
            jax.ShapeDtypeStruct((length, chans), f32),
        ],
        compiler_params=params(),
        name="mixer_backward",
    )(me, grad_gated, proj, proj, proj, response, spec, taps9, skip, filt_spec, dft, inverse)


class Plain:
    def __init__(self, size):
        self.size = size

    def origin(self):
        return jnp.zeros((1,), jnp.int32)

    def gather(self, block):
        return [lax.all_gather(block, "mp", axis=0)]

    def scatter(self, groups):
        (partial_sums,) = groups
        return lax.psum_scatter(partial_sums.astype(bf16), "mp", scatter_dimension=0).astype(f32)


class Square:
    def __init__(self):
        self.size = 8

    def origin(self):
        return lax.axis_index("mp").astype(jnp.int32).reshape(1)

    def swap(self, block, bit):
        return lax.ppermute(block, "mp", [(i, i ^ bit) for i in range(8)])

    def gather(self, block):
        half = block.shape[0] // 2
        low, high = block[:half], block[half:]
        x_low, y_high = self.swap(low, 2), self.swap(high, 4)
        sibling = self.swap(block, 1)
        x_high, y_low = self.swap(high, 2), self.swap(low, 4)
        d_low, d_high = self.swap(x_low, 4), self.swap(y_high, 2)
        x_all = jnp.concatenate([x_low, x_high], axis=0)
        y_all = jnp.concatenate([y_low, y_high], axis=0)
        d_all = jnp.concatenate([d_low, d_high], axis=0)
        near = jnp.stack([block, sibling], axis=0)
        side = jnp.stack([x_all, self.swap(x_all, 1), y_all, self.swap(y_all, 1)], axis=0)
        far = jnp.stack([d_all, self.swap(d_all, 1)], axis=0)
        return [near, side, far]

    def scatter(self, groups):
        near, side, far = groups
        half = near.shape[1] // 2

        def both(mine, other):
            return mine.astype(f32) + self.swap(other, 1).astype(f32)

        far_sum = both(far[0], far[1])
        far_low, far_high = far_sum[:half].astype(bf16), far_sum[half:].astype(bf16)
        from_far_low, from_far_high = self.swap(far_low, 2), self.swap(far_high, 4)
        x_sum = both(side[0], side[1])
        y_sum = both(side[2], side[3])
        own_low_x = self.swap(x_sum[:half].astype(bf16), 2)
        own_high_y = self.swap(y_sum[half:].astype(bf16), 4)
        y_low = (y_sum[:half] + from_far_low.astype(f32)).astype(bf16)
        x_high = (x_sum[half:] + from_far_high.astype(f32)).astype(bf16)
        own_low_y = self.swap(y_low, 4)
        own_high_x = self.swap(x_high, 2)
        own = both(near[0], near[1])
        low = own[:half] + own_low_x.astype(f32) + own_low_y.astype(f32)
        high = own[half:] + own_high_y.astype(f32) + own_high_x.astype(f32)
        return jnp.concatenate([low, high], axis=0)


def local(
    links, tokens, lengths, norm_gain, in_proj, short_taps, conv_skip, filter_residue, filter_rate, filter_freq,
    out_proj, mlp_gain, gate_proj, up_proj, down_proj, cotangent,
):
    micro, rows, per_dev, width = tokens.shape
    seqs = micro * per_dev
    chans = in_proj.shape[2]
    hidden_units = gate_proj.shape[1]
    length = rows * links.size
    in_flat = in_proj.reshape(width, 3 * chans)
    table = dft_matrix(length)
    dft = jnp.asarray(table, bf16)
    inverse = jnp.asarray(table.T / length, bf16)
    me = links.origin()

    def by_sequence(array):
        return array.transpose(0, 2, 1, 3).reshape(seqs, rows, array.shape[3])

    def by_position(array):
        return array.reshape(micro, per_dev, rows, array.shape[2]).transpose(0, 2, 1, 3)

    def flat(array):
        return array.reshape(-1, array.shape[-1])

    def grouped(array, like):
        return array.reshape(like.shape[:-1] + (array.shape[-1],))

    positions = lax.axis_index("mp") * rows + jnp.arange(rows)
    valid = (positions[None, :] < lengths.reshape(seqs)[:, None]).astype(f32)[:, :, None]

    rows_in = by_sequence(tokens).astype(f32)
    scale_in = row_scale(rows_in)
    normed = (rows_in * scale_in * norm_gain).astype(bf16)
    normed_groups = links.gather(normed)
    grad_final = by_sequence(cotangent).astype(f32) * valid
    grad_final_all = flat(jnp.concatenate(links.gather(grad_final.astype(bf16)), axis=0))

    high = (STEP * jnp.arange(length // STEP)).astype(f32)[:, None, None]
    low = jnp.arange(STEP).astype(f32)[None, :, None]
    rate_t, freq_t, residue_t = filter_rate.T, filter_freq.T, filter_residue.T
    decay_high, turn_high = jnp.exp(-rate_t * high), freq_t * high
    decay_low, turn_low = jnp.exp(-rate_t[:, None, :] * low), freq_t[:, None, :] * low
    tables = (
        decay_high * jnp.cos(turn_high),
        decay_high * jnp.sin(turn_high),
        decay_low * jnp.cos(turn_low),
        decay_low * jnp.sin(turn_low),
    )
    filt_spec = make_filter(tables, residue_t, dft)

    proj = jnp.concatenate(
        [grouped(dot32(flat(group), in_flat), group) for group in normed_groups], axis=0
    )
    taps9 = short_taps.reshape(9, chans)
    skip = conv_skip.reshape(1, chans)
    gated, response, spec = mixer(me, proj, taps9, skip, filt_spec, dft, inverse)

    counts = [group.shape[0] for group in normed_groups]
    starts = [sum(counts[:i]) for i in range(len(counts))]

    def product_groups(left, right, dot):
        out = [None] * len(counts)
        for i in reversed(range(len(counts))):
            part = left[starts[i] : starts[i] + counts[i]]
            out[i] = grouped(dot(flat(part), right).astype(bf16), part)
        return out

    second = rows_in + links.scatter(product_groups(gated, out_proj, dot32))
    scale_second = row_scale(second)
    mlp_normed = (second * scale_second * mlp_gain).astype(bf16)
    mlp_groups = links.gather(mlp_normed)
    gate = jnp.concatenate([dot32(flat(group), gate_proj) for group in mlp_groups], axis=0)
    up = jnp.concatenate([dot32(flat(group), up_proj) for group in mlp_groups], axis=0)
    sig = jax.nn.sigmoid(gate)
    silu = gate * sig
    hidden = (silu * up).astype(bf16)

    grad_hidden = contract_cols(grad_final_all, down_proj)
    grad_gate = (grad_hidden * up * sig * (1.0 + gate * (1.0 - sig))).astype(bf16)
    grad_up = (grad_hidden * silu).astype(bf16)
    mlp_all = flat(jnp.concatenate(mlp_groups, axis=0))
    grad_down = contract_rows(hidden, grad_final_all).astype(bf16)
    grad_gate_proj = contract_rows(mlp_all, grad_gate)
    grad_up_proj = contract_rows(mlp_all, grad_up)

    chain = [None]

    def over_dp(*arrays):
        if chain[0] is not None:
            arrays = lax.optimization_barrier((arrays, chain[0]))[0]
        summed = lax.psum(arrays, "dp")
        chain[0] = summed
        return summed

    (sum_down,) = over_dp(grad_down)
    sum_gate, sum_up = over_dp(grad_gate_proj.astype(bf16), grad_up_proj.astype(bf16))

    shape4 = gated.shape[:3]
    grad_gate4 = grad_gate.reshape(shape4 + (hidden_units,))
    grad_up4 = grad_up.reshape(shape4 + (hidden_units,))
    partial_groups = []
    for start, count in zip(starts, counts):
        gate_rows = flat(grad_gate4[start : start + count])
        up_rows = flat(grad_up4[start : start + count])
        both = contract_cols(gate_rows, gate_proj) + contract_cols(up_rows, up_proj)
        partial_groups.append(both.astype(bf16).reshape((count,) + shape4[1:] + (width,)))
    grad_mlp_normed = links.scatter(partial_groups)
    grad_second = grad_final + norm_back(grad_mlp_normed, second, scale_second, mlp_gain)
    gain_two = jnp.sum(grad_mlp_normed * second * scale_second, axis=(0, 1))

    grad_branch_groups = links.gather(grad_second.astype(bf16))
    grad_gated = jnp.concatenate(
        [grouped(contract_cols(flat(group), out_proj), group) for group in grad_branch_groups], axis=0
    )
    mlp_out = links.scatter(product_groups(hidden.reshape(shape4 + (hidden_units,)), down_proj, dot32))
    layer_out = ((second + mlp_out) * valid).astype(bf16)

    grad_branch_all = flat(jnp.concatenate(grad_branch_groups, axis=0))
    grad_out = contract_rows(flat(gated), grad_branch_all)
    (sum_out,) = over_dp(grad_out.astype(bf16))
    grad_proj, grad_taps, grad_skip, grad_filt = mixer_back(
        me, grad_gated, proj, response, spec, taps9, skip, filt_spec, dft, inverse
    )
    grad_normed = links.scatter(product_groups(grad_proj, in_flat, contract_cols))
    normed_all = flat(jnp.concatenate(normed_groups, axis=0))
    grad_in = contract_rows(normed_all, flat(grad_proj))
    pole_sum, pole_re, pole_im = pole_gradients(grad_filt, tables)
    grad_tokens = grad_second + norm_back(grad_normed, rows_in, scale_in, norm_gain)
    gain_one = jnp.sum(grad_normed * rows_in * scale_in, axis=(0, 1))

    small = jnp.concatenate(
        [grad_taps, grad_skip, pole_sum, -residue_t * pole_re, -residue_t * pole_im], axis=0
    )
    sum_in, sum_small = over_dp(grad_in.astype(bf16), small.astype(bf16))
    sum_in, sum_small = sum_in.astype(f32), sum_small.astype(f32)
    gains = lax.psum((gain_one, gain_two), ("dp", "mp"))
    poles = filter_residue.shape[1]
    pole_grads = [
        sum_small[10 + poles * i : 10 + poles * (i + 1)].T for i in range(3)
    ]
    return (
        by_position(layer_out),
        by_position(grad_tokens),
        gains[0],
        sum_in.reshape(width, 3, chans),
        sum_small[:9].reshape(3, 3, chans),
        sum_small[9],
        pole_grads[0],
        pole_grads[1],
        pole_grads[2],
        sum_out.astype(f32),
        gains[1],
        sum_gate.astype(f32),
        sum_up.astype(f32),
        sum_down.astype(f32),
    )


def solution(mesh):
    links = Square() if mesh.shape["mp"] == 8 else Plain(mesh.shape["mp"])
    wide = P(None, "mp", "dp", None)
    chan = P("mp", None)
    return jax.shard_map(
        partial(local, links),
        mesh=mesh,
        in_specs=(
            wide, P(None, "dp"), P(), P(None, None, "mp"), P(None, None, "mp"), P("mp"), chan, chan, chan,
            chan, P(), P(None, "mp"), P(None, "mp"), chan, wide,
        ),
        out_specs=(
            wide, wide, P(), P(None, None, "mp"), P(None, None, "mp"), P("mp"), chan, chan, chan,
            chan, P(), P(None, "mp"), P(None, "mp"), chan,
        ),
        check_vma=False,
    )
```

time: 3630 us -> 860 us (0.24)
  local copies, waits for them, and re-layouts: 1850 us -> 99.4 us
  matrix products: 550 us -> 135 us
  waiting for transfers between devices: 717 us -> 363 us
  other arithmetic: 406 us -> 65.4 us
  Pallas kernels: 0 us -> 57 us
  starting transfers between devices: 1.55 us -> 57.6 us
    reshape x21 -> x2, local copies, waits for them, and re-layouts: 740 us -> 0.62 us  [the longest x1 0.61 us: local(): sum_small[:9].reshape(3, 3, chans)]
    unnamed x331 -> x213, local copies, waits for them, and re-layouts: 494 us -> 65.4 us
    dot_general x54 -> x15, matrix products: 429 us -> 42.6 us  [dot32(): return jnp.dot(left, right, preferred_element_type=f32)]
    reduce_scatter x8 -> x0, waiting for transfers between devices: 382 us -> none  [the longest x2 143 us: local(): lax.psum_scatter(jnp.dot(gated_low, out_proj, preferred_element_type=jnp....]
    pad x16 -> x0, local copies, waits for them, and re-layouts: 272 us -> none  [the longest x8 150 us: lag_fold(): wide = jnp.pad(grad_table, ((0, 0), (0, 0), (0, block_len - 1)))]
    ppermute x0 -> x80, waiting for transfers between devices: none -> 187 us  [swap(): return lax.ppermute(block, 'mp', [(i, i ^ bit) for i in range(8)])]
    all_gather x8 -> x0, waiting for transfers between devices: 162 us -> none  [the longest x2 62.1 us: local(): lax.all_gather(mlp_normed, 'mp', axis=0, tiled=True)]
    reduce_sum x33 -> x4, other arithmetic: 155 us -> 3.37 us  [the longest x2 2.02 us: row_scale(): jnp.mean(rows_in * rows_in, axis=-1, keepdims=True) + epsilon]
  transfers between devices with their start and end apart: 17 -> 84, of which waited for: 13 -> 33; matrix products, arithmetic and copies ran while one was open for 61% -> 23% of each run, Pallas kernels for 0% -> 7%
where the time goes in v1:
time: 860 us; the launch traced here: 854 us
  waiting for transfers between devices  363 us (42%)
  matrix products  135 us (16%)
  local copies, waits for them, and re-layouts  99.4 us (12%)
  other arithmetic  65.4 us (8%)
  blocking collectives  61.4 us (7%)
  starting transfers between devices  57.6 us (7%)
  Pallas kernels  57 us (7%)
  between operations  15.7 us (2%)
    ppermute x80, waiting for transfers between devices, swap(): return lax.ppermute(block, 'mp', [(i, i ^ bit) for i in range(8)])  187 us
    psum x4, waiting for transfers between devices, over_dp(): summed = lax.psum(arrays, 'dp')  176 us
    unnamed x213, local copies, waits for them, and re-layouts  65.4 us
    ppermute x80, starting transfers between devices, swap(): return lax.ppermute(block, 'mp', [(i, i ^ bit) for i in range(8)])  57.4 us
    dot_general x13, matrix products, contract_cols(): lax.dot_general(left, right, (((1,), (1,)), ((), ())), preferred_element_...  54.4 us
    dot_general x15, matrix products, dot32(): return jnp.dot(left, right, preferred_element_type=f32)  42.6 us
    psum x1, blocking collectives, local(): gains = lax.psum((gain_one, gain_two), ('dp', 'mp'))  42.2 us
    dot_general x5, matrix products, contract_rows(): lax.dot_general(left, right, (((0,), (0,)), ((), ())), preferred_element_...  37.9 us
  transfers between devices with their start and end apart: 84, of which 33 were waited for; matrix products, arithmetic and copies ran while one was open for 23% of the time, Pallas kernels for 7%

profile of v1, /device:TPU:0, one launch (start us, length us, event | category | flops | bytes accessed | tf_op | source)
XLA Modules:
  0.0 854.4 jit_solution(9569551189414911813)
XLA Ops:
  13.1 3.0 collective-permute-start.4
  26.7 2.8 fusion.111
  29.5 3.1 fusion.109
  32.6 4.7 copy.39
  39.4 8.5 modal_filter.1.filt_ref
  54.8 5.6 collective-permute-done.44
  63.2 3.0 collective-permute-done.42
  67.9 7.0 collective-permute-done.45
  82.5 7.4 collective-permute-done.7
  90.0 9.9 %collective-permute-done.47 = bf16[1,128,2048]{2,1,0:T(8,128)(2,1)S(1)} collective-permute-done((bf16[1,128,2048]{2,1,0:T(8,128)(2,1)}, bf16[1,128,2048]{2,1,0:T(8,128)(2,1)S(1)}, u32[]{:S(2)}, u32[]{:S(2)}) %collective-permute-start.47) | collective-permute-done | bytes 524320 | tf_op jit(solution)/shard_map/ppermute | solution.py:378
  101.5 12.9 %collective-permute-done.48 = bf16[1,128,2048]{2,1,0:T(8,128)(2,1)S(1)} collective-permute-done((bf16[1,128,2048]{2,1,0:T(8,128)(2,1)S(1)}, bf16[1,128,2048]{2,1,0:T(8,128)(2,1)S(1)}, u32[]{:S(2)}, u32[]{:S(2)}) %collective-permute-start.48) | collective-permute-done | bytes 524320 | tf_op jit(solution)/shard_map/ppermute | solution.py:378
  123.8 3.5 fusion.1
  129.1 3.4 pad_maximum_fusion.q_ref.k_ref.v_ref
  132.5 16.9 %mixer_forward.1 = (bf16[8,2,128,256]{3,2,1,0:T(8,128)(2,1)S(1)}, f32[2,1024,256]{2,1,0:T(8,128)}, f32[2,2048,256]{2,1,0:T(8,128)}) custom-call(s32[1]{0:T(128)} %bitcast.2.me_ref, f32[8,2,128,768]{3,2,1,0:T(8,128)} %pad_maximum_fusion.q_ref.k_ref.v_ref, f32[8,2,128,768]{3,2,1,0:T(8,128)} %pad_maximum_fusion.q_ref.k_ref.v_ref, ...), custom_call_target="tpu_custom_call" | custom-call | tf_op jit(solution)/shard_map/mixer_forward/pallas_call | solution.py:280
  162.2 9.7 %collective-permute-done.18 = bf16[1,128,2048]{2,1,0:T(8,128)(2,1)S(1)} collective-permute-done((bf16[1,128,2048]{2,1,0:T(8,128)(2,1)S(1)}, bf16[1,128,2048]{2,1,0:T(8,128)(2,1)S(1)}, u32[]{:S(2)}, u32[]{:S(2)}) %collective-permute-start.18) | collective-permute-done | bytes 524320 | tf_op jit(solution)/shard_map/ppermute | solution.py:378
  174.8 9.9 %collective-permute-done.12 = bf16[1,128,2048]{2,1,0:T(8,128)(2,1)S(1)} collective-permute-done((bf16[1,128,2048]{2,1,0:T(8,128)(2,1)S(1)}, bf16[1,128,2048]{2,1,0:T(8,128)(2,1)S(1)}, u32[]{:S(2)}, u32[]{:S(2)}) %collective-permute-start.12) | collective-permute-done | bytes 524320 | tf_op jit(solution)/shard_map/ppermute | solution.py:378
  184.7 10.0 %collective-permute-done.19 = bf16[1,128,2048]{2,1,0:T(8,128)(2,1)S(1)} collective-permute-done((bf16[1,128,2048]{2,1,0:T(8,128)(2,1)S(1)}, bf16[1,128,2048]{2,1,0:T(8,128)(2,1)S(1)}, u32[]{:S(2)}, u32[]{:S(2)}) %collective-permute-start.19) | collective-permute-done | bytes 524320 | tf_op jit(solution)/shard_map/ppermute | solution.py:378
  201.5 10.3 %collective-permute-done.21 = bf16[1,128,2048]{2,1,0:T(8,128)(2,1)S(1)} collective-permute-done((bf16[1,128,2048]{2,1,0:T(8,128)(2,1)S(1)}, bf16[1,128,2048]{2,1,0:T(8,128)(2,1)S(1)}, u32[]{:S(2)}, u32[]{:S(2)}) %collective-permute-start.21) | collective-permute-done | bytes 524320 | tf_op jit(solution)/shard_map/ppermute | solution.py:378
  212.3 10.3 %collective-permute-done.22 = bf16[1,128,2048]{2,1,0:T(8,128)(2,1)S(1)} collective-permute-done((bf16[1,128,2048]{2,1,0:T(8,128)(2,1)S(1)}, bf16[1,128,2048]{2,1,0:T(8,128)(2,1)S(1)}, u32[]{:S(2)}, u32[]{:S(2)}) %collective-permute-start.22) | collective-permute-done | bytes 524320 | tf_op jit(solution)/shard_map/ppermute | solution.py:378
  225.3 8.9 %collective-permute-done.27 = bf16[1,128,2048]{2,1,0:T(8,128)(2,1)S(1)} collective-permute-done((bf16[1,128,2048]{2,1,0:T(8,128)(2,1)S(1)}, bf16[1,128,2048]{2,1,0:T(8,128)(2,1)S(1)}, u32[]{:S(2)}, u32[]{:S(2)}) %collective-permute-start.27) | collective-permute-done | bytes 524320 | tf_op jit(solution)/shard_map/ppermute | solution.py:378
  234.2 2.9 collective-permute-done.28
  244.6 4.8 fusion.143
  249.6 4.8 fusion.146
  254.6 2.8 fusion.144
  257.4 2.9 fusion.147
  260.3 15.7 %multiply_convert_fusion = (bf16[2048,704]{0,1:T(8,128)(2,1)}, bf16[2048,704]{0,1:T(8,128)(2,1)}, bf16[2048,704]{0,1:T(8,128)(2,1)}) fusion(f32[512,704]{0,1:T(8,128)} %fusion.144, f32[1024,704]{0,1:T(8,128)} %fusion.143, f32[512,704]{0,1:T(8,128)S(1)} %fusion.142, f32[512,704]{0,1:T(8,128)} %fusion.147, f32[1024,704]{0,1:T(8,128)} %fusion.146, ...), kind=kOutput, calls=%fused_computation.5 | convolution fusion | flops 5932974080 | bytes 31457280 | tf_op jit(solution)/shard_map/dot_general | solution.py:34
  276.0 7.2 fusion.75
  283.2 3.8 fusion.101
  287.1 3.9 fusion.104
  291.0 7.5 convolution_convert_fusion.5
  298.5 6.7 convolution_convert_fusion
  305.2 3.2 convolution_convert_fusion.10
  308.4 3.2 convolution_convert_fusion.11
  312.6 11.0 %convolution_convert_fusion.4 = bf16[2048,704]{0,1:T(8,128)(2,1)} fusion(bf16[2048,704]{0,1:T(8,128)(2,1)S(1)} %copy-done.54, bf16[2048,2048]{1,0:T(8,128)(2,1)} %bitcast.418), kind=kOutput, calls=%fused_computation.42 | convolution fusion | flops 5907021824 | bytes 14155776 | tf_op jit(solution)/shard_map/dot_general | solution.py:30
  323.6 7.4 convolution_convert_fusion.3
  332.9 6.9 add_convert_fusion
  363.0 7.8 collective-permute-done.58
  371.4 11.6 %collective-permute-done.55 = bf16[1,128,2048]{2,1,0:T(8,128)(2,1)S(1)} collective-permute-done((bf16[1,128,2048]{2,1,0:T(8,128)(2,1)S(1)}, bf16[1,128,2048]{2,1,0:T(8,128)(2,1)S(1)}, u32[]{:S(2)}, u32[]{:S(2)}) %collective-permute-start.55) | collective-permute-done | bytes 524320 | tf_op jit(solution)/shard_map/ppermute | solution.py:378
  383.7 8.7 %collective-permute-done.38 = bf16[1,128,2048]{2,1,0:T(8,128)(2,1)S(1)} collective-permute-done((bf16[1,128,2048]{2,1,0:T(8,128)(2,1)S(1)}, bf16[1,128,2048]{2,1,0:T(8,128)(2,1)S(1)}, u32[]{:S(2)}, u32[]{:S(2)}) %collective-permute-start.38) | collective-permute-done | bytes 524320 | tf_op jit(solution)/shard_map/ppermute | solution.py:378
  398.0 7.5 collective-permute-done.59
  412.8 3.9 collective-permute-done.32
  419.0 9.0 %collective-permute-done.39 = bf16[1,128,2048]{2,1,0:T(8,128)(2,1)S(1)} collective-permute-done((bf16[1,128,2048]{2,1,0:T(8,128)(2,1)S(1)}, bf16[1,128,2048]{2,1,0:T(8,128)(2,1)S(1)}, u32[]{:S(2)}, u32[]{:S(2)}) %collective-permute-start.39) | collective-permute-done | bytes 524320 | tf_op jit(solution)/shard_map/ppermute | solution.py:378
  434.7 4.4 collective-permute-done.61
  440.0 9.2 %collective-permute-done.62 = bf16[1,128,2048]{2,1,0:T(8,128)(2,1)S(1)} collective-permute-done((bf16[1,128,2048]{2,1,0:T(8,128)(2,1)S(1)}, bf16[1,128,2048]{2,1,0:T(8,128)(2,1)S(1)}, u32[]{:S(2)}, u32[]{:S(2)}) %collective-permute-start.62) | collective-permute-done | bytes 524320 | tf_op jit(solution)/shard_map/ppermute | solution.py:378
  455.4 5.1 convert_element_type.591
  460.6 2.8 constant_dynamic-update-slice_fusion.38
  477.9 3.1 fusion.9
  483.3 24.9 %mixer_backward.1 = (bf16[8,2,128,768]{3,2,1,0:T(8,128)(2,1)}, f32[9,256]{1,0:T(8,128)S(1)}, f32[1,256]{1,0:T(1,128)S(1)}, f32[1024,256]{1,0:T(8,128)S(1)}) custom-call(s32[1]{0:T(128)} %bitcast.2.me_ref, f32[8,2,128,256]{3,2,1,0:T(8,128)} %pad_maximum_fusion.7.gg_ref, f32[8,2,128,768]{3,2,1,0:T(8,128)} %pad_maximum_fusion.q_ref.k_ref.v_ref, ...), custom_call_target="tpu_custom_call" | custom-call | tf_op jit(solution)/shard_map/mixer_backward/pallas_call | solution.py:317
  512.8 6.8 pole_gradients.1
  519.6 3.6 convolution_convert_fusion.2
  533.2 8.6 %bitcast_convert_fusion = bf16[2048,768]{1,0:T(8,128)(2,1)} fusion(bf16[8,2,128,2048]{3,2,1,0:T(8,128)(2,1)S(1)} %bitcast.413, bf16[8,2,128,768]{3,2,1,0:T(8,128)(2,1)S(1)} %copy-done.45), kind=kOutput, calls=%fused_computation.2 | convolution fusion | flops 6444023808 | bytes 14680064 | tf_op jit(solution)/shard_map/dot_general | solution.py:30
  541.9 3.4 fusion.24
  549.7 112.4 %all-reduce.13.cloned.1.call-done = (bf16[2048,704]{0,1:T(8,128)(2,1)}, bf16[2048,704]{0,1:T(8,128)(2,1)}) async-done(((bf16[2048,704]{0,1:T(8,128)(2,1)}, bf16[2048,704]{0,1:T(8,128)(2,1)}), (bf16[2048,704]{0,1:T(8,128)(2,1)}, bf16[2048,704]{0,1:T(8,128)(2,1)})) %all-reduce.13.cloned.1.call-update) | async-done | bytes 5767184 | tf_op jit(solution)/shard_map/psum | solution.py:509
  672.4 43.0 %all-reduce.9.cloned.1.call-done = bf16[256,2048]{1,0:T(8,128)(2,1)} async-done(((bf16[256,2048]{1,0:T(8,128)(2,1)}), bf16[256,2048]{1,0:T(8,128)(2,1)}) %all-reduce.9.cloned.1.call-update) | async-done | bytes 1048592 | tf_op jit(solution)/shard_map/psum | solution.py:509
  715.3 4.6 copy.47
  727.4 7.8 collective-permute-done.79
  743.5 3.5 copy.48
  747.0 42.2 %all-reduce = (f32[2048]{0:T(1024)}, f32[2048]{0:T(1024)}) all-reduce(f32[2048]{0:T(1024)S(1)} %get-tuple-element.74, f32[2048]{0:T(1024)S(1)} %get-tuple-element.72), channel_id=1, replica_groups=mesh['dp'=4,'mp'=8] {'dp','mp'}, use_global_device_ids=true, to_apply=%region_5.0 | all-reduce | flops 4096 | bytes 32768 | tf_op jit(solution)/shard_map/psum | solution.py:554
  789.3 5.3 convert_element_type.589
  794.6 3.3 convert_element_type.590
  797.9 19.1 %psum.62 = bf16[58,256]{1,0:T(8,128)(2,1)S(1)} all-reduce(bf16[58,256]{1,0:T(8,128)(2,1)S(1)} %concatenate.187), channel_id=1, replica_groups=mesh['dp'=4,'mp'=8] {'dp'}, use_global_device_ids=true, to_apply=%region_11.0 | all-reduce | flops 14848 | bytes 59392 | tf_op jit(solution)/shard_map/psum | solution.py:509
  818.2 2.8 convert_element_type.588
  821.6 20.7 %all-reduce.11.cloned.1.call-done = bf16[2048,3,256]{0,2,1:T(8,128)(2,1)} async-done(((bf16[2048,3,256]{0,2,1:T(8,128)(2,1)}), bf16[2048,3,256]{0,2,1:T(8,128)(2,1)}) %all-reduce.11.cloned.1.call-update) | async-done | bytes 3145744 | tf_op jit(solution)/shard_map/psum | solution.py:509
  842.3 5.4 copy.49
  (485 shorter events, 202.8 us)
Async XLA Ops:
  7.2 448.1 %all-reduce.7.cloned.1.call-start = ((), (), s32[]{:S(2)}) async-start(), calls=%async_computation | async-start | bytes 5767168 | tf_op jit(solution)/shard_map/psum | solution.py:509
  13.1 34.9 %collective-permute-start.4 = (bf16[1,128,2048]{2,1,0:T(8,128)(2,1)}, bf16[1,128,2048]{2,1,0:T(8,128)(2,1)}, u32[]{:S(2)}, u32[]{:S(2)}) collective-permute-start(bf16[1,128,2048]{2,1,0:T(8,128)(2,1)} %get-tuple-element.148), channel_id=1, source_target_pairs={{0,4},{1,5},{2,6},{3,7},{4,0},{5,1},{6,2},{7,3},{8,12},{9,13},{10,... | collective-permute-start | bytes 1572872 | tf_op jit(solution)/shard_map/ppermute | solution.py:378
  16.0 34.5 %collective-permute-start.1 = (bf16[1,128,2048]{2,1,0:T(8,128)(2,1)}, bf16[1,128,2048]{2,1,0:T(8,128)(2,1)}, u32[]{:S(2)}, u32[]{:S(2)}) collective-permute-start(bf16[1,128,2048]{2,1,0:T(8,128)(2,1)} %get-tuple-element.148), channel_id=1, source_target_pairs={{0,2},{1,3},{2,0},{3,1},{4,6},{5,7},{6,4},{7,5},{8,10},{9,11},{10,... | collective-permute-start | bytes 1572872 | tf_op jit(solution)/shard_map/ppermute | solution.py:378
  17.5 42.9 %collective-permute-start.5 = (bf16[1,128,2048]{2,1,0:T(8,128)(2,1)}, bf16[1,128,2048]{2,1,0:T(8,128)(2,1)}, u32[]{:S(2)}, u32[]{:S(2)}) collective-permute-start(bf16[1,128,2048]{2,1,0:T(8,128)(2,1)} %get-tuple-element.147), channel_id=1, source_target_pairs={{0,4},{1,5},{2,6},{3,7},{4,0},{5,1},{6,2},{7,3},{8,12},{9,13},{10,... | collective-permute-start | bytes 1572872 | tf_op jit(solution)/shard_map/ppermute | solution.py:378
  18.0 48.2 %collective-permute-start.2 = (bf16[1,128,2048]{2,1,0:T(8,128)(2,1)}, bf16[1,128,2048]{2,1,0:T(8,128)(2,1)}, u32[]{:S(2)}, u32[]{:S(2)}) collective-permute-start(bf16[1,128,2048]{2,1,0:T(8,128)(2,1)} %get-tuple-element.147), channel_id=1, source_target_pairs={{0,2},{1,3},{2,0},{3,1},{4,6},{5,7},{6,4},{7,5},{8,10},{9,11},{10,... | collective-permute-start | bytes 1572872 | tf_op jit(solution)/shard_map/ppermute | solution.py:378
  21.8 30.4 %collective-permute-start.41 = (bf16[1,128,2048]{2,1,0:T(8,128)(2,1)}, bf16[1,128,2048]{2,1,0:T(8,128)(2,1)}, u32[]{:S(2)}, u32[]{:S(2)}) collective-permute-start(bf16[1,128,2048]{2,1,0:T(8,128)(2,1)} %get-tuple-element.138), channel_id=1, source_target_pairs={{0,2},{1,3},{2,0},{3,1},{4,6},{5,7},{6,4},{7,5},{8,10},{9,11},{10,... | collective-permute-start | bytes 1572872 | tf_op jit(solution)/shard_map/ppermute | solution.py:378
  50.6 28.7 %collective-permute-start = (bf16[2,128,2048]{2,1,0:T(8,128)(2,1)S(1)}, bf16[2,128,2048]{2,1,0:T(8,128)(2,1)S(1)}, u32[]{:S(2)}, u32[]{:S(2)}) collective-permute-start(bf16[2,128,2048]{2,1,0:T(8,128)(2,1)S(1)} %copy-done.34), channel_id=1, source_target_pairs={{0,1},{1,0},{2,3},{3,2},{4,5},{5,4},{6,7},{7,6},{8,9},{9,8},{10,11... | collective-permute-start | bytes 3145736 | tf_op jit(solution)/shard_map/ppermute | solution.py:378
  60.4 16.1 %collective-permute-start.40 = (bf16[2,128,2048]{2,1,0:T(8,128)(2,1)S(1)}, bf16[2,128,2048]{2,1,0:T(8,128)(2,1)S(1)}, u32[]{:S(2)}, u32[]{:S(2)}) collective-permute-start(bf16[2,128,2048]{2,1,0:T(8,128)(2,1)S(1)} %copy-done.36), channel_id=1, source_target_pairs={{0,1},{1,0},{2,3},{3,2},{4,5},{5,4},{6,7},{7,6},{8,9},{9,8},{10,11... | collective-permute-start | bytes 3145736 | tf_op jit(solution)/shard_map/ppermute | solution.py:378
  60.5 14.4 %collective-permute-start.45 = (bf16[1,128,2048]{2,1,0:T(8,128)(2,1)S(1)}, bf16[1,128,2048]{2,1,0:T(8,128)(2,1)S(1)}, u32[]{:S(2)}, u32[]{:S(2)}) collective-permute-start(bf16[1,128,2048]{2,1,0:T(8,128)(2,1)S(1)} %copy-done.55), channel_id=1, source_target_pairs={{0,4},{1,5},{2,6},{3,7},{4,0},{5,1},{6,2},{7,3},{8,12},{9,13},{10,... | collective-permute-start | bytes 1572872 | tf_op jit(solution)/shard_map/ppermute | solution.py:378
  66.1 55.4 %collective-permute-start.6 = (bf16[2,128,2048]{2,1,0:T(8,128)(2,1)S(1)}, bf16[2,128,2048]{2,1,0:T(8,128)(2,1)S(1)}, u32[]{:S(2)}, u32[]{:S(2)}) collective-permute-start(bf16[2,128,2048]{2,1,0:T(8,128)(2,1)S(1)} %constant_dynamic-update-slice_fusion.2), channel_id=1, source_target_pairs={{0,1},{1,0},{2,3},{3,2},{4,5},{5,4},{6,7},{7,6},{8,9},{9,8},{10,11... | collective-permute-start | bytes 3145736 | tf_op jit(solution)/shard_map/ppermute | solution.py:378
  66.2 48.2 %collective-permute-start.43 = (bf16[2,128,2048]{2,1,0:T(8,128)(2,1)S(1)}, bf16[2,128,2048]{2,1,0:T(8,128)(2,1)S(1)}, u32[]{:S(2)}, u32[]{:S(2)}) collective-permute-start(bf16[2,128,2048]{2,1,0:T(8,128)(2,1)S(1)} %constant_dynamic-update-slice_fusion.12), channel_id=1, source_target_pairs={{0,1},{1,0},{2,3},{3,2},{4,5},{5,4},{6,7},{7,6},{8,9},{9,8},{10,11... | collective-permute-start | bytes 3145736 | tf_op jit(solution)/shard_map/ppermute | solution.py:378
  74.9 15.0 %collective-permute-start.7 = (bf16[1,128,2048]{2,1,0:T(8,128)(2,1)}, bf16[1,128,2048]{2,1,0:T(8,128)(2,1)S(1)}, u32[]{:S(2)}, u32[]{:S(2)}) collective-permute-start(bf16[1,128,2048]{2,1,0:T(8,128)(2,1)} %collective-permute-done.1), channel_id=1, source_target_pairs={{0,4},{1,5},{2,6},{3,7},{4,0},{5,1},{6,2},{7,3},{8,12},{9,13},{10,... | collective-permute-start | bytes 1572872 | tf_op jit(solution)/shard_map/ppermute | solution.py:378
  76.5 23.5 %collective-permute-start.8 = (bf16[1,128,2048]{2,1,0:T(8,128)(2,1)}, bf16[1,128,2048]{2,1,0:T(8,128)(2,1)S(1)}, u32[]{:S(2)}, u32[]{:S(2)}) collective-permute-start(bf16[1,128,2048]{2,1,0:T(8,128)(2,1)} %collective-permute-done.5), channel_id=1, source_target_pairs={{0,2},{1,3},{2,0},{3,1},{4,6},{5,7},{6,4},{7,5},{8,10},{9,11},{10,... | collective-permute-start | bytes 1572872 | tf_op jit(solution)/shard_map/ppermute | solution.py:378
  79.3 20.6 %collective-permute-start.47 = (bf16[1,128,2048]{2,1,0:T(8,128)(2,1)}, bf16[1,128,2048]{2,1,0:T(8,128)(2,1)S(1)}, u32[]{:S(2)}, u32[]{:S(2)}) collective-permute-start(bf16[1,128,2048]{2,1,0:T(8,128)(2,1)} %collective-permute-done.41), channel_id=1, source_target_pairs={{0,4},{1,5},{2,6},{3,7},{4,0},{5,1},{6,2},{7,3},{8,12},{9,13},{10,... | collective-permute-start | bytes 1572872 | tf_op jit(solution)/shard_map/ppermute | solution.py:378
  89.9 29.5 %collective-permute-start.3 = (bf16[2,128,2048]{2,1,0:T(8,128)(2,1)S(1)}, bf16[2,128,2048]{2,1,0:T(8,128)(2,1)S(1)}, u32[]{:S(2)}, u32[]{:S(2)}) collective-permute-start(bf16[2,128,2048]{2,1,0:T(8,128)(2,1)S(1)} %constant_dynamic-update-slice_fusion), channel_id=1, source_target_pairs={{0,1},{1,0},{2,3},{3,2},{4,5},{5,4},{6,7},{7,6},{8,9},{9,8},{10,11... | collective-permute-start | bytes 3145736 | tf_op jit(solution)/shard_map/ppermute | solution.py:378
  99.9 17.2 %collective-permute-start.46 = (bf16[2,128,2048]{2,1,0:T(8,128)(2,1)S(1)}, bf16[2,128,2048]{2,1,0:T(8,128)(2,1)S(1)}, u32[]{:S(2)}, u32[]{:S(2)}) collective-permute-start(bf16[2,128,2048]{2,1,0:T(8,128)(2,1)S(1)} %constant_dynamic-update-slice_fusion.14), channel_id=1, source_target_pairs={{0,1},{1,0},{2,3},{3,2},{4,5},{5,4},{6,7},{7,6},{8,9},{9,8},{10,11... | collective-permute-start | bytes 3145736 | tf_op jit(solution)/shard_map/ppermute | solution.py:378
  100.0 14.4 %collective-permute-start.48 = (bf16[1,128,2048]{2,1,0:T(8,128)(2,1)S(1)}, bf16[1,128,2048]{2,1,0:T(8,128)(2,1)S(1)}, u32[]{:S(2)}, u32[]{:S(2)}) collective-permute-start(bf16[1,128,2048]{2,1,0:T(8,128)(2,1)S(1)} %collective-permute-done.45), channel_id=1, source_target_pairs={{0,2},{1,3},{2,0},{3,1},{4,6},{5,7},{6,4},{7,5},{8,10},{9,11},{10,... | collective-permute-start | bytes 1572872 | tf_op jit(solution)/shard_map/ppermute | solution.py:378
  114.4 41.1 %collective-permute-start.49 = (bf16[2,128,2048]{2,1,0:T(8,128)(2,1)S(1)}, bf16[2,128,2048]{2,1,0:T(8,128)(2,1)S(1)}, u32[]{:S(2)}, u32[]{:S(2)}) collective-permute-start(bf16[2,128,2048]{2,1,0:T(8,128)(2,1)S(1)} %constant_dynamic-update-slice_fusion.16), channel_id=1, source_target_pairs={{0,1},{1,0},{2,3},{3,2},{4,5},{5,4},{6,7},{7,6},{8,9},{9,8},{10,11... | collective-permute-start | bytes 3145736 | tf_op jit(solution)/shard_map/ppermute | solution.py:378
  154.0 20.4 %collective-permute-start.10 = (bf16[2,128,2048]{2,1,0:T(8,128)(2,1)S(1)}, bf16[2,128,2048]{2,1,0:T(8,128)(2,1)S(1)}, u32[]{:S(2)}, u32[]{:S(2)}) collective-permute-start(bf16[2,128,2048]{2,1,0:T(8,128)(2,1)S(1)} %bitcast.397), channel_id=1, source_target_pairs={{0,1},{1,0},{2,3},{3,2},{4,5},{5,4},{6,7},{7,6},{8,9},{9,8},{10,11... | collective-permute-start | bytes 3145736 | tf_op jit(solution)/shard_map/ppermute | solution.py:378
  157.1 14.8 %collective-permute-start.18 = (bf16[1,128,2048]{2,1,0:T(8,128)(2,1)S(1)}, bf16[1,128,2048]{2,1,0:T(8,128)(2,1)S(1)}, u32[]{:S(2)}, u32[]{:S(2)}) collective-permute-start(bf16[1,128,2048]{2,1,0:T(8,128)(2,1)S(1)} %get-tuple-element.144), channel_id=1, source_target_pairs={{0,4},{1,5},{2,6},{3,7},{4,0},{5,1},{6,2},{7,3},{8,12},{9,13},{10,... | collective-permute-start | bytes 1572872 | tf_op jit(solution)/shard_map/ppermute | solution.py:378
  158.7 14.8 %collective-permute-start.15 = (bf16[1,128,2048]{2,1,0:T(8,128)(2,1)S(1)}, bf16[1,128,2048]{2,1,0:T(8,128)(2,1)S(1)}, u32[]{:S(2)}, u32[]{:S(2)}) collective-permute-start(bf16[1,128,2048]{2,1,0:T(8,128)(2,1)S(1)} %get-tuple-element.143), channel_id=1, source_target_pairs={{0,2},{1,3},{2,0},{3,1},{4,6},{5,7},{6,4},{7,5},{8,10},{9,11},{10,... | collective-permute-start | bytes 1572872 | tf_op jit(solution)/shard_map/ppermute | solution.py:378
  159.6 25.1 %collective-permute-start.12 = (bf16[1,128,2048]{2,1,0:T(8,128)(2,1)S(1)}, bf16[1,128,2048]{2,1,0:T(8,128)(2,1)S(1)}, u32[]{:S(2)}, u32[]{:S(2)}) collective-permute-start(bf16[1,128,2048]{2,1,0:T(8,128)(2,1)S(1)} %slice.599), channel_id=1, source_target_pairs={{0,2},{1,3},{2,0},{3,1},{4,6},{5,7},{6,4},{7,5},{8,10},{9,11},{10,... | collective-permute-start | bytes 1572872 | tf_op jit(solution)/shard_map/ppermute | solution.py:378
  161.6 23.1 %collective-permute-start.17 = (bf16[1,128,2048]{2,1,0:T(8,128)(2,1)S(1)}, bf16[1,128,2048]{2,1,0:T(8,128)(2,1)S(1)}, u32[]{:S(2)}, u32[]{:S(2)}) collective-permute-start(bf16[1,128,2048]{2,1,0:T(8,128)(2,1)S(1)} %slice.598), channel_id=1, source_target_pairs={{0,4},{1,5},{2,6},{3,7},{4,0},{5,1},{6,2},{7,3},{8,12},{9,13},{10,... | collective-permute-start | bytes 1572872 | tf_op jit(solution)/shard_map/ppermute | solution.py:378
  172.1 22.7 %collective-permute-start.19 = (bf16[1,128,2048]{2,1,0:T(8,128)(2,1)S(1)}, bf16[1,128,2048]{2,1,0:T(8,128)(2,1)S(1)}, u32[]{:S(2)}, u32[]{:S(2)}) collective-permute-start(bf16[1,128,2048]{2,1,0:T(8,128)(2,1)S(1)} %fusion.93), channel_id=1, source_target_pairs={{0,2},{1,3},{2,0},{3,1},{4,6},{5,7},{6,4},{7,5},{8,10},{9,11},{10,... | collective-permute-start | bytes 1572872 | tf_op jit(solution)/shard_map/ppermute | solution.py:378
  173.6 21.2 %collective-permute-start.16 = (bf16[1,128,2048]{2,1,0:T(8,128)(2,1)S(1)}, bf16[1,128,2048]{2,1,0:T(8,128)(2,1)S(1)}, u32[]{:S(2)}, u32[]{:S(2)}) collective-permute-start(bf16[1,128,2048]{2,1,0:T(8,128)(2,1)S(1)} %fusion.95), channel_id=1, source_target_pairs={{0,4},{1,5},{2,6},{3,7},{4,0},{5,1},{6,2},{7,3},{8,12},{9,13},{10,... | collective-permute-start | bytes 1572872 | tf_op jit(solution)/shard_map/ppermute | solution.py:378
  196.8 40.4 %collective-permute-start.20 = (bf16[2,128,2048]{2,1,0:T(8,128)(2,1)S(1)}, bf16[2,128,2048]{2,1,0:T(8,128)(2,1)S(1)}, u32[]{:S(2)}, u32[]{:S(2)}) collective-permute-start(bf16[2,128,2048]{2,1,0:T(8,128)(2,1)S(1)} %multiply_convert_fusion.3), channel_id=1, source_target_pairs={{0,1},{1,0},{2,3},{3,2},{4,5},{5,4},{6,7},{7,6},{8,9},{9,8},{10,11... | collective-permute-start | bytes 3145736 | tf_op jit(solution)/shard_map/ppermute | solution.py:378
  197.0 14.8 %collective-permute-start.21 = (bf16[1,128,2048]{2,1,0:T(8,128)(2,1)S(1)}, bf16[1,128,2048]{2,1,0:T(8,128)(2,1)S(1)}, u32[]{:S(2)}, u32[]{:S(2)}) collective-permute-start(bf16[1,128,2048]{2,1,0:T(8,128)(2,1)S(1)} %get-tuple-element.142), channel_id=1, source_target_pairs={{0,2},{1,3},{2,0},{3,1},{4,6},{5,7},{6,4},{7,5},{8,10},{9,11},{10,... | collective-permute-start | bytes 1572872 | tf_op jit(solution)/shard_map/ppermute | solution.py:378
  197.6 27.5 %collective-permute-start.24 = (bf16[1,128,2048]{2,1,0:T(8,128)(2,1)S(1)}, bf16[1,128,2048]{2,1,0:T(8,128)(2,1)S(1)}, u32[]{:S(2)}, u32[]{:S(2)}) collective-permute-start(bf16[1,128,2048]{2,1,0:T(8,128)(2,1)S(1)} %get-tuple-element.142), channel_id=1, source_target_pairs={{0,4},{1,5},{2,6},{3,7},{4,0},{5,1},{6,2},{7,3},{8,12},{9,13},{10,... | collective-permute-start | bytes 1572872 | tf_op jit(solution)/shard_map/ppermute | solution.py:378
  198.0 24.7 %collective-permute-start.22 = (bf16[1,128,2048]{2,1,0:T(8,128)(2,1)S(1)}, bf16[1,128,2048]{2,1,0:T(8,128)(2,1)S(1)}, u32[]{:S(2)}, u32[]{:S(2)}) collective-permute-start(bf16[1,128,2048]{2,1,0:T(8,128)(2,1)S(1)} %get-tuple-element.141), channel_id=1, source_target_pairs={{0,2},{1,3},{2,0},{3,1},{4,6},{5,7},{6,4},{7,5},{8,10},{9,11},{10,... | collective-permute-start | bytes 1572872 | tf_op jit(solution)/shard_map/ppermute | solution.py:378
  199.6 24.0 %collective-permute-start.25 = (bf16[1,128,2048]{2,1,0:T(8,128)(2,1)S(1)}, bf16[1,128,2048]{2,1,0:T(8,128)(2,1)S(1)}, u32[]{:S(2)}, u32[]{:S(2)}) collective-permute-start(bf16[1,128,2048]{2,1,0:T(8,128)(2,1)S(1)} %get-tuple-element.141), channel_id=1, source_target_pairs={{0,4},{1,5},{2,6},{3,7},{4,0},{5,1},{6,2},{7,3},{8,12},{9,13},{10,... | collective-permute-start | bytes 1572872 | tf_op jit(solution)/shard_map/ppermute | solution.py:378
  211.8 22.3 %collective-permute-start.27 = (bf16[1,128,2048]{2,1,0:T(8,128)(2,1)S(1)}, bf16[1,128,2048]{2,1,0:T(8,128)(2,1)S(1)}, u32[]{:S(2)}, u32[]{:S(2)}) collective-permute-start(bf16[1,128,2048]{2,1,0:T(8,128)(2,1)S(1)} %collective-permute-done.21), channel_id=1, source_target_pairs={{0,4},{1,5},{2,6},{3,7},{4,0},{5,1},{6,2},{7,3},{8,12},{9,13},{10,... | collective-permute-start | bytes 1572872 | tf_op jit(solution)/shard_map/ppermute | solution.py:378
  222.7 21.0 %collective-permute-start.23 = (bf16[2,128,2048]{2,1,0:T(8,128)(2,1)S(1)}, bf16[2,128,2048]{2,1,0:T(8,128)(2,1)S(1)}, u32[]{:S(2)}, u32[]{:S(2)}) collective-permute-start(bf16[2,128,2048]{2,1,0:T(8,128)(2,1)S(1)} %constant_dynamic-update-slice_fusion.6), channel_id=1, source_target_pairs={{0,1},{1,0},{2,3},{3,2},{4,5},{5,4},{6,7},{7,6},{8,9},{9,8},{10,11... | collective-permute-start | bytes 3145736 | tf_op jit(solution)/shard_map/ppermute | solution.py:378
  225.2 18.9 %collective-permute-start.26 = (bf16[2,128,2048]{2,1,0:T(8,128)(2,1)S(1)}, bf16[2,128,2048]{2,1,0:T(8,128)(2,1)S(1)}, u32[]{:S(2)}, u32[]{:S(2)}) collective-permute-start(bf16[2,128,2048]{2,1,0:T(8,128)(2,1)S(1)} %constant_dynamic-update-slice_fusion.8), channel_id=1, source_target_pairs={{0,1},{1,0},{2,3},{3,2},{4,5},{5,4},{6,7},{7,6},{8,9},{9,8},{10,11... | collective-permute-start | bytes 3145736 | tf_op jit(solution)/shard_map/ppermute | solution.py:378
  237.1 17.3 %collective-permute-start.29 = (bf16[2,128,2048]{2,1,0:T(8,128)(2,1)S(1)}, bf16[2,128,2048]{2,1,0:T(8,128)(2,1)S(1)}, u32[]{:S(2)}, u32[]{:S(2)}) collective-permute-start(bf16[2,128,2048]{2,1,0:T(8,128)(2,1)S(1)} %constant_dynamic-update-slice_fusion.10), channel_id=1, source_target_pairs={{0,1},{1,0},{2,3},{3,2},{4,5},{5,4},{6,7},{7,6},{8,9},{9,8},{10,11... | collective-permute-start | bytes 3145736 | tf_op jit(solution)/shard_map/ppermute | solution.py:378
  331.1 331.1 %all-reduce.13.cloned.1.call-start = ((), (), s32[]{:S(2)}) async-start(), calls=%async_computation.3 | async-start | bytes 11534336 | tf_op jit(solution)/shard_map/psum | solution.py:509
  355.9 14.8 %collective-permute-start.58 = (bf16[1,128,2048]{2,1,0:T(8,128)(2,1)S(1)}, bf16[1,128,2048]{2,1,0:T(8,128)(2,1)S(1)}, u32[]{:S(2)}, u32[]{:S(2)}) collective-permute-start(bf16[1,128,2048]{2,1,0:T(8,128)(2,1)S(1)} %get-tuple-element.136), channel_id=1, source_target_pairs={{0,4},{1,5},{2,6},{3,7},{4,0},{5,1},{6,2},{7,3},{8,12},{9,13},{10,... | collective-permute-start | bytes 1572872 | tf_op jit(solution)/shard_map/ppermute | solution.py:378
  356.9 38.1 %collective-permute-start.52 = (bf16[1,128,2048]{2,1,0:T(8,128)(2,1)S(1)}, bf16[1,128,2048]{2,1,0:T(8,128)(2,1)S(1)}, u32[]{:S(2)}, u32[]{:S(2)}) collective-permute-start(bf16[1,128,2048]{2,1,0:T(8,128)(2,1)S(1)} %slice.595), channel_id=1, source_target_pairs={{0,2},{1,3},{2,0},{3,1},{4,6},{5,7},{6,4},{7,5},{8,10},{9,11},{10,... | collective-permute-start | bytes 1572872 | tf_op jit(solution)/shard_map/ppermute | solution.py:378
  357.9 25.1 %collective-permute-start.55 = (bf16[1,128,2048]{2,1,0:T(8,128)(2,1)S(1)}, bf16[1,128,2048]{2,1,0:T(8,128)(2,1)S(1)}, u32[]{:S(2)}, u32[]{:S(2)}) collective-permute-start(bf16[1,128,2048]{2,1,0:T(8,128)(2,1)S(1)} %get-tuple-element.135), channel_id=1, source_target_pairs={{0,2},{1,3},{2,0},{3,1},{4,6},{5,7},{6,4},{7,5},{8,10},{9,11},{10,... | collective-permute-start | bytes 1572872 | tf_op jit(solution)/shard_map/ppermute | solution.py:378
  360.0 36.6 %collective-permute-start.57 = (bf16[1,128,2048]{2,1,0:T(8,128)(2,1)S(1)}, bf16[1,128,2048]{2,1,0:T(8,128)(2,1)S(1)}, u32[]{:S(2)}, u32[]{:S(2)}) collective-permute-start(bf16[1,128,2048]{2,1,0:T(8,128)(2,1)S(1)} %slice.594), channel_id=1, source_target_pairs={{0,4},{1,5},{2,6},{3,7},{4,0},{5,1},{6,2},{7,3},{8,12},{9,13},{10,... | collective-permute-start | bytes 1572872 | tf_op jit(solution)/shard_map/ppermute | solution.py:378
  361.9 30.5 %collective-permute-start.38 = (bf16[1,128,2048]{2,1,0:T(8,128)(2,1)S(1)}, bf16[1,128,2048]{2,1,0:T(8,128)(2,1)S(1)}, u32[]{:S(2)}, u32[]{:S(2)}) collective-permute-start(bf16[1,128,2048]{2,1,0:T(8,128)(2,1)S(1)} %get-tuple-element.140), channel_id=1, source_target_pairs={{0,4},{1,5},{2,6},{3,7},{4,0},{5,1},{6,2},{7,3},{8,12},{9,13},{10,... | collective-permute-start | bytes 1572872 | tf_op jit(solution)/shard_map/ppermute | solution.py:378
  370.8 23.5 %collective-permute-start.35 = (bf16[1,128,2048]{2,1,0:T(8,128)(2,1)S(1)}, bf16[1,128,2048]{2,1,0:T(8,128)(2,1)S(1)}, u32[]{:S(2)}, u32[]{:S(2)}) collective-permute-start(bf16[1,128,2048]{2,1,0:T(8,128)(2,1)S(1)} %get-tuple-element.139), channel_id=1, source_target_pairs={{0,2},{1,3},{2,0},{3,1},{4,6},{5,7},{6,4},{7,5},{8,10},{9,11},{10,... | collective-permute-start | bytes 1572872 | tf_op jit(solution)/shard_map/ppermute | solution.py:378
  383.0 22.5 %collective-permute-start.59 = (bf16[1,128,2048]{2,1,0:T(8,128)(2,1)S(1)}, bf16[1,128,2048]{2,1,0:T(8,128)(2,1)S(1)}, u32[]{:S(2)}, u32[]{:S(2)}) collective-permute-start(bf16[1,128,2048]{2,1,0:T(8,128)(2,1)S(1)} %fusion.83), channel_id=1, source_target_pairs={{0,2},{1,3},{2,0},{3,1},{4,6},{5,7},{6,4},{7,5},{8,10},{9,11},{10,... | collective-permute-start | bytes 1572872 | tf_op jit(solution)/shard_map/ppermute | solution.py:378
  392.3 14.9 %collective-permute-start.56 = (bf16[1,128,2048]{2,1,0:T(8,128)(2,1)S(1)}, bf16[1,128,2048]{2,1,0:T(8,128)(2,1)S(1)}, u32[]{:S(2)}, u32[]{:S(2)}) collective-permute-start(bf16[1,128,2048]{2,1,0:T(8,128)(2,1)S(1)} %fusion.85), channel_id=1, source_target_pairs={{0,4},{1,5},{2,6},{3,7},{4,0},{5,1},{6,2},{7,3},{8,12},{9,13},{10,... | collective-permute-start | bytes 1572872 | tf_op jit(solution)/shard_map/ppermute | solution.py:378
  394.2 22.5 %collective-permute-start.32 = (bf16[1,128,2048]{2,1,0:T(8,128)(2,1)S(1)}, bf16[1,128,2048]{2,1,0:T(8,128)(2,1)S(1)}, u32[]{:S(2)}, u32[]{:S(2)}) collective-permute-start(bf16[1,128,2048]{2,1,0:T(8,128)(2,1)S(1)} %slice.597), channel_id=1, source_target_pairs={{0,2},{1,3},{2,0},{3,1},{4,6},{5,7},{6,4},{7,5},{8,10},{9,11},{10,... | collective-permute-start | bytes 1572872 | tf_op jit(solution)/shard_map/ppermute | solution.py:378
  395.0 23.5 %collective-permute-start.37 = (bf16[1,128,2048]{2,1,0:T(8,128)(2,1)S(1)}, bf16[1,128,2048]{2,1,0:T(8,128)(2,1)S(1)}, u32[]{:S(2)}, u32[]{:S(2)}) collective-permute-start(bf16[1,128,2048]{2,1,0:T(8,128)(2,1)S(1)} %slice.596), channel_id=1, source_target_pairs={{0,4},{1,5},{2,6},{3,7},{4,0},{5,1},{6,2},{7,3},{8,12},{9,13},{10,... | collective-permute-start | bytes 1572872 | tf_op jit(solution)/shard_map/ppermute | solution.py:378
  396.6 31.4 %collective-permute-start.39 = (bf16[1,128,2048]{2,1,0:T(8,128)(2,1)S(1)}, bf16[1,128,2048]{2,1,0:T(8,128)(2,1)S(1)}, u32[]{:S(2)}, u32[]{:S(2)}) collective-permute-start(bf16[1,128,2048]{2,1,0:T(8,128)(2,1)S(1)} %fusion.87), channel_id=1, source_target_pairs={{0,2},{1,3},{2,0},{3,1},{4,6},{5,7},{6,4},{7,5},{8,10},{9,11},{10,... | collective-permute-start | bytes 1572872 | tf_op jit(solution)/shard_map/ppermute | solution.py:378
  405.5 24.2 %collective-permute-start.36 = (bf16[1,128,2048]{2,1,0:T(8,128)(2,1)S(1)}, bf16[1,128,2048]{2,1,0:T(8,128)(2,1)S(1)}, u32[]{:S(2)}, u32[]{:S(2)}) collective-permute-start(bf16[1,128,2048]{2,1,0:T(8,128)(2,1)S(1)} %fusion.90), channel_id=1, source_target_pairs={{0,4},{1,5},{2,6},{3,7},{4,0},{5,1},{6,2},{7,3},{8,12},{9,13},{10,... | collective-permute-start | bytes 1572872 | tf_op jit(solution)/shard_map/ppermute | solution.py:378
  411.6 49.0 %collective-permute-start.60 = (bf16[2,128,2048]{2,1,0:T(8,128)(2,1)}, bf16[2,128,2048]{2,1,0:T(8,128)(2,1)}, u32[]{:S(2)}, u32[]{:S(2)}) collective-permute-start(bf16[2,128,2048]{2,1,0:T(8,128)(2,1)} %fusion.36), channel_id=1, source_target_pairs={{0,1},{1,0},{2,3},{3,2},{4,5},{5,4},{6,7},{7,6},{8,9},{9,8},{10,11... | collective-permute-start | bytes 3145736 | tf_op jit(solution)/shard_map/ppermute | solution.py:378
  416.7 22.5 %collective-permute-start.61 = (bf16[1,128,2048]{2,1,0:T(8,128)(2,1)S(1)}, bf16[1,128,2048]{2,1,0:T(8,128)(2,1)S(1)}, u32[]{:S(2)}, u32[]{:S(2)}) collective-permute-start(bf16[1,128,2048]{2,1,0:T(8,128)(2,1)S(1)} %get-tuple-element.134), channel_id=1, source_target_pairs={{0,2},{1,3},{2,0},{3,1},{4,6},{5,7},{6,4},{7,5},{8,10},{9,11},{10,... | collective-permute-start | bytes 1572872 | tf_op jit(solution)/shard_map/ppermute | solution.py:378
  418.4 31.6 %collective-permute-start.64 = (bf16[1,128,2048]{2,1,0:T(8,128)(2,1)S(1)}, bf16[1,128,2048]{2,1,0:T(8,128)(2,1)S(1)}, u32[]{:S(2)}, u32[]{:S(2)}) collective-permute-start(bf16[1,128,2048]{2,1,0:T(8,128)(2,1)S(1)} %get-tuple-element.134), channel_id=1, source_target_pairs={{0,4},{1,5},{2,6},{3,7},{4,0},{5,1},{6,2},{7,3},{8,12},{9,13},{10,... | collective-permute-start | bytes 1572872 | tf_op jit(solution)/shard_map/ppermute | solution.py:378
  427.9 21.3 %collective-permute-start.62 = (bf16[1,128,2048]{2,1,0:T(8,128)(2,1)S(1)}, bf16[1,128,2048]{2,1,0:T(8,128)(2,1)S(1)}, u32[]{:S(2)}, u32[]{:S(2)}) collective-permute-start(bf16[1,128,2048]{2,1,0:T(8,128)(2,1)S(1)} %get-tuple-element.133), channel_id=1, source_target_pairs={{0,2},{1,3},{2,0},{3,1},{4,6},{5,7},{6,4},{7,5},{8,10},{9,11},{10,... | collective-permute-start | bytes 1572872 | tf_op jit(solution)/shard_map/ppermute | solution.py:378
  429.7 21.2 %collective-permute-start.65 = (bf16[1,128,2048]{2,1,0:T(8,128)(2,1)S(1)}, bf16[1,128,2048]{2,1,0:T(8,128)(2,1)}, u32[]{:S(2)}, u32[]{:S(2)}) collective-permute-start(bf16[1,128,2048]{2,1,0:T(8,128)(2,1)S(1)} %get-tuple-element.133), channel_id=1, source_target_pairs={{0,4},{1,5},{2,6},{3,7},{4,0},{5,1},{6,2},{7,3},{8,12},{9,13},{10,... | collective-permute-start | bytes 1572872 | tf_op jit(solution)/shard_map/ppermute | solution.py:378
  450.1 19.8 %collective-permute-start.63 = (bf16[2,128,2048]{2,1,0:T(8,128)(2,1)}, bf16[2,128,2048]{2,1,0:T(8,128)(2,1)}, u32[]{:S(2)}, u32[]{:S(2)}) collective-permute-start(bf16[2,128,2048]{2,1,0:T(8,128)(2,1)} %constant_dynamic-update-slice_fusion.18), channel_id=1, source_target_pairs={{0,1},{1,0},{2,3},{3,2},{4,5},{5,4},{6,7},{7,6},{8,9},{9,8},{10,11... | collective-permute-start | bytes 3145736 | tf_op jit(solution)/shard_map/ppermute | solution.py:378
  452.8 21.7 %collective-permute-start.66 = (bf16[2,128,2048]{2,1,0:T(8,128)(2,1)}, bf16[2,128,2048]{2,1,0:T(8,128)(2,1)}, u32[]{:S(2)}, u32[]{:S(2)}) collective-permute-start(bf16[2,128,2048]{2,1,0:T(8,128)(2,1)} %constant_dynamic-update-slice_fusion.20), channel_id=1, source_target_pairs={{0,1},{1,0},{2,3},{3,2},{4,5},{5,4},{6,7},{7,6},{8,9},{9,8},{10,11... | collective-permute-start | bytes 3145736 | tf_op jit(solution)/shard_map/ppermute | solution.py:378
  455.4 260.0 %all-reduce.9.cloned.1.call-start = ((), (), s32[]{:S(2)}) async-start(), calls=%async_computation.1 | async-start | bytes 2097152 | tf_op jit(solution)/shard_map/psum | solution.py:509
  525.4 136.8 %collective-permute-start.71 = (bf16[2,128,2048]{2,1,0:T(8,128)(2,1)}, bf16[2,128,2048]{2,1,0:T(8,128)(2,1)}, u32[]{:S(2)}, u32[]{:S(2)}) collective-permute-start(bf16[2,128,2048]{2,1,0:T(8,128)(2,1)} %bitcast.93), channel_id=1, source_target_pairs={{0,1},{1,0},{2,3},{3,2},{4,5},{5,4},{6,7},{7,6},{8,9},{9,8},{10,11... | collective-permute-start | bytes 3145736 | tf_op jit(solution)/shard_map/ppermute | solution.py:378
  529.4 16.3 %collective-permute-start.74 = (bf16[2,128,2048]{2,1,0:T(8,128)(2,1)}, bf16[2,128,2048]{2,1,0:T(8,128)(2,1)}, u32[]{:S(2)}, u32[]{:S(2)}) collective-permute-start(bf16[2,128,2048]{2,1,0:T(8,128)(2,1)} %bitcast.98), channel_id=1, source_target_pairs={{0,1},{1,0},{2,3},{3,2},{4,5},{5,4},{6,7},{7,6},{8,9},{9,8},{10,11... | collective-permute-start | bytes 3145736 | tf_op jit(solution)/shard_map/ppermute | solution.py:378
  529.4 137.7 %collective-permute-start.73 = (bf16[2,128,2048]{2,1,0:T(8,128)(2,1)}, bf16[2,128,2048]{2,1,0:T(8,128)(2,1)}, u32[]{:S(2)}, u32[]{:S(2)}) collective-permute-start(bf16[2,128,2048]{2,1,0:T(8,128)(2,1)} %bitcast.95), channel_id=1, source_target_pairs={{0,1},{1,0},{2,3},{3,2},{4,5},{5,4},{6,7},{7,6},{8,9},{9,8},{10,11... | collective-permute-start | bytes 3145736 | tf_op jit(solution)/shard_map/ppermute | solution.py:378
  533.1 192.7 %collective-permute-start.70 = (bf16[2,128,2048]{2,1,0:T(8,128)(2,1)}, bf16[2,128,2048]{2,1,0:T(8,128)(2,1)}, u32[]{:S(2)}, u32[]{:S(2)}) collective-permute-start(bf16[2,128,2048]{2,1,0:T(8,128)(2,1)} %bitcast.90), channel_id=1, source_target_pairs={{0,1},{1,0},{2,3},{3,2},{4,5},{5,4},{6,7},{7,6},{8,9},{9,8},{10,11... | collective-permute-start | bytes 3145736 | tf_op jit(solution)/shard_map/ppermute | solution.py:378
  548.8 171.3 %collective-permute-start.78 = (bf16[1,128,2048]{2,1,0:T(8,128)(2,1)}, bf16[1,128,2048]{2,1,0:T(8,128)(2,1)}, u32[]{:S(2)}, u32[]{:S(2)}) collective-permute-start(bf16[1,128,2048]{2,1,0:T(8,128)(2,1)} %get-tuple-element.132), channel_id=1, source_target_pairs={{0,4},{1,5},{2,6},{3,7},{4,0},{5,1},{6,2},{7,3},{8,12},{9,13},{10,... | collective-permute-start | bytes 1572872 | tf_op jit(solution)/shard_map/ppermute | solution.py:378
  662.2 180.2 %all-reduce.11.cloned.1.call-start = ((), (), s32[]{:S(2)}) async-start(), calls=%async_computation.2 | async-start | bytes 6291456 | tf_op jit(solution)/shard_map/psum | solution.py:509
  665.1 62.3 %collective-permute-start.72 = (bf16[1,128,2048]{2,1,0:T(8,128)(2,1)}, bf16[1,128,2048]{2,1,0:T(8,128)(2,1)}, u32[]{:S(2)}, u32[]{:S(2)}) collective-permute-start(bf16[1,128,2048]{2,1,0:T(8,128)(2,1)} %slice.593), channel_id=1, source_target_pairs={{0,2},{1,3},{2,0},{3,1},{4,6},{5,7},{6,4},{7,5},{8,10},{9,11},{10,... | collective-permute-start | bytes 1572872 | tf_op jit(solution)/shard_map/ppermute | solution.py:378
  666.6 56.2 %collective-permute-start.75 = (bf16[1,128,2048]{2,1,0:T(8,128)(2,1)}, bf16[1,128,2048]{2,1,0:T(8,128)(2,1)}, u32[]{:S(2)}, u32[]{:S(2)}) collective-permute-start(bf16[1,128,2048]{2,1,0:T(8,128)(2,1)} %get-tuple-element.131), channel_id=1, source_target_pairs={{0,2},{1,3},{2,0},{3,1},{4,6},{5,7},{6,4},{7,5},{8,10},{9,11},{10,... | collective-permute-start | bytes 1572872 | tf_op jit(solution)/shard_map/ppermute | solution.py:378
  670.9 56.5 %collective-permute-start.77 = (bf16[1,128,2048]{2,1,0:T(8,128)(2,1)}, bf16[1,128,2048]{2,1,0:T(8,128)(2,1)}, u32[]{:S(2)}, u32[]{:S(2)}) collective-permute-start(bf16[1,128,2048]{2,1,0:T(8,128)(2,1)} %slice.592), channel_id=1, source_target_pairs={{0,4},{1,5},{2,6},{3,7},{4,0},{5,1},{6,2},{7,3},{8,12},{9,13},{10,... | collective-permute-start | bytes 1572872 | tf_op jit(solution)/shard_map/ppermute | solution.py:378
  (107 other events, 1000.2 us)
Sparse Core Ops, SparseCore 0:
  331.2 112.0 all-reduce.6
  455.5 206.5 all-reduce.12
  664.5 50.7 all-reduce.8
  720.1 122.1 all-reduce.10

commit v2 on v1

--- a/solution.py
+++ b/solution.py
@@ -93,12 +93,12 @@
         vim_ref[pole : pole + 1, :] = jnp.sum(hre * wim + him * wre, axis=0, keepdims=True)
 
 
-def load_padded(me, parts, pad):
-    blocks, _, rows, _ = parts[0].shape
+def load_padded(parts, pad):
     for index, part in enumerate(parts):
-        pad[index, 0:8, :] = jnp.zeros((8, pad.shape[2]), f32)
+        blocks, _, rows, chans = part.shape
+        pad[index, 0:8, :] = jnp.zeros((8, chans), f32)
         for block in range(blocks):
-            pad[index, 8 + block * rows : 8 + (block + 1) * rows, :] = part[me ^ block, 0].astype(f32)
+            pad[index, 8 + block * rows : 8 + (block + 1) * rows, :] = part[block, 0]
 
 
 def short_rows(pad, taps, index, start, count):
@@ -111,12 +111,12 @@
 
 def mixer_kernel(
     me_ref, q_ref, k_ref, v_ref, taps_ref, skip_ref, filt_ref, dft_ref, inv_ref,
-    gated_ref, resp_ref, spec_ref, pad, mixed, product, conv,
+    gated_ref, ordered_ref, resp_ref, spec_ref, pad, mixed, product, conv,
 ):
     me = me_ref[0]
     blocks, _, rows, chans = q_ref.shape
     length = blocks * rows
-    load_padded(me, (q_ref, k_ref, v_ref), pad)
+    load_padded((q_ref, k_ref, v_ref), pad)
     taps = taps_ref[...]
     skip = skip_ref[...]
     for block in range(blocks):
@@ -138,18 +138,19 @@
         response = conv[start : start + rows, :] + skip * mixed[start : start + rows, :].astype(f32)
         resp_ref[0, start : start + rows, :] = response
         query = short_rows(pad, taps, 0, start, rows)
-        gated_ref[me ^ block, 0] = (query * response).astype(bf16)
+        gated = (query * response).astype(bf16)
+        gated_ref[me ^ block, 0] = gated
+        ordered_ref[block, 0] = gated
 
 
 def mixer_back_kernel(
-    me_ref, gg_ref, q_ref, k_ref, v_ref, resp_ref, spec_ref, taps_ref, skip_ref, filt_ref, dft_ref, inv_ref,
+    gg_ref, q_ref, k_ref, v_ref, resp_ref, spec_ref, taps_ref, skip_ref, filt_ref, dft_ref, inv_ref,
     gproj_ref, gtaps_ref, gskip_ref, gfilt_ref, pad, late, response_grad, grad_conv, spectrum, product, lags, conv,
 ):
-    me = me_ref[0]
     sequence = pl.program_id(0)
     blocks, _, rows, chans = q_ref.shape
     length = blocks * rows
-    load_padded(me, (q_ref, k_ref, v_ref), pad)
+    load_padded((q_ref, k_ref, v_ref), pad)
     taps = taps_ref[...]
     skip = skip_ref[...]
 
@@ -164,7 +165,7 @@
     for block in range(blocks):
         start = block * rows
         at = slice(start, start + rows)
-        incoming = gg_ref[me ^ block, 0].astype(f32)
+        incoming = gg_ref[block, 0].astype(f32)
         query = short_rows(pad, taps, 0, start, rows)
         key = short_rows(pad, taps, 1, start, rows)
         value = short_rows(pad, taps, 2, start, rows)
@@ -207,7 +208,7 @@
             for back in (1, 2):
                 tap = taps[3 * back + index : 3 * back + index + 1]
                 total = total + tap * late[index, start + back : start + back + rows, :]
-            gproj_ref[me ^ block, 0, :, index * chans : (index + 1) * chans] = total.astype(bf16)
+            gproj_ref[index, block, 0] = total.astype(bf16)
             for back in range(3):
                 shifted = pad[index, 8 + start - back : 8 + start - back + rows, :]
                 sums[3 * back + index] = sums[3 * back + index] + jnp.sum(
@@ -224,6 +225,10 @@
 
 def whole(shape):
     return pl.BlockSpec(shape, lambda *_: (0,) * len(shape), pipeline_mode=pl.Buffered(1))
+
+
+def cost(flops, nbytes):
+    return pl.CostEstimate(flops=flops, bytes_accessed=nbytes, transcendentals=0)
 
 
 def params():
@@ -273,6 +278,7 @@
     blocks, seqs, rows, triple = proj.shape
     chans = triple // 3
     length = blocks * rows
+    fixed = (taps9, skip, filt_spec, dft, inverse)
 
     def part(index):
         return pl.BlockSpec((blocks, 1, rows, chans), lambda s, m: (0, s, 0, index))
@@ -282,10 +288,10 @@
         grid_spec=pltpu.PrefetchScalarGridSpec(
             num_scalar_prefetch=1,
             grid=(seqs,),
-            in_specs=[part(0), part(1), part(2), whole(taps9.shape), whole(skip.shape),
-                      whole(filt_spec.shape), whole(dft.shape), whole(inverse.shape)],
+            in_specs=[part(0), part(1), part(2)] + [whole(op.shape) for op in fixed],
             out_specs=[
-                pl.BlockSpec((blocks, 1, rows, chans), lambda s, m: (0, s, 0, 0)),
+                part(0),
+                part(0),
                 pl.BlockSpec((1, length, chans), lambda s, m: (s, 0, 0)),
                 pl.BlockSpec((1, 2 * length, chans), lambda s, m: (s, 0, 0)),
             ],
@@ -298,122 +304,343 @@
         ),
         out_shape=[
             jax.ShapeDtypeStruct((blocks, seqs, rows, chans), bf16),
+            jax.ShapeDtypeStruct((blocks, seqs, rows, chans), bf16),
             jax.ShapeDtypeStruct((seqs, length, chans), f32),
             jax.ShapeDtypeStruct((seqs, 2 * length, chans), f32),
         ],
         compiler_params=params(),
+        cost_estimate=cost(1000, 1000),
         name="mixer_forward",
-    )(me, proj, proj, proj, taps9, skip, filt_spec, dft, inverse)
-
-
-def mixer_back(me, grad_gated, proj, response, spec, taps9, skip, filt_spec, dft, inverse):
+    )(me, proj, proj, proj, *fixed)
+
+
+def mixer_back(grad_gated, proj, response, spec, taps9, skip, filt_spec, dft, inverse):
     blocks, seqs, rows, triple = proj.shape
     chans = triple // 3
     length = blocks * rows
+    fixed = (taps9, skip, filt_spec, dft, inverse)
 
     def part(index):
-        return pl.BlockSpec((blocks, 1, rows, chans), lambda s, m: (0, s, 0, index))
+        return pl.BlockSpec((blocks, 1, rows, chans), lambda s: (0, s, 0, index))
 
     return pl.pallas_call(
         mixer_back_kernel,
-        grid_spec=pltpu.PrefetchScalarGridSpec(
-            num_scalar_prefetch=1,
-            grid=(seqs,),
-            in_specs=[part(0), part(0), part(1), part(2),
-                      pl.BlockSpec((1, length, chans), lambda s, m: (s, 0, 0)),
-                      pl.BlockSpec((1, 2 * length, chans), lambda s, m: (s, 0, 0)),
-                      whole(taps9.shape), whole(skip.shape),
-                      whole(filt_spec.shape), whole(dft.shape), whole(inverse.shape)],
-            out_specs=[
-                pl.BlockSpec((blocks, 1, rows, triple), lambda s, m: (0, s, 0, 0)),
-                whole(taps9.shape),
-                whole(skip.shape),
-                whole((length, chans)),
-            ],
-            scratch_shapes=[
-                pltpu.VMEM((3, length + 8, chans), f32),
-                pltpu.VMEM((3, length + 8, chans), f32),
-                pltpu.VMEM((length, chans), f32),
-                pltpu.VMEM((length, chans), bf16),
-                pltpu.VMEM((2 * length, chans), f32),
-                pltpu.VMEM((2 * length, chans), bf16),
-                pltpu.VMEM((2 * length, chans), f32),
-                pltpu.VMEM((length, chans), f32),
-            ],
-        ),
+        grid=(seqs,),
+        in_specs=[part(0), part(0), part(1), part(2)]
+        + [
+            pl.BlockSpec((1, length, chans), lambda s: (s, 0, 0)),
+            pl.BlockSpec((1, 2 * length, chans), lambda s: (s, 0, 0)),
+        ]
+        + [whole(op.shape) for op in fixed],
+        out_specs=[
+            pl.BlockSpec((3, blocks, 1, rows, chans), lambda s: (0, 0, s, 0, 0)),
+            whole(taps9.shape),
+            whole(skip.shape),
+            whole((length, chans)),
+        ],
+        scratch_shapes=[
+            pltpu.VMEM((3, length + 8, chans), f32),
+            pltpu.VMEM((3, length + 8, chans), f32),
+            pltpu.VMEM((length, chans), f32),
+            pltpu.VMEM((length, chans), bf16),
+            pltpu.VMEM((2 * length, chans), f32),
+            pltpu.VMEM((2 * length, chans), bf16),
+            pltpu.VMEM((2 * length, chans), f32),
+            pltpu.VMEM((length, chans), f32),
+        ],
         out_shape=[
-            jax.ShapeDtypeStruct((blocks, seqs, rows, triple), bf16),
+            jax.ShapeDtypeStruct((3, blocks, seqs, rows, chans), bf16),
             jax.ShapeDtypeStruct(taps9.shape, f32),
             jax.ShapeDtypeStruct(skip.shape, f32),
             jax.ShapeDtypeStruct((length, chans), f32),
         ],
         compiler_params=params(),
+        cost_estimate=cost(1000, 1000),
         name="mixer_backward",
-    )(me, grad_gated, proj, proj, proj, response, spec, taps9, skip, filt_spec, dft, inverse)
+    )(grad_gated, proj, proj, proj, response, spec, *fixed)
+
+
+def arrived(refs, counts, step, use):
+    at = 0
+    for index, count in enumerate(counts):
+        block = refs[at : at + count]
+        at += count
+
+        @pl.when(step == index)
+        def _(block=block):
+            rows = [ref[...].reshape(-1, ref.shape[-1]) for ref in block]
+            use(rows[0] if len(rows) == 1 else jnp.concatenate(rows, axis=0))
+
+
+def project_kernel(counts, given, me_ref, *refs):
+    pieces = sum(counts)
+    weight_ref = refs[pieces]
+    out_ref, rows_ref = refs[pieces + 1 + given :]
+    chans = weight_ref.shape[2]
+
+    def use(rows):
+        rows_ref[0] = rows
+        for part in range(3):
+            out_ref[0, :, part * chans : (part + 1) * chans] = dot32(rows, weight_ref[part])
+
+    arrived(refs, counts, pl.program_id(0), use)
+
+
+def hidden_back_kernel(counts, given, me_ref, *refs):
+    pieces = sum(counts)
+    weight_ref = refs[pieces]
+    out_ref, rows_ref = refs[pieces + 1 + given :]
+
+    def use(rows):
+        rows_ref[0] = rows
+        out_ref[0] = contract_cols(rows, weight_ref[...])
+
+    arrived(refs, counts, pl.program_id(0), use)
+
+
+def feed_kernel(counts, given, me_ref, *refs):
+    pieces = sum(counts)
+    gate_w, up_w, back_ref = refs[pieces : pieces + 3]
+    hidden_ref, ggate_ref, gup_ref, rows_ref = refs[pieces + 3 + given :]
+
+    def use(rows):
+        rows_ref[0] = rows
+        gate = contract_cols(rows, gate_w[...])
+        up = contract_cols(rows, up_w[...])
+        sig = jax.nn.sigmoid(gate)
+        silu = gate * sig
+        hidden_ref[0] = (silu * up).astype(bf16)
+        back = back_ref[0]
+        ggate_ref[0] = (back * up * sig * (1.0 + gate * (1.0 - sig))).astype(bf16)
+        gup_ref[0] = (back * silu).astype(bf16)
+
+    arrived(refs, counts, pl.program_id(0), use)
+
+
+def on_arrival(kernel, me, group, start, total, fixed, per_block, outputs, filled):
+    pieces = [piece for block in group for piece in block]
+    rows = sum(piece.shape[0] * piece.shape[1] for piece in group[0])
+
+    def at_index(i, m):
+        return (m[0] ^ (start + i), 0, 0)
+
+    operands = [me, *pieces, *fixed, *per_block, *filled]
+    first = len(operands) - len(filled)
+    return pl.pallas_call(
+        partial(kernel, [len(block) for block in group], len(filled)),
+        grid_spec=pltpu.PrefetchScalarGridSpec(
+            num_scalar_prefetch=1,
+            grid=(len(group),),
+            in_specs=[whole(op.shape) for op in (*pieces, *fixed)]
+            + [pl.BlockSpec((1,) + op.shape[1:], at_index) for op in per_block]
+            + [pl.BlockSpec(memory_space=pl.ANY)] * len(filled),
+            out_specs=[pl.BlockSpec((1, rows, width), at_index) for width, _ in outputs],
+        ),
+        out_shape=[jax.ShapeDtypeStruct((total, rows, width), dtype) for width, dtype in outputs],
+        input_output_aliases={first + i: i for i in range(len(filled))},
+        compiler_params=params(),
+        cost_estimate=cost(1000, 1000),
+        name=kernel.__name__.removesuffix("_kernel"),
+    )(*operands)
+
+
+def sum_products(rights, transposed):
+    def kernel(*refs):
+        count = len(rights)
+        dot = contract_cols if transposed else dot32
+        total = dot(refs[0][0], refs[count][...])
+        for left, right in zip(refs[1:count], refs[count + 1 : 2 * count]):
+            total = total + dot(left[0], right[...])
+        refs[2 * count][0] = total.astype(bf16)
+
+    def call(*lefts):
+        blocks, rows, depth = lefts[0].shape
+        width = rights[0].shape[0 if transposed else 1]
+        return pl.pallas_call(
+            kernel,
+            grid=(blocks,),
+            in_specs=[pl.BlockSpec((1, rows, depth), lambda i: (i, 0, 0))] * len(lefts)
+            + [whole(right.shape) for right in rights],
+            out_specs=pl.BlockSpec((1, rows, width), lambda i: (i, 0, 0)),
+            out_shape=jax.ShapeDtypeStruct((blocks, rows, width), bf16),
+            compiler_params=params(),
+            cost_estimate=cost(1000, 1000),
+            name="sum_products",
+        )(*lefts, *rights)
+
+    return call
+
+
+def gather_whole(block):
+    return lax.all_gather(block, "mp", axis=0)
+
+
+def scatter_whole(partial_sums):
+    return lax.psum_scatter(partial_sums, "mp", scatter_dimension=0).astype(f32)
+
+
+def together(*values):
+    return lax.optimization_barrier(values)
+
+
+def together(*values):
+    return lax.optimization_barrier(values)
+
+
+class WholeGather:
+    def __init__(self, block):
+        blocks = gather_whole(block)
+        self.blocks = [(blocks[i],) for i in range(blocks.shape[0])]
+
+    def tie(self, names, *values):
+        return values
+
+    def reach(self):
+        pass
+
+    def near(self):
+        return self.blocks
+
+    def side(self):
+        return []
+
+    def far(self):
+        return []
 
 
 class Plain:
-    def __init__(self, size):
-        self.size = size
+    def __init__(self):
+        self.parts = []
+
+    def counts(self, size):
+        return (size, 0, 0)
 
     def origin(self):
         return jnp.zeros((1,), jnp.int32)
 
     def gather(self, block):
-        return [lax.all_gather(block, "mp", axis=0)]
-
-    def scatter(self, groups):
-        (partial_sums,) = groups
-        return lax.psum_scatter(partial_sums.astype(bf16), "mp", scatter_dimension=0).astype(f32)
+        return WholeGather(block)
+
+    def scatter(self, groups, given, compute):
+        return scatter_whole(groups[0]), compute(given)
+
+    def sum_mp(self, part):
+        return lax.psum(part, "mp")
+
+    def push(self, part):
+        self.parts.append(part)
+
+    def hop(self, *values):
+        return values
+
+    def sums(self):
+        return [lax.psum(part, "dp") for part in self.parts]
+
+
+def swap(block, bit):
+    return lax.ppermute(block, "mp", [(i, i ^ bit) for i in range(8)])
+
+
+class SquareGather:
+    def __init__(self, block):
+        cut = block.shape[0] // 2
+        low, high = block[:cut], block[cut:]
+        x_low, y_high = swap(low, 2), swap(high, 4)
+        sibling = swap(block, 1)
+        low, high, sibling = together(low, high, sibling)
+        x_high, y_low = swap(high, 2), swap(low, 4)
+        self.here = {"near": (block, sibling), "lead": (x_low, y_high), "rest": (x_high, y_low)}
+
+    def tie(self, names, *values):
+        held, values = together([self.here[name] for name in names], values)
+        self.here.update(zip(names, held))
+        return values
+
+    def reach(self):
+        x_low, y_high = self.here["lead"]
+        self.here["far"] = (swap(x_low, 4), swap(y_high, 2))
+
+    def near(self):
+        return [(block,) for block in self.here["near"]]
+
+    def side(self):
+        (x_low, y_high), (x_high, y_low) = self.here["lead"], self.here["rest"]
+        return self.twins((x_low, x_high)) + self.twins((y_low, y_high))
+
+    def far(self):
+        return self.twins(self.here["far"])
+
+    def twins(self, halves):
+        return [halves, tuple(swap(half, 1) for half in halves)]
 
 
 class Square:
     def __init__(self):
-        self.size = 8
+        self.queue, self.half, self.total, self.done = [], None, None, []
+
+    def counts(self, size):
+        return (2, 4, 2)
 
     def origin(self):
         return lax.axis_index("mp").astype(jnp.int32).reshape(1)
 
-    def swap(self, block, bit):
-        return lax.ppermute(block, "mp", [(i, i ^ bit) for i in range(8)])
-
     def gather(self, block):
-        half = block.shape[0] // 2
-        low, high = block[:half], block[half:]
-        x_low, y_high = self.swap(low, 2), self.swap(high, 4)
-        sibling = self.swap(block, 1)
-        x_high, y_low = self.swap(high, 2), self.swap(low, 4)
-        d_low, d_high = self.swap(x_low, 4), self.swap(y_high, 2)
-        x_all = jnp.concatenate([x_low, x_high], axis=0)
-        y_all = jnp.concatenate([y_low, y_high], axis=0)
-        d_all = jnp.concatenate([d_low, d_high], axis=0)
-        near = jnp.stack([block, sibling], axis=0)
-        side = jnp.stack([x_all, self.swap(x_all, 1), y_all, self.swap(y_all, 1)], axis=0)
-        far = jnp.stack([d_all, self.swap(d_all, 1)], axis=0)
-        return [near, side, far]
-
-    def scatter(self, groups):
+        return SquareGather(block)
+
+    def scatter(self, groups, given, compute):
         near, side, far = groups
         half = near.shape[1] // 2
 
         def both(mine, other):
-            return mine.astype(f32) + self.swap(other, 1).astype(f32)
+            return mine.astype(f32) + swap(other, 1).astype(f32)
 
         far_sum = both(far[0], far[1])
         far_low, far_high = far_sum[:half].astype(bf16), far_sum[half:].astype(bf16)
-        from_far_low, from_far_high = self.swap(far_low, 2), self.swap(far_high, 4)
+        from_far_low, from_far_high = swap(far_low, 2), swap(far_high, 4)
         x_sum = both(side[0], side[1])
         y_sum = both(side[2], side[3])
-        own_low_x = self.swap(x_sum[:half].astype(bf16), 2)
-        own_high_y = self.swap(y_sum[half:].astype(bf16), 4)
+        own_low_x = swap(x_sum[:half].astype(bf16), 2)
+        own_high_y = swap(y_sum[half:].astype(bf16), 4)
+        own = both(near[0], near[1])
+        own, x_sum, y_sum, given = together(own, x_sum, y_sum, given)
+        beside = compute(given)
+        from_far_low, from_far_high, beside = together(from_far_low, from_far_high, beside)
         y_low = (y_sum[:half] + from_far_low.astype(f32)).astype(bf16)
         x_high = (x_sum[half:] + from_far_high.astype(f32)).astype(bf16)
-        own_low_y = self.swap(y_low, 4)
-        own_high_x = self.swap(x_high, 2)
-        own = both(near[0], near[1])
+        own_low_y = swap(y_low, 4)
+        own_high_x = swap(x_high, 2)
         low = own[:half] + own_low_x.astype(f32) + own_low_y.astype(f32)
         high = own[half:] + own_high_y.astype(f32) + own_high_x.astype(f32)
-        return jnp.concatenate([low, high], axis=0)
+        return jnp.concatenate([low, high], axis=0), beside
+
+    def sum_mp(self, part):
+        for bit in (1, 2, 4):
+            part = part + swap(part, bit)
+        return part
+
+    def push(self, part):
+        self.queue.append((part, lax.ppermute(part, "dp", [(0, 1), (3, 2)])))
+
+    def hop(self, *values):
+        part = inward = across = outward = None
+        if self.queue:
+            part, inward = self.queue.pop(0)
+        if self.total is not None:
+            outward = lax.ppermute(self.total, "dp", [(1, 0), (2, 3)])
+        if self.half is not None:
+            across = lax.ppermute(self.half, "dp", [(1, 2), (2, 1)])
+        inward, across, outward, values = together(inward, across, outward, values)
+        if outward is not None:
+            place = lax.axis_index("dp")
+            self.done.append(jnp.where((place == 0) | (place == 3), outward, self.total))
+        self.total = None if across is None else (self.half.astype(f32) + across.astype(f32)).astype(bf16)
+        self.half = None if inward is None else (part.astype(f32) + inward.astype(f32)).astype(bf16)
+        return values
+
+    def sums(self):
+        while self.queue or self.half is not None or self.total is not None:
+            self.hop()
+        return self.done
 
 
 def local(
@@ -424,8 +651,9 @@
     seqs = micro * per_dev
     chans = in_proj.shape[2]
     hidden_units = gate_proj.shape[1]
-    length = rows * links.size
-    in_flat = in_proj.reshape(width, 3 * chans)
+    length = rows * lax.axis_size("mp")
+    in_parts = in_proj.transpose(1, 0, 2)
+    gate_t, up_t = gate_proj.T, up_proj.T
     table = dft_matrix(length)
     dft = jnp.asarray(table, bf16)
     inverse = jnp.asarray(table.T / length, bf16)
@@ -449,9 +677,7 @@
     rows_in = by_sequence(tokens).astype(f32)
     scale_in = row_scale(rows_in)
     normed = (rows_in * scale_in * norm_gain).astype(bf16)
-    normed_groups = links.gather(normed)
-    grad_final = by_sequence(cotangent).astype(f32) * valid
-    grad_final_all = flat(jnp.concatenate(links.gather(grad_final.astype(bf16)), axis=0))
+    coming = links.gather(normed)
 
     high = (STEP * jnp.arange(length // STEP)).astype(f32)[:, None, None]
     low = jnp.arange(STEP).astype(f32)[None, :, None]
@@ -465,117 +691,167 @@
         decay_low * jnp.sin(turn_low),
     )
     filt_spec = make_filter(tables, residue_t, dft)
-
-    proj = jnp.concatenate(
-        [grouped(dot32(flat(group), in_flat), group) for group in normed_groups], axis=0
-    )
+    grad_final = by_sequence(cotangent).astype(f32) * valid
+    grad_final_low = grad_final.astype(bf16)
+    filt_spec, grad_final_low = coming.tie(["lead"], filt_spec, grad_final_low)
+    coming.reach()
+
+    blocks = lax.axis_size("mp")
+    counts = links.counts(blocks)
+    starts = [sum(counts[:i]) for i in range(len(counts))]
+
+    def arrive(kernel, group, number, fixed, per_block, outputs, filled):
+        if not group:
+            return filled
+        return on_arrival(kernel, me, group, starts[number], blocks, fixed, per_block, outputs, filled)
+
+    def projected(group, number, filled):
+        return arrive(project_kernel, group, number, (in_parts,), (), ((3 * chans, f32), (width, bf16)), filled)
+
+    filled = projected(coming.near(), 0, ())
+    (filled,) = coming.tie(["lead", "rest"], filled)
+    filled = projected(coming.side(), 1, filled)
+    filled, grad_final_low = coming.tie(["far"], filled, grad_final_low)
+    grad_coming = links.gather(grad_final_low)
+    proj, normed_all = projected(coming.far(), 2, filled)
+    (proj,) = grad_coming.tie(["lead"], proj)
+    grad_coming.reach()
+    proj = proj.reshape(blocks, seqs, rows, 3 * chans)
     taps9 = short_taps.reshape(9, chans)
     skip = conv_skip.reshape(1, chans)
-    gated, response, spec = mixer(me, proj, taps9, skip, filt_spec, dft, inverse)
-
-    counts = [group.shape[0] for group in normed_groups]
-    starts = [sum(counts[:i]) for i in range(len(counts))]
-
-    def product_groups(left, right, dot):
-        out = [None] * len(counts)
-        for i in reversed(range(len(counts))):
-            part = left[starts[i] : starts[i] + counts[i]]
-            out[i] = grouped(dot(flat(part), right).astype(bf16), part)
-        return out
-
-    second = rows_in + links.scatter(product_groups(gated, out_proj, dot32))
+    gated, gated_ordered, response, spec = mixer(me, proj, taps9, skip, filt_spec, dft, inverse)
+    (gated,) = grad_coming.tie(["lead", "rest"], gated)
+
+    mixed_groups = [None] * len(counts)
+    for i in reversed(range(len(counts))):
+        if counts[i]:
+            part = gated[starts[i] : starts[i] + counts[i]]
+            mixed_groups[i] = grouped(dot32(flat(part), out_proj).astype(bf16), part)
+
+    def hidden_backed(group, number, filled):
+        return arrive(hidden_back_kernel, group, number, (down_proj,), (), ((hidden_units, f32), (width, bf16)), filled)
+
+    def beside_scatter(held):
+        near, side = held
+        return hidden_backed(side, 1, hidden_backed(near, 0, ()))
+
+    mixed_sum, filled = links.scatter(mixed_groups, (grad_coming.near(), grad_coming.side()), beside_scatter)
+    second = rows_in + mixed_sum
     scale_second = row_scale(second)
     mlp_normed = (second * scale_second * mlp_gain).astype(bf16)
-    mlp_groups = links.gather(mlp_normed)
-    gate = jnp.concatenate([dot32(flat(group), gate_proj) for group in mlp_groups], axis=0)
-    up = jnp.concatenate([dot32(flat(group), up_proj) for group in mlp_groups], axis=0)
-    sig = jax.nn.sigmoid(gate)
-    silu = gate * sig
-    hidden = (silu * up).astype(bf16)
-
-    grad_hidden = contract_cols(grad_final_all, down_proj)
-    grad_gate = (grad_hidden * up * sig * (1.0 + gate * (1.0 - sig))).astype(bf16)
-    grad_up = (grad_hidden * silu).astype(bf16)
-    mlp_all = flat(jnp.concatenate(mlp_groups, axis=0))
-    grad_down = contract_rows(hidden, grad_final_all).astype(bf16)
-    grad_gate_proj = contract_rows(mlp_all, grad_gate)
-    grad_up_proj = contract_rows(mlp_all, grad_up)
-
-    chain = [None]
-
-    def over_dp(*arrays):
-        if chain[0] is not None:
-            arrays = lax.optimization_barrier((arrays, chain[0]))[0]
-        summed = lax.psum(arrays, "dp")
-        chain[0] = summed
-        return summed
-
-    (sum_down,) = over_dp(grad_down)
-    sum_gate, sum_up = over_dp(grad_gate_proj.astype(bf16), grad_up_proj.astype(bf16))
-
-    shape4 = gated.shape[:3]
-    grad_gate4 = grad_gate.reshape(shape4 + (hidden_units,))
-    grad_up4 = grad_up.reshape(shape4 + (hidden_units,))
-    partial_groups = []
-    for start, count in zip(starts, counts):
-        gate_rows = flat(grad_gate4[start : start + count])
-        up_rows = flat(grad_up4[start : start + count])
-        both = contract_cols(gate_rows, gate_proj) + contract_cols(up_rows, up_proj)
-        partial_groups.append(both.astype(bf16).reshape((count,) + shape4[1:] + (width,)))
-    grad_mlp_normed = links.scatter(partial_groups)
+    coming = links.gather(mlp_normed)
+    filled, mlp_normed = grad_coming.tie(["far"], filled, mlp_normed) if counts[2] else (filled, mlp_normed)
+    grad_hidden, grad_final_all = hidden_backed(grad_coming.far(), 2, filled)
+    (grad_hidden,) = coming.tie(["lead"], grad_hidden)
+    coming.reach()
+
+    def fed(group, number, filled):
+        outputs = ((hidden_units, bf16),) * 3 + ((width, bf16),)
+        return arrive(feed_kernel, group, number, (gate_t, up_t), (grad_hidden,), outputs, filled)
+
+    filled = fed(coming.near(), 0, ())
+    (filled,) = coming.tie(["lead", "rest"], filled)
+    filled = fed(coming.side(), 1, filled)
+    if counts[2]:
+        (filled,) = coming.tie(["far"], filled)
+    hidden, grad_gate, grad_up, mlp_all = fed(coming.far(), 2, filled)
+
+    def weight_gradient(left, right, number=0, count=1):
+        left, right = flat(left), flat(right)
+        total = left.shape[1]
+        left = left[:, number * total // count : (number + 1) * total // count]
+        return contract_rows(left, right).astype(bf16)
+
+    def blocked(array):
+        return array.reshape(blocks, seqs, rows, array.shape[-1])
+
+    down_one, hidden, grad_gate = together(weight_gradient(hidden, grad_final_all, 0, 2), hidden, grad_gate)
+    links.push(down_one)
+    down_two = weight_gradient(hidden, grad_final_all, 1, 2)
+    mlp_back = blocked(sum_products((gate_t, up_t), False)(grad_gate, grad_up))
+    mlp_back, down_two, grad_gate = links.hop(mlp_back, down_two, grad_gate)
+    links.push(down_two)
+    grad_mlp_normed = scatter_whole(mlp_back)
+    links.push(weight_gradient(grad_gate, mlp_all, 0, 2))
+    gate_two = weight_gradient(grad_gate, mlp_all, 1, 2)
+    gate_two, hidden, grad_up = links.hop(gate_two, hidden, grad_up)
+    links.push(gate_two)
+    up_one = weight_gradient(grad_up, mlp_all, 0, 2)
+    up_one, grad_up, second = links.hop(up_one, grad_up, second)
+    links.push(up_one)
     grad_second = grad_final + norm_back(grad_mlp_normed, second, scale_second, mlp_gain)
+    grad_branch_all = gather_whole(grad_second.astype(bf16))
     gain_two = jnp.sum(grad_mlp_normed * second * scale_second, axis=(0, 1))
-
-    grad_branch_groups = links.gather(grad_second.astype(bf16))
-    grad_gated = jnp.concatenate(
-        [grouped(contract_cols(flat(group), out_proj), group) for group in grad_branch_groups], axis=0
+    up_two = weight_gradient(grad_up, mlp_all, 1, 2)
+    up_two, gain_two, hidden = links.hop(up_two, gain_two, hidden)
+    links.push(up_two)
+    mlp_part = blocked(dot32(flat(hidden), down_proj).astype(bf16))
+    mlp_part, gated_ordered, out_here = links.hop(mlp_part, gated_ordered, out_proj)
+
+    grad_gated = blocked(contract_cols(flat(grad_branch_all), out_here))
+    links.push(weight_gradient(gated_ordered, grad_branch_all))
+    grad_gated, mlp_part = links.hop(grad_gated, mlp_part)
+    mlp_out = scatter_whole(mlp_part)
+    grad_proj, grad_taps, grad_skip, grad_filt = mixer_back(
+        grad_gated, proj, response, spec, taps9, skip, filt_spec, dft, inverse
     )
-    mlp_out = links.scatter(product_groups(hidden.reshape(shape4 + (hidden_units,)), down_proj, dot32))
+    grad_parts = [part.reshape(blocks, seqs * rows, chans) for part in grad_proj]
+    grad_q = weight_gradient(normed_all, grad_parts[0])
+    links.push(grad_q)
+    grad_parts, gain_two = links.hop(grad_parts, gain_two)
+    grad_in_rows = blocked(sum_products(tuple(in_parts), True)(*grad_parts))
+    grad_k = weight_gradient(normed_all, grad_parts[1])
+    links.push(grad_k)
+    grad_v = weight_gradient(normed_all, grad_parts[2])
+    grad_in_rows, grad_v, grad_filt, mlp_out = links.hop(grad_in_rows, grad_v, grad_filt, mlp_out)
+    grad_normed = scatter_whole(grad_in_rows)
+
+    ones = jnp.ones((8, chans), bf16)
+    against = sum(
+        contract_cols(ones, (grad.astype(f32) * part.astype(f32)).astype(bf16))[0]
+        for grad, part in zip((grad_q, grad_k, grad_v), in_parts)
+    )
+    gains = links.sum_mp(jnp.stack([against / norm_gain, gain_two], axis=0))
+    pole_sum, pole_re, pole_im = pole_gradients(grad_filt, tables)
+    poles = filter_residue.shape[1]
+    small = jnp.concatenate(
+        [grad_taps, grad_skip, pole_sum, -residue_t * pole_re, -residue_t * pole_im, gains.reshape(-1, chans)], axis=0
+    )
+    small_rows = small.shape[0]
+    small = jnp.pad(small.astype(bf16), ((0, -small_rows % 32), (0, 0)))
+    links.push(jnp.concatenate([grad_v, small], axis=0))
+    (mlp_out,) = links.hop(mlp_out)
     layer_out = ((second + mlp_out) * valid).astype(bf16)
-
-    grad_branch_all = flat(jnp.concatenate(grad_branch_groups, axis=0))
-    grad_out = contract_rows(flat(gated), grad_branch_all)
-    (sum_out,) = over_dp(grad_out.astype(bf16))
-    grad_proj, grad_taps, grad_skip, grad_filt = mixer_back(
-        me, grad_gated, proj, response, spec, taps9, skip, filt_spec, dft, inverse
-    )
-    grad_normed = links.scatter(product_groups(grad_proj, in_flat, contract_cols))
-    normed_all = flat(jnp.concatenate(normed_groups, axis=0))
-    grad_in = contract_rows(normed_all, flat(grad_proj))
-    pole_sum, pole_re, pole_im = pole_gradients(grad_filt, tables)
+    layer_out, grad_second = links.hop(layer_out, grad_second)
     grad_tokens = grad_second + norm_back(grad_normed, rows_in, scale_in, norm_gain)
-    gain_one = jnp.sum(grad_normed * rows_in * scale_in, axis=(0, 1))
-
-    small = jnp.concatenate(
-        [grad_taps, grad_skip, pole_sum, -residue_t * pole_re, -residue_t * pole_im], axis=0
-    )
-    sum_in, sum_small = over_dp(grad_in.astype(bf16), small.astype(bf16))
-    sum_in, sum_small = sum_in.astype(f32), sum_small.astype(f32)
-    gains = lax.psum((gain_one, gain_two), ("dp", "mp"))
-    poles = filter_residue.shape[1]
-    pole_grads = [
-        sum_small[10 + poles * i : 10 + poles * (i + 1)].T for i in range(3)
-    ]
+    (grad_tokens,) = links.hop(by_position(grad_tokens))
+
+    sums = links.sums()
+    sum_small = sums[-1][width:].astype(f32)
+    pole_grads = [sum_small[10 + poles * i : 10 + poles * (i + 1)].T for i in range(3)]
+    gains = sum_small[10 + 3 * poles : small_rows].reshape(2, width)
+    sum_in = jnp.stack([sums[7], sums[8], sums[9][:width]], axis=0).astype(f32)
     return (
         by_position(layer_out),
-        by_position(grad_tokens),
+        grad_tokens,
         gains[0],
-        sum_in.reshape(width, 3, chans),
+        sum_in.transpose(1, 0, 2),
         sum_small[:9].reshape(3, 3, chans),
         sum_small[9],
         pole_grads[0],
         pole_grads[1],
         pole_grads[2],
-        sum_out.astype(f32),
+        sums[6].astype(f32),
         gains[1],
-        sum_gate.astype(f32),
-        sum_up.astype(f32),
-        sum_down.astype(f32),
+        jnp.concatenate(sums[2:4], axis=0).astype(f32).T,
+        jnp.concatenate(sums[4:6], axis=0).astype(f32).T,
+        jnp.concatenate(sums[:2], axis=0).astype(f32),
     )
 
 
 def solution(mesh):
-    links = Square() if mesh.shape["mp"] == 8 else Plain(mesh.shape["mp"])
+    square = mesh.shape["mp"] == 8 and mesh.shape["dp"] == 4
+    links = Square() if square else Plain()
     wide = P(None, "mp", "dp", None)
     chan = P("mp", None)
     return jax.shard_map(

time: 860 us -> 724 us (0.84)
  waiting for transfers between devices: 363 us -> 197 us
  Pallas kernels: 57 us -> 159 us
  starting transfers between devices: 57.6 us -> 125 us
  blocking collectives: 61.4 us -> 0 us
  local copies, waits for them, and re-layouts: 99.4 us -> 40.1 us
  matrix products: 135 us -> 85.5 us
  other arithmetic: 65.4 us -> 89.1 us
    psum x4 -> x0, waiting for transfers between devices: 176 us -> none  [over_dp(): summed = lax.psum(arrays, 'dp')]
    ppermute x0 -> x30, waiting for transfers between devices: none -> 151 us  [the longest x10 78.7 us: push(): self.queue.append((part, lax.ppermute(part, 'dp', [(0, 1), (3, 2)])))]
    ppermute x80 -> x52, waiting for transfers between devices: 187 us -> 46.6 us  [swap(): return lax.ppermute(block, 'mp', [(i, i ^ bit) for i in range(8)])]
    pallas_call x1 -> x12, Pallas kernels: 24.9 us -> 126 us  [the longest x9 70.7 us: on_arrival(): pl.pallas_call(partial(kernel, [len(block) for block in group], len(fille...]
    ppermute x0 -> x30, starting transfers between devices: none -> 90.3 us  [the longest x10 62.5 us: push(): self.queue.append((part, lax.ppermute(part, 'dp', [(0, 1), (3, 2)])))]
    psum x2 -> x0, blocking collectives: 61.4 us -> none  [the longest x1 42.2 us: local(): gains = lax.psum((gain_one, gain_two), ('dp', 'mp'))]
    dot_general x13 -> x4, matrix products: 54.4 us -> 11.5 us  [contract_cols(): lax.dot_general(left, right, (((1,), (1,)), ((), ())), preferred_element_...]
    unnamed x213 -> x206, local copies, waits for them, and re-layouts: 65.4 us -> 24.5 us
  transfers between devices with their start and end apart: 84 -> 86, of which waited for: 33 -> 38; matrix products, arithmetic and copies ran while one was open for 23% -> 24% of each run, Pallas kernels for 7% -> 21%
where the time goes in v2:
time: 724 us; the launch traced here: 712 us
  waiting for transfers between devices  197 us (27%)
  Pallas kernels  159 us (22%)
  starting transfers between devices  125 us (17%)
  other arithmetic  89.1 us (12%)
  matrix products  85.5 us (12%)
  local copies, waits for them, and re-layouts  40.1 us (6%)
  between operations  15.8 us (2%)
    ppermute x10, waiting for transfers between devices, push(): self.queue.append((part, lax.ppermute(part, 'dp', [(0, 1), (3, 2)])))  78.7 us
    ppermute x10, waiting for transfers between devices, hop(): outward = lax.ppermute(self.total, 'dp', [(1, 0), (2, 3)])  71.9 us
    pallas_call x9, Pallas kernels, on_arrival(): pl.pallas_call(partial(kernel, [len(block) for block in group], len(fille...  70.7 us
    ppermute x10, starting transfers between devices, push(): self.queue.append((part, lax.ppermute(part, 'dp', [(0, 1), (3, 2)])))  62.5 us
    dot_general x10, matrix products, contract_rows(): lax.dot_general(left, right, (((0,), (0,)), ((), ())), preferred_element_...  62.5 us
    ppermute x52, waiting for transfers between devices, swap(): return lax.ppermute(block, 'mp', [(i, i ^ bit) for i in range(8)])  46.6 us
    ppermute x52, starting transfers between devices, swap(): return lax.ppermute(block, 'mp', [(i, i ^ bit) for i in range(8)])  34.8 us
    pallas_call x2, Pallas kernels, call(): pl.pallas_call(kernel, grid=(blocks,), in_specs=[pl.BlockSpec((1, rows, d...  30.6 us
  transfers between devices with their start and end apart: 86, of which 38 were waited for; matrix products, arithmetic and copies ran while one was open for 24% of the time, Pallas kernels for 21%

profile of v2, /device:TPU:0, one launch (start us, length us, event | category | flops | bytes accessed | tf_op | source)
XLA Modules:
  0.0 711.7 jit_solution(7433955309103104709)
XLA Ops:
  23.0 9.0 %modal_filter.1.filt_ref = f32[2048,256]{1,0:T(8,128)} custom-call(f32[32,16,256]{2,1,0:T(8,128)S(1)} %get-tuple-element.414.hre_ref, f32[32,16,256]{2,1,0:T(8,128)S(1)} %get-tuple-element.413.him_ref, f32[16,32,256]{2,1,0:T(8,128)S(1)} %get-tuple-element.412.lre_ref, f32[16,32,256]{2,1,0:T(8,128)} %get-tuple-element.411.lim_ref, f32[16,256]{1,0:T(8,128)S(1)} %bitcast.167, ...), custom_call_target="tpu_custom_call" | custom-call | tf_op jit(solution)/shard_map/modal_filter/pallas_call | solution.py:243
  32.3 5.5 project.3
  46.3 8.5 %project.4 = (f32[8,256,768]{2,1,0:T(8,128)}, bf16[8,256,2048]{2,1,0:T(8,128)(2,1)}) custom-call(s32[1]{0:T(128)} %bitcast.me_ref, bf16[1,128,2048]{2,1,0:T(8,128)(2,1)} %collective-permute-done.refs_0_, bf16[1,128,2048]{2,1,0:T(8,128)(2,1)S(1)} %collective-permute-done.5.refs_1_, ...), custom_call_target="tpu_custom_call", output_to_operand_aliasing={{0}: (10, {}), {1}: (11, {})} | custom-call | flops 1000 | bytes 1000 | tf_op jit(solution)/shard_map/project/pallas_call | solution.py:429
  66.2 5.5 project.5
  74.7 16.9 %mixer_forward.1 = (bf16[8,2,128,256]{3,2,1,0:T(8,128)(2,1)S(1)}, bf16[8,2,128,256]{3,2,1,0:T(8,128)(2,1)}, f32[2,1024,256]{2,1,0:T(8,128)}, f32[2,2048,256]{2,1,0:T(8,128)}) custom-call(s32[1]{0:T(128)} %bitcast.me_ref, f32[8,2,128,768]{3,2,1,0:T(8,128)} %bitcast.170, f32[8,2,128,768]{3,2,1,0:T(8,128)} %bitcast.171, f32[8,2,128,768]{3,2,1,0:T(8,128)} %bitcast.172, ...), custom_call_target="tpu_custom_call" | custom-call | flops 1000 | bytes 1000 | tf_op jit(solution)/shard_map/mixer_forward/pallas_call | solution.py:286
  98.3 4.8 collective-permute-done.26
  112.3 5.6 hidden_back.3
  117.9 8.8 %hidden_back.4 = (f32[8,256,704]{2,1,0:T(8,128)}, bf16[8,256,2048]{2,1,0:T(8,128)(2,1)}) custom-call(s32[1]{0:T(128)} %bitcast.me_ref, bf16[1,128,2048]{2,1,0:T(8,128)(2,1)S(1)} %collective-permute-done.13.refs_0_, bf16[1,128,2048]{2,1,0:T(8,128)(2,1)S(1)} %collective-permute-done.16.refs_1_, ...), custom_call_target="tpu_custom_call", output_to_operand_aliasing={{0}: (10, {}), {1}: (11, {})} | custom-call | flops 1000 | bytes 1000 | tf_op jit(solution)/shard_map/hidden_back/pallas_call | solution.py:429
  133.6 9.1 %collective-permute-done.31 = bf16[1,128,2048]{2,1,0:T(8,128)(2,1)S(1)} collective-permute-done((bf16[1,128,2048]{2,1,0:T(8,128)(2,1)S(1)}, bf16[1,128,2048]{2,1,0:T(8,128)(2,1)S(1)}, u32[]{:S(2)}, u32[]{:S(2)}) %collective-permute-start.31) | collective-permute-done | bytes 524320 | tf_op jit(solution)/shard_map/ppermute | solution.py:541
  147.1 7.5 %collective-permute-done.34.refs_0_ = bf16[1,128,2048]{2,1,0:T(8,128)(2,1)S(1)} collective-permute-done((bf16[1,128,2048]{2,1,0:T(8,128)(2,1)S(1)}, bf16[1,128,2048]{2,1,0:T(8,128)(2,1)S(1)}, u32[]{:S(2)}, u32[]{:S(2)}) %collective-permute-start.34) | collective-permute-done | bytes 524320 | tf_op jit(solution)/shard_map/ppermute | solution.py:541
  160.2 5.4 hidden_back.5
  165.6 4.5 collective-permute-done.32.refs_0_
  170.6 8.9 %feed.3 = (bf16[8,256,704]{2,1,0:T(8,128)(2,1)}, bf16[8,256,704]{2,1,0:T(8,128)(2,1)}, bf16[8,256,704]{2,1,0:T(8,128)(2,1)}, bf16[8,256,2048]{2,1,0:T(8,128)(2,1)}) custom-call(s32[1]{0:T(128)} %bitcast.me_ref, bf16[2,128,2048]{2,1,0:T(8,128)(2,1)S(1)} %multiply_convert_fusion.2.refs_0_, bf16[2,128,2048]{2,1,0:T(8,128)(2,1)} %copy-done.71, ...), custom_call_target="tpu_custom_call" | custom-call | flops 1000 | bytes 1000 | tf_op jit(solution)/shard_map/feed/pallas_call | solution.py:429
  186.5 13.9 %feed.4 = (bf16[8,256,704]{2,1,0:T(8,128)(2,1)}, bf16[8,256,704]{2,1,0:T(8,128)(2,1)}, bf16[8,256,704]{2,1,0:T(8,128)(2,1)}, bf16[8,256,2048]{2,1,0:T(8,128)(2,1)}) custom-call(s32[1]{0:T(128)} %bitcast.me_ref, ...), custom_call_target="tpu_custom_call", output_to_operand_aliasing={{0}: (12, {}), {1}: (13, {}), {2}: (14, {}), {3}: (15, {})} | custom-call | flops 1000 | bytes 1000 | tf_op jit(solution)/shard_map/feed/pallas_call | solution.py:429
  204.0 8.6 %feed.5 = (bf16[8,256,704]{2,1,0:T(8,128)(2,1)}, bf16[8,256,704]{2,1,0:T(8,128)(2,1)}, bf16[8,256,704]{2,1,0:T(8,128)(2,1)}, bf16[8,256,2048]{2,1,0:T(8,128)(2,1)}) custom-call(s32[1]{0:T(128)} %bitcast.me_ref, bf16[1,128,2048]{2,1,0:T(8,128)(2,1)S(1)} %collective-permute-done.38.refs_0_, ...), custom_call_target="tpu_custom_call", output_to_operand_aliasing={{0}: (8, {}), {1}: (9, {}), {2}: (10, {}), {3}: (11, {})} | custom-call | flops 1000 | bytes 1000 | tf_op jit(solution)/shard_map/feed/pallas_call | solution.py:429
  212.7 5.8 convolution_convert_fusion.9
  218.4 4.8 collective-permute-start.49
  223.2 18.4 %sum_products.2 = bf16[8,256,2048]{2,1,0:T(8,128)(2,1)} custom-call(bf16[8,256,704]{2,1,0:T(8,128)(2,1)} %get-tuple-element.279.refs_0_, bf16[8,256,704]{2,1,0:T(8,128)(2,1)} %get-tuple-element.287.refs_1_, bf16[704,2048]{1,0:T(8,128)(2,1)} %bitcast.186, bf16[704,2048]{1,0:T(8,128)(2,1)} %bitcast.190), custom_call_target="tpu_custom_call" | custom-call | flops 1000 | bytes 1000 | tf_op jit(solution)/shard_map/sum_products/pallas_call | solution.py:459
  241.6 5.1 convolution_convert_fusion.8
  246.7 6.6 collective-permute-done.49
  256.8 7.2 %collective-permute-start.50 = (bf16[352,2048]{1,0:T(8,128)(2,1)S(1)}, bf16[352,2048]{1,0:T(8,128)(2,1)S(1)}, u32[]{:S(2)}, u32[]{:S(2)}) collective-permute-start(bf16[352,2048]{1,0:T(8,128)(2,1)S(1)} %convolution_convert_fusion.8), channel_id=1, source_target_pairs={{0,8},{24,16},{1,9},{25,17},{2,10},{26,18},{3,11},{27,19},{4,12},{... | collective-permute-start | bytes 4325384 | tf_op jit(solution)/shard_map/ppermute | solution.py:622
  264.0 9.0 %convolution_convert_fusion.6 = bf16[352,2048]{1,0:T(8,128)(2,1)S(1)} fusion(bf16[2048,2048]{1,0:T(8,128)(2,1)} %bitcast.200, bf16[2048,704]{1,0:T(8,128)(2,1)} %bitcast.206), kind=kOutput, calls=%fused_computation.27 | convolution fusion | flops 2953510912 | bytes 11403264 | tf_op jit(solution)/shard_map/dot_general | solution.py:30
  274.5 5.0 convolution_convert_fusion.7
  279.4 16.5 %collective-permute-done.50 = bf16[352,2048]{1,0:T(8,128)(2,1)S(1)} collective-permute-done((bf16[352,2048]{1,0:T(8,128)(2,1)S(1)}, bf16[352,2048]{1,0:T(8,128)(2,1)S(1)}, u32[]{:S(2)}, u32[]{:S(2)}) %collective-permute-start.50) | collective-permute-done | bytes 1441824 | tf_op jit(solution)/shard_map/ppermute | solution.py:622
  300.7 4.2 convolution_convert_fusion.5
  305.0 19.9 %collective-permute-done.53 = bf16[352,2048]{1,0:T(8,128)(2,1)S(1)} collective-permute-done((bf16[352,2048]{1,0:T(8,128)(2,1)S(1)}, bf16[352,2048]{1,0:T(8,128)(2,1)S(1)}, u32[]{:S(2)}, u32[]{:S(2)}) %collective-permute-start.53) | collective-permute-done | bytes 1441824 | tf_op jit(solution)/shard_map/ppermute | solution.py:622
  324.8 3.7 collective-permute-done.55
  334.3 5.6 collective-permute-start.52
  339.9 2.8 add_convert_fusion.7
  345.7 6.0 collective-permute-start.59
  351.7 7.9 %convolution_convert_fusion.4 = bf16[352,2048]{1,0:T(8,128)(2,1)} fusion(bf16[2048,2048]{1,0:T(8,128)(2,1)} %bitcast.201, bf16[2048,704]{1,0:T(8,128)(2,1)S(1)} %bitcast.209), kind=kOutput, calls=%fused_computation.25 | convolution fusion | flops 2953510912 | bytes 11403264 | tf_op jit(solution)/shard_map/dot_general | solution.py:30
  359.7 12.5 %collective-permute-done.52 = bf16[352,2048]{1,0:T(8,128)(2,1)S(1)} collective-permute-done((bf16[352,2048]{1,0:T(8,128)(2,1)}, bf16[352,2048]{1,0:T(8,128)(2,1)S(1)}, u32[]{:S(2)}, u32[]{:S(2)}) %collective-permute-start.52) | collective-permute-done | bytes 1441824 | tf_op jit(solution)/shard_map/ppermute | solution.py:622
  377.4 8.4 %collective-permute-start.58 = (bf16[352,2048]{1,0:T(8,128)(2,1)}, bf16[352,2048]{1,0:T(8,128)(2,1)}, u32[]{:S(2)}, u32[]{:S(2)}) collective-permute-start(bf16[352,2048]{1,0:T(8,128)(2,1)} %convolution_convert_fusion.4), channel_id=1, source_target_pairs={{0,8},{24,16},{1,9},{25,17},{2,10},{26,18},{3,11},{27,19},{4,12},{... | collective-permute-start | bytes 4325384 | tf_op jit(solution)/shard_map/ppermute | solution.py:622
  385.8 8.8 %convolution_convert_fusion = bf16[2048,2048]{1,0:T(8,128)(2,1)} fusion(bf16[2048,704]{1,0:T(8,128)(2,1)S(1)} %bitcast.212, bf16[704,2048]{1,0:T(8,128)(2,1)S(1)} %copy-done.23), kind=kOutput, calls=%fused_computation | convolution fusion | flops 5909774336 | bytes 14155776 | tf_op jit(solution)/shard_map/dot_general | solution.py:26
  394.6 8.3 %collective-permute-done.59 = bf16[352,2048]{1,0:T(8,128)(2,1)S(1)} collective-permute-done((bf16[352,2048]{1,0:T(8,128)(2,1)S(1)}, bf16[352,2048]{1,0:T(8,128)(2,1)S(1)}, u32[]{:S(2)}, u32[]{:S(2)}) %collective-permute-start.59) | collective-permute-done | bytes 1441824 | tf_op jit(solution)/shard_map/ppermute | solution.py:622
  406.5 3.7 add_convert_fusion.3
  414.9 7.1 fusion.36.gg_ref
  422.0 5.9 collective-permute-done.58
  427.9 11.2 %collective-permute-done.63 = bf16[352,2048]{1,0:T(8,128)(2,1)} collective-permute-done((bf16[352,2048]{1,0:T(8,128)(2,1)}, bf16[352,2048]{1,0:T(8,128)(2,1)}, u32[]{:S(2)}, u32[]{:S(2)}) %collective-permute-start.63) | collective-permute-done | bytes 1441824 | tf_op jit(solution)/shard_map/ppermute | solution.py:629
  439.2 3.5 slice_bitcast_fusion.1
  450.0 7.3 %fusion = bf16[256,2048]{1,0:T(8,128)(2,1)S(1)} fusion(bf16[8,2,128,256]{3,2,1,0:T(8,128)(2,1)S(1)} %copy-done.66, bf16[8,2,128,2048]{3,2,1,0:T(8,128)(2,1)} %bitcast.214), kind=kOutput, calls=%fused_computation.40 | convolution fusion | flops 2148007936 | bytes 10485760 | tf_op jit(solution)/shard_map/dot_general | solution.py:30
  457.3 10.6 %collective-permute-start.65 = (bf16[256,2048]{1,0:T(8,128)(2,1)S(1)}, bf16[256,2048]{1,0:T(8,128)(2,1)S(1)}, u32[]{:S(2)}, u32[]{:S(2)}) collective-permute-start(bf16[256,2048]{1,0:T(8,128)(2,1)S(1)} %fusion), channel_id=1, source_target_pairs={{0,8},{24,16},{1,9},{25,17},{2,10},{26,18},{3,11},{27,19},{4,12},{... | collective-permute-start | bytes 3145736 | tf_op jit(solution)/shard_map/ppermute | solution.py:622
  468.0 25.0 %mixer_backward.1 = (bf16[3,8,2,128,256]{4,3,2,1,0:T(8,128)(2,1)}, f32[9,256]{1,0:T(8,128)S(1)}, f32[1,256]{1,0:T(1,128)S(1)}, f32[1024,256]{1,0:T(8,128)S(1)}) custom-call(f32[8,2,128,256]{3,2,1,0:T(8,128)} %fusion.36.gg_ref, f32[8,2,128,768]{3,2,1,0:T(8,128)} %bitcast.173, f32[8,2,128,768]{3,2,1,0:T(8,128)} %bitcast.174, f32[8,2,128,768]{3,2,1,0:T(8,128)} %bitcast.175, ...), custom_call_target="tpu_custom_call" | custom-call | flops 1000 | bytes 1000 | tf_op jit(solution)/shard_map/mixer_backward/pallas_call | solution.py:326
  493.9 3.6 fusion.52
  497.5 7.6 %convolution_convert_fusion.10 = bf16[2048,256]{1,0:T(8,128)(2,1)} fusion(bf16[2048,2048]{1,0:T(8,128)(2,1)} %bitcast.191, bf16[2048,256]{1,0:T(8,128)(2,1)S(1)} %bitcast.165), kind=kOutput, calls=%fused_computation.43 | convolution fusion | flops 2148007936 | bytes 10485760 | tf_op jit(solution)/shard_map/dot_general | solution.py:30
  513.7 12.2 %sum_products.3 = bf16[8,256,2048]{2,1,0:T(8,128)(2,1)} custom-call(bf16[8,256,256]{2,1,0:T(8,128)(2,1)S(1)} %bitcast.166, bf16[8,256,256]{2,1,0:T(8,128)(2,1)} %bitcast.216, bf16[8,256,256]{2,1,0:T(8,128)(2,1)} %bitcast.218, bf16[2048,256]{1,0:T(8,128)(2,1)} %get-tuple-element.386.refs_3_, bf16[2048,256]{1,0:T(8,128)(2,1)} %get-tuple-element.385.refs_4_, ...), custom_call_target="tpu_custom_call" | custom-call | flops 1000 | bytes 1000 | tf_op jit(solution)/shard_map/sum_products/pallas_call | solution.py:459
  525.9 6.9 fusion.1
  532.8 2.8 bitcast_convert_fusion
  538.1 3.7 maximum_convert_fusion
  547.5 2.9 broadcast_select_fusion.4
  550.5 3.6 fusion.2
  554.1 9.2 %collective-permute-start.74 = (bf16[2048,256]{1,0:T(8,128)(2,1)}, bf16[2048,256]{1,0:T(8,128)(2,1)}, u32[]{:S(2)}, u32[]{:S(2)}) collective-permute-start(bf16[2048,256]{1,0:T(8,128)(2,1)} %fusion.2), channel_id=1, source_target_pairs={{0,8},{24,16},{1,9},{25,17},{2,10},{26,18},{3,11},{27,19},{4,12},{... | collective-permute-start | bytes 3145736 | tf_op jit(solution)/shard_map/ppermute | solution.py:622
  570.1 3.0 add_convert_fusion.16
  576.3 2.8 fusion.10
  581.1 6.4 pole_gradients.1
  588.3 3.1 collective-permute-done.72
  593.3 7.1 collective-permute-start.73
  607.3 5.2 convert_bitcast_fusion.1
  613.7 8.9 %collective-permute-done.73 = bf16[2144,256]{1,0:T(8,128)(2,1)S(1)} collective-permute-done((bf16[2144,256]{1,0:T(8,128)(2,1)S(1)}, bf16[2144,256]{1,0:T(8,128)(2,1)S(1)}, u32[]{:S(2)}, u32[]{:S(2)}) %collective-permute-start.73) | collective-permute-done | bytes 1097760 | tf_op jit(solution)/shard_map/ppermute | solution.py:622
  622.6 13.3 %collective-permute-done.78 = bf16[2048,256]{1,0:T(8,128)(2,1)S(1)} collective-permute-done((bf16[2048,256]{1,0:T(8,128)(2,1)S(1)}, bf16[2048,256]{1,0:T(8,128)(2,1)S(1)}, u32[]{:S(2)}, u32[]{:S(2)}) %collective-permute-start.78) | collective-permute-done | bytes 1048608 | tf_op jit(solution)/shard_map/ppermute | solution.py:629
  644.4 24.8 %collective-permute-done.80 = bf16[2048,256]{1,0:T(8,128)(2,1)} collective-permute-done((bf16[2048,256]{1,0:T(8,128)(2,1)}, bf16[2048,256]{1,0:T(8,128)(2,1)}, u32[]{:S(2)}, u32[]{:S(2)}) %collective-permute-start.80) | collective-permute-done | bytes 1048608 | tf_op jit(solution)/shard_map/ppermute | solution.py:629
  675.0 3.5 copy.60
  679.8 16.3 %collective-permute-done.81 = bf16[2144,256]{1,0:T(8,128)(2,1)S(1)} collective-permute-done((bf16[2144,256]{1,0:T(8,128)(2,1)S(1)}, bf16[2144,256]{1,0:T(8,128)(2,1)S(1)}, u32[]{:S(2)}, u32[]{:S(2)}) %collective-permute-start.81) | collective-permute-done | bytes 1097760 | tf_op jit(solution)/shard_map/ppermute | solution.py:629
  700.4 4.4 convert_bitcast_fusion
  (448 shorter events, 181.2 us)
Async XLA Ops:
  7.2 322.5 %reduce-scatter.4.cloned.1.call-start = ((), (), s32[]{:S(2)}) async-start(), calls=%async_computation.3 | async-start | bytes 9437184 | tf_op jit(solution)/shard_map/reduce_scatter | solution.py:479
  11.6 10.4 %collective-permute-start.4 = (bf16[2,128,2048]{2,1,0:T(8,128)(2,1)S(1)}, bf16[2,128,2048]{2,1,0:T(8,128)(2,1)S(1)}, u32[]{:S(2)}, u32[]{:S(2)}) collective-permute-start(bf16[2,128,2048]{2,1,0:T(8,128)(2,1)S(1)} %fusion.17.refs_0_), channel_id=1, source_target_pairs={{0,1},{1,0},{2,3},{3,2},{4,5},{5,4},{6,7},{7,6},{8,9},{9,8},{10,11... | collective-permute-start | bytes 3145736 | tf_op jit(solution)/shard_map/ppermute | solution.py:541
  13.1 19.2 %collective-permute-start = (bf16[1,128,2048]{2,1,0:T(8,128)(2,1)}, bf16[1,128,2048]{2,1,0:T(8,128)(2,1)}, u32[]{:S(2)}, u32[]{:S(2)}) collective-permute-start(bf16[1,128,2048]{2,1,0:T(8,128)(2,1)} %get-tuple-element.183), channel_id=1, source_target_pairs={{0,2},{1,3},{2,0},{3,1},{4,6},{5,7},{6,4},{7,5},{8,10},{9,11},{10,... | collective-permute-start | bytes 1572872 | tf_op jit(solution)/shard_map/ppermute | solution.py:541
  15.6 16.7 %collective-permute-start.1 = (bf16[1,128,2048]{2,1,0:T(8,128)(2,1)}, bf16[1,128,2048]{2,1,0:T(8,128)(2,1)}, u32[]{:S(2)}, u32[]{:S(2)}) collective-permute-start(bf16[1,128,2048]{2,1,0:T(8,128)(2,1)} %get-tuple-element.182), channel_id=1, source_target_pairs={{0,4},{1,5},{2,6},{3,7},{4,0},{5,1},{6,2},{7,3},{8,12},{9,13},{10,... | collective-permute-start | bytes 1572872 | tf_op jit(solution)/shard_map/ppermute | solution.py:541
  22.0 17.7 %collective-permute-start.5 = (bf16[1,128,2048]{2,1,0:T(8,128)(2,1)}, bf16[1,128,2048]{2,1,0:T(8,128)(2,1)S(1)}, u32[]{:S(2)}, u32[]{:S(2)}) collective-permute-start(bf16[1,128,2048]{2,1,0:T(8,128)(2,1)} %get-tuple-element.182), channel_id=1, source_target_pairs={{0,2},{1,3},{2,0},{3,1},{4,6},{5,7},{6,4},{7,5},{8,10},{9,11},{10,... | collective-permute-start | bytes 1572872 | tf_op jit(solution)/shard_map/ppermute | solution.py:541
  22.6 18.5 %collective-permute-start.6 = (bf16[1,128,2048]{2,1,0:T(8,128)(2,1)}, bf16[1,128,2048]{2,1,0:T(8,128)(2,1)S(1)}, u32[]{:S(2)}, u32[]{:S(2)}) collective-permute-start(bf16[1,128,2048]{2,1,0:T(8,128)(2,1)} %get-tuple-element.183), channel_id=1, source_target_pairs={{0,4},{1,5},{2,6},{3,7},{4,0},{5,1},{6,2},{7,3},{8,12},{9,13},{10,... | collective-permute-start | bytes 1572872 | tf_op jit(solution)/shard_map/ppermute | solution.py:541
  42.1 14.0 %collective-permute-start.2 = (bf16[1,128,2048]{2,1,0:T(8,128)(2,1)}, bf16[1,128,2048]{2,1,0:T(8,128)(2,1)S(1)}, u32[]{:S(2)}, u32[]{:S(2)}) collective-permute-start(bf16[1,128,2048]{2,1,0:T(8,128)(2,1)} %collective-permute-done.refs_0_), channel_id=1, source_target_pairs={{0,4},{1,5},{2,6},{3,7},{4,0},{5,1},{6,2},{7,3},{8,12},{9,13},{10,... | collective-permute-start | bytes 1572872 | tf_op jit(solution)/shard_map/ppermute | solution.py:541
  43.6 13.9 %collective-permute-start.3 = (bf16[1,128,2048]{2,1,0:T(8,128)(2,1)}, bf16[1,128,2048]{2,1,0:T(8,128)(2,1)}, u32[]{:S(2)}, u32[]{:S(2)}) collective-permute-start(bf16[1,128,2048]{2,1,0:T(8,128)(2,1)} %collective-permute-done.1.refs_5_), channel_id=1, source_target_pairs={{0,2},{1,3},{2,0},{3,1},{4,6},{5,7},{6,4},{7,5},{8,10},{9,11},{10,... | collective-permute-start | bytes 1572872 | tf_op jit(solution)/shard_map/ppermute | solution.py:541
  59.1 14.9 %collective-permute-start.13 = (bf16[1,128,2048]{2,1,0:T(8,128)(2,1)}, bf16[1,128,2048]{2,1,0:T(8,128)(2,1)S(1)}, u32[]{:S(2)}, u32[]{:S(2)}) collective-permute-start(bf16[1,128,2048]{2,1,0:T(8,128)(2,1)} %get-tuple-element.206), channel_id=1, source_target_pairs={{0,2},{1,3},{2,0},{3,1},{4,6},{5,7},{6,4},{7,5},{8,10},{9,11},{10,... | collective-permute-start | bytes 1572872 | tf_op jit(solution)/shard_map/ppermute | solution.py:541
  59.7 15.1 %collective-permute-start.14 = (bf16[1,128,2048]{2,1,0:T(8,128)(2,1)}, bf16[1,128,2048]{2,1,0:T(8,128)(2,1)}, u32[]{:S(2)}, u32[]{:S(2)}) collective-permute-start(bf16[1,128,2048]{2,1,0:T(8,128)(2,1)} %get-tuple-element.205), channel_id=1, source_target_pairs={{0,4},{1,5},{2,6},{3,7},{4,0},{5,1},{6,2},{7,3},{8,12},{9,13},{10,... | collective-permute-start | bytes 1572872 | tf_op jit(solution)/shard_map/ppermute | solution.py:541
  61.2 30.4 %collective-permute-start.16 = (bf16[1,128,2048]{2,1,0:T(8,128)(2,1)}, bf16[1,128,2048]{2,1,0:T(8,128)(2,1)S(1)}, u32[]{:S(2)}, u32[]{:S(2)}) collective-permute-start(bf16[1,128,2048]{2,1,0:T(8,128)(2,1)} %get-tuple-element.205), channel_id=1, source_target_pairs={{0,2},{1,3},{2,0},{3,1},{4,6},{5,7},{6,4},{7,5},{8,10},{9,11},{10,... | collective-permute-start | bytes 1572872 | tf_op jit(solution)/shard_map/ppermute | solution.py:541
  63.5 28.1 %collective-permute-start.17 = (bf16[1,128,2048]{2,1,0:T(8,128)(2,1)}, bf16[1,128,2048]{2,1,0:T(8,128)(2,1)}, u32[]{:S(2)}, u32[]{:S(2)}) collective-permute-start(bf16[1,128,2048]{2,1,0:T(8,128)(2,1)} %get-tuple-element.206), channel_id=1, source_target_pairs={{0,4},{1,5},{2,6},{3,7},{4,0},{5,1},{6,2},{7,3},{8,12},{9,13},{10,... | collective-permute-start | bytes 1572872 | tf_op jit(solution)/shard_map/ppermute | solution.py:541
  95.1 11.9 %collective-permute-start.18 = (bf16[2,128,2048]{2,1,0:T(8,128)(2,1)S(1)}, bf16[2,128,2048]{2,1,0:T(8,128)(2,1)S(1)}, u32[]{:S(2)}, u32[]{:S(2)}) collective-permute-start(bf16[2,128,2048]{2,1,0:T(8,128)(2,1)S(1)} %bitcast.226), channel_id=1, source_target_pairs={{0,1},{1,0},{2,3},{3,2},{4,5},{5,4},{6,7},{7,6},{8,9},{9,8},{10,11... | collective-permute-start | bytes 3145736 | tf_op jit(solution)/shard_map/ppermute | solution.py:541
  95.7 13.2 %collective-permute-start.22 = (bf16[1,128,2048]{2,1,0:T(8,128)(2,1)S(1)}, bf16[1,128,2048]{2,1,0:T(8,128)(2,1)S(1)}, u32[]{:S(2)}, u32[]{:S(2)}) collective-permute-start(bf16[1,128,2048]{2,1,0:T(8,128)(2,1)S(1)} %collective-permute-done.16.refs_1_), channel_id=1, source_target_pairs={{0,1},{1,0},{2,3},{3,2},{4,5},{5,4},{6,7},{7,6},{8,9},{9,8},{10,11... | collective-permute-start | bytes 1572872 | tf_op jit(solution)/shard_map/ppermute | solution.py:541
  97.8 11.9 %collective-permute-start.23 = (bf16[1,128,2048]{2,1,0:T(8,128)(2,1)}, bf16[1,128,2048]{2,1,0:T(8,128)(2,1)S(1)}, u32[]{:S(2)}, u32[]{:S(2)}) collective-permute-start(bf16[1,128,2048]{2,1,0:T(8,128)(2,1)} %collective-permute-done.17.refs_4_), channel_id=1, source_target_pairs={{0,1},{1,0},{2,3},{3,2},{4,5},{5,4},{6,7},{7,6},{8,9},{9,8},{10,11... | collective-permute-start | bytes 1572872 | tf_op jit(solution)/shard_map/ppermute | solution.py:541
  105.4 21.3 %collective-permute-start.27 = (bf16[1,128,2048]{2,1,0:T(8,128)(2,1)S(1)}, bf16[1,128,2048]{2,1,0:T(8,128)(2,1)S(1)}, u32[]{:S(2)}, u32[]{:S(2)}) collective-permute-start(bf16[1,128,2048]{2,1,0:T(8,128)(2,1)S(1)} %get-tuple-element.401), channel_id=1, source_target_pairs={{0,2},{1,3},{2,0},{3,1},{4,6},{5,7},{6,4},{7,5},{8,10},{9,11},{10,... | collective-permute-start | bytes 1572872 | tf_op jit(solution)/shard_map/ppermute | solution.py:541
  107.0 19.7 %collective-permute-start.28 = (bf16[1,128,2048]{2,1,0:T(8,128)(2,1)S(1)}, bf16[1,128,2048]{2,1,0:T(8,128)(2,1)}, u32[]{:S(2)}, u32[]{:S(2)}) collective-permute-start(bf16[1,128,2048]{2,1,0:T(8,128)(2,1)S(1)} %get-tuple-element.400), channel_id=1, source_target_pairs={{0,4},{1,5},{2,6},{3,7},{4,0},{5,1},{6,2},{7,3},{8,12},{9,13},{10,... | collective-permute-start | bytes 1572872 | tf_op jit(solution)/shard_map/ppermute | solution.py:541
  111.3 21.8 %collective-permute-start.30 = (bf16[1,128,2048]{2,1,0:T(8,128)(2,1)}, bf16[1,128,2048]{2,1,0:T(8,128)(2,1)}, u32[]{:S(2)}, u32[]{:S(2)}) collective-permute-start(bf16[1,128,2048]{2,1,0:T(8,128)(2,1)} %slice.251), channel_id=1, source_target_pairs={{0,4},{1,5},{2,6},{3,7},{4,0},{5,1},{6,2},{7,3},{8,12},{9,13},{10,... | collective-permute-start | bytes 1572872 | tf_op jit(solution)/shard_map/ppermute | solution.py:541
  111.8 21.8 %collective-permute-start.25 = (bf16[1,128,2048]{2,1,0:T(8,128)(2,1)}, bf16[1,128,2048]{2,1,0:T(8,128)(2,1)}, u32[]{:S(2)}, u32[]{:S(2)}) collective-permute-start(bf16[1,128,2048]{2,1,0:T(8,128)(2,1)} %slice.252), channel_id=1, source_target_pairs={{0,2},{1,3},{2,0},{3,1},{4,6},{5,7},{6,4},{7,5},{8,10},{9,11},{10,... | collective-permute-start | bytes 1572872 | tf_op jit(solution)/shard_map/ppermute | solution.py:541
  127.8 14.9 %collective-permute-start.31 = (bf16[1,128,2048]{2,1,0:T(8,128)(2,1)S(1)}, bf16[1,128,2048]{2,1,0:T(8,128)(2,1)S(1)}, u32[]{:S(2)}, u32[]{:S(2)}) collective-permute-start(bf16[1,128,2048]{2,1,0:T(8,128)(2,1)S(1)} %add_convert_fusion.18), channel_id=1, source_target_pairs={{0,2},{1,3},{2,0},{3,1},{4,6},{5,7},{6,4},{7,5},{8,10},{9,11},{10,... | collective-permute-start | bytes 1572872 | tf_op jit(solution)/shard_map/ppermute | solution.py:541
  129.4 14.9 %collective-permute-start.29 = (bf16[1,128,2048]{2,1,0:T(8,128)(2,1)S(1)}, bf16[1,128,2048]{2,1,0:T(8,128)(2,1)S(1)}, u32[]{:S(2)}, u32[]{:S(2)}) collective-permute-start(bf16[1,128,2048]{2,1,0:T(8,128)(2,1)S(1)} %add_convert_fusion.19), channel_id=1, source_target_pairs={{0,4},{1,5},{2,6},{3,7},{4,0},{5,1},{6,2},{7,3},{8,12},{9,13},{10,... | collective-permute-start | bytes 1572872 | tf_op jit(solution)/shard_map/ppermute | solution.py:541
  131.1 23.5 %collective-permute-start.34 = (bf16[1,128,2048]{2,1,0:T(8,128)(2,1)S(1)}, bf16[1,128,2048]{2,1,0:T(8,128)(2,1)S(1)}, u32[]{:S(2)}, u32[]{:S(2)}) collective-permute-start(bf16[1,128,2048]{2,1,0:T(8,128)(2,1)S(1)} %collective-permute-done.13.refs_0_), channel_id=1, source_target_pairs={{0,4},{1,5},{2,6},{3,7},{4,0},{5,1},{6,2},{7,3},{8,12},{9,13},{10,... | collective-permute-start | bytes 1572872 | tf_op jit(solution)/shard_map/ppermute | solution.py:541
  133.1 21.5 %collective-permute-start.35 = (bf16[1,128,2048]{2,1,0:T(8,128)(2,1)}, bf16[1,128,2048]{2,1,0:T(8,128)(2,1)S(1)}, u32[]{:S(2)}, u32[]{:S(2)}) collective-permute-start(bf16[1,128,2048]{2,1,0:T(8,128)(2,1)} %collective-permute-done.14.refs_5_), channel_id=1, source_target_pairs={{0,2},{1,3},{2,0},{3,1},{4,6},{5,7},{6,4},{7,5},{8,10},{9,11},{10,... | collective-permute-start | bytes 1572872 | tf_op jit(solution)/shard_map/ppermute | solution.py:541
  147.0 10.4 %collective-permute-start.40 = (bf16[2,128,2048]{2,1,0:T(8,128)(2,1)S(1)}, bf16[2,128,2048]{2,1,0:T(8,128)(2,1)S(1)}, u32[]{:S(2)}, u32[]{:S(2)}) collective-permute-start(bf16[2,128,2048]{2,1,0:T(8,128)(2,1)S(1)} %multiply_convert_fusion.2.refs_0_), channel_id=1, source_target_pairs={{0,1},{1,0},{2,3},{3,2},{4,5},{5,4},{6,7},{7,6},{8,9},{9,8},{10,11... | collective-permute-start | bytes 3145736 | tf_op jit(solution)/shard_map/ppermute | solution.py:541
  155.2 14.8 %collective-permute-start.32 = (bf16[1,128,2048]{2,1,0:T(8,128)(2,1)S(1)}, bf16[1,128,2048]{2,1,0:T(8,128)(2,1)S(1)}, u32[]{:S(2)}, u32[]{:S(2)}) collective-permute-start(bf16[1,128,2048]{2,1,0:T(8,128)(2,1)S(1)} %get-tuple-element.245), channel_id=1, source_target_pairs={{0,2},{1,3},{2,0},{3,1},{4,6},{5,7},{6,4},{7,5},{8,10},{9,11},{10,... | collective-permute-start | bytes 1572872 | tf_op jit(solution)/shard_map/ppermute | solution.py:541
  155.8 14.8 %collective-permute-start.33 = (bf16[1,128,2048]{2,1,0:T(8,128)(2,1)S(1)}, bf16[1,128,2048]{2,1,0:T(8,128)(2,1)S(1)}, u32[]{:S(2)}, u32[]{:S(2)}) collective-permute-start(bf16[1,128,2048]{2,1,0:T(8,128)(2,1)S(1)} %get-tuple-element.244), channel_id=1, source_target_pairs={{0,4},{1,5},{2,6},{3,7},{4,0},{5,1},{6,2},{7,3},{8,12},{9,13},{10,... | collective-permute-start | bytes 1572872 | tf_op jit(solution)/shard_map/ppermute | solution.py:541
  157.3 23.1 %collective-permute-start.41 = (bf16[1,128,2048]{2,1,0:T(8,128)(2,1)S(1)}, bf16[1,128,2048]{2,1,0:T(8,128)(2,1)S(1)}, u32[]{:S(2)}, u32[]{:S(2)}) collective-permute-start(bf16[1,128,2048]{2,1,0:T(8,128)(2,1)S(1)} %get-tuple-element.244), channel_id=1, source_target_pairs={{0,2},{1,3},{2,0},{3,1},{4,6},{5,7},{6,4},{7,5},{8,10},{9,11},{10,... | collective-permute-start | bytes 1572872 | tf_op jit(solution)/shard_map/ppermute | solution.py:541
  158.8 21.8 %collective-permute-start.42 = (bf16[1,128,2048]{2,1,0:T(8,128)(2,1)S(1)}, bf16[1,128,2048]{2,1,0:T(8,128)(2,1)S(1)}, u32[]{:S(2)}, u32[]{:S(2)}) collective-permute-start(bf16[1,128,2048]{2,1,0:T(8,128)(2,1)S(1)} %get-tuple-element.245), channel_id=1, source_target_pairs={{0,4},{1,5},{2,6},{3,7},{4,0},{5,1},{6,2},{7,3},{8,12},{9,13},{10,... | collective-permute-start | bytes 1572872 | tf_op jit(solution)/shard_map/ppermute | solution.py:541
  181.7 18.7 %collective-permute-start.38 = (bf16[1,128,2048]{2,1,0:T(8,128)(2,1)S(1)}, bf16[1,128,2048]{2,1,0:T(8,128)(2,1)S(1)}, u32[]{:S(2)}, u32[]{:S(2)}) collective-permute-start(bf16[1,128,2048]{2,1,0:T(8,128)(2,1)S(1)} %collective-permute-done.32.refs_0_), channel_id=1, source_target_pairs={{0,4},{1,5},{2,6},{3,7},{4,0},{5,1},{6,2},{7,3},{8,12},{9,13},{10,... | collective-permute-start | bytes 1572872 | tf_op jit(solution)/shard_map/ppermute | solution.py:541
  183.2 17.2 %collective-permute-start.39 = (bf16[1,128,2048]{2,1,0:T(8,128)(2,1)S(1)}, bf16[1,128,2048]{2,1,0:T(8,128)(2,1)S(1)}, u32[]{:S(2)}, u32[]{:S(2)}) collective-permute-start(bf16[1,128,2048]{2,1,0:T(8,128)(2,1)S(1)} %collective-permute-done.33.refs_5_), channel_id=1, source_target_pairs={{0,2},{1,3},{2,0},{3,1},{4,6},{5,7},{6,4},{7,5},{8,10},{9,11},{10,... | collective-permute-start | bytes 1572872 | tf_op jit(solution)/shard_map/ppermute | solution.py:541
  218.4 34.9 %collective-permute-start.49 = (bf16[352,2048]{1,0:T(8,128)(2,1)}, bf16[352,2048]{1,0:T(8,128)(2,1)}, u32[]{:S(2)}, u32[]{:S(2)}) collective-permute-start(bf16[352,2048]{1,0:T(8,128)(2,1)} %convolution_convert_fusion.9), channel_id=1, source_target_pairs={{0,8},{24,16},{1,9},{25,17},{2,10},{26,18},{3,11},{27,19},{4,12},{... | collective-permute-start | bytes 4325384 | tf_op jit(solution)/shard_map/ppermute | solution.py:622
  253.4 161.5 %all-gather.3.cloned.1.call-start = ((), (), s32[]{:S(2)}) async-start(), calls=%async_computation.6 | async-start | bytes 9437184 | tf_op jit(solution)/shard_map/all_gather | solution.py:475
  256.0 23.4 %collective-permute-start.51 = (bf16[352,2048]{1,0:T(8,128)(2,1)S(1)}, bf16[352,2048]{1,0:T(8,128)(2,1)S(1)}, u32[]{:S(2)}, u32[]{:S(2)}) collective-permute-start(bf16[352,2048]{1,0:T(8,128)(2,1)S(1)} %add_convert_fusion.11), channel_id=1, source_target_pairs={{8,16},{16,8},{9,17},{17,9},{10,18},{18,10},{11,19},{19,11},{12,20... | collective-permute-start | bytes 4325384 | tf_op jit(solution)/shard_map/ppermute | solution.py:631
  256.8 39.1 %collective-permute-start.50 = (bf16[352,2048]{1,0:T(8,128)(2,1)S(1)}, bf16[352,2048]{1,0:T(8,128)(2,1)S(1)}, u32[]{:S(2)}, u32[]{:S(2)}) collective-permute-start(bf16[352,2048]{1,0:T(8,128)(2,1)S(1)} %convolution_convert_fusion.8), channel_id=1, source_target_pairs={{0,8},{24,16},{1,9},{25,17},{2,10},{26,18},{3,11},{27,19},{4,12},{... | collective-permute-start | bytes 4325384 | tf_op jit(solution)/shard_map/ppermute | solution.py:622
  273.0 51.8 %collective-permute-start.53 = (bf16[352,2048]{1,0:T(8,128)(2,1)S(1)}, bf16[352,2048]{1,0:T(8,128)(2,1)S(1)}, u32[]{:S(2)}, u32[]{:S(2)}) collective-permute-start(bf16[352,2048]{1,0:T(8,128)(2,1)S(1)} %convolution_convert_fusion.6), channel_id=1, source_target_pairs={{0,8},{24,16},{1,9},{25,17},{2,10},{26,18},{3,11},{27,19},{4,12},{... | collective-permute-start | bytes 4325384 | tf_op jit(solution)/shard_map/ppermute | solution.py:622
  296.5 32.0 %collective-permute-start.55 = (bf16[352,2048]{1,0:T(8,128)(2,1)S(1)}, bf16[352,2048]{1,0:T(8,128)(2,1)S(1)}, u32[]{:S(2)}, u32[]{:S(2)}) collective-permute-start(bf16[352,2048]{1,0:T(8,128)(2,1)S(1)} %add_convert_fusion.9), channel_id=1, source_target_pairs={{8,0},{16,24},{9,1},{17,25},{10,2},{18,26},{11,3},{19,27},{12,4},{... | collective-permute-start | bytes 4325384 | tf_op jit(solution)/shard_map/ppermute | solution.py:629
  298.7 30.9 %collective-permute-start.54 = (bf16[352,2048]{1,0:T(8,128)(2,1)S(1)}, bf16[352,2048]{1,0:T(8,128)(2,1)}, u32[]{:S(2)}, u32[]{:S(2)}) collective-permute-start(bf16[352,2048]{1,0:T(8,128)(2,1)S(1)} %add_convert_fusion.10), channel_id=1, source_target_pairs={{8,16},{16,8},{9,17},{17,9},{10,18},{18,10},{11,19},{19,11},{12,20... | collective-permute-start | bytes 4325384 | tf_op jit(solution)/shard_map/ppermute | solution.py:631
  334.2 198.5 %reduce-scatter.6.cloned.1.call-start = ((), (), s32[]{:S(2)}) async-start(), calls=%async_computation.4 | async-start | bytes 9437184 | tf_op jit(solution)/shard_map/reduce_scatter | solution.py:479
  334.3 37.9 %collective-permute-start.52 = (bf16[352,2048]{1,0:T(8,128)(2,1)}, bf16[352,2048]{1,0:T(8,128)(2,1)S(1)}, u32[]{:S(2)}, u32[]{:S(2)}) collective-permute-start(bf16[352,2048]{1,0:T(8,128)(2,1)} %convolution_convert_fusion.7), channel_id=1, source_target_pairs={{0,8},{24,16},{1,9},{25,17},{2,10},{26,18},{3,11},{27,19},{4,12},{... | collective-permute-start | bytes 4325384 | tf_op jit(solution)/shard_map/ppermute | solution.py:622
  342.8 30.0 %collective-permute-start.57 = (bf16[352,2048]{1,0:T(8,128)(2,1)S(1)}, bf16[352,2048]{1,0:T(8,128)(2,1)S(1)}, u32[]{:S(2)}, u32[]{:S(2)}) collective-permute-start(bf16[352,2048]{1,0:T(8,128)(2,1)S(1)} %add_convert_fusion.7), channel_id=1, source_target_pairs={{8,0},{16,24},{9,1},{17,25},{10,2},{18,26},{11,3},{19,27},{12,4},{... | collective-permute-start | bytes 4325384 | tf_op jit(solution)/shard_map/ppermute | solution.py:629
  344.9 27.9 %collective-permute-start.56 = (bf16[352,2048]{1,0:T(8,128)(2,1)S(1)}, bf16[352,2048]{1,0:T(8,128)(2,1)S(1)}, u32[]{:S(2)}, u32[]{:S(2)}) collective-permute-start(bf16[352,2048]{1,0:T(8,128)(2,1)S(1)} %add_convert_fusion.8), channel_id=1, source_target_pairs={{8,16},{16,8},{9,17},{17,9},{10,18},{18,10},{11,19},{19,11},{12,20... | collective-permute-start | bytes 4325384 | tf_op jit(solution)/shard_map/ppermute | solution.py:631
  345.7 57.3 %collective-permute-start.59 = (bf16[352,2048]{1,0:T(8,128)(2,1)S(1)}, bf16[352,2048]{1,0:T(8,128)(2,1)S(1)}, u32[]{:S(2)}, u32[]{:S(2)}) collective-permute-start(bf16[352,2048]{1,0:T(8,128)(2,1)S(1)} %copy-done.56), channel_id=1, source_target_pairs={{0,8},{24,16},{1,9},{25,17},{2,10},{26,18},{3,11},{27,19},{4,12},{... | collective-permute-start | bytes 4325384 | tf_op jit(solution)/shard_map/ppermute | solution.py:622
  374.4 29.8 %collective-permute-start.61 = (bf16[352,2048]{1,0:T(8,128)(2,1)S(1)}, bf16[352,2048]{1,0:T(8,128)(2,1)S(1)}, u32[]{:S(2)}, u32[]{:S(2)}) collective-permute-start(bf16[352,2048]{1,0:T(8,128)(2,1)S(1)} %add_convert_fusion.5), channel_id=1, source_target_pairs={{8,0},{16,24},{9,1},{17,25},{10,2},{18,26},{11,3},{19,27},{12,4},{... | collective-permute-start | bytes 4325384 | tf_op jit(solution)/shard_map/ppermute | solution.py:629
  376.6 27.6 %collective-permute-start.60 = (bf16[352,2048]{1,0:T(8,128)(2,1)S(1)}, bf16[352,2048]{1,0:T(8,128)(2,1)S(1)}, u32[]{:S(2)}, u32[]{:S(2)}) collective-permute-start(bf16[352,2048]{1,0:T(8,128)(2,1)S(1)} %add_convert_fusion.6), channel_id=1, source_target_pairs={{8,16},{16,8},{9,17},{17,9},{10,18},{18,10},{11,19},{19,11},{12,20... | collective-permute-start | bytes 4325384 | tf_op jit(solution)/shard_map/ppermute | solution.py:631
  377.4 50.5 %collective-permute-start.58 = (bf16[352,2048]{1,0:T(8,128)(2,1)}, bf16[352,2048]{1,0:T(8,128)(2,1)}, u32[]{:S(2)}, u32[]{:S(2)}) collective-permute-start(bf16[352,2048]{1,0:T(8,128)(2,1)} %convolution_convert_fusion.4), channel_id=1, source_target_pairs={{0,8},{24,16},{1,9},{25,17},{2,10},{26,18},{3,11},{27,19},{4,12},{... | collective-permute-start | bytes 4325384 | tf_op jit(solution)/shard_map/ppermute | solution.py:622
  410.2 28.9 %collective-permute-start.63 = (bf16[352,2048]{1,0:T(8,128)(2,1)}, bf16[352,2048]{1,0:T(8,128)(2,1)}, u32[]{:S(2)}, u32[]{:S(2)}) collective-permute-start(bf16[352,2048]{1,0:T(8,128)(2,1)} %add_convert_fusion.3), channel_id=1, source_target_pairs={{8,0},{16,24},{9,1},{17,25},{10,2},{18,26},{11,3},{19,27},{12,4},{... | collective-permute-start | bytes 4325384 | tf_op jit(solution)/shard_map/ppermute | solution.py:629
  413.1 26.0 %collective-permute-start.62 = (bf16[352,2048]{1,0:T(8,128)(2,1)}, bf16[352,2048]{1,0:T(8,128)(2,1)}, u32[]{:S(2)}, u32[]{:S(2)}) collective-permute-start(bf16[352,2048]{1,0:T(8,128)(2,1)} %add_convert_fusion.4), channel_id=1, source_target_pairs={{8,16},{16,8},{9,17},{17,9},{10,18},{18,10},{11,19},{19,11},{12,20... | collective-permute-start | bytes 4325384 | tf_op jit(solution)/shard_map/ppermute | solution.py:631
  439.2 201.5 %reduce-scatter.8.cloned.1.call-start = ((), (), s32[]{:S(2)}) async-start(), calls=%async_computation.5 | async-start | bytes 9437184 | tf_op jit(solution)/shard_map/reduce_scatter | solution.py:479
  445.2 62.2 %collective-permute-start.67 = (bf16[352,2048]{1,0:T(8,128)(2,1)S(1)}, bf16[352,2048]{1,0:T(8,128)(2,1)S(1)}, u32[]{:S(2)}, u32[]{:S(2)}) collective-permute-start(bf16[352,2048]{1,0:T(8,128)(2,1)S(1)} %add_convert_fusion.1), channel_id=1, source_target_pairs={{8,0},{16,24},{9,1},{17,25},{10,2},{18,26},{11,3},{19,27},{12,4},{... | collective-permute-start | bytes 4325384 | tf_op jit(solution)/shard_map/ppermute | solution.py:629
  449.2 58.2 %collective-permute-start.66 = (bf16[352,2048]{1,0:T(8,128)(2,1)S(1)}, bf16[352,2048]{1,0:T(8,128)(2,1)S(1)}, u32[]{:S(2)}, u32[]{:S(2)}) collective-permute-start(bf16[352,2048]{1,0:T(8,128)(2,1)S(1)} %add_convert_fusion.2), channel_id=1, source_target_pairs={{8,16},{16,8},{9,17},{17,9},{10,18},{18,10},{11,19},{19,11},{12,20... | collective-permute-start | bytes 4325384 | tf_op jit(solution)/shard_map/ppermute | solution.py:631
  457.3 50.0 %collective-permute-start.65 = (bf16[256,2048]{1,0:T(8,128)(2,1)S(1)}, bf16[256,2048]{1,0:T(8,128)(2,1)S(1)}, u32[]{:S(2)}, u32[]{:S(2)}) collective-permute-start(bf16[256,2048]{1,0:T(8,128)(2,1)S(1)} %fusion), channel_id=1, source_target_pairs={{0,8},{24,16},{1,9},{25,17},{2,10},{26,18},{3,11},{27,19},{4,12},{... | collective-permute-start | bytes 3145736 | tf_op jit(solution)/shard_map/ppermute | solution.py:622
  505.1 30.5 %collective-permute-start.64 = (bf16[2048,256]{1,0:T(8,128)(2,1)}, bf16[2048,256]{1,0:T(8,128)(2,1)}, u32[]{:S(2)}, u32[]{:S(2)}) collective-permute-start(bf16[2048,256]{1,0:T(8,128)(2,1)} %convolution_convert_fusion.10), channel_id=1, source_target_pairs={{0,8},{24,16},{1,9},{25,17},{2,10},{26,18},{3,11},{27,19},{4,12},{... | collective-permute-start | bytes 3145736 | tf_op jit(solution)/shard_map/ppermute | solution.py:622
  509.1 26.5 %collective-permute-start.69 = (bf16[352,2048]{1,0:T(8,128)(2,1)}, bf16[352,2048]{1,0:T(8,128)(2,1)}, u32[]{:S(2)}, u32[]{:S(2)}) collective-permute-start(bf16[352,2048]{1,0:T(8,128)(2,1)} %add_convert_fusion), channel_id=1, source_target_pairs={{8,0},{16,24},{9,1},{17,25},{10,2},{18,26},{11,3},{19,27},{12,4},{... | collective-permute-start | bytes 4325384 | tf_op jit(solution)/shard_map/ppermute | solution.py:629
  512.0 23.5 %collective-permute-start.68 = (bf16[256,2048]{1,0:T(8,128)(2,1)}, bf16[256,2048]{1,0:T(8,128)(2,1)}, u32[]{:S(2)}, u32[]{:S(2)}) collective-permute-start(bf16[256,2048]{1,0:T(8,128)(2,1)} %add_convert_fusion.17), channel_id=1, source_target_pairs={{8,16},{16,8},{9,17},{17,9},{10,18},{18,10},{11,19},{19,11},{12,20... | collective-permute-start | bytes 3145736 | tf_op jit(solution)/shard_map/ppermute | solution.py:631
  554.1 46.2 %collective-permute-start.74 = (bf16[2048,256]{1,0:T(8,128)(2,1)}, bf16[2048,256]{1,0:T(8,128)(2,1)}, u32[]{:S(2)}, u32[]{:S(2)}) collective-permute-start(bf16[2048,256]{1,0:T(8,128)(2,1)} %fusion.2), channel_id=1, source_target_pairs={{0,8},{24,16},{1,9},{25,17},{2,10},{26,18},{3,11},{27,19},{4,12},{... | collective-permute-start | bytes 3145736 | tf_op jit(solution)/shard_map/ppermute | solution.py:622
  573.1 27.9 %collective-permute-start.76 = (bf16[256,2048]{1,0:T(8,128)(2,1)}, bf16[256,2048]{1,0:T(8,128)(2,1)}, u32[]{:S(2)}, u32[]{:S(2)}) collective-permute-start(bf16[256,2048]{1,0:T(8,128)(2,1)} %add_convert_fusion.16), channel_id=1, source_target_pairs={{8,0},{16,24},{9,1},{17,25},{10,2},{18,26},{11,3},{19,27},{12,4},{... | collective-permute-start | bytes 3145736 | tf_op jit(solution)/shard_map/ppermute | solution.py:629
  574.5 13.0 %collective-permute-start.71 = (f32[2,2048]{1,0:T(2,128)S(1)}, f32[2,2048]{1,0:T(2,128)S(1)}, u32[]{:S(2)}, u32[]{:S(2)}) collective-permute-start(f32[2,2048]{1,0:T(2,128)S(1)} %fusion.48), channel_id=1, source_target_pairs={{0,2},{1,3},{2,0},{3,1},{4,6},{5,7},{6,4},{7,5},{8,10},{9,11},{10,... | collective-permute-start | bytes 49160 | tf_op jit(solution)/shard_map/ppermute | solution.py:541
  579.1 21.9 %collective-permute-start.75 = (bf16[2048,256]{1,0:T(8,128)(2,1)}, bf16[2048,256]{1,0:T(8,128)(2,1)}, u32[]{:S(2)}, u32[]{:S(2)}) collective-permute-start(bf16[2048,256]{1,0:T(8,128)(2,1)} %fusion.10), channel_id=1, source_target_pairs={{8,16},{16,8},{9,17},{17,9},{10,18},{18,10},{11,19},{19,11},{12,20... | collective-permute-start | bytes 3145736 | tf_op jit(solution)/shard_map/ppermute | solution.py:631
  593.3 29.4 %collective-permute-start.73 = (bf16[2144,256]{1,0:T(8,128)(2,1)S(1)}, bf16[2144,256]{1,0:T(8,128)(2,1)S(1)}, u32[]{:S(2)}, u32[]{:S(2)}) collective-permute-start(bf16[2144,256]{1,0:T(8,128)(2,1)S(1)} %fusion.32), channel_id=1, source_target_pairs={{0,8},{24,16},{1,9},{25,17},{2,10},{26,18},{3,11},{27,19},{4,12},{... | collective-permute-start | bytes 3293192 | tf_op jit(solution)/shard_map/ppermute | solution.py:622
  603.0 32.9 %collective-permute-start.78 = (bf16[2048,256]{1,0:T(8,128)(2,1)S(1)}, bf16[2048,256]{1,0:T(8,128)(2,1)S(1)}, u32[]{:S(2)}, u32[]{:S(2)}) collective-permute-start(bf16[2048,256]{1,0:T(8,128)(2,1)S(1)} %add_convert_fusion.15), channel_id=1, source_target_pairs={{8,0},{16,24},{9,1},{17,25},{10,2},{18,26},{11,3},{19,27},{12,4},{... | collective-permute-start | bytes 3145736 | tf_op jit(solution)/shard_map/ppermute | solution.py:629
  606.4 29.5 %collective-permute-start.77 = (bf16[2048,256]{1,0:T(8,128)(2,1)S(1)}, bf16[2048,256]{1,0:T(8,128)(2,1)S(1)}, u32[]{:S(2)}, u32[]{:S(2)}) collective-permute-start(bf16[2048,256]{1,0:T(8,128)(2,1)S(1)} %fusion.12), channel_id=1, source_target_pairs={{8,16},{16,8},{9,17},{17,9},{10,18},{18,10},{11,19},{19,11},{12,20... | collective-permute-start | bytes 3145736 | tf_op jit(solution)/shard_map/ppermute | solution.py:631
  636.3 32.9 %collective-permute-start.79 = (bf16[2144,256]{1,0:T(8,128)(2,1)S(1)}, bf16[2144,256]{1,0:T(8,128)(2,1)}, u32[]{:S(2)}, u32[]{:S(2)}) collective-permute-start(bf16[2144,256]{1,0:T(8,128)(2,1)S(1)} %add_convert_fusion.13), channel_id=1, source_target_pairs={{8,16},{16,8},{9,17},{17,9},{10,18},{18,10},{11,19},{19,11},{12,20... | collective-permute-start | bytes 3293192 | tf_op jit(solution)/shard_map/ppermute | solution.py:631
  639.3 29.9 %collective-permute-start.80 = (bf16[2048,256]{1,0:T(8,128)(2,1)}, bf16[2048,256]{1,0:T(8,128)(2,1)}, u32[]{:S(2)}, u32[]{:S(2)}) collective-permute-start(bf16[2048,256]{1,0:T(8,128)(2,1)} %add_convert_fusion.14), channel_id=1, source_target_pairs={{8,0},{16,24},{9,1},{17,25},{10,2},{18,26},{11,3},{19,27},{12,4},{... | collective-permute-start | bytes 3145736 | tf_op jit(solution)/shard_map/ppermute | solution.py:629
  670.8 25.4 %collective-permute-start.81 = (bf16[2144,256]{1,0:T(8,128)(2,1)S(1)}, bf16[2144,256]{1,0:T(8,128)(2,1)S(1)}, u32[]{:S(2)}, u32[]{:S(2)}) collective-permute-start(bf16[2144,256]{1,0:T(8,128)(2,1)S(1)} %add_convert_fusion.12), channel_id=1, source_target_pairs={{8,0},{16,24},{9,1},{17,25},{10,2},{18,26},{11,3},{19,27},{12,4},{... | collective-permute-start | bytes 3293192 | tf_op jit(solution)/shard_map/ppermute | solution.py:629
  (123 other events, 810.4 us)
Sparse Core Ops, SparseCore 0:
  253.5 71.6 reduce-scatter.3
  334.4 54.5 all-gather.2
  439.3 75.0 reduce-scatter.5
  535.8 74.2 reduce-scatter.7

commit v3 on v2

--- a/solution.py
+++ b/solution.py
@@ -1,3 +1,4 @@
+import math
 from functools import partial
 
 import jax
@@ -143,23 +144,20 @@
         ordered_ref[block, 0] = gated
 
 
-def mixer_back_kernel(
-    gg_ref, q_ref, k_ref, v_ref, resp_ref, spec_ref, taps_ref, skip_ref, filt_ref, dft_ref, inv_ref,
-    gproj_ref, gtaps_ref, gskip_ref, gfilt_ref, pad, late, response_grad, grad_conv, spectrum, product, lags, conv,
-):
-    sequence = pl.program_id(0)
+def mixer_back_kernel(first, last, *refs):
+    gg_ref, q_ref, k_ref, v_ref, resp_ref, spec_ref, taps_ref, skip_ref, filt_ref, dft_ref, inv_ref = refs[:11]
+    refs = refs[11:]
+    if not first:
+        taps_before, lags_before = refs[3:5]
+        refs = refs[5:]
+    gq_ref, gk_ref, gv_ref, gtaps_ref, result_ref, pad, late, response_grad, grad_conv, spectrum, product, conv = refs
     blocks, _, rows, chans = q_ref.shape
     length = blocks * rows
     load_padded((q_ref, k_ref, v_ref), pad)
     taps = taps_ref[...]
     skip = skip_ref[...]
 
-    @pl.when(sequence == 0)
-    def _():
-        gtaps_ref[...] = jnp.zeros_like(gtaps_ref)
-        gskip_ref[...] = jnp.zeros_like(gskip_ref)
-        lags[...] = jnp.zeros_like(lags)
-
+    gtaps_ref[...] = jnp.zeros_like(gtaps_ref) if first else taps_before[...]
     late[:, length : length + 8, :] = jnp.zeros((3, 8, chans), f32)
     skip_sum = jnp.zeros((1, chans), f32)
     for block in range(blocks):
@@ -175,7 +173,7 @@
         grad_conv[at, :] = grad.astype(bf16)
         late[0, at, :] = incoming * resp_ref[0, at, :]
         skip_sum = skip_sum + jnp.sum(grad * mixed, axis=0, keepdims=True)
-    gskip_ref[...] += skip_sum
+    gtaps_ref[9:10, :] += skip_sum
 
     spectrum[...] = dot32(dft_ref[...], grad_conv[...])
     for block in range(blocks):
@@ -186,8 +184,14 @@
         mre, mim = spec_ref[0, re, :], spec_ref[0, im, :]
         product[re, :] = (gre * hre + gim * him).astype(bf16)
         product[im, :] = (gim * hre - gre * him).astype(bf16)
-        lags[re, :] += gre * mre + gim * mim
-        lags[im, :] += gim * mre - gre * mim
+        lag_re = gre * mre + gim * mim
+        lag_im = gim * mre - gre * mim
+        if not first:
+            lag_re = lag_re + lags_before[re, :]
+            lag_im = lag_im + lags_before[im, :]
+        lags = spectrum if last else result_ref
+        lags[re, :] = lag_re
+        lags[im, :] = lag_im
     conv[...] = dot32(inv_ref[...], product[...])
 
     for block in range(blocks):
@@ -208,7 +212,7 @@
             for back in (1, 2):
                 tap = taps[3 * back + index : 3 * back + index + 1]
                 total = total + tap * late[index, start + back : start + back + rows, :]
-            gproj_ref[index, block, 0] = total.astype(bf16)
+            (gq_ref, gk_ref, gv_ref)[index][block, 0] = total.astype(bf16)
             for back in range(3):
                 shifted = pad[index, 8 + start - back : 8 + start - back + rows, :]
                 sums[3 * back + index] = sums[3 * back + index] + jnp.sum(
@@ -217,10 +221,9 @@
     for index in range(9):
         gtaps_ref[index : index + 1, :] += sums[index]
 
-    @pl.when(sequence == pl.num_programs(0) - 1)
-    def _():
-        product[...] = lags[...].astype(bf16)
-        gfilt_ref[...] = dot32(inv_ref[...], product[...])
+    if last:
+        product[...] = spectrum[...].astype(bf16)
+        result_ref[...] = dot32(inv_ref[...], product[...])
 
 
 def whole(shape):
@@ -309,35 +312,33 @@
             jax.ShapeDtypeStruct((seqs, 2 * length, chans), f32),
         ],
         compiler_params=params(),
-        cost_estimate=cost(1000, 1000),
+        cost_estimate=cost(8 * length * length * chans * seqs, 40 * length * chans * seqs),
         name="mixer_forward",
     )(me, proj, proj, proj, *fixed)
 
 
-def mixer_back(grad_gated, proj, response, spec, taps9, skip, filt_spec, dft, inverse):
+def mixer_back(number, before, grad_gated, proj, response, spec, taps9, skip, filt_spec, dft, inverse):
     blocks, seqs, rows, triple = proj.shape
     chans = triple // 3
     length = blocks * rows
     fixed = (taps9, skip, filt_spec, dft, inverse)
+    first, last = number == 0, number == seqs - 1
+    result = (length, chans) if last else (2 * length, chans)
 
     def part(index):
-        return pl.BlockSpec((blocks, 1, rows, chans), lambda s: (0, s, 0, index))
+        return pl.BlockSpec((blocks, 1, rows, chans), lambda i: (0, number, 0, index))
 
     return pl.pallas_call(
-        mixer_back_kernel,
-        grid=(seqs,),
+        partial(mixer_back_kernel, first, last),
+        grid=(1,),
         in_specs=[part(0), part(0), part(1), part(2)]
         + [
-            pl.BlockSpec((1, length, chans), lambda s: (s, 0, 0)),
-            pl.BlockSpec((1, 2 * length, chans), lambda s: (s, 0, 0)),
+            pl.BlockSpec((1, length, chans), lambda i: (number, 0, 0)),
+            pl.BlockSpec((1, 2 * length, chans), lambda i: (number, 0, 0)),
         ]
-        + [whole(op.shape) for op in fixed],
-        out_specs=[
-            pl.BlockSpec((3, blocks, 1, rows, chans), lambda s: (0, 0, s, 0, 0)),
-            whole(taps9.shape),
-            whole(skip.shape),
-            whole((length, chans)),
-        ],
+        + [whole(op.shape) for op in fixed]
+        + ([] if first else [pl.BlockSpec(memory_space=pl.ANY)] * 3 + [whole(op.shape) for op in before[3:]]),
+        out_specs=[part(0), part(0), part(0), whole((16, chans)), whole(result)],
         scratch_shapes=[
             pltpu.VMEM((3, length + 8, chans), f32),
             pltpu.VMEM((3, length + 8, chans), f32),
@@ -345,19 +346,15 @@
             pltpu.VMEM((length, chans), bf16),
             pltpu.VMEM((2 * length, chans), f32),
             pltpu.VMEM((2 * length, chans), bf16),
-            pltpu.VMEM((2 * length, chans), f32),
             pltpu.VMEM((length, chans), f32),
         ],
-        out_shape=[
-            jax.ShapeDtypeStruct((3, blocks, seqs, rows, chans), bf16),
-            jax.ShapeDtypeStruct(taps9.shape, f32),
-            jax.ShapeDtypeStruct(skip.shape, f32),
-            jax.ShapeDtypeStruct((length, chans), f32),
-        ],
+        out_shape=[jax.ShapeDtypeStruct((blocks, seqs, rows, chans), bf16)] * 3
+        + [jax.ShapeDtypeStruct((16, chans), f32), jax.ShapeDtypeStruct(result, f32)],
+        input_output_aliases={} if first else {11: 0, 12: 1, 13: 2},
         compiler_params=params(),
-        cost_estimate=cost(1000, 1000),
+        cost_estimate=cost(12 * length * length * chans, 80 * length * chans),
         name="mixer_backward",
-    )(grad_gated, proj, proj, proj, response, spec, *fixed)
+    )(grad_gated, proj, proj, proj, response, spec, *fixed, *before)
 
 
 def arrived(refs, counts, step, use):
@@ -393,7 +390,7 @@
 
     def use(rows):
         rows_ref[0] = rows
-        out_ref[0] = contract_cols(rows, weight_ref[...])
+        out_ref[...] = contract_cols(weight_ref[...], rows)
 
     arrived(refs, counts, pl.program_id(0), use)
 
@@ -405,14 +402,14 @@
 
     def use(rows):
         rows_ref[0] = rows
-        gate = contract_cols(rows, gate_w[...])
-        up = contract_cols(rows, up_w[...])
+        gate = contract_cols(gate_w[...], rows)
+        up = contract_cols(up_w[...], rows)
         sig = jax.nn.sigmoid(gate)
         silu = gate * sig
-        hidden_ref[0] = (silu * up).astype(bf16)
-        back = back_ref[0]
-        ggate_ref[0] = (back * up * sig * (1.0 + gate * (1.0 - sig))).astype(bf16)
-        gup_ref[0] = (back * silu).astype(bf16)
+        hidden_ref[...] = (silu * up).astype(bf16)
+        back = back_ref[...]
+        ggate_ref[...] = (back * up * sig * (1.0 + gate * (1.0 - sig))).astype(bf16)
+        gup_ref[...] = (back * silu).astype(bf16)
 
     arrived(refs, counts, pl.program_id(0), use)
 
@@ -421,9 +418,19 @@
     pieces = [piece for block in group for piece in block]
     rows = sum(piece.shape[0] * piece.shape[1] for piece in group[0])
 
-    def at_index(i, m):
+    def at_rows(i, m):
         return (m[0] ^ (start + i), 0, 0)
 
+    def at_cols(i, m):
+        return (0, m[0] ^ (start + i))
+
+    def out_spec(width, dtype, turned):
+        return pl.BlockSpec((width, rows), at_cols) if turned else pl.BlockSpec((1, rows, width), at_rows)
+
+    def out_type(width, dtype, turned):
+        return jax.ShapeDtypeStruct((width, total * rows) if turned else (total, rows, width), dtype)
+
+    work = sum(2 * op.size for op in fixed)
     operands = [me, *pieces, *fixed, *per_block, *filled]
     first = len(operands) - len(filled)
     return pl.pallas_call(
@@ -432,51 +439,123 @@
             num_scalar_prefetch=1,
             grid=(len(group),),
             in_specs=[whole(op.shape) for op in (*pieces, *fixed)]
-            + [pl.BlockSpec((1,) + op.shape[1:], at_index) for op in per_block]
+            + [pl.BlockSpec((op.shape[0], rows), at_cols) for op in per_block]
             + [pl.BlockSpec(memory_space=pl.ANY)] * len(filled),
-            out_specs=[pl.BlockSpec((1, rows, width), at_index) for width, _ in outputs],
+            out_specs=[out_spec(*output) for output in outputs],
         ),
-        out_shape=[jax.ShapeDtypeStruct((total, rows, width), dtype) for width, dtype in outputs],
+        out_shape=[out_type(*output) for output in outputs],
         input_output_aliases={first + i: i for i in range(len(filled))},
         compiler_params=params(),
-        cost_estimate=cost(1000, 1000),
+        cost_estimate=cost(len(group) * rows * work, sum(op.size * 2 for op in fixed)),
         name=kernel.__name__.removesuffix("_kernel"),
     )(*operands)
 
 
-def sum_products(rights, transposed):
+def sum_products(dot, rights, dtype, turned):
     def kernel(*refs):
         count = len(rights)
-        dot = contract_cols if transposed else dot32
-        total = dot(refs[0][0], refs[count][...])
-        for left, right in zip(refs[1:count], refs[count + 1 : 2 * count]):
-            total = total + dot(left[0], right[...])
-        refs[2 * count][0] = total.astype(bf16)
-
-    def call(*lefts):
-        blocks, rows, depth = lefts[0].shape
-        width = rights[0].shape[0 if transposed else 1]
+        lefts = [ref[...] if turned else ref[0] for ref in refs[:count]]
+        total = dot(lefts[0], refs[count][...])
+        for left, right in zip(lefts[1:], refs[count + 1 : 2 * count]):
+            total = total + dot(left, right[...])
+        refs[2 * count][0] = total.astype(dtype)
+
+    def call(blocks, *lefts):
+        if turned:
+            depth, rows = lefts[0].shape[0], lefts[0].shape[1] // blocks
+            left_spec = pl.BlockSpec((depth, rows), lambda i: (0, i))
+        else:
+            _, rows, depth = lefts[0].shape
+            left_spec = pl.BlockSpec((1, rows, depth), lambda i: (i, 0, 0))
+        width = rights[0].shape[0 if dot is contract_cols else 1]
         return pl.pallas_call(
             kernel,
             grid=(blocks,),
-            in_specs=[pl.BlockSpec((1, rows, depth), lambda i: (i, 0, 0))] * len(lefts)
-            + [whole(right.shape) for right in rights],
+            in_specs=[left_spec] * len(lefts) + [whole(right.shape) for right in rights],
             out_specs=pl.BlockSpec((1, rows, width), lambda i: (i, 0, 0)),
-            out_shape=jax.ShapeDtypeStruct((blocks, rows, width), bf16),
+            out_shape=jax.ShapeDtypeStruct((blocks, rows, width), dtype),
             compiler_params=params(),
-            cost_estimate=cost(1000, 1000),
+            cost_estimate=cost(sum(2 * left.size * width for left in lefts), 2 * blocks * rows * width),
             name="sum_products",
         )(*lefts, *rights)
 
     return call
 
 
+def outer_kernel(left_ref, right_ref, out_ref):
+    out_ref[...] = dot32(left_ref[...], right_ref[...]).astype(bf16)
+
+
+def outer(left, right, number, count):
+    height, depth = left.shape[0] // count, left.shape[1]
+    width = right.shape[1]
+    tile = math.gcd(width, 512)
+    return pl.pallas_call(
+        outer_kernel,
+        grid=(width // tile,),
+        in_specs=[
+            pl.BlockSpec((height, depth), lambda j: (number, 0)),
+            pl.BlockSpec((depth, tile), lambda j: (0, j)),
+        ],
+        out_specs=pl.BlockSpec((height, tile), lambda j: (0, j)),
+        out_shape=jax.ShapeDtypeStruct((height, width), bf16),
+        compiler_params=params(),
+        cost_estimate=cost(2 * height * depth * width, 2 * depth * width),
+        name="weight_gradient",
+    )(left, right)
+
+
 def gather_whole(block):
     return lax.all_gather(block, "mp", axis=0)
 
 
 def scatter_whole(partial_sums):
     return lax.psum_scatter(partial_sums, "mp", scatter_dimension=0).astype(f32)
+
+
+def finish_kernel(end_ref, outward_ref, total_ref, *refs):
+    refs[-1][...] = jnp.where(end_ref[0] == 1, outward_ref[...].astype(f32), total_ref[...].astype(f32))
+
+
+def finish(end, outward, total, start, used, height, filled):
+    width = total.shape[1]
+    rows = math.gcd(start, used) if start else used
+    rows = rows // 2 if rows * width > 512 * 1024 and rows % 32 == 0 else rows
+    piece = pl.BlockSpec((rows, width), lambda i, e: (i, 0))
+    return pl.pallas_call(
+        finish_kernel,
+        grid_spec=pltpu.PrefetchScalarGridSpec(
+            num_scalar_prefetch=1,
+            grid=(used // rows,),
+            in_specs=[piece, piece] + [pl.BlockSpec(memory_space=pl.ANY)] * len(filled),
+            out_specs=pl.BlockSpec((rows, width), lambda i, e: (start // rows + i, 0)),
+        ),
+        out_shape=jax.ShapeDtypeStruct((height, width), f32),
+        input_output_aliases={3: 0} if filled else {},
+        compiler_params=params(),
+        cost_estimate=cost(1000, 8 * used * width),
+        name="finish",
+    )(end, outward, total, *filled)
+
+
+def add_kernel(left_ref, right_ref, out_ref):
+    out_ref[...] = (left_ref[...].astype(f32) + right_ref[...].astype(f32)).astype(bf16)
+
+
+def add(left, right):
+    height, width = left.shape
+    rows = height // 2 if height % 32 == 0 and height > 128 else height
+    piece = pl.BlockSpec((rows, width), lambda i: (i, 0))
+    return pl.pallas_call(
+        add_kernel,
+        grid=(height // rows,),
+        in_specs=[piece, piece],
+        out_specs=piece,
+        out_shape=jax.ShapeDtypeStruct(left.shape, bf16),
+        compiler_params=params(),
+        cost_estimate=cost(1000, 1000),
+        name="add",
+    )(left, right)
 
 
 def together(*values):
@@ -521,8 +600,8 @@
     def gather(self, block):
         return WholeGather(block)
 
-    def scatter(self, groups, given, compute):
-        return scatter_whole(groups[0]), compute(given)
+    def scatter(self, array, product, coming, compute):
+        return scatter_whole(product(array)), compute(coming)
 
     def sum_mp(self, part):
         return lax.psum(part, "mp")
@@ -530,12 +609,28 @@
     def push(self, part):
         self.parts.append(part)
 
-    def hop(self, *values):
+    def hop_in(self, *values):
         return values
+
+    def hop_out(self, *values, keep=0):
+        return values
+
+    def come(self, *values):
+        return values
+
+    def sums_so_far(self):
+        return self.sums()
 
     def sums(self):
         return [lax.psum(part, "dp") for part in self.parts]
 
+    def join(self, sums, total=None, before=None, number=0):
+        joined = jnp.concatenate(([] if before is None else [before]) + [part.astype(f32) for part in sums], axis=0)
+        return joined
+
+    def plain(self, total):
+        return total.astype(f32)
+
 
 def swap(block, bit):
     return lax.ppermute(block, "mp", [(i, i ^ bit) for i in range(8)])
@@ -543,13 +638,7 @@
 
 class SquareGather:
     def __init__(self, block):
-        cut = block.shape[0] // 2
-        low, high = block[:cut], block[cut:]
-        x_low, y_high = swap(low, 2), swap(high, 4)
-        sibling = swap(block, 1)
-        low, high, sibling = together(low, high, sibling)
-        x_high, y_low = swap(high, 2), swap(low, 4)
-        self.here = {"near": (block, sibling), "lead": (x_low, y_high), "rest": (x_high, y_low)}
+        self.here = {"near": (block, swap(block, 1)), "side": (swap(block, 2), swap(block, 4))}
 
     def tie(self, names, *values):
         held, values = together([self.here[name] for name in names], values)
@@ -557,26 +646,24 @@
         return values
 
     def reach(self):
-        x_low, y_high = self.here["lead"]
-        self.here["far"] = (swap(x_low, 4), swap(y_high, 2))
+        x_all, y_all = self.here["side"]
+        cut = x_all.shape[0] // 2
+        self.here["far"] = (swap(x_all[:cut], 4), swap(y_all[cut:], 2))
 
     def near(self):
         return [(block,) for block in self.here["near"]]
 
     def side(self):
-        (x_low, y_high), (x_high, y_low) = self.here["lead"], self.here["rest"]
-        return self.twins((x_low, x_high)) + self.twins((y_low, y_high))
+        return [(block,) for here in self.here["side"] for block in (here, swap(here, 1))]
 
     def far(self):
-        return self.twins(self.here["far"])
-
-    def twins(self, halves):
+        halves = self.here["far"]
         return [halves, tuple(swap(half, 1) for half in halves)]
 
 
 class Square:
     def __init__(self):
-        self.queue, self.half, self.total, self.done = [], None, None, []
+        self.queue, self.middle, self.sent, self.done = [], [], [], []
 
     def counts(self, size):
         return (2, 4, 2)
@@ -587,14 +674,14 @@
     def gather(self, block):
         return SquareGather(block)
 
-    def scatter(self, groups, given, compute):
-        near, side, far = groups
-        half = near.shape[1] // 2
-
+    def scatter(self, array, product, coming, compute):
         def both(mine, other):
             return mine.astype(f32) + swap(other, 1).astype(f32)
 
+        far, array = together(product(array[6:8]), array)
+        half = far.shape[1] // 2
         far_sum = both(far[0], far[1])
+        side, near, far_sum = together(product(array[2:6]), product(array[0:2]), far_sum)
         far_low, far_high = far_sum[:half].astype(bf16), far_sum[half:].astype(bf16)
         from_far_low, from_far_high = swap(far_low, 2), swap(far_high, 4)
         x_sum = both(side[0], side[1])
@@ -602,9 +689,11 @@
         own_low_x = swap(x_sum[:half].astype(bf16), 2)
         own_high_y = swap(y_sum[half:].astype(bf16), 4)
         own = both(near[0], near[1])
-        own, x_sum, y_sum, given = together(own, x_sum, y_sum, given)
-        beside = compute(given)
-        from_far_low, from_far_high, beside = together(from_far_low, from_far_high, beside)
+        own, x_sum, y_sum = coming.tie(["near", "side", "far"], own, x_sum, y_sum)
+        beside = compute(coming)
+        from_far_low, from_far_high, own_low_x, own_high_y, beside = together(
+            from_far_low, from_far_high, own_low_x, own_high_y, beside
+        )
         y_low = (y_sum[:half] + from_far_low.astype(f32)).astype(bf16)
         x_high = (x_sum[half:] + from_far_high.astype(f32)).astype(bf16)
         own_low_y = swap(y_low, 4)
@@ -621,26 +710,49 @@
     def push(self, part):
         self.queue.append((part, lax.ppermute(part, "dp", [(0, 1), (3, 2)])))
 
-    def hop(self, *values):
-        part = inward = across = outward = None
-        if self.queue:
-            part, inward = self.queue.pop(0)
-        if self.total is not None:
-            outward = lax.ppermute(self.total, "dp", [(1, 0), (2, 3)])
-        if self.half is not None:
-            across = lax.ppermute(self.half, "dp", [(1, 2), (2, 1)])
-        inward, across, outward, values = together(inward, across, outward, values)
-        if outward is not None:
-            place = lax.axis_index("dp")
-            self.done.append(jnp.where((place == 0) | (place == 3), outward, self.total))
-        self.total = None if across is None else (self.half.astype(f32) + across.astype(f32)).astype(bf16)
-        self.half = None if inward is None else (part.astype(f32) + inward.astype(f32)).astype(bf16)
+    def hop_in(self, *values):
+        part, inward = self.queue.pop(0)
+        inward, values = together(inward, values)
+        half = add(part, inward)
+        self.middle.append((half, lax.ppermute(half, "dp", [(1, 2), (2, 1)])))
         return values
 
+    def hop_out(self, *values, keep=0):
+        half, across = self.middle.pop(0)
+        ready = len(self.sent) - keep
+        outward = [sent for _, sent in self.sent[:ready]]
+        across, outward, values = together(across, outward, values)
+        self.done += list(zip(outward, [total for total, _ in self.sent[:ready]]))
+        total = add(half, across)
+        self.sent = self.sent[ready:] + [(total, lax.ppermute(total, "dp", [(1, 0), (2, 3)]))]
+        return values
+
+    def come(self, *values):
+        (total, outward), self.sent = self.sent[0], self.sent[1:]
+        outward, values = together(outward, values)
+        self.done.append((outward, total))
+        return values
+
+    def sums_so_far(self):
+        return self.done
+
     def sums(self):
-        while self.queue or self.half is not None or self.total is not None:
-            self.hop()
-        return self.done
+        return self.done + [(outward, total) for total, outward in self.sent]
+
+    def join(self, sums, total=None, before=None, number=0):
+        place = lax.axis_index("dp")
+        end = ((place == 0) | (place == 3)).astype(jnp.int32).reshape(1)
+        height = sums[0][1].shape[0]
+        filled = () if before is None else (before,)
+        for outward, part in sums:
+            filled = (finish(end, outward, part, number * height, height, height * (total or len(sums)), filled),)
+            number += 1
+        return filled[0]
+
+    def plain(self, pair):
+        place = lax.axis_index("dp")
+        outward, total = pair
+        return jnp.where((place == 0) | (place == 3), outward, total).astype(f32)
 
 
 def local(
@@ -693,9 +805,6 @@
     filt_spec = make_filter(tables, residue_t, dft)
     grad_final = by_sequence(cotangent).astype(f32) * valid
     grad_final_low = grad_final.astype(bf16)
-    filt_spec, grad_final_low = coming.tie(["lead"], filt_spec, grad_final_low)
-    coming.reach()
-
     blocks = lax.axis_size("mp")
     counts = links.counts(blocks)
     starts = [sum(counts[:i]) for i in range(len(counts))]
@@ -706,146 +815,158 @@
         return on_arrival(kernel, me, group, starts[number], blocks, fixed, per_block, outputs, filled)
 
     def projected(group, number, filled):
-        return arrive(project_kernel, group, number, (in_parts,), (), ((3 * chans, f32), (width, bf16)), filled)
+        return arrive(project_kernel, group, number, (in_parts,), (), ((3 * chans, f32, False), (width, bf16, False)), filled)
 
     filled = projected(coming.near(), 0, ())
-    (filled,) = coming.tie(["lead", "rest"], filled)
+    filled, filt_spec, grad_final_low = coming.tie(["side"], filled, filt_spec, grad_final_low)
+    coming.reach()
     filled = projected(coming.side(), 1, filled)
     filled, grad_final_low = coming.tie(["far"], filled, grad_final_low)
     grad_coming = links.gather(grad_final_low)
     proj, normed_all = projected(coming.far(), 2, filled)
-    (proj,) = grad_coming.tie(["lead"], proj)
-    grad_coming.reach()
     proj = proj.reshape(blocks, seqs, rows, 3 * chans)
     taps9 = short_taps.reshape(9, chans)
     skip = conv_skip.reshape(1, chans)
     gated, gated_ordered, response, spec = mixer(me, proj, taps9, skip, filt_spec, dft, inverse)
-    (gated,) = grad_coming.tie(["lead", "rest"], gated)
-
-    mixed_groups = [None] * len(counts)
-    for i in reversed(range(len(counts))):
-        if counts[i]:
-            part = gated[starts[i] : starts[i] + counts[i]]
-            mixed_groups[i] = grouped(dot32(flat(part), out_proj).astype(bf16), part)
+    (gated,) = grad_coming.tie(["side"], gated)
+    grad_coming.reach()
+
+    def mixed_out(part):
+        return grouped(dot32(flat(part), out_proj).astype(bf16), part)
 
     def hidden_backed(group, number, filled):
-        return arrive(hidden_back_kernel, group, number, (down_proj,), (), ((hidden_units, f32), (width, bf16)), filled)
-
-    def beside_scatter(held):
-        near, side = held
-        return hidden_backed(side, 1, hidden_backed(near, 0, ()))
-
-    mixed_sum, filled = links.scatter(mixed_groups, (grad_coming.near(), grad_coming.side()), beside_scatter)
+        return arrive(hidden_back_kernel, group, number, (down_proj,), (), ((hidden_units, f32, True), (width, bf16, False)), filled)
+
+    def beside_scatter(grad_coming):
+        return hidden_backed(grad_coming.side(), 1, hidden_backed(grad_coming.near(), 0, ()))
+
+    mixed_sum, filled = links.scatter(gated, mixed_out, grad_coming, beside_scatter)
     second = rows_in + mixed_sum
     scale_second = row_scale(second)
     mlp_normed = (second * scale_second * mlp_gain).astype(bf16)
     coming = links.gather(mlp_normed)
-    filled, mlp_normed = grad_coming.tie(["far"], filled, mlp_normed) if counts[2] else (filled, mlp_normed)
     grad_hidden, grad_final_all = hidden_backed(grad_coming.far(), 2, filled)
-    (grad_hidden,) = coming.tie(["lead"], grad_hidden)
+
+    def fed(group, number, filled):
+        outputs = ((hidden_units, bf16, True),) * 3 + ((width, bf16, False),)
+        return arrive(feed_kernel, group, number, (gate_t, up_t), (grad_hidden,), outputs, filled)
+
+    (filled,) = coming.tie(["side"], fed(coming.near(), 0, ()))
     coming.reach()
-
-    def fed(group, number, filled):
-        outputs = ((hidden_units, bf16),) * 3 + ((width, bf16),)
-        return arrive(feed_kernel, group, number, (gate_t, up_t), (grad_hidden,), outputs, filled)
-
-    filled = fed(coming.near(), 0, ())
-    (filled,) = coming.tie(["lead", "rest"], filled)
     filled = fed(coming.side(), 1, filled)
-    if counts[2]:
-        (filled,) = coming.tie(["far"], filled)
+    (filled,) = coming.tie(["far"], filled)
     hidden, grad_gate, grad_up, mlp_all = fed(coming.far(), 2, filled)
 
-    def weight_gradient(left, right, number=0, count=1):
-        left, right = flat(left), flat(right)
-        total = left.shape[1]
-        left = left[:, number * total // count : (number + 1) * total // count]
-        return contract_rows(left, right).astype(bf16)
+    def weight_gradient(left, right):
+        return contract_rows(flat(left), flat(right)).astype(bf16)
 
     def blocked(array):
         return array.reshape(blocks, seqs, rows, array.shape[-1])
 
-    down_one, hidden, grad_gate = together(weight_gradient(hidden, grad_final_all, 0, 2), hidden, grad_gate)
-    links.push(down_one)
-    down_two = weight_gradient(hidden, grad_final_all, 1, 2)
-    mlp_back = blocked(sum_products((gate_t, up_t), False)(grad_gate, grad_up))
-    mlp_back, down_two, grad_gate = links.hop(mlp_back, down_two, grad_gate)
+    grad_final_all, mlp_all = flat(grad_final_all), flat(mlp_all)
+    links.push(outer(hidden, grad_final_all, 0, 2))
+    down_two, grad_gate, grad_up = together(outer(hidden, grad_final_all, 1, 2), grad_gate, grad_up)
     links.push(down_two)
+    mlp_back = blocked(sum_products(contract_rows, (gate_t, up_t), bf16, True)(blocks, grad_gate, grad_up))
+    gate_one = outer(grad_gate, mlp_all, 0, 2)
+    mlp_back, gate_one, grad_gate = links.hop_in(mlp_back, gate_one, grad_gate)
+    links.push(gate_one)
     grad_mlp_normed = scatter_whole(mlp_back)
-    links.push(weight_gradient(grad_gate, mlp_all, 0, 2))
-    gate_two = weight_gradient(grad_gate, mlp_all, 1, 2)
-    gate_two, hidden, grad_up = links.hop(gate_two, hidden, grad_up)
+    gate_two = outer(grad_gate, mlp_all, 1, 2)
+    gate_two, grad_up = links.hop_in(gate_two, grad_up)
     links.push(gate_two)
-    up_one = weight_gradient(grad_up, mlp_all, 0, 2)
-    up_one, grad_up, second = links.hop(up_one, grad_up, second)
+    (grad_up,) = links.hop_out(grad_up)
+    up_one = outer(grad_up, mlp_all, 0, 2)
+    up_one, grad_up = links.hop_in(up_one, grad_up)
     links.push(up_one)
+    grad_up, hidden, second = links.hop_out(grad_up, hidden, second)
     grad_second = grad_final + norm_back(grad_mlp_normed, second, scale_second, mlp_gain)
+    gain_two = jnp.sum(grad_mlp_normed * second * scale_second, axis=(0, 1))
     grad_branch_all = gather_whole(grad_second.astype(bf16))
-    gain_two = jnp.sum(grad_mlp_normed * second * scale_second, axis=(0, 1))
-    up_two = weight_gradient(grad_up, mlp_all, 1, 2)
-    up_two, gain_two, hidden = links.hop(up_two, gain_two, hidden)
+    up_two = outer(grad_up, mlp_all, 1, 2)
+    up_two, gain_two, hidden = links.hop_in(up_two, gain_two, hidden)
     links.push(up_two)
-    mlp_part = blocked(dot32(flat(hidden), down_proj).astype(bf16))
-    mlp_part, gated_ordered, out_here = links.hop(mlp_part, gated_ordered, out_proj)
-
-    grad_gated = blocked(contract_cols(flat(grad_branch_all), out_here))
-    links.push(weight_gradient(gated_ordered, grad_branch_all))
-    grad_gated, mlp_part = links.hop(grad_gated, mlp_part)
+    mlp_part = blocked(sum_products(contract_rows, (down_proj,), bf16, True)(blocks, hidden))
+    (mlp_part,) = links.hop_out(mlp_part)
+    (gated_ordered,) = links.hop_in(gated_ordered)
+
+    grad_gated = blocked(
+        sum_products(contract_cols, (out_proj,), f32, False)(blocks, grad_branch_all.reshape(blocks, -1, width))
+    )
+    grads_out = weight_gradient(gated_ordered, grad_branch_all)
+    grads_out, grad_gated, mlp_part = links.hop_out(grads_out, grad_gated, mlp_part)
+    links.push(grads_out)
     mlp_out = scatter_whole(mlp_part)
-    grad_proj, grad_taps, grad_skip, grad_filt = mixer_back(
-        grad_gated, proj, response, spec, taps9, skip, filt_spec, dft, inverse
+    back = ()
+    for number in range(seqs - 1):
+        back = mixer_back(number, back, grad_gated, proj, response, spec, taps9, skip, filt_spec, dft, inverse)
+    back, grad_gated = links.hop_in(back, grad_gated)
+    back, grad_gated = links.hop_out(back, grad_gated)
+    *grad_parts, grad_taps, grad_filt = mixer_back(
+        seqs - 1, tuple(back), grad_gated, proj, response, spec, taps9, skip, filt_spec, dft, inverse
     )
-    grad_parts = [part.reshape(blocks, seqs * rows, chans) for part in grad_proj]
+    grad_parts = [part.reshape(blocks, seqs * rows, chans) for part in grad_parts]
     grad_q = weight_gradient(normed_all, grad_parts[0])
     links.push(grad_q)
-    grad_parts, gain_two = links.hop(grad_parts, gain_two)
-    grad_in_rows = blocked(sum_products(tuple(in_parts), True)(*grad_parts))
+    grad_q, grad_parts, grad_filt = links.hop_in(grad_q, grad_parts, grad_filt)
+    grad_parts, grad_filt = links.hop_out(grad_parts, grad_filt)
     grad_k = weight_gradient(normed_all, grad_parts[1])
     links.push(grad_k)
     grad_v = weight_gradient(normed_all, grad_parts[2])
-    grad_in_rows, grad_v, grad_filt, mlp_out = links.hop(grad_in_rows, grad_v, grad_filt, mlp_out)
+    links.push(grad_v)
+    grads_in, grad_parts, grad_filt = links.hop_in((grad_q, grad_k, grad_v), grad_parts, grad_filt)
+    grad_in_rows = blocked(sum_products(contract_cols, tuple(in_parts), bf16, False)(blocks, *grad_parts))
+    grad_in_rows, grads_in, grad_filt = links.hop_in(grad_in_rows, grads_in, grad_filt)
     grad_normed = scatter_whole(grad_in_rows)
+    grads_in, grad_filt = links.hop_out(grads_in, grad_filt)
 
     ones = jnp.ones((8, chans), bf16)
     against = sum(
         contract_cols(ones, (grad.astype(f32) * part.astype(f32)).astype(bf16))[0]
-        for grad, part in zip((grad_q, grad_k, grad_v), in_parts)
+        for grad, part in zip(grads_in, in_parts)
     )
-    gains = links.sum_mp(jnp.stack([against / norm_gain, gain_two], axis=0))
+    gains = jnp.stack([against / norm_gain, gain_two], axis=0)
+    gains, grad_filt = links.hop_in(gains, grad_filt)
+    gains, grad_filt = links.hop_out(gains, grad_filt, keep=1)
     pole_sum, pole_re, pole_im = pole_gradients(grad_filt, tables)
+    gains, pole_sum = links.hop_out(links.sum_mp(gains), pole_sum, keep=1)
     poles = filter_residue.shape[1]
-    small = jnp.concatenate(
-        [grad_taps, grad_skip, pole_sum, -residue_t * pole_re, -residue_t * pole_im, gains.reshape(-1, chans)], axis=0
-    )
-    small_rows = small.shape[0]
-    small = jnp.pad(small.astype(bf16), ((0, -small_rows % 32), (0, 0)))
-    links.push(jnp.concatenate([grad_v, small], axis=0))
-    (mlp_out,) = links.hop(mlp_out)
+    small = [grad_taps, pole_sum, -residue_t * pole_re, -residue_t * pole_im, gains.reshape(-1, chans)]
+    small = [jnp.pad(rows_of, ((0, -rows_of.shape[0] % 8), (0, 0))) for rows_of in small]
+    bounds = np.cumsum([0] + [rows_of.shape[0] for rows_of in small])
+    small = jnp.pad(jnp.concatenate(small, axis=0), ((0, -int(bounds[-1]) % 16), (0, 0))).astype(bf16)
+    links.push(small)
+    sum_down = links.join(links.sums_so_far()[:2])
+    sum_down, grad_second = links.hop_out(sum_down, grad_second, keep=1)
+    sum_gate = links.join(links.sums_so_far()[2:4])
+    sum_gate, grad_second = links.hop_in(sum_gate, grad_second)
+    sum_up, sum_out = links.join(links.sums_so_far()[4:6]), links.join(links.sums_so_far()[6:7])
+    sum_up, sum_out, mlp_out = links.come(sum_up, sum_out, mlp_out)
+    sum_in = links.join(links.sums_so_far()[7:9], 3)
     layer_out = ((second + mlp_out) * valid).astype(bf16)
-    layer_out, grad_second = links.hop(layer_out, grad_second)
-    grad_tokens = grad_second + norm_back(grad_normed, rows_in, scale_in, norm_gain)
-    (grad_tokens,) = links.hop(by_position(grad_tokens))
+    grad_tokens = by_position(grad_second + norm_back(grad_normed, rows_in, scale_in, norm_gain))
+    sum_in, layer_out, grad_tokens = links.hop_out(sum_in, layer_out, grad_tokens, keep=1)
 
     sums = links.sums()
-    sum_small = sums[-1][width:].astype(f32)
-    pole_grads = [sum_small[10 + poles * i : 10 + poles * (i + 1)].T for i in range(3)]
-    gains = sum_small[10 + 3 * poles : small_rows].reshape(2, width)
-    sum_in = jnp.stack([sums[7], sums[8], sums[9][:width]], axis=0).astype(f32)
+    sum_in = links.join(sums[9:10], 3, sum_in, 2).reshape(3, width, chans)
+    sum_small = links.plain(sums[10])
+    small = [sum_small[low:high] for low, high in zip(bounds[:-1], bounds[1:])]
+    gains = small[4][: 2 * width // chans].reshape(2, width)
     return (
         by_position(layer_out),
         grad_tokens,
         gains[0],
         sum_in.transpose(1, 0, 2),
-        sum_small[:9].reshape(3, 3, chans),
-        sum_small[9],
-        pole_grads[0],
-        pole_grads[1],
-        pole_grads[2],
-        sums[6].astype(f32),
+        small[0][:9].reshape(3, 3, chans),
+        small[0][9],
+        small[1][:poles].T,
+        small[2][:poles].T,
+        small[3][:poles].T,
+        sum_out,
         gains[1],
-        jnp.concatenate(sums[2:4], axis=0).astype(f32).T,
-        jnp.concatenate(sums[4:6], axis=0).astype(f32).T,
-        jnp.concatenate(sums[:2], axis=0).astype(f32),
+        sum_gate.T,
+        sum_up.T,
+        sum_down,
     )
 
 

time: 724 us -> 697 us (0.963)
  Pallas kernels: 159 us -> 300 us
  matrix products: 85.5 us -> 25 us
  other arithmetic: 89.1 us -> 29.6 us
  waiting for transfers between devices: 197 us -> 149 us
    pallas_call x3 -> x44, Pallas kernels: 55.7 us -> 198 us  [the longest x4 52.7 us: call(): pl.pallas_call(kernel, grid=(blocks,), in_specs=[left_spec] * len(lefts)...]
    dot_general x10 -> x4, matrix products: 62.5 us -> 19.9 us  [contract_rows(): lax.dot_general(left, right, (((0,), (0,)), ((), ())), preferred_element_...]
    convert_element_type x23 -> x1, other arithmetic: 40.6 us -> 0.01 us  [plain(): return jnp.where((place == 0) | (place == 3), outward, total).astype(f32)]
    ppermute x20 -> x22, waiting for transfers between devices: 71.9 us -> 33 us  [the longest x11 32.9 us: hop_out(): lax.ppermute(total, 'dp', [(1, 0), (2, 3)])]
    ppermute x10 -> x11, waiting for transfers between devices: 78.7 us -> 67.1 us  [push(): self.queue.append((part, lax.ppermute(part, 'dp', [(0, 1), (3, 2)])))]
    select_n x7 -> x0, other arithmetic: 10 us -> none  [hop(): jnp.where((place == 0) | (place == 3), outward, self.total)]
    transpose x2 -> x0, other arithmetic: 9.6 us -> none  [the longest x1 5.19 us: local(): jnp.concatenate(sums[4:6], axis=0).astype(f32)]
    dot_general x4 -> x3, matrix products: 11.5 us -> 2.42 us  [contract_cols(): lax.dot_general(left, right, (((1,), (1,)), ((), ())), preferred_element_...]
  transfers between devices with their start and end apart: 86 -> 77, of which waited for: 38 -> 38; matrix products, arithmetic and copies ran while one was open for 24% -> 7% of each run, Pallas kernels for 21% -> 42%
where the time goes in v3:
time: 697 us; the launch traced here: 685 us
  Pallas kernels  300 us (43%)
  waiting for transfers between devices  149 us (21%)
  starting transfers between devices  128 us (18%)
  local copies, waits for them, and re-layouts  36.9 us (5%)
  other arithmetic  29.6 us (4%)
  matrix products  25 us (4%)
  between operations  16 us (2%)
    ppermute x11, starting transfers between devices, push(): self.queue.append((part, lax.ppermute(part, 'dp', [(0, 1), (3, 2)])))  70.5 us
    pallas_call x9, Pallas kernels, on_arrival(): pl.pallas_call(partial(kernel, [len(block) for block in group], len(fille...  69 us
    ppermute x11, waiting for transfers between devices, push(): self.queue.append((part, lax.ppermute(part, 'dp', [(0, 1), (3, 2)])))  67.1 us
    pallas_call x4, Pallas kernels, call(): pl.pallas_call(kernel, grid=(blocks,), in_specs=[left_spec] * len(lefts)...  52.7 us
    ppermute x40, waiting for transfers between devices, swap(): return lax.ppermute(block, 'mp', [(i, i ^ bit) for i in range(8)])  49.2 us
    pallas_call x6, Pallas kernels, outer(): pl.pallas_call(outer_kernel, grid=(width // tile,), in_specs=[pl.BlockSpe...  41.8 us
    pallas_call x22, Pallas kernels, add(): pl.pallas_call(add_kernel, grid=(height // rows,), in_specs=[piece, piece...  41.6 us
    ppermute x11, waiting for transfers between devices, hop_out(): lax.ppermute(total, 'dp', [(1, 0), (2, 3)])  32.9 us
  transfers between devices with their start and end apart: 77, of which 38 were waited for; matrix products, arithmetic and copies ran while one was open for 7% of the time, Pallas kernels for 42%

profile of v3, /device:TPU:0, one launch (start us, length us, event | category | flops | bytes accessed | tf_op | source)
XLA Modules:
  0.0 685.1 jit_solution(14379314102935539748)
XLA Ops:
  16.3 2.8 fusion.24
  21.2 9.3 %modal_filter.1.filt_ref.refs_8_ = f32[2048,256]{1,0:T(8,128)} custom-call(f32[32,16,256]{2,1,0:T(8,128)S(1)} %get-tuple-element.453.hre_ref, f32[32,16,256]{2,1,0:T(8,128)S(1)} %get-tuple-element.452.him_ref, f32[16,32,256]{2,1,0:T(8,128)S(1)} %get-tuple-element.451.lre_ref, f32[16,32,256]{2,1,0:T(8,128)} %get-tuple-element.450.lim_ref, ...), custom_call_target="tpu_custom_call" | custom-call | tf_op jit(solution)/shard_map/modal_filter/pallas_call | solution.py:246
  31.8 5.9 project.3
  46.5 8.5 %project.4 = (f32[8,256,768]{2,1,0:T(8,128)}, bf16[8,256,2048]{2,1,0:T(8,128)(2,1)}) custom-call(s32[1]{0:T(128)} %bitcast.me_ref, bf16[2,128,2048]{2,1,0:T(8,128)(2,1)S(1)} %collective-permute-done.refs_0_, bf16[2,128,2048]{2,1,0:T(8,128)(2,1)} %copy-done.82, ...), custom_call_target="tpu_custom_call", output_to_operand_aliasing={{0}: (6, {}), {1}: (7, {})} | custom-call | flops 3221225472 | bytes 3145728 | tf_op jit(solution)/shard_map/project/pallas_call | solution.py:436
  60.0 5.4 project.5
  65.4 17.0 %mixer_forward.1 = (bf16[8,2,128,256]{3,2,1,0:T(8,128)(2,1)S(1)}, bf16[8,2,128,256]{3,2,1,0:T(8,128)(2,1)}, f32[2,1024,256]{2,1,0:T(8,128)}, f32[2,2048,256]{2,1,0:T(8,128)}) custom-call(s32[1]{0:T(128)} %bitcast.me_ref, f32[8,2,128,768]{3,2,1,0:T(8,128)} %bitcast.158, f32[8,2,128,768]{3,2,1,0:T(8,128)} %bitcast.159, f32[8,2,128,768]{3,2,1,0:T(8,128)} %bitcast.160, ...), custom_call_target="tpu_custom_call" | custom-call | flops 4294967296 | bytes 20971520 | tf_op jit(solution)/shard_map/mixer_forward/pallas_call | solution.py:289
  95.1 7.7 %collective-permute-done.12.refs_0_ = bf16[1,128,2048]{2,1,0:T(8,128)(2,1)S(1)} collective-permute-done((bf16[1,128,2048]{2,1,0:T(8,128)(2,1)S(1)}, bf16[1,128,2048]{2,1,0:T(8,128)(2,1)S(1)}, u32[]{:S(2)}, u32[]{:S(2)}) %collective-permute-start.12) | collective-permute-done | bytes 524320 | tf_op jit(solution)/shard_map/ppermute | solution.py:636
  111.7 5.7 hidden_back.3
  117.4 8.7 %hidden_back.4 = (f32[704,2048]{1,0:T(8,128)}, bf16[8,256,2048]{2,1,0:T(8,128)(2,1)}) custom-call(s32[1]{0:T(128)} %bitcast.me_ref, bf16[2,128,2048]{2,1,0:T(8,128)(2,1)S(1)} %collective-permute-done.8.refs_0_, bf16[2,128,2048]{2,1,0:T(8,128)(2,1)} %copy-done.79, ...), custom_call_target="tpu_custom_call", output_to_operand_aliasing={{0}: (6, {}), {1}: (7, {})} | custom-call | flops 2952790016 | bytes 2883584 | tf_op jit(solution)/shard_map/hidden_back/pallas_call | solution.py:436
  126.1 5.0 collective-permute-done.20
  137.1 9.3 %collective-permute-done.25 = bf16[1,128,2048]{2,1,0:T(8,128)(2,1)S(1)} collective-permute-done((bf16[1,128,2048]{2,1,0:T(8,128)(2,1)S(1)}, bf16[1,128,2048]{2,1,0:T(8,128)(2,1)S(1)}, u32[]{:S(2)}, u32[]{:S(2)}) %collective-permute-start.25) | collective-permute-done | bytes 524320 | tf_op jit(solution)/shard_map/ppermute | solution.py:636
  157.1 5.2 hidden_back.5
  163.3 8.4 %feed.3 = (bf16[704,2048]{1,0:T(8,128)(2,1)}, bf16[704,2048]{1,0:T(8,128)(2,1)}, bf16[704,2048]{1,0:T(8,128)(2,1)}, bf16[8,256,2048]{2,1,0:T(8,128)(2,1)}) custom-call(s32[1]{0:T(128)} %bitcast.me_ref, bf16[2,128,2048]{2,1,0:T(8,128)(2,1)S(1)} %multiply_convert_fusion.4.refs_0_, bf16[2,128,2048]{2,1,0:T(8,128)(2,1)} %copy-done.84, ...), custom_call_target="tpu_custom_call" | custom-call | flops 2952790016 | bytes 5767168 | tf_op jit(solution)/shard_map/feed/pallas_call | solution.py:436
  171.7 4.5 collective-permute-done.26.refs_0_
  182.5 13.1 %feed.4 = (bf16[704,2048]{1,0:T(8,128)(2,1)}, bf16[704,2048]{1,0:T(8,128)(2,1)}, bf16[704,2048]{1,0:T(8,128)(2,1)}, bf16[8,256,2048]{2,1,0:T(8,128)(2,1)}) custom-call(s32[1]{0:T(128)} %bitcast.me_ref, bf16[2,128,2048]{2,1,0:T(8,128)(2,1)S(1)} %collective-permute-done.26.refs_0_, ...), custom_call_target="tpu_custom_call", output_to_operand_aliasing={{0}: (8, {}), {1}: (9, {}), {2}: (10, {}), {3}: (11, {})} | custom-call | flops 5905580032 | bytes 5767168 | tf_op jit(solution)/shard_map/feed/pallas_call | solution.py:436
  199.1 8.2 %feed.5 = (bf16[704,2048]{1,0:T(8,128)(2,1)}, bf16[704,2048]{1,0:T(8,128)(2,1)}, bf16[704,2048]{1,0:T(8,128)(2,1)}, bf16[8,256,2048]{2,1,0:T(8,128)(2,1)}) custom-call(s32[1]{0:T(128)} %bitcast.me_ref, bf16[1,128,2048]{2,1,0:T(8,128)(2,1)S(1)} %collective-permute-done.31.refs_0_, ...), custom_call_target="tpu_custom_call", output_to_operand_aliasing={{0}: (8, {}), {1}: (9, {}), {2}: (10, {}), {3}: (11, {})} | custom-call | flops 2952790016 | bytes 5767168 | tf_op jit(solution)/shard_map/feed/pallas_call | solution.py:436
  207.3 6.6 weight_gradient.6.left_ref
  213.9 3.6 collective-permute-start.37
  217.4 6.6 weight_gradient.7.left_ref
  224.0 8.0 %weight_gradient.8.left_ref = bf16[352,2048]{1,0:T(8,128)(2,1)} custom-call(bf16[704,2048]{1,0:T(8,128)(2,1)} %get-tuple-element.282.refs_0_.left_ref, bf16[2048,2048]{1,0:T(8,128)(2,1)} %bitcast.167), custom_call_target="tpu_custom_call" | custom-call | flops 2952790016 | bytes 8388608 | tf_op jit(solution)/shard_map/weight_gradient/pallas_call | solution.py:493
  232.0 18.6 %sum_products.4 = bf16[8,256,2048]{2,1,0:T(8,128)(2,1)} custom-call(bf16[704,2048]{1,0:T(8,128)(2,1)} %get-tuple-element.282.refs_0_.left_ref, bf16[704,2048]{1,0:T(8,128)(2,1)} %get-tuple-element.292.refs_1_.left_ref, bf16[704,2048]{1,0:T(8,128)(2,1)} %bitcast.191, bf16[704,2048]{1,0:T(8,128)(2,1)} %bitcast.195), custom_call_target="tpu_custom_call" | custom-call | flops 11811160064 | bytes 8388608 | tf_op jit(solution)/shard_map/sum_products/pallas_call | solution.py:471
  257.0 7.6 %weight_gradient.9.left_ref = bf16[352,2048]{1,0:T(8,128)(2,1)S(1)} custom-call(bf16[704,2048]{1,0:T(8,128)(2,1)} %get-tuple-element.282.refs_0_.left_ref, bf16[2048,2048]{1,0:T(8,128)(2,1)} %bitcast.168), custom_call_target="tpu_custom_call" | custom-call | flops 2952790016 | bytes 8388608 | tf_op jit(solution)/shard_map/weight_gradient/pallas_call | solution.py:493
  265.7 18.8 %collective-permute-done.40.right_ref = bf16[352,2048]{1,0:T(8,128)(2,1)S(1)} collective-permute-done((bf16[352,2048]{1,0:T(8,128)(2,1)S(1)}, bf16[352,2048]{1,0:T(8,128)(2,1)S(1)}, u32[]{:S(2)}, u32[]{:S(2)}) %collective-permute-start.40) | collective-permute-done | bytes 1441824 | tf_op jit(solution)/shard_map/ppermute | solution.py:711
  288.3 7.2 %collective-permute-start.38 = (bf16[352,2048]{1,0:T(8,128)(2,1)}, bf16[352,2048]{1,0:T(8,128)(2,1)S(1)}, u32[]{:S(2)}, u32[]{:S(2)}) collective-permute-start(bf16[352,2048]{1,0:T(8,128)(2,1)} %weight_gradient.8.left_ref), channel_id=1, source_target_pairs={{0,8},{24,16},{1,9},{25,17},{2,10},{26,18},{3,11},{27,19},{4,12},{... | collective-permute-start | bytes 4325384 | tf_op jit(solution)/shard_map/ppermute | solution.py:711
  299.9 6.6 weight_gradient.10.left_ref
  306.5 18.5 %collective-permute-done.38.right_ref = bf16[352,2048]{1,0:T(8,128)(2,1)S(1)} collective-permute-done((bf16[352,2048]{1,0:T(8,128)(2,1)}, bf16[352,2048]{1,0:T(8,128)(2,1)S(1)}, u32[]{:S(2)}, u32[]{:S(2)}) %collective-permute-start.38) | collective-permute-done | bytes 1441824 | tf_op jit(solution)/shard_map/ppermute | solution.py:711
  327.3 4.7 collective-permute-done.45.outward_ref
  333.2 2.6 fusion.7
  336.0 3.7 fusion.31
  347.7 5.7 collective-permute-start.41
  353.4 6.6 weight_gradient.11.left_ref
  360.0 13.5 %collective-permute-done.43.right_ref = bf16[352,2048]{1,0:T(8,128)(2,1)S(1)} collective-permute-done((bf16[352,2048]{1,0:T(8,128)(2,1)}, bf16[352,2048]{1,0:T(8,128)(2,1)S(1)}, u32[]{:S(2)}, u32[]{:S(2)}) %collective-permute-start.43) | collective-permute-done | bytes 1441824 | tf_op jit(solution)/shard_map/ppermute | solution.py:711
  373.5 12.3 %sum_products.5 = bf16[8,256,2048]{2,1,0:T(8,128)(2,1)} custom-call(bf16[704,2048]{1,0:T(8,128)(2,1)} %get-tuple-element.299.left_ref.refs_0_, bf16[704,2048]{1,0:T(8,128)(2,1)} %refs_1_.2), custom_call_target="tpu_custom_call" | custom-call | flops 5905580032 | bytes 8388608 | tf_op jit(solution)/shard_map/sum_products/pallas_call | solution.py:471
  388.1 2.8 add.183.total_ref
  392.2 2.8 add.180.left_ref
  396.9 3.6 collective-permute-done.41.right_ref
  400.5 9.6 %sum_products.6 = f32[8,256,256]{2,1,0:T(8,128)} custom-call(bf16[8,256,2048]{2,1,0:T(8,128)(2,1)} %bitcast.184, bf16[256,2048]{1,0:T(8,128)(2,1)S(1)} %copy-done), custom_call_target="tpu_custom_call" | custom-call | flops 2147483648 | bytes 1048576 | tf_op jit(solution)/shard_map/sum_products/pallas_call | solution.py:471
  410.1 3.3 fusion.left_ref
  413.5 5.9 collective-permute-done.49.outward_ref
  420.7 9.5 %collective-permute-start.51 = (bf16[352,2048]{1,0:T(8,128)(2,1)S(1)}, bf16[352,2048]{1,0:T(8,128)(2,1)S(1)}, u32[]{:S(2)}, u32[]{:S(2)}) collective-permute-start(bf16[352,2048]{1,0:T(8,128)(2,1)S(1)} %copy-done.4), channel_id=1, source_target_pairs={{0,8},{24,16},{1,9},{25,17},{2,10},{26,18},{3,11},{27,19},{4,12},{... | collective-permute-start | bytes 4325384 | tf_op jit(solution)/shard_map/ppermute | solution.py:711
  437.3 16.6 %mixer_backward.2 = (bf16[8,2,128,256]{3,2,1,0:T(8,128)(2,1)S(1)}, bf16[8,2,128,256]{3,2,1,0:T(8,128)(2,1)}, bf16[8,2,128,256]{3,2,1,0:T(8,128)(2,1)}, f32[16,256]{1,0:T(8,128)S(1)}, f32[2048,256]{1,0:T(8,128)}) custom-call(f32[8,2,128,256]{3,2,1,0:T(8,128)} %bitcast.198, f32[8,2,128,768]{3,2,1,0:T(8,128)} %bitcast.161, f32[8,2,128,768]{3,2,1,0:T(8,128)} %bitcast.162, ...), custom_call_target="tpu_custom_call" | custom-call | flops 3221225472 | bytes 20971520 | tf_op jit(solution)/shard_map/mixer_backward/pallas_call | solution.py:331
  467.5 5.0 collective-permute-start.54
  472.5 16.1 %mixer_backward.3 = (bf16[8,2,128,256]{3,2,1,0:T(8,128)(2,1)S(1)}, bf16[8,2,128,256]{3,2,1,0:T(8,128)(2,1)}, bf16[8,2,128,256]{3,2,1,0:T(8,128)(2,1)}, f32[16,256]{1,0:T(8,128)S(1)}, f32[1024,256]{1,0:T(8,128)}) custom-call(f32[8,2,128,256]{3,2,1,0:T(8,128)} %bitcast.199, ...), custom_call_target="tpu_custom_call", output_to_operand_aliasing={{0}: (11, {}), {1}: (12, {}), {2}: (13, {})} | custom-call | flops 3221225472 | bytes 20971520 | tf_op jit(solution)/shard_map/mixer_backward/pallas_call | solution.py:331
  488.6 6.1 convolution_convert_fusion.3.left_ref
  496.3 6.9 %fusion.1.left_ref = bf16[2048,256]{1,0:T(8,128)(2,1)S(1)} fusion(bf16[8,256,2048]{2,1,0:T(8,128)(2,1)} %get-tuple-element.326, bf16[8,256,256]{2,1,0:T(8,128)(2,1)S(1)} %bitcast.209), kind=kOutput, calls=%fused_computation.14 | convolution fusion | flops 2148007936 | bytes 10485760 | tf_op jit(solution)/shard_map/dot_general | solution.py:31
  504.6 3.6 fusion.2.left_ref
  508.3 11.3 %collective-permute-done.56.right_ref = bf16[2048,256]{1,0:T(8,128)(2,1)S(1)} collective-permute-done((bf16[2048,256]{1,0:T(8,128)(2,1)S(1)}, bf16[2048,256]{1,0:T(8,128)(2,1)S(1)}, u32[]{:S(2)}, u32[]{:S(2)}) %collective-permute-start.56) | collective-permute-done | bytes 1048608 | tf_op jit(solution)/shard_map/ppermute | solution.py:711
  520.5 12.1 %sum_products.7 = bf16[8,256,2048]{2,1,0:T(8,128)(2,1)} custom-call(bf16[8,256,256]{2,1,0:T(8,128)(2,1)S(1)} %bitcast.153, bf16[8,256,256]{2,1,0:T(8,128)(2,1)} %bitcast.208, bf16[8,256,256]{2,1,0:T(8,128)(2,1)} %bitcast.210, bf16[2048,256]{1,0:T(8,128)(2,1)} %get-tuple-element.440.refs_3_, bf16[2048,256]{1,0:T(8,128)(2,1)} %get-tuple-element.439.refs_4_, ...), custom_call_target="tpu_custom_call" | custom-call | flops 6442450944 | bytes 8388608 | tf_op jit(solution)/shard_map/sum_products/pallas_call | solution.py:471
  541.8 6.9 %collective-permute-start.62 = (bf16[2048,256]{1,0:T(8,128)(2,1)S(1)}, bf16[2048,256]{1,0:T(8,128)(2,1)}, u32[]{:S(2)}, u32[]{:S(2)}) collective-permute-start(bf16[2048,256]{1,0:T(8,128)(2,1)S(1)} %copy-done.57), channel_id=1, source_target_pairs={{0,8},{24,16},{1,9},{25,17},{2,10},{26,18},{3,11},{27,19},{4,12},{... | collective-permute-start | bytes 3145736 | tf_op jit(solution)/shard_map/ppermute | solution.py:711
  555.8 10.9 %collective-permute-done.59.outward_ref = bf16[352,2048]{1,0:T(8,128)(2,1)S(1)} collective-permute-done((bf16[352,2048]{1,0:T(8,128)(2,1)S(1)}, bf16[352,2048]{1,0:T(8,128)(2,1)S(1)}, u32[]{:S(2)}, u32[]{:S(2)}) %collective-permute-start.59) | collective-permute-done | bytes 1441824 | tf_op jit(solution)/shard_map/ppermute | solution.py:727
  583.4 6.4 pole_gradients.1
  594.3 25.7 %collective-permute-start.66 = (bf16[80,256]{1,0:T(8,128)(2,1)S(1)}, bf16[80,256]{1,0:T(8,128)(2,1)S(1)}, u32[]{:S(2)}, u32[]{:S(2)}) collective-permute-start(bf16[80,256]{1,0:T(8,128)(2,1)S(1)} %constant_dynamic-update-slice_fusion.left_ref), channel_id=1, source_target_pairs={{0,8},{24,16},{1,9},{25,17},{2,10},{26,18},{3,11},{27,19},{4,12},{... | collective-permute-start | bytes 122888 | tf_op jit(solution)/shard_map/ppermute | solution.py:711
  621.4 2.9 finish.12.refs_0_
  624.3 2.8 finish.13
  627.2 3.2 finish.10.refs_0_
  630.3 2.9 finish.11
  633.3 2.9 finish.14.refs_0_
  636.2 2.8 finish.15
  642.2 2.8 finish.16
  644.9 3.1 finish.17.refs_0_
  650.2 3.2 finish.18.refs_0_
  659.9 9.0 %collective-permute-done.72.outward_ref = bf16[2048,256]{1,0:T(8,128)(2,1)S(1)} collective-permute-done((bf16[2048,256]{1,0:T(8,128)(2,1)S(1)}, bf16[2048,256]{1,0:T(8,128)(2,1)S(1)}, u32[]{:S(2)}, u32[]{:S(2)}) %collective-permute-start.72) | collective-permute-done | bytes 1048608 | tf_op jit(solution)/shard_map/ppermute | solution.py:727
  668.9 2.8 finish.19
  671.6 3.5 copy.68
  (426 shorter events, 186.3 us)
Async XLA Ops:
  7.2 326.0 %reduce-scatter.4.cloned.1.call-start = ((), (), s32[]{:S(2)}) async-start(), calls=%async_computation.3 | async-start | bytes 9437184 | tf_op jit(solution)/shard_map/reduce_scatter | solution.py:513
  11.9 20.0 %collective-permute-start.2 = (bf16[2,128,2048]{2,1,0:T(8,128)(2,1)}, bf16[2,128,2048]{2,1,0:T(8,128)(2,1)}, u32[]{:S(2)}, u32[]{:S(2)}) collective-permute-start(bf16[2,128,2048]{2,1,0:T(8,128)(2,1)} %fusion.12.refs_0_), channel_id=1, source_target_pairs={{0,1},{1,0},{2,3},{3,2},{4,5},{5,4},{6,7},{7,6},{8,9},{9,8},{10,11... | collective-permute-start | bytes 3145736 | tf_op jit(solution)/shard_map/ppermute | solution.py:636
  12.3 26.5 %collective-permute-start = (bf16[2,128,2048]{2,1,0:T(8,128)(2,1)}, bf16[2,128,2048]{2,1,0:T(8,128)(2,1)S(1)}, u32[]{:S(2)}, u32[]{:S(2)}) collective-permute-start(bf16[2,128,2048]{2,1,0:T(8,128)(2,1)} %fusion.12.refs_0_), channel_id=1, source_target_pairs={{0,2},{1,3},{2,0},{3,1},{4,6},{5,7},{6,4},{7,5},{8,10},{9,11},{10,... | collective-permute-start | bytes 3145736 | tf_op jit(solution)/shard_map/ppermute | solution.py:636
  14.8 25.6 %collective-permute-start.1 = (bf16[2,128,2048]{2,1,0:T(8,128)(2,1)}, bf16[2,128,2048]{2,1,0:T(8,128)(2,1)}, u32[]{:S(2)}, u32[]{:S(2)}) collective-permute-start(bf16[2,128,2048]{2,1,0:T(8,128)(2,1)} %fusion.12.refs_0_), channel_id=1, source_target_pairs={{0,4},{1,5},{2,6},{3,7},{4,0},{5,1},{6,2},{7,3},{8,12},{9,13},{10,... | collective-permute-start | bytes 3145736 | tf_op jit(solution)/shard_map/ppermute | solution.py:636
  42.1 13.9 %collective-permute-start.3 = (bf16[1,128,2048]{2,1,0:T(8,128)(2,1)S(1)}, bf16[1,128,2048]{2,1,0:T(8,128)(2,1)S(1)}, u32[]{:S(2)}, u32[]{:S(2)}) collective-permute-start(bf16[1,128,2048]{2,1,0:T(8,128)(2,1)S(1)} %slice.117), channel_id=1, source_target_pairs={{0,4},{1,5},{2,6},{3,7},{4,0},{5,1},{6,2},{7,3},{8,12},{9,13},{10,... | collective-permute-start | bytes 1572872 | tf_op jit(solution)/shard_map/ppermute | solution.py:636
  43.6 13.6 %collective-permute-start.4 = (bf16[1,128,2048]{2,1,0:T(8,128)(2,1)S(1)}, bf16[1,128,2048]{2,1,0:T(8,128)(2,1)S(1)}, u32[]{:S(2)}, u32[]{:S(2)}) collective-permute-start(bf16[1,128,2048]{2,1,0:T(8,128)(2,1)S(1)} %slice.118), channel_id=1, source_target_pairs={{0,2},{1,3},{2,0},{3,1},{4,6},{5,7},{6,4},{7,5},{8,10},{9,11},{10,... | collective-permute-start | bytes 1572872 | tf_op jit(solution)/shard_map/ppermute | solution.py:636
  57.7 25.3 %collective-permute-start.8 = (bf16[2,128,2048]{2,1,0:T(8,128)(2,1)}, bf16[2,128,2048]{2,1,0:T(8,128)(2,1)S(1)}, u32[]{:S(2)}, u32[]{:S(2)}) collective-permute-start(bf16[2,128,2048]{2,1,0:T(8,128)(2,1)} %fusion.19.refs_0_), channel_id=1, source_target_pairs={{0,2},{1,3},{2,0},{3,1},{4,6},{5,7},{6,4},{7,5},{8,10},{9,11},{10,... | collective-permute-start | bytes 3145736 | tf_op jit(solution)/shard_map/ppermute | solution.py:636
  58.2 25.1 %collective-permute-start.9 = (bf16[2,128,2048]{2,1,0:T(8,128)(2,1)}, bf16[2,128,2048]{2,1,0:T(8,128)(2,1)}, u32[]{:S(2)}, u32[]{:S(2)}) collective-permute-start(bf16[2,128,2048]{2,1,0:T(8,128)(2,1)} %fusion.19.refs_0_), channel_id=1, source_target_pairs={{0,4},{1,5},{2,6},{3,7},{4,0},{5,1},{6,2},{7,3},{8,12},{9,13},{10,... | collective-permute-start | bytes 3145736 | tf_op jit(solution)/shard_map/ppermute | solution.py:636
  87.7 5.5 collective-permute-start.17
  88.2 6.5 collective-permute-start.15
  88.4 6.7 collective-permute-start.7
  88.8 14.0 %collective-permute-start.12 = (bf16[1,128,2048]{2,1,0:T(8,128)(2,1)S(1)}, bf16[1,128,2048]{2,1,0:T(8,128)(2,1)S(1)}, u32[]{:S(2)}, u32[]{:S(2)}) collective-permute-start(bf16[1,128,2048]{2,1,0:T(8,128)(2,1)S(1)} %slice.119), channel_id=1, source_target_pairs={{0,4},{1,5},{2,6},{3,7},{4,0},{5,1},{6,2},{7,3},{8,12},{9,13},{10,... | collective-permute-start | bytes 1572872 | tf_op jit(solution)/shard_map/ppermute | solution.py:636
  90.3 13.9 %collective-permute-start.13 = (bf16[1,128,2048]{2,1,0:T(8,128)(2,1)S(1)}, bf16[1,128,2048]{2,1,0:T(8,128)(2,1)S(1)}, u32[]{:S(2)}, u32[]{:S(2)}) collective-permute-start(bf16[1,128,2048]{2,1,0:T(8,128)(2,1)S(1)} %slice.120), channel_id=1, source_target_pairs={{0,2},{1,3},{2,0},{3,1},{4,6},{5,7},{6,4},{7,5},{8,10},{9,11},{10,... | collective-permute-start | bytes 1572872 | tf_op jit(solution)/shard_map/ppermute | solution.py:636
  104.2 6.9 %collective-permute-start.22 = (bf16[2,128,2048]{2,1,0:T(8,128)(2,1)S(1)}, bf16[2,128,2048]{2,1,0:T(8,128)(2,1)S(1)}, u32[]{:S(2)}, u32[]{:S(2)}) collective-permute-start(bf16[2,128,2048]{2,1,0:T(8,128)(2,1)S(1)} %collective-permute-done.8.refs_0_), channel_id=1, source_target_pairs={{0,1},{1,0},{2,3},{3,2},{4,5},{5,4},{6,7},{7,6},{8,9},{9,8},{10,11... | collective-permute-start | bytes 3145736 | tf_op jit(solution)/shard_map/ppermute | solution.py:636
  104.2 13.1 %collective-permute-start.23 = (bf16[2,128,2048]{2,1,0:T(8,128)(2,1)}, bf16[2,128,2048]{2,1,0:T(8,128)(2,1)}, u32[]{:S(2)}, u32[]{:S(2)}) collective-permute-start(bf16[2,128,2048]{2,1,0:T(8,128)(2,1)} %collective-permute-done.9.refs_2_), channel_id=1, source_target_pairs={{0,1},{1,0},{2,3},{3,2},{4,5},{5,4},{6,7},{7,6},{8,9},{9,8},{10,11... | collective-permute-start | bytes 3145736 | tf_op jit(solution)/shard_map/ppermute | solution.py:636
  105.9 20.3 %collective-permute-start.18 = (bf16[1,128,2048]{2,1,0:T(8,128)(2,1)}, bf16[1,128,2048]{2,1,0:T(8,128)(2,1)}, u32[]{:S(2)}, u32[]{:S(2)}) collective-permute-start(bf16[1,128,2048]{2,1,0:T(8,128)(2,1)} %get-tuple-element.444), channel_id=1, source_target_pairs={{0,2},{1,3},{2,0},{3,1},{4,6},{5,7},{6,4},{7,5},{8,10},{9,11},{10,... | collective-permute-start | bytes 1572872 | tf_op jit(solution)/shard_map/ppermute | solution.py:636
  107.4 18.7 %collective-permute-start.19 = (bf16[1,128,2048]{2,1,0:T(8,128)(2,1)}, bf16[1,128,2048]{2,1,0:T(8,128)(2,1)}, u32[]{:S(2)}, u32[]{:S(2)}) collective-permute-start(bf16[1,128,2048]{2,1,0:T(8,128)(2,1)} %get-tuple-element.443), channel_id=1, source_target_pairs={{0,4},{1,5},{2,6},{3,7},{4,0},{5,1},{6,2},{7,3},{8,12},{9,13},{10,... | collective-permute-start | bytes 1572872 | tf_op jit(solution)/shard_map/ppermute | solution.py:636
  110.6 20.5 %collective-permute-start.20 = (bf16[1,128,2048]{2,1,0:T(8,128)(2,1)}, bf16[1,128,2048]{2,1,0:T(8,128)(2,1)S(1)}, u32[]{:S(2)}, u32[]{:S(2)}) collective-permute-start(bf16[1,128,2048]{2,1,0:T(8,128)(2,1)} %slice.189), channel_id=1, source_target_pairs={{0,2},{1,3},{2,0},{3,1},{4,6},{5,7},{6,4},{7,5},{8,10},{9,11},{10,... | collective-permute-start | bytes 1572872 | tf_op jit(solution)/shard_map/ppermute | solution.py:636
  111.2 21.2 %collective-permute-start.21 = (bf16[1,128,2048]{2,1,0:T(8,128)(2,1)}, bf16[1,128,2048]{2,1,0:T(8,128)(2,1)S(1)}, u32[]{:S(2)}, u32[]{:S(2)}) collective-permute-start(bf16[1,128,2048]{2,1,0:T(8,128)(2,1)} %slice.188), channel_id=1, source_target_pairs={{0,4},{1,5},{2,6},{3,7},{4,0},{5,1},{6,2},{7,3},{8,12},{9,13},{10,... | collective-permute-start | bytes 1572872 | tf_op jit(solution)/shard_map/ppermute | solution.py:636
  133.7 12.7 %collective-permute-start.25 = (bf16[1,128,2048]{2,1,0:T(8,128)(2,1)S(1)}, bf16[1,128,2048]{2,1,0:T(8,128)(2,1)S(1)}, u32[]{:S(2)}, u32[]{:S(2)}) collective-permute-start(bf16[1,128,2048]{2,1,0:T(8,128)(2,1)S(1)} %add_convert_fusion), channel_id=1, source_target_pairs={{0,2},{1,3},{2,0},{3,1},{4,6},{5,7},{6,4},{7,5},{8,10},{9,11},{10,... | collective-permute-start | bytes 1572872 | tf_op jit(solution)/shard_map/ppermute | solution.py:636
  135.5 12.5 %collective-permute-start.24 = (bf16[1,128,2048]{2,1,0:T(8,128)(2,1)S(1)}, bf16[1,128,2048]{2,1,0:T(8,128)(2,1)S(1)}, u32[]{:S(2)}, u32[]{:S(2)}) collective-permute-start(bf16[1,128,2048]{2,1,0:T(8,128)(2,1)S(1)} %add_convert_fusion.1), channel_id=1, source_target_pairs={{0,4},{1,5},{2,6},{3,7},{4,0},{5,1},{6,2},{7,3},{8,12},{9,13},{10,... | collective-permute-start | bytes 1572872 | tf_op jit(solution)/shard_map/ppermute | solution.py:636
  150.5 11.7 %collective-permute-start.28 = (bf16[2,128,2048]{2,1,0:T(8,128)(2,1)S(1)}, bf16[2,128,2048]{2,1,0:T(8,128)(2,1)S(1)}, u32[]{:S(2)}, u32[]{:S(2)}) collective-permute-start(bf16[2,128,2048]{2,1,0:T(8,128)(2,1)S(1)} %multiply_convert_fusion.4.refs_0_), channel_id=1, source_target_pairs={{0,1},{1,0},{2,3},{3,2},{4,5},{5,4},{6,7},{7,6},{8,9},{9,8},{10,11... | collective-permute-start | bytes 3145736 | tf_op jit(solution)/shard_map/ppermute | solution.py:636
  150.6 25.6 %collective-permute-start.26 = (bf16[2,128,2048]{2,1,0:T(8,128)(2,1)S(1)}, bf16[2,128,2048]{2,1,0:T(8,128)(2,1)S(1)}, u32[]{:S(2)}, u32[]{:S(2)}) collective-permute-start(bf16[2,128,2048]{2,1,0:T(8,128)(2,1)S(1)} %multiply_convert_fusion.4.refs_0_), channel_id=1, source_target_pairs={{0,2},{1,3},{2,0},{3,1},{4,6},{5,7},{6,4},{7,5},{8,10},{9,11},{10,... | collective-permute-start | bytes 3145736 | tf_op jit(solution)/shard_map/ppermute | solution.py:636
  152.1 25.2 %collective-permute-start.27 = (bf16[2,128,2048]{2,1,0:T(8,128)(2,1)S(1)}, bf16[2,128,2048]{2,1,0:T(8,128)(2,1)S(1)}, u32[]{:S(2)}, u32[]{:S(2)}) collective-permute-start(bf16[2,128,2048]{2,1,0:T(8,128)(2,1)S(1)} %multiply_convert_fusion.4.refs_0_), channel_id=1, source_target_pairs={{0,4},{1,5},{2,6},{3,7},{4,0},{5,1},{6,2},{7,3},{8,12},{9,13},{10,... | collective-permute-start | bytes 3145736 | tf_op jit(solution)/shard_map/ppermute | solution.py:636
  177.9 17.6 %collective-permute-start.31 = (bf16[1,128,2048]{2,1,0:T(8,128)(2,1)S(1)}, bf16[1,128,2048]{2,1,0:T(8,128)(2,1)S(1)}, u32[]{:S(2)}, u32[]{:S(2)}) collective-permute-start(bf16[1,128,2048]{2,1,0:T(8,128)(2,1)S(1)} %slice.140), channel_id=1, source_target_pairs={{0,4},{1,5},{2,6},{3,7},{4,0},{5,1},{6,2},{7,3},{8,12},{9,13},{10,... | collective-permute-start | bytes 1572872 | tf_op jit(solution)/shard_map/ppermute | solution.py:636
  179.5 16.0 %collective-permute-start.32 = (bf16[1,128,2048]{2,1,0:T(8,128)(2,1)S(1)}, bf16[1,128,2048]{2,1,0:T(8,128)(2,1)S(1)}, u32[]{:S(2)}, u32[]{:S(2)}) collective-permute-start(bf16[1,128,2048]{2,1,0:T(8,128)(2,1)S(1)} %slice.141), channel_id=1, source_target_pairs={{0,2},{1,3},{2,0},{3,1},{4,6},{5,7},{6,4},{7,5},{8,10},{9,11},{10,... | collective-permute-start | bytes 1572872 | tf_op jit(solution)/shard_map/ppermute | solution.py:636
  213.9 36.7 %collective-permute-start.37 = (bf16[352,2048]{1,0:T(8,128)(2,1)S(1)}, bf16[352,2048]{1,0:T(8,128)(2,1)S(1)}, u32[]{:S(2)}, u32[]{:S(2)}) collective-permute-start(bf16[352,2048]{1,0:T(8,128)(2,1)S(1)} %weight_gradient.6.left_ref), channel_id=1, source_target_pairs={{0,8},{24,16},{1,9},{25,17},{2,10},{26,18},{3,11},{27,19},{4,12},{... | collective-permute-start | bytes 4325384 | tf_op jit(solution)/shard_map/ppermute | solution.py:711
  251.7 148.7 %all-gather.3.cloned.1.call-start = ((), (), s32[]{:S(2)}) async-start(), calls=%async_computation.6 | async-start | bytes 9437184 | tf_op jit(solution)/shard_map/all_gather | solution.py:509
  251.8 32.7 %collective-permute-start.40 = (bf16[352,2048]{1,0:T(8,128)(2,1)S(1)}, bf16[352,2048]{1,0:T(8,128)(2,1)S(1)}, u32[]{:S(2)}, u32[]{:S(2)}) collective-permute-start(bf16[352,2048]{1,0:T(8,128)(2,1)S(1)} %weight_gradient.7.left_ref), channel_id=1, source_target_pairs={{0,8},{24,16},{1,9},{25,17},{2,10},{26,18},{3,11},{27,19},{4,12},{... | collective-permute-start | bytes 4325384 | tf_op jit(solution)/shard_map/ppermute | solution.py:711
  256.2 39.4 %collective-permute-start.39 = (bf16[352,2048]{1,0:T(8,128)(2,1)S(1)}, bf16[352,2048]{1,0:T(8,128)(2,1)S(1)}, u32[]{:S(2)}, u32[]{:S(2)}) collective-permute-start(bf16[352,2048]{1,0:T(8,128)(2,1)S(1)} %add.176.left_ref), channel_id=1, source_target_pairs={{8,16},{16,8},{9,17},{17,9},{10,18},{18,10},{11,19},{19,11},{12,20... | collective-permute-start | bytes 4325384 | tf_op jit(solution)/shard_map/ppermute | solution.py:717
  287.6 37.5 %collective-permute-start.44 = (bf16[352,2048]{1,0:T(8,128)(2,1)S(1)}, bf16[352,2048]{1,0:T(8,128)(2,1)S(1)}, u32[]{:S(2)}, u32[]{:S(2)}) collective-permute-start(bf16[352,2048]{1,0:T(8,128)(2,1)S(1)} %add.178.left_ref), channel_id=1, source_target_pairs={{8,16},{16,8},{9,17},{17,9},{10,18},{18,10},{11,19},{19,11},{12,20... | collective-permute-start | bytes 4325384 | tf_op jit(solution)/shard_map/ppermute | solution.py:717
  288.3 36.7 %collective-permute-start.38 = (bf16[352,2048]{1,0:T(8,128)(2,1)}, bf16[352,2048]{1,0:T(8,128)(2,1)S(1)}, u32[]{:S(2)}, u32[]{:S(2)}) collective-permute-start(bf16[352,2048]{1,0:T(8,128)(2,1)} %weight_gradient.8.left_ref), channel_id=1, source_target_pairs={{0,8},{24,16},{1,9},{25,17},{2,10},{26,18},{3,11},{27,19},{4,12},{... | collective-permute-start | bytes 4325384 | tf_op jit(solution)/shard_map/ppermute | solution.py:711
  298.6 33.4 %collective-permute-start.45 = (bf16[352,2048]{1,0:T(8,128)(2,1)S(1)}, bf16[352,2048]{1,0:T(8,128)(2,1)S(1)}, u32[]{:S(2)}, u32[]{:S(2)}) collective-permute-start(bf16[352,2048]{1,0:T(8,128)(2,1)S(1)} %add.179.total_ref), channel_id=1, source_target_pairs={{8,0},{16,24},{9,1},{17,25},{10,2},{18,26},{11,3},{19,27},{12,4},{... | collective-permute-start | bytes 4325384 | tf_op jit(solution)/shard_map/ppermute | solution.py:727
  339.7 309.0 %reduce-scatter.6.cloned.1.call-start = ((), (), s32[]{:S(2)}) async-start(), calls=%async_computation.4 | async-start | bytes 9437184 | tf_op jit(solution)/shard_map/reduce_scatter | solution.py:513
  339.7 33.8 %collective-permute-start.43 = (bf16[352,2048]{1,0:T(8,128)(2,1)}, bf16[352,2048]{1,0:T(8,128)(2,1)S(1)}, u32[]{:S(2)}, u32[]{:S(2)}) collective-permute-start(bf16[352,2048]{1,0:T(8,128)(2,1)} %copy-done.2), channel_id=1, source_target_pairs={{0,8},{24,16},{1,9},{25,17},{2,10},{26,18},{3,11},{27,19},{4,12},{... | collective-permute-start | bytes 4325384 | tf_op jit(solution)/shard_map/ppermute | solution.py:711
  343.2 42.6 %collective-permute-start.47 = (bf16[352,2048]{1,0:T(8,128)(2,1)S(1)}, bf16[352,2048]{1,0:T(8,128)(2,1)S(1)}, u32[]{:S(2)}, u32[]{:S(2)}) collective-permute-start(bf16[352,2048]{1,0:T(8,128)(2,1)S(1)} %add.181.left_ref), channel_id=1, source_target_pairs={{8,16},{16,8},{9,17},{17,9},{10,18},{18,10},{11,19},{19,11},{12,20... | collective-permute-start | bytes 4325384 | tf_op jit(solution)/shard_map/ppermute | solution.py:717
  346.4 39.5 %collective-permute-start.48 = (bf16[352,2048]{1,0:T(8,128)(2,1)S(1)}, bf16[352,2048]{1,0:T(8,128)(2,1)S(1)}, u32[]{:S(2)}, u32[]{:S(2)}) collective-permute-start(bf16[352,2048]{1,0:T(8,128)(2,1)S(1)} %add.182.total_ref), channel_id=1, source_target_pairs={{8,0},{16,24},{9,1},{17,25},{10,2},{18,26},{11,3},{19,27},{12,4},{... | collective-permute-start | bytes 4325384 | tf_op jit(solution)/shard_map/ppermute | solution.py:727
  347.7 52.8 %collective-permute-start.41 = (bf16[352,2048]{1,0:T(8,128)(2,1)S(1)}, bf16[352,2048]{1,0:T(8,128)(2,1)}, u32[]{:S(2)}, u32[]{:S(2)}) collective-permute-start(bf16[352,2048]{1,0:T(8,128)(2,1)S(1)} %weight_gradient.10.left_ref), channel_id=1, source_target_pairs={{0,8},{24,16},{1,9},{25,17},{2,10},{26,18},{3,11},{27,19},{4,12},{... | collective-permute-start | bytes 4325384 | tf_op jit(solution)/shard_map/ppermute | solution.py:711
  391.0 28.4 %collective-permute-start.49 = (bf16[352,2048]{1,0:T(8,128)(2,1)}, bf16[352,2048]{1,0:T(8,128)(2,1)}, u32[]{:S(2)}, u32[]{:S(2)}) collective-permute-start(bf16[352,2048]{1,0:T(8,128)(2,1)} %add.183.total_ref), channel_id=1, source_target_pairs={{8,0},{16,24},{9,1},{17,25},{10,2},{18,26},{11,3},{19,27},{12,4},{... | collective-permute-start | bytes 4325384 | tf_op jit(solution)/shard_map/ppermute | solution.py:727
  395.0 24.3 %collective-permute-start.46 = (bf16[352,2048]{1,0:T(8,128)(2,1)}, bf16[352,2048]{1,0:T(8,128)(2,1)}, u32[]{:S(2)}, u32[]{:S(2)}) collective-permute-start(bf16[352,2048]{1,0:T(8,128)(2,1)} %add.180.left_ref), channel_id=1, source_target_pairs={{8,16},{16,8},{9,17},{17,9},{10,18},{18,10},{11,19},{19,11},{12,20... | collective-permute-start | bytes 4325384 | tf_op jit(solution)/shard_map/ppermute | solution.py:717
  419.4 235.2 %reduce-scatter.8.cloned.1.call-start = ((), (), s32[]{:S(2)}) async-start(), calls=%async_computation.5 | async-start | bytes 9437184 | tf_op jit(solution)/shard_map/reduce_scatter | solution.py:513
  420.7 33.2 %collective-permute-start.51 = (bf16[352,2048]{1,0:T(8,128)(2,1)S(1)}, bf16[352,2048]{1,0:T(8,128)(2,1)S(1)}, u32[]{:S(2)}, u32[]{:S(2)}) collective-permute-start(bf16[352,2048]{1,0:T(8,128)(2,1)S(1)} %copy-done.4), channel_id=1, source_target_pairs={{0,8},{24,16},{1,9},{25,17},{2,10},{26,18},{3,11},{27,19},{4,12},{... | collective-permute-start | bytes 4325384 | tf_op jit(solution)/shard_map/ppermute | solution.py:711
  432.3 26.8 %collective-permute-start.42 = (bf16[352,2048]{1,0:T(8,128)(2,1)S(1)}, bf16[352,2048]{1,0:T(8,128)(2,1)S(1)}, u32[]{:S(2)}, u32[]{:S(2)}) collective-permute-start(bf16[352,2048]{1,0:T(8,128)(2,1)S(1)} %add.177.left_ref), channel_id=1, source_target_pairs={{8,16},{16,8},{9,17},{17,9},{10,18},{18,10},{11,19},{19,11},{12,20... | collective-permute-start | bytes 4325384 | tf_op jit(solution)/shard_map/ppermute | solution.py:717
  435.6 26.0 %collective-permute-start.50 = (bf16[352,2048]{1,0:T(8,128)(2,1)S(1)}, bf16[352,2048]{1,0:T(8,128)(2,1)S(1)}, u32[]{:S(2)}, u32[]{:S(2)}) collective-permute-start(bf16[352,2048]{1,0:T(8,128)(2,1)S(1)} %add.184.total_ref), channel_id=1, source_target_pairs={{8,0},{16,24},{9,1},{17,25},{10,2},{18,26},{11,3},{19,27},{12,4},{... | collective-permute-start | bytes 4325384 | tf_op jit(solution)/shard_map/ppermute | solution.py:727
  457.3 39.0 %collective-permute-start.52 = (bf16[352,2048]{1,0:T(8,128)(2,1)S(1)}, bf16[352,2048]{1,0:T(8,128)(2,1)}, u32[]{:S(2)}, u32[]{:S(2)}) collective-permute-start(bf16[352,2048]{1,0:T(8,128)(2,1)S(1)} %add.185.left_ref), channel_id=1, source_target_pairs={{8,16},{16,8},{9,17},{17,9},{10,18},{18,10},{11,19},{19,11},{12,20... | collective-permute-start | bytes 4325384 | tf_op jit(solution)/shard_map/ppermute | solution.py:717
  464.1 32.2 %collective-permute-start.53 = (bf16[352,2048]{1,0:T(8,128)(2,1)S(1)}, bf16[352,2048]{1,0:T(8,128)(2,1)S(1)}, u32[]{:S(2)}, u32[]{:S(2)}) collective-permute-start(bf16[352,2048]{1,0:T(8,128)(2,1)S(1)} %add.186.total_ref), channel_id=1, source_target_pairs={{8,0},{16,24},{9,1},{17,25},{10,2},{18,26},{11,3},{19,27},{12,4},{... | collective-permute-start | bytes 4325384 | tf_op jit(solution)/shard_map/ppermute | solution.py:727
  467.5 28.8 %collective-permute-start.54 = (bf16[256,2048]{1,0:T(8,128)(2,1)S(1)}, bf16[256,2048]{1,0:T(8,128)(2,1)S(1)}, u32[]{:S(2)}, u32[]{:S(2)}) collective-permute-start(bf16[256,2048]{1,0:T(8,128)(2,1)S(1)} %copy-done.56), channel_id=1, source_target_pairs={{0,8},{24,16},{1,9},{25,17},{2,10},{26,18},{3,11},{27,19},{4,12},{... | collective-permute-start | bytes 3145736 | tf_op jit(solution)/shard_map/ppermute | solution.py:711
  494.7 24.9 %collective-permute-start.56 = (bf16[2048,256]{1,0:T(8,128)(2,1)S(1)}, bf16[2048,256]{1,0:T(8,128)(2,1)S(1)}, u32[]{:S(2)}, u32[]{:S(2)}) collective-permute-start(bf16[2048,256]{1,0:T(8,128)(2,1)S(1)} %convolution_convert_fusion.3.left_ref), channel_id=1, source_target_pairs={{0,8},{24,16},{1,9},{25,17},{2,10},{26,18},{3,11},{27,19},{4,12},{... | collective-permute-start | bytes 3145736 | tf_op jit(solution)/shard_map/ppermute | solution.py:711
  503.2 30.7 %collective-permute-start.55 = (bf16[2048,256]{1,0:T(8,128)(2,1)S(1)}, bf16[2048,256]{1,0:T(8,128)(2,1)S(1)}, u32[]{:S(2)}, u32[]{:S(2)}) collective-permute-start(bf16[2048,256]{1,0:T(8,128)(2,1)S(1)} %fusion.1.left_ref), channel_id=1, source_target_pairs={{0,8},{24,16},{1,9},{25,17},{2,10},{26,18},{3,11},{27,19},{4,12},{... | collective-permute-start | bytes 3145736 | tf_op jit(solution)/shard_map/ppermute | solution.py:711
  536.9 29.8 %collective-permute-start.59 = (bf16[352,2048]{1,0:T(8,128)(2,1)S(1)}, bf16[352,2048]{1,0:T(8,128)(2,1)S(1)}, u32[]{:S(2)}, u32[]{:S(2)}) collective-permute-start(bf16[352,2048]{1,0:T(8,128)(2,1)S(1)} %add.189.total_ref), channel_id=1, source_target_pairs={{8,0},{16,24},{9,1},{17,25},{10,2},{18,26},{11,3},{19,27},{12,4},{... | collective-permute-start | bytes 4325384 | tf_op jit(solution)/shard_map/ppermute | solution.py:727
  540.2 15.7 %collective-permute-start.58 = (bf16[256,2048]{1,0:T(8,128)(2,1)S(1)}, bf16[256,2048]{1,0:T(8,128)(2,1)}, u32[]{:S(2)}, u32[]{:S(2)}) collective-permute-start(bf16[256,2048]{1,0:T(8,128)(2,1)S(1)} %add.188.left_ref), channel_id=1, source_target_pairs={{8,16},{16,8},{9,17},{17,9},{10,18},{18,10},{11,19},{19,11},{12,20... | collective-permute-start | bytes 3145736 | tf_op jit(solution)/shard_map/ppermute | solution.py:717
  541.8 31.0 %collective-permute-start.62 = (bf16[2048,256]{1,0:T(8,128)(2,1)S(1)}, bf16[2048,256]{1,0:T(8,128)(2,1)}, u32[]{:S(2)}, u32[]{:S(2)}) collective-permute-start(bf16[2048,256]{1,0:T(8,128)(2,1)S(1)} %copy-done.57), channel_id=1, source_target_pairs={{0,8},{24,16},{1,9},{25,17},{2,10},{26,18},{3,11},{27,19},{4,12},{... | collective-permute-start | bytes 3145736 | tf_op jit(solution)/shard_map/ppermute | solution.py:711
  550.7 22.1 %collective-permute-start.61 = (bf16[2048,256]{1,0:T(8,128)(2,1)S(1)}, bf16[2048,256]{1,0:T(8,128)(2,1)}, u32[]{:S(2)}, u32[]{:S(2)}) collective-permute-start(bf16[2048,256]{1,0:T(8,128)(2,1)S(1)} %add.191.left_ref), channel_id=1, source_target_pairs={{8,16},{16,8},{9,17},{17,9},{10,18},{18,10},{11,19},{19,11},{12,20... | collective-permute-start | bytes 3145736 | tf_op jit(solution)/shard_map/ppermute | solution.py:717
  554.1 35.8 %collective-permute-start.57 = (bf16[2048,256]{1,0:T(8,128)(2,1)S(1)}, bf16[2048,256]{1,0:T(8,128)(2,1)}, u32[]{:S(2)}, u32[]{:S(2)}) collective-permute-start(bf16[2048,256]{1,0:T(8,128)(2,1)S(1)} %add.187.left_ref), channel_id=1, source_target_pairs={{8,16},{16,8},{9,17},{17,9},{10,18},{18,10},{11,19},{19,11},{12,20... | collective-permute-start | bytes 3145736 | tf_op jit(solution)/shard_map/ppermute | solution.py:717
  569.0 20.9 %collective-permute-start.60 = (bf16[256,2048]{1,0:T(8,128)(2,1)S(1)}, bf16[256,2048]{1,0:T(8,128)(2,1)S(1)}, u32[]{:S(2)}, u32[]{:S(2)}) collective-permute-start(bf16[256,2048]{1,0:T(8,128)(2,1)S(1)} %add.190.total_ref), channel_id=1, source_target_pairs={{8,0},{16,24},{9,1},{17,25},{10,2},{18,26},{11,3},{19,27},{12,4},{... | collective-permute-start | bytes 3145736 | tf_op jit(solution)/shard_map/ppermute | solution.py:727
  574.1 8.6 %collective-permute-start.64 = (f32[2,2048]{1,0:T(2,128)S(1)}, f32[2,2048]{1,0:T(2,128)S(1)}, u32[]{:S(2)}, u32[]{:S(2)}) collective-permute-start(f32[2,2048]{1,0:T(2,128)S(1)} %add.140), channel_id=1, source_target_pairs={{0,2},{1,3},{2,0},{3,1},{4,6},{5,7},{6,4},{7,5},{8,10},{9,11},{10,... | collective-permute-start | bytes 49160 | tf_op jit(solution)/shard_map/ppermute | solution.py:636
  577.6 61.5 %collective-permute-start.68 = (bf16[2048,256]{1,0:T(8,128)(2,1)S(1)}, bf16[2048,256]{1,0:T(8,128)(2,1)}, u32[]{:S(2)}, u32[]{:S(2)}) collective-permute-start(bf16[2048,256]{1,0:T(8,128)(2,1)S(1)} %add.193.total_ref), channel_id=1, source_target_pairs={{8,0},{16,24},{9,1},{17,25},{10,2},{18,26},{11,3},{19,27},{12,4},{... | collective-permute-start | bytes 3145736 | tf_op jit(solution)/shard_map/ppermute | solution.py:727
  580.8 58.3 %collective-permute-start.67 = (bf16[2048,256]{1,0:T(8,128)(2,1)S(1)}, bf16[2048,256]{1,0:T(8,128)(2,1)}, u32[]{:S(2)}, u32[]{:S(2)}) collective-permute-start(bf16[2048,256]{1,0:T(8,128)(2,1)S(1)} %add.192.left_ref), channel_id=1, source_target_pairs={{8,16},{16,8},{9,17},{17,9},{10,18},{18,10},{11,19},{19,11},{12,20... | collective-permute-start | bytes 3145736 | tf_op jit(solution)/shard_map/ppermute | solution.py:717
  582.7 7.1 %collective-permute-start.65 = (f32[2,2048]{1,0:T(2,128)S(1)}, f32[2,2048]{1,0:T(2,128)S(1)}, u32[]{:S(2)}, u32[]{:S(2)}) collective-permute-start(f32[2,2048]{1,0:T(2,128)S(1)} %add.141), channel_id=1, source_target_pairs={{0,4},{1,5},{2,6},{3,7},{4,0},{5,1},{6,2},{7,3},{8,12},{9,13},{10,... | collective-permute-start | bytes 49160 | tf_op jit(solution)/shard_map/ppermute | solution.py:636
  593.0 57.2 %collective-permute-start.70 = (bf16[2048,256]{1,0:T(8,128)(2,1)S(1)}, bf16[2048,256]{1,0:T(8,128)(2,1)}, u32[]{:S(2)}, u32[]{:S(2)}) collective-permute-start(bf16[2048,256]{1,0:T(8,128)(2,1)S(1)} %add.195.total_ref), channel_id=1, source_target_pairs={{8,0},{16,24},{9,1},{17,25},{10,2},{18,26},{11,3},{19,27},{12,4},{... | collective-permute-start | bytes 3145736 | tf_op jit(solution)/shard_map/ppermute | solution.py:727
  594.3 53.7 %collective-permute-start.66 = (bf16[80,256]{1,0:T(8,128)(2,1)S(1)}, bf16[80,256]{1,0:T(8,128)(2,1)S(1)}, u32[]{:S(2)}, u32[]{:S(2)}) collective-permute-start(bf16[80,256]{1,0:T(8,128)(2,1)S(1)} %constant_dynamic-update-slice_fusion.left_ref), channel_id=1, source_target_pairs={{0,8},{24,16},{1,9},{25,17},{2,10},{26,18},{3,11},{27,19},{4,12},{... | collective-permute-start | bytes 122888 | tf_op jit(solution)/shard_map/ppermute | solution.py:711
  640.8 28.0 %collective-permute-start.72 = (bf16[2048,256]{1,0:T(8,128)(2,1)S(1)}, bf16[2048,256]{1,0:T(8,128)(2,1)S(1)}, u32[]{:S(2)}, u32[]{:S(2)}) collective-permute-start(bf16[2048,256]{1,0:T(8,128)(2,1)S(1)} %add.197.total_ref), channel_id=1, source_target_pairs={{8,0},{16,24},{9,1},{17,25},{10,2},{18,26},{11,3},{19,27},{12,4},{... | collective-permute-start | bytes 3145736 | tf_op jit(solution)/shard_map/ppermute | solution.py:727
  648.0 10.6 %collective-permute-start.69 = (bf16[80,256]{1,0:T(8,128)(2,1)S(1)}, bf16[80,256]{1,0:T(8,128)(2,1)S(1)}, u32[]{:S(2)}, u32[]{:S(2)}) collective-permute-start(bf16[80,256]{1,0:T(8,128)(2,1)S(1)} %add.194.left_ref), channel_id=1, source_target_pairs={{8,16},{16,8},{9,17},{17,9},{10,18},{18,10},{11,19},{19,11},{12,20... | collective-permute-start | bytes 122888 | tf_op jit(solution)/shard_map/ppermute | solution.py:717
  658.6 16.5 %collective-permute-start.71 = (bf16[80,256]{1,0:T(8,128)(2,1)S(1)}, bf16[80,256]{1,0:T(8,128)(2,1)S(1)}, u32[]{:S(2)}, u32[]{:S(2)}) collective-permute-start(bf16[80,256]{1,0:T(8,128)(2,1)S(1)} %add.196), channel_id=1, source_target_pairs={{8,0},{16,24},{9,1},{17,25},{10,2},{18,26},{11,3},{19,27},{12,4},{... | collective-permute-start | bytes 122888 | tf_op jit(solution)/shard_map/ppermute | solution.py:727
  (113 other events, 757.3 us)
Sparse Core Ops, SparseCore 0:
  251.9 70.5 reduce-scatter.3
  339.8 52.4 all-gather.2
  419.5 76.0 reduce-scatter.5
  535.1 71.8 reduce-scatter.7

commit v4 on v3

--- a/solution.py
+++ b/solution.py
@@ -148,9 +148,9 @@
     gg_ref, q_ref, k_ref, v_ref, resp_ref, spec_ref, taps_ref, skip_ref, filt_ref, dft_ref, inv_ref = refs[:11]
     refs = refs[11:]
     if not first:
-        taps_before, lags_before = refs[3:5]
-        refs = refs[5:]
-    gq_ref, gk_ref, gv_ref, gtaps_ref, result_ref, pad, late, response_grad, grad_conv, spectrum, product, conv = refs
+        taps_before, lags_before = refs[1:3]
+        refs = refs[3:]
+    gproj_ref, gtaps_ref, result_ref, pad, late, response_grad, grad_conv, spectrum, product, conv = refs
     blocks, _, rows, chans = q_ref.shape
     length = blocks * rows
     load_padded((q_ref, k_ref, v_ref), pad)
@@ -212,7 +212,7 @@
             for back in (1, 2):
                 tap = taps[3 * back + index : 3 * back + index + 1]
                 total = total + tap * late[index, start + back : start + back + rows, :]
-            (gq_ref, gk_ref, gv_ref)[index][block, 0] = total.astype(bf16)
+            gproj_ref[block, 0, :, index * chans : (index + 1) * chans] = total.astype(bf16)
             for back in range(3):
                 shifted = pad[index, 8 + start - back : 8 + start - back + rows, :]
                 sums[3 * back + index] = sums[3 * back + index] + jnp.sum(
@@ -337,8 +337,12 @@
             pl.BlockSpec((1, 2 * length, chans), lambda i: (number, 0, 0)),
         ]
         + [whole(op.shape) for op in fixed]
-        + ([] if first else [pl.BlockSpec(memory_space=pl.ANY)] * 3 + [whole(op.shape) for op in before[3:]]),
-        out_specs=[part(0), part(0), part(0), whole((16, chans)), whole(result)],
+        + ([] if first else [pl.BlockSpec(memory_space=pl.ANY)] + [whole(op.shape) for op in before[1:]]),
+        out_specs=[
+            pl.BlockSpec((blocks, 1, rows, triple), lambda i: (0, number, 0, 0)),
+            whole((16, chans)),
+            whole(result),
+        ],
         scratch_shapes=[
             pltpu.VMEM((3, length + 8, chans), f32),
             pltpu.VMEM((3, length + 8, chans), f32),
@@ -348,9 +352,12 @@
             pltpu.VMEM((2 * length, chans), bf16),
             pltpu.VMEM((length, chans), f32),
         ],
-        out_shape=[jax.ShapeDtypeStruct((blocks, seqs, rows, chans), bf16)] * 3
-        + [jax.ShapeDtypeStruct((16, chans), f32), jax.ShapeDtypeStruct(result, f32)],
-        input_output_aliases={} if first else {11: 0, 12: 1, 13: 2},
+        out_shape=[
+            jax.ShapeDtypeStruct((blocks, seqs, rows, triple), bf16),
+            jax.ShapeDtypeStruct((16, chans), f32),
+            jax.ShapeDtypeStruct(result, f32),
+        ],
+        input_output_aliases={} if first else {11: 0},
         compiler_params=params(),
         cost_estimate=cost(12 * length * length * chans, 80 * length * chans),
         name="mixer_backward",
@@ -482,6 +489,28 @@
     return call
 
 
+def token_grad_kernel(grad_ref, rows_ref, second_ref, gain_ref, out_ref):
+    rows_in = rows_ref[0].astype(f32)
+    scale = row_scale(rows_in)
+    total = second_ref[0] + norm_back(grad_ref[0].astype(f32), rows_in, scale, gain_ref[...])
+    out_ref[0, :, 0, :] = total
+
+
+def token_grad(grad_normed, rows_in, grad_second, gain):
+    seqs, rows, width = grad_normed.shape
+    part = pl.BlockSpec((1, rows, width), lambda i: (i, 0, 0))
+    return pl.pallas_call(
+        token_grad_kernel,
+        grid=(seqs,),
+        in_specs=[part, part, part, whole((1, width))],
+        out_specs=pl.BlockSpec((1, rows, 1, width), lambda i: (i, 0, 0, 0)),
+        out_shape=jax.ShapeDtypeStruct((seqs, rows, 1, width), f32),
+        compiler_params=params(),
+        cost_estimate=cost(1000, 1000),
+        name="token_grad",
+    )(grad_normed, rows_in, grad_second, gain.reshape(1, width))
+
+
 def outer_kernel(left_ref, right_ref, out_ref):
     out_ref[...] = dot32(left_ref[...], right_ref[...]).astype(bf16)
 
@@ -513,29 +542,33 @@
     return lax.psum_scatter(partial_sums, "mp", scatter_dimension=0).astype(f32)
 
 
-def finish_kernel(end_ref, outward_ref, total_ref, *refs):
-    refs[-1][...] = jnp.where(end_ref[0] == 1, outward_ref[...].astype(f32), total_ref[...].astype(f32))
-
-
-def finish(end, outward, total, start, used, height, filled):
-    width = total.shape[1]
-    rows = math.gcd(start, used) if start else used
-    rows = rows // 2 if rows * width > 512 * 1024 and rows % 32 == 0 else rows
-    piece = pl.BlockSpec((rows, width), lambda i, e: (i, 0))
+def finish_kernel(end_ref, *refs):
+    out_ref = refs[-1]
+    count = len(refs) // 2
+    for number in range(count):
+
+        @pl.when(pl.program_id(0) == number)
+        def _(number=number):
+            outward, total = refs[2 * number][...].astype(f32), refs[2 * number + 1][...].astype(f32)
+            out_ref[...] = jnp.where(end_ref[0] == 1, outward, total)
+
+
+def finish(end, pairs):
+    height, width = pairs[0][1].shape
+    operands = [array for pair in pairs for array in pair]
     return pl.pallas_call(
         finish_kernel,
         grid_spec=pltpu.PrefetchScalarGridSpec(
             num_scalar_prefetch=1,
-            grid=(used // rows,),
-            in_specs=[piece, piece] + [pl.BlockSpec(memory_space=pl.ANY)] * len(filled),
-            out_specs=pl.BlockSpec((rows, width), lambda i, e: (start // rows + i, 0)),
+            grid=(len(pairs),),
+            in_specs=[whole(op.shape) for op in operands],
+            out_specs=pl.BlockSpec((height, width), lambda i, e: (i, 0)),
         ),
-        out_shape=jax.ShapeDtypeStruct((height, width), f32),
-        input_output_aliases={3: 0} if filled else {},
+        out_shape=jax.ShapeDtypeStruct((height * len(pairs), width), f32),
         compiler_params=params(),
-        cost_estimate=cost(1000, 8 * used * width),
+        cost_estimate=cost(1000, 1000),
         name="finish",
-    )(end, outward, total, *filled)
+    )(end, *operands)
 
 
 def add_kernel(left_ref, right_ref, out_ref):
@@ -558,6 +591,25 @@
     )(left, right)
 
 
+def merge_kernel(end_ref, part_ref, left_ref, right_ref, out_ref):
+    total = (left_ref[...].astype(f32) + right_ref[...].astype(f32)).astype(bf16)
+    out_ref[...] = jnp.where(end_ref[0] == 1, part_ref[...].astype(f32), total.astype(f32)).astype(bf16)
+
+
+def merge(end, part, left, right):
+    piece = pl.BlockSpec(left.shape, lambda i, e: (0, 0))
+    return pl.pallas_call(
+        merge_kernel,
+        grid_spec=pltpu.PrefetchScalarGridSpec(
+            num_scalar_prefetch=1, grid=(1,), in_specs=[piece] * 3, out_specs=piece
+        ),
+        out_shape=jax.ShapeDtypeStruct(left.shape, bf16),
+        compiler_params=params(),
+        cost_estimate=cost(1000, 1000),
+        name="merge",
+    )(end, part, left, right)
+
+
 def together(*values):
     return lax.optimization_barrier(values)
 
@@ -568,8 +620,7 @@
 
 class WholeGather:
     def __init__(self, block):
-        blocks = gather_whole(block)
-        self.blocks = [(blocks[i],) for i in range(blocks.shape[0])]
+        self.here = gather_whole(block)
 
     def tie(self, names, *values):
         return values
@@ -578,7 +629,7 @@
         pass
 
     def near(self):
-        return self.blocks
+        return [(self.here[i],) for i in range(self.here.shape[0])]
 
     def side(self):
         return []
@@ -600,36 +651,34 @@
     def gather(self, block):
         return WholeGather(block)
 
-    def scatter(self, array, product, coming, compute):
-        return scatter_whole(product(array)), compute(coming)
+    def scatter(self, array, product, coming):
+        return scatter_whole(product(array))
 
     def sum_mp(self, part):
         return lax.psum(part, "mp")
 
-    def push(self, part):
-        self.parts.append(part)
-
-    def hop_in(self, *values):
+    def hop(self, *values, part=None, last=False):
+        if part is not None:
+            self.parts.append(lax.psum(part, "dp"))
         return values
 
-    def hop_out(self, *values, keep=0):
-        return values
-
-    def come(self, *values):
-        return values
-
-    def sums_so_far(self):
-        return self.sums()
-
     def sums(self):
-        return [lax.psum(part, "dp") for part in self.parts]
-
-    def join(self, sums, total=None, before=None, number=0):
-        joined = jnp.concatenate(([] if before is None else [before]) + [part.astype(f32) for part in sums], axis=0)
-        return joined
-
-    def plain(self, total):
-        return total.astype(f32)
+        return self.parts
+
+    def join(self, first, last):
+        return jnp.concatenate([part.astype(f32) for part in self.parts[first:last]], axis=0)
+
+    def inward(self, part):
+        return lax.psum(part, "dp")
+
+    def across(self, part, came):
+        return came, came
+
+    def outward(self, half, came):
+        return came, came
+
+    def settled(self, total, came):
+        return came.astype(f32)
 
 
 def swap(block, bit):
@@ -661,9 +710,35 @@
         return [halves, tuple(swap(half, 1) for half in halves)]
 
 
+class Lane:
+    def __init__(self):
+        self.queue, self.flight, self.done = [], {}, []
+        self.part = self.half = self.total = None
+
+    def advance(self, end):
+        flight = self.flight
+        if "out" in flight:
+            self.done.append((flight["out"], self.total))
+        half = add(self.part, flight["in"]) if "in" in flight else None
+        self.part = self.queue.pop(0) if self.queue else None
+        started = {}
+        if "across" in flight and self.part is not None and self.part.shape == self.half.shape:
+            self.total = merge(end, self.part, self.half, flight["across"])
+            started["in"] = started["out"] = lax.ppermute(self.total, "dp", [(0, 1), (3, 2), (1, 0), (2, 3)])
+        else:
+            if self.part is not None:
+                started["in"] = lax.ppermute(self.part, "dp", [(0, 1), (3, 2)])
+            if "across" in flight:
+                self.total = add(self.half, flight["across"])
+                started["out"] = lax.ppermute(self.total, "dp", [(1, 0), (2, 3)])
+        if half is not None:
+            started["across"] = lax.ppermute(half, "dp", [(1, 2), (2, 1)])
+        self.half, self.flight = half, started
+
+
 class Square:
     def __init__(self):
-        self.queue, self.middle, self.sent, self.done = [], [], [], []
+        self.lanes, self.turn = (Lane(), Lane()), 0
 
     def counts(self, size):
         return (2, 4, 2)
@@ -674,85 +749,73 @@
     def gather(self, block):
         return SquareGather(block)
 
-    def scatter(self, array, product, coming, compute):
+    def scatter(self, array, product, coming):
         def both(mine, other):
             return mine.astype(f32) + swap(other, 1).astype(f32)
 
         far, array = together(product(array[6:8]), array)
         half = far.shape[1] // 2
         far_sum = both(far[0], far[1])
-        side, near, far_sum = together(product(array[2:6]), product(array[0:2]), far_sum)
         far_low, far_high = far_sum[:half].astype(bf16), far_sum[half:].astype(bf16)
+        side, near, far_low, far_high = together(product(array[2:6]), product(array[0:2]), far_low, far_high)
         from_far_low, from_far_high = swap(far_low, 2), swap(far_high, 4)
         x_sum = both(side[0], side[1])
         y_sum = both(side[2], side[3])
+        x_sum, y_sum = coming.tie(["far"], x_sum, y_sum)
         own_low_x = swap(x_sum[:half].astype(bf16), 2)
         own_high_y = swap(y_sum[half:].astype(bf16), 4)
         own = both(near[0], near[1])
-        own, x_sum, y_sum = coming.tie(["near", "side", "far"], own, x_sum, y_sum)
-        beside = compute(coming)
-        from_far_low, from_far_high, own_low_x, own_high_y, beside = together(
-            from_far_low, from_far_high, own_low_x, own_high_y, beside
-        )
         y_low = (y_sum[:half] + from_far_low.astype(f32)).astype(bf16)
         x_high = (x_sum[half:] + from_far_high.astype(f32)).astype(bf16)
         own_low_y = swap(y_low, 4)
         own_high_x = swap(x_high, 2)
         low = own[:half] + own_low_x.astype(f32) + own_low_y.astype(f32)
         high = own[half:] + own_high_y.astype(f32) + own_high_x.astype(f32)
-        return jnp.concatenate([low, high], axis=0), beside
+        return jnp.concatenate([low, high], axis=0)
 
     def sum_mp(self, part):
         for bit in (1, 2, 4):
             part = part + swap(part, bit)
         return part
 
-    def push(self, part):
-        self.queue.append((part, lax.ppermute(part, "dp", [(0, 1), (3, 2)])))
-
-    def hop_in(self, *values):
-        part, inward = self.queue.pop(0)
-        inward, values = together(inward, values)
-        half = add(part, inward)
-        self.middle.append((half, lax.ppermute(half, "dp", [(1, 2), (2, 1)])))
+    def end(self):
+        place = lax.axis_index("dp")
+        return ((place == 0) | (place == 3)).astype(jnp.int32).reshape(1)
+
+    def hop(self, *values, part=None, last=False):
+        lane = self.lanes[self.turn]
+        self.turn = 1 - self.turn
+        if last:
+            done = [each.done for each in self.lanes]
+            lane.flight, done, values = together(lane.flight, done, values)
+            for each, sums in zip(self.lanes, done):
+                each.done = list(sums)
+        else:
+            lane.flight, part, values = together(lane.flight, part, values)
+        if part is not None:
+            cut = part.shape[0] // 2
+            for each, half in zip(self.lanes, (part[:cut], part[cut:])):
+                each.queue.append(half)
+        lane.advance(self.end())
         return values
 
-    def hop_out(self, *values, keep=0):
-        half, across = self.middle.pop(0)
-        ready = len(self.sent) - keep
-        outward = [sent for _, sent in self.sent[:ready]]
-        across, outward, values = together(across, outward, values)
-        self.done += list(zip(outward, [total for total, _ in self.sent[:ready]]))
-        total = add(half, across)
-        self.sent = self.sent[ready:] + [(total, lax.ppermute(total, "dp", [(1, 0), (2, 3)]))]
-        return values
-
-    def come(self, *values):
-        (total, outward), self.sent = self.sent[0], self.sent[1:]
-        outward, values = together(outward, values)
-        self.done.append((outward, total))
-        return values
-
-    def sums_so_far(self):
-        return self.done
-
-    def sums(self):
-        return self.done + [(outward, total) for total, outward in self.sent]
-
-    def join(self, sums, total=None, before=None, number=0):
-        place = lax.axis_index("dp")
-        end = ((place == 0) | (place == 3)).astype(jnp.int32).reshape(1)
-        height = sums[0][1].shape[0]
-        filled = () if before is None else (before,)
-        for outward, part in sums:
-            filled = (finish(end, outward, part, number * height, height, height * (total or len(sums)), filled),)
-            number += 1
-        return filled[0]
-
-    def plain(self, pair):
-        place = lax.axis_index("dp")
-        outward, total = pair
-        return jnp.where((place == 0) | (place == 3), outward, total).astype(f32)
+    def join(self, first, last):
+        return finish(self.end(), [lane.done[number] for number in range(first, last) for lane in self.lanes])
+
+
+    def inward(self, part):
+        return lax.ppermute(part, "dp", [(0, 1), (3, 2)])
+
+    def across(self, part, came):
+        half = add(part, came)
+        return half, lax.ppermute(half, "dp", [(1, 2), (2, 1)])
+
+    def outward(self, half, came):
+        total = add(half, came)
+        return total, lax.ppermute(total, "dp", [(1, 0), (2, 3)])
+
+    def settled(self, total, came):
+        return jnp.where(self.end()[0] == 1, came, total).astype(f32)
 
 
 def local(
@@ -765,6 +828,7 @@
     hidden_units = gate_proj.shape[1]
     length = rows * lax.axis_size("mp")
     in_parts = in_proj.transpose(1, 0, 2)
+    in_flat = in_proj.reshape(width, 3 * chans)
     gate_t, up_t = gate_proj.T, up_proj.T
     table = dft_matrix(length)
     dft = jnp.asarray(table, bf16)
@@ -818,7 +882,7 @@
         return arrive(project_kernel, group, number, (in_parts,), (), ((3 * chans, f32, False), (width, bf16, False)), filled)
 
     filled = projected(coming.near(), 0, ())
-    filled, filt_spec, grad_final_low = coming.tie(["side"], filled, filt_spec, grad_final_low)
+    filled, filt_spec, grad_final_low, in_flat = coming.tie(["side"], filled, filt_spec, grad_final_low, in_flat)
     coming.reach()
     filled = projected(coming.side(), 1, filled)
     filled, grad_final_low = coming.tie(["far"], filled, grad_final_low)
@@ -837,22 +901,22 @@
     def hidden_backed(group, number, filled):
         return arrive(hidden_back_kernel, group, number, (down_proj,), (), ((hidden_units, f32, True), (width, bf16, False)), filled)
 
-    def beside_scatter(grad_coming):
-        return hidden_backed(grad_coming.side(), 1, hidden_backed(grad_coming.near(), 0, ()))
-
-    mixed_sum, filled = links.scatter(gated, mixed_out, grad_coming, beside_scatter)
-    second = rows_in + mixed_sum
+    second = rows_in + links.scatter(gated, mixed_out, grad_coming)
     scale_second = row_scale(second)
     mlp_normed = (second * scale_second * mlp_gain).astype(bf16)
+    mlp_normed, grad_coming.here = together(mlp_normed, grad_coming.here)
     coming = links.gather(mlp_normed)
+    filled = hidden_backed(grad_coming.near(), 0, ())
+    filled = hidden_backed(grad_coming.side(), 1, filled)
     grad_hidden, grad_final_all = hidden_backed(grad_coming.far(), 2, filled)
+    (grad_hidden,) = coming.tie(["side"], grad_hidden)
 
     def fed(group, number, filled):
         outputs = ((hidden_units, bf16, True),) * 3 + ((width, bf16, False),)
         return arrive(feed_kernel, group, number, (gate_t, up_t), (grad_hidden,), outputs, filled)
 
-    (filled,) = coming.tie(["side"], fed(coming.near(), 0, ()))
     coming.reach()
+    filled = fed(coming.near(), 0, ())
     filled = fed(coming.side(), 1, filled)
     (filled,) = coming.tie(["far"], filled)
     hidden, grad_gate, grad_up, mlp_all = fed(coming.far(), 2, filled)
@@ -864,61 +928,47 @@
         return array.reshape(blocks, seqs, rows, array.shape[-1])
 
     grad_final_all, mlp_all = flat(grad_final_all), flat(mlp_all)
-    links.push(outer(hidden, grad_final_all, 0, 2))
-    down_two, grad_gate, grad_up = together(outer(hidden, grad_final_all, 1, 2), grad_gate, grad_up)
-    links.push(down_two)
+    links.hop(part=outer(hidden, grad_final_all, 0, 2))
+    links.hop()
+    grad_gate, grad_up, hidden = links.hop(
+        grad_gate, grad_up, hidden, part=outer(hidden, grad_final_all, 1, 2)
+    )
     mlp_back = blocked(sum_products(contract_rows, (gate_t, up_t), bf16, True)(blocks, grad_gate, grad_up))
-    gate_one = outer(grad_gate, mlp_all, 0, 2)
-    mlp_back, gate_one, grad_gate = links.hop_in(mlp_back, gate_one, grad_gate)
-    links.push(gate_one)
+    mlp_back, grad_gate = links.hop(mlp_back, grad_gate)
     grad_mlp_normed = scatter_whole(mlp_back)
-    gate_two = outer(grad_gate, mlp_all, 1, 2)
-    gate_two, grad_up = links.hop_in(gate_two, grad_up)
-    links.push(gate_two)
-    (grad_up,) = links.hop_out(grad_up)
-    up_one = outer(grad_up, mlp_all, 0, 2)
-    up_one, grad_up = links.hop_in(up_one, grad_up)
-    links.push(up_one)
-    grad_up, hidden, second = links.hop_out(grad_up, hidden, second)
+    grad_gate, grad_up = links.hop(grad_gate, grad_up, part=outer(grad_gate, mlp_all, 0, 2))
+    gate_two, grad_up = links.hop(outer(grad_gate, mlp_all, 1, 2), grad_up)
+    up_one, grad_up = links.hop(outer(grad_up, mlp_all, 0, 2), grad_up, part=gate_two)
+    up_two, second = links.hop(outer(grad_up, mlp_all, 1, 2), second)
+    second, hidden = links.hop(second, hidden, part=up_one)
     grad_second = grad_final + norm_back(grad_mlp_normed, second, scale_second, mlp_gain)
     gain_two = jnp.sum(grad_mlp_normed * second * scale_second, axis=(0, 1))
     grad_branch_all = gather_whole(grad_second.astype(bf16))
-    up_two = outer(grad_up, mlp_all, 1, 2)
-    up_two, gain_two, hidden = links.hop_in(up_two, gain_two, hidden)
-    links.push(up_two)
     mlp_part = blocked(sum_products(contract_rows, (down_proj,), bf16, True)(blocks, hidden))
-    (mlp_part,) = links.hop_out(mlp_part)
-    (gated_ordered,) = links.hop_in(gated_ordered)
+    mlp_part, gain_two = links.hop(mlp_part, gain_two)
+    mlp_part, gated_ordered = links.hop(mlp_part, gated_ordered, part=up_two)
+    mlp_part, gated_ordered = links.hop(mlp_part, gated_ordered)
 
     grad_gated = blocked(
         sum_products(contract_cols, (out_proj,), f32, False)(blocks, grad_branch_all.reshape(blocks, -1, width))
     )
-    grads_out = weight_gradient(gated_ordered, grad_branch_all)
-    grads_out, grad_gated, mlp_part = links.hop_out(grads_out, grad_gated, mlp_part)
-    links.push(grads_out)
+    grad_out = weight_gradient(gated_ordered, grad_branch_all)
+    grad_gated, mlp_part = links.hop(grad_gated, mlp_part, part=grad_out)
     mlp_out = scatter_whole(mlp_part)
     back = ()
     for number in range(seqs - 1):
         back = mixer_back(number, back, grad_gated, proj, response, spec, taps9, skip, filt_spec, dft, inverse)
-    back, grad_gated = links.hop_in(back, grad_gated)
-    back, grad_gated = links.hop_out(back, grad_gated)
-    *grad_parts, grad_taps, grad_filt = mixer_back(
+    back, grad_gated = links.hop(back, grad_gated)
+    grad_proj, grad_taps, grad_filt = mixer_back(
         seqs - 1, tuple(back), grad_gated, proj, response, spec, taps9, skip, filt_spec, dft, inverse
     )
-    grad_parts = [part.reshape(blocks, seqs * rows, chans) for part in grad_parts]
-    grad_q = weight_gradient(normed_all, grad_parts[0])
-    links.push(grad_q)
-    grad_q, grad_parts, grad_filt = links.hop_in(grad_q, grad_parts, grad_filt)
-    grad_parts, grad_filt = links.hop_out(grad_parts, grad_filt)
-    grad_k = weight_gradient(normed_all, grad_parts[1])
-    links.push(grad_k)
-    grad_v = weight_gradient(normed_all, grad_parts[2])
-    links.push(grad_v)
-    grads_in, grad_parts, grad_filt = links.hop_in((grad_q, grad_k, grad_v), grad_parts, grad_filt)
-    grad_in_rows = blocked(sum_products(contract_cols, tuple(in_parts), bf16, False)(blocks, *grad_parts))
-    grad_in_rows, grads_in, grad_filt = links.hop_in(grad_in_rows, grads_in, grad_filt)
+    grad_in = weight_gradient(normed_all, grad_proj)
+    grads_in = [grad_in[:, part * chans : (part + 1) * chans] for part in range(3)]
+    grads_in, grad_proj, grad_filt = links.hop(grads_in, grad_proj, grad_filt, part=grads_in[0])
+    grad_in_rows = blocked(contract_cols(flat(grad_proj), in_flat).astype(bf16).reshape(blocks, -1, width))
+    grad_in_rows, grads_in = links.hop(grad_in_rows, grads_in)
+    grads_in, grad_filt = links.hop(grads_in, grad_filt, part=grads_in[1])
     grad_normed = scatter_whole(grad_in_rows)
-    grads_in, grad_filt = links.hop_out(grads_in, grad_filt)
 
     ones = jnp.ones((8, chans), bf16)
     against = sum(
@@ -926,30 +976,32 @@
         for grad, part in zip(grads_in, in_parts)
     )
     gains = jnp.stack([against / norm_gain, gain_two], axis=0)
-    gains, grad_filt = links.hop_in(gains, grad_filt)
-    gains, grad_filt = links.hop_out(gains, grad_filt, keep=1)
+    gains, grad_filt = links.hop(gains, grad_filt)
     pole_sum, pole_re, pole_im = pole_gradients(grad_filt, tables)
-    gains, pole_sum = links.hop_out(links.sum_mp(gains), pole_sum, keep=1)
+    gains, pole_sum = links.hop(links.sum_mp(gains), pole_sum, part=grads_in[2])
     poles = filter_residue.shape[1]
     small = [grad_taps, pole_sum, -residue_t * pole_re, -residue_t * pole_im, gains.reshape(-1, chans)]
     small = [jnp.pad(rows_of, ((0, -rows_of.shape[0] % 8), (0, 0))) for rows_of in small]
     bounds = np.cumsum([0] + [rows_of.shape[0] for rows_of in small])
-    small = jnp.pad(jnp.concatenate(small, axis=0), ((0, -int(bounds[-1]) % 16), (0, 0))).astype(bf16)
-    links.push(small)
-    sum_down = links.join(links.sums_so_far()[:2])
-    sum_down, grad_second = links.hop_out(sum_down, grad_second, keep=1)
-    sum_gate = links.join(links.sums_so_far()[2:4])
-    sum_gate, grad_second = links.hop_in(sum_gate, grad_second)
-    sum_up, sum_out = links.join(links.sums_so_far()[4:6]), links.join(links.sums_so_far()[6:7])
-    sum_up, sum_out, mlp_out = links.come(sum_up, sum_out, mlp_out)
-    sum_in = links.join(links.sums_so_far()[7:9], 3)
+    small = jnp.pad(jnp.concatenate(small, axis=0), ((0, -int(bounds[-1]) % 32), (0, 0))).astype(bf16)
+    (small,) = links.hop(small)
+    came = links.inward(small)
+    links.hop()
+    (came,) = links.hop(came)
+    half, came = links.across(small, came)
+    grad_second, mlp_out = links.hop(grad_second, mlp_out)
     layer_out = ((second + mlp_out) * valid).astype(bf16)
-    grad_tokens = by_position(grad_second + norm_back(grad_normed, rows_in, scale_in, norm_gain))
-    sum_in, layer_out, grad_tokens = links.hop_out(sum_in, layer_out, grad_tokens, keep=1)
-
-    sums = links.sums()
-    sum_in = links.join(sums[9:10], 3, sum_in, 2).reshape(3, width, chans)
-    sum_small = links.plain(sums[10])
+    half, came, layer_out, grad_second = links.hop(half, came, layer_out, grad_second, last=True)
+    total, came = links.outward(half, came)
+    if per_dev == 1:
+        grad_tokens = token_grad(grad_normed, by_sequence(tokens), grad_second, norm_gain)
+    else:
+        grad_tokens = by_position(grad_second + norm_back(grad_normed, rows_in, scale_in, norm_gain))
+    sum_down, sum_gate, sum_up, sum_out = (links.join(*at) for at in ((0, 2), (2, 4), (4, 6), (6, 7)))
+    grad_tokens, total = links.hop(grad_tokens, total)
+    came, sum_down, sum_gate, sum_up, sum_out = links.hop(came, sum_down, sum_gate, sum_up, sum_out)
+    sum_small = links.settled(total, came)
+    sum_in = links.join(7, 10).reshape(3, width, chans)
     small = [sum_small[low:high] for low, high in zip(bounds[:-1], bounds[1:])]
     gains = small[4][: 2 * width // chans].reshape(2, width)
     return (

time: 697 us -> 680 us (0.976)
  the two profiles are of different devices: /device:TPU:0 before, /device:TPU:8 now
where the time goes in v4:
time: 680 us; the launch traced here: 667 us
  Pallas kernels  297 us (44%)
  starting transfers between devices  135 us (20%)
  waiting for transfers between devices  127 us (19%)
  local copies, waits for them, and re-layouts  37.4 us (6%)
  matrix products  29.7 us (4%)
  other arithmetic  25 us (4%)
  between operations  16.3 us (2%)
    pallas_call x9, Pallas kernels, on_arrival(): pl.pallas_call(partial(kernel, [len(block) for block in group], len(fille...  68.9 us
    ppermute x20, starting transfers between devices, advance(): started['across'] = lax.ppermute(half, 'dp', [(1, 2), (2, 1)])  57.3 us
    ppermute x40, waiting for transfers between devices, swap(): return lax.ppermute(block, 'mp', [(i, i ^ bit) for i in range(8)])  53.8 us
    pallas_call x6, Pallas kernels, outer(): pl.pallas_call(outer_kernel, grid=(width // tile,), in_specs=[pl.BlockSpe...  40.2 us
    pallas_call x3, Pallas kernels, call(): pl.pallas_call(kernel, grid=(blocks,), in_specs=[left_spec] * len(lefts)...  39.8 us
    pallas_call x32, Pallas kernels, add(): pl.pallas_call(add_kernel, grid=(height // rows,), in_specs=[piece, piece...  35.3 us
    pallas_call x2, Pallas kernels, mixer_back(): pl.pallas_call(partial(mixer_back_kernel, first, last), grid=(1,), in_spe...  34.2 us
    ppermute x10, starting transfers between devices, advance(): started['out'] = lax.ppermute(self.total, 'dp', [(1, 0), (2, 3)])  29.4 us
  transfers between devices with their start and end apart: 97, of which 41 were waited for; matrix products, arithmetic and copies ran while one was open for 8% of the time, Pallas kernels for 41%

profile of v4, /device:TPU:8, one launch (start us, length us, event | category | flops | bytes accessed | tf_op | source)
XLA Modules:
  0.0 667.5 jit_solution(9696783397675226302)
XLA Ops:
  14.3 2.8 fusion.25
  19.2 5.0 copy.56
  24.2 8.0 %modal_filter.1.filt_ref.refs_8_ = f32[2048,256]{1,0:T(8,128)} custom-call(f32[32,16,256]{2,1,0:T(8,128)S(1)} %get-tuple-element.581.hre_ref, f32[32,16,256]{2,1,0:T(8,128)S(1)} %get-tuple-element.580.him_ref, f32[16,32,256]{2,1,0:T(8,128)S(1)} %get-tuple-element.579.lre_ref, f32[16,32,256]{2,1,0:T(8,128)} %get-tuple-element.578.lim_ref, ...), custom_call_target="tpu_custom_call" | custom-call | tf_op jit(solution)/shard_map/modal_filter/pallas_call | solution.py:246
  33.6 5.9 project.3
  44.8 8.4 %project.4 = (f32[8,256,768]{2,1,0:T(8,128)}, bf16[8,256,2048]{2,1,0:T(8,128)(2,1)}) custom-call(s32[1]{0:T(128)} %bitcast.me_ref, bf16[2,128,2048]{2,1,0:T(8,128)(2,1)S(1)} %collective-permute-done.refs_0_, bf16[2,128,2048]{2,1,0:T(8,128)(2,1)} %copy-done.82, ...), custom_call_target="tpu_custom_call", output_to_operand_aliasing={{0}: (6, {}), {1}: (7, {})} | custom-call | flops 3221225472 | bytes 3145728 | tf_op jit(solution)/shard_map/project/pallas_call | solution.py:443
  58.7 5.4 project.5
  64.1 17.0 %mixer_forward.1 = (bf16[8,2,128,256]{3,2,1,0:T(8,128)(2,1)S(1)}, bf16[8,2,128,256]{3,2,1,0:T(8,128)(2,1)}, f32[2,1024,256]{2,1,0:T(8,128)}, f32[2,2048,256]{2,1,0:T(8,128)}) custom-call(s32[1]{0:T(128)} %bitcast.me_ref, f32[8,2,128,768]{3,2,1,0:T(8,128)} %bitcast.143, f32[8,2,128,768]{3,2,1,0:T(8,128)} %bitcast.144, f32[8,2,128,768]{3,2,1,0:T(8,128)} %bitcast.145, ...), custom_call_target="tpu_custom_call" | custom-call | flops 4294967296 | bytes 20971520 | tf_op jit(solution)/shard_map/mixer_forward/pallas_call | solution.py:289
  92.5 8.6 %collective-permute-done.13.refs_0_ = bf16[1,128,2048]{2,1,0:T(8,128)(2,1)S(1)} collective-permute-done((bf16[1,128,2048]{2,1,0:T(8,128)(2,1)S(1)}, bf16[1,128,2048]{2,1,0:T(8,128)(2,1)S(1)}, u32[]{:S(2)}, u32[]{:S(2)}) %collective-permute-start.13) | collective-permute-done | bytes 524320 | tf_op jit(solution)/shard_map/ppermute | solution.py:685
  103.9 7.7 %collective-permute-done.21 = bf16[1,128,2048]{2,1,0:T(8,128)(2,1)S(1)} collective-permute-done((bf16[1,128,2048]{2,1,0:T(8,128)(2,1)S(1)}, bf16[1,128,2048]{2,1,0:T(8,128)(2,1)S(1)}, u32[]{:S(2)}, u32[]{:S(2)}) %collective-permute-start.21) | collective-permute-done | bytes 524320 | tf_op jit(solution)/shard_map/ppermute | solution.py:685
  116.7 9.9 %collective-permute-done.22 = bf16[1,128,2048]{2,1,0:T(8,128)(2,1)S(1)} collective-permute-done((bf16[1,128,2048]{2,1,0:T(8,128)(2,1)S(1)}, bf16[1,128,2048]{2,1,0:T(8,128)(2,1)S(1)}, u32[]{:S(2)}, u32[]{:S(2)}) %collective-permute-start.22) | collective-permute-done | bytes 524320 | tf_op jit(solution)/shard_map/ppermute | solution.py:685
  126.6 9.8 %collective-permute-done.17 = bf16[1,128,2048]{2,1,0:T(8,128)(2,1)S(1)} collective-permute-done((bf16[1,128,2048]{2,1,0:T(8,128)(2,1)S(1)}, bf16[1,128,2048]{2,1,0:T(8,128)(2,1)S(1)}, u32[]{:S(2)}, u32[]{:S(2)}) %collective-permute-start.17) | collective-permute-done | bytes 524320 | tf_op jit(solution)/shard_map/ppermute | solution.py:685
  143.9 6.1 hidden_back.3
  151.0 8.2 %hidden_back.4 = (f32[704,2048]{1,0:T(8,128)}, bf16[8,256,2048]{2,1,0:T(8,128)(2,1)}) custom-call(s32[1]{0:T(128)} %bitcast.me_ref, bf16[2,128,2048]{2,1,0:T(8,128)(2,1)S(1)} %collective-permute-done.7.refs_0_, bf16[2,128,2048]{2,1,0:T(8,128)(2,1)} %copy-done.78, ...), custom_call_target="tpu_custom_call", output_to_operand_aliasing={{0}: (6, {}), {1}: (7, {})} | custom-call | flops 2952790016 | bytes 2883584 | tf_op jit(solution)/shard_map/hidden_back/pallas_call | solution.py:443
  160.0 5.2 hidden_back.5
  170.8 8.5 %feed.3 = (bf16[704,2048]{1,0:T(8,128)(2,1)}, bf16[704,2048]{1,0:T(8,128)(2,1)}, bf16[704,2048]{1,0:T(8,128)(2,1)}, bf16[8,256,2048]{2,1,0:T(8,128)(2,1)}) custom-call(s32[1]{0:T(128)} %bitcast.me_ref, bf16[2,128,2048]{2,1,0:T(8,128)(2,1)S(1)} %multiply_convert_fusion.1.refs_0_, bf16[2,128,2048]{2,1,0:T(8,128)(2,1)} %copy-done.84, ...), custom_call_target="tpu_custom_call" | custom-call | flops 2952790016 | bytes 5767168 | tf_op jit(solution)/shard_map/feed/pallas_call | solution.py:443
  180.7 13.0 %feed.4 = (bf16[704,2048]{1,0:T(8,128)(2,1)}, bf16[704,2048]{1,0:T(8,128)(2,1)}, bf16[704,2048]{1,0:T(8,128)(2,1)}, bf16[8,256,2048]{2,1,0:T(8,128)(2,1)}) custom-call(s32[1]{0:T(128)} %bitcast.me_ref, bf16[2,128,2048]{2,1,0:T(8,128)(2,1)S(1)} %collective-permute-done.24.refs_0_, ...), custom_call_target="tpu_custom_call", output_to_operand_aliasing={{0}: (8, {}), {1}: (9, {}), {2}: (10, {}), {3}: (11, {})} | custom-call | flops 5905580032 | bytes 5767168 | tf_op jit(solution)/shard_map/feed/pallas_call | solution.py:443
  197.3 8.3 %feed.5 = (bf16[704,2048]{1,0:T(8,128)(2,1)}, bf16[704,2048]{1,0:T(8,128)(2,1)}, bf16[704,2048]{1,0:T(8,128)(2,1)}, bf16[8,256,2048]{2,1,0:T(8,128)(2,1)}) custom-call(s32[1]{0:T(128)} %bitcast.me_ref, bf16[1,128,2048]{2,1,0:T(8,128)(2,1)S(1)} %collective-permute-done.30.refs_0_, ...), custom_call_target="tpu_custom_call", output_to_operand_aliasing={{0}: (8, {}), {1}: (9, {}), {2}: (10, {}), {3}: (11, {})} | custom-call | flops 2952790016 | bytes 5767168 | tf_op jit(solution)/shard_map/feed/pallas_call | solution.py:443
  205.5 6.6 weight_gradient.6
  214.9 6.6 weight_gradient.7
  221.5 11.7 %collective-permute-done.37.right_ref = bf16[176,2048]{1,0:T(8,128)(2,1)S(1)} collective-permute-done((bf16[176,2048]{1,0:T(8,128)(2,1)S(1)}, bf16[176,2048]{1,0:T(8,128)(2,1)S(1)}, u32[]{:S(2)}, u32[]{:S(2)}) %collective-permute-start.37) | collective-permute-done | bytes 720928 | tf_op jit(solution)/shard_map/ppermute | solution.py:730
  233.1 18.8 %sum_products.3 = bf16[8,256,2048]{2,1,0:T(8,128)(2,1)} custom-call(bf16[704,2048]{1,0:T(8,128)(2,1)} %get-tuple-element.327.refs_0_.left_ref, bf16[704,2048]{1,0:T(8,128)(2,1)} %get-tuple-element.337.refs_1_.left_ref, bf16[704,2048]{1,0:T(8,128)(2,1)} %bitcast.172, bf16[704,2048]{1,0:T(8,128)(2,1)} %bitcast.176), custom_call_target="tpu_custom_call" | custom-call | flops 11811160064 | bytes 8388608 | tf_op jit(solution)/shard_map/sum_products/pallas_call | solution.py:478
  255.1 3.5 collective-permute-start.38
  267.1 7.1 %weight_gradient.8 = bf16[352,2048]{1,0:T(8,128)(2,1)S(1)} custom-call(bf16[704,2048]{1,0:T(8,128)(2,1)} %get-tuple-element.327.refs_0_.left_ref, bf16[2048,2048]{1,0:T(8,128)(2,1)} %bitcast.152), custom_call_target="tpu_custom_call" | custom-call | flops 2952790016 | bytes 8388608 | tf_op jit(solution)/shard_map/weight_gradient/pallas_call | solution.py:522
  276.3 4.5 collective-permute-done.39.right_ref
  286.7 6.7 %weight_gradient.9 = bf16[352,2048]{1,0:T(8,128)(2,1)S(1)} custom-call(bf16[704,2048]{1,0:T(8,128)(2,1)} %get-tuple-element.327.refs_0_.left_ref, bf16[2048,2048]{1,0:T(8,128)(2,1)} %bitcast.153), custom_call_target="tpu_custom_call" | custom-call | flops 2952790016 | bytes 8388608 | tf_op jit(solution)/shard_map/weight_gradient/pallas_call | solution.py:522
  302.0 6.6 weight_gradient.10
  317.4 6.7 weight_gradient.11
  327.1 12.7 %collective-permute-done.46.right_ref.refs_4_ = bf16[176,2048]{1,0:T(8,128)(2,1)S(1)} collective-permute-done((bf16[176,2048]{1,0:T(8,128)(2,1)S(1)}, bf16[176,2048]{1,0:T(8,128)(2,1)S(1)}, u32[]{:S(2)}, u32[]{:S(2)}) %collective-permute-start.46) | collective-permute-done | bytes 720928 | tf_op jit(solution)/shard_map/ppermute | solution.py:727
  343.5 3.7 fusion.32
  358.9 3.3 collective-permute-start.49
  362.2 11.9 %sum_products.4 = bf16[8,256,2048]{2,1,0:T(8,128)(2,1)} custom-call(bf16[704,2048]{1,0:T(8,128)(2,1)} %get-tuple-element.346.left_ref.refs_0_, bf16[704,2048]{1,0:T(8,128)(2,1)} %refs_1_.2), custom_call_target="tpu_custom_call" | custom-call | flops 5905580032 | bytes 8388608 | tf_op jit(solution)/shard_map/sum_products/pallas_call | solution.py:478
  379.1 3.0 collective-permute-start.55
  382.9 3.1 collective-permute-done.49.right_ref
  394.0 4.3 collective-permute-done.56.right_ref.refs_2_
  401.6 9.1 %sum_products.5 = f32[8,256,256]{2,1,0:T(8,128)} custom-call(bf16[8,256,2048]{2,1,0:T(8,128)(2,1)} %bitcast.165, bf16[256,2048]{1,0:T(8,128)(2,1)S(1)} %copy-done.2), custom_call_target="tpu_custom_call" | custom-call | flops 2147483648 | bytes 1048576 | tf_op jit(solution)/shard_map/sum_products/pallas_call | solution.py:478
  410.6 3.6 fusion
  417.9 3.1 collective-permute-start.60
  422.8 18.2 %mixer_backward.2 = (bf16[8,2,128,768]{3,2,1,0:T(8,128)(2,1)}, f32[16,256]{1,0:T(8,128)S(1)}, f32[2048,256]{1,0:T(8,128)}) custom-call(f32[8,2,128,256]{3,2,1,0:T(8,128)} %bitcast.177, f32[8,2,128,768]{3,2,1,0:T(8,128)} %bitcast.146, f32[8,2,128,768]{3,2,1,0:T(8,128)} %bitcast.147, f32[8,2,128,768]{3,2,1,0:T(8,128)} %bitcast.148, ...), custom_call_target="tpu_custom_call" | custom-call | flops 3221225472 | bytes 20971520 | tf_op jit(solution)/shard_map/mixer_backward/pallas_call | solution.py:331
  445.6 3.2 collective-permute-start.57
  450.1 2.9 collective-permute-start.67
  454.3 3.5 collective-permute-start.65
  457.8 16.0 %mixer_backward.3 = (bf16[8,2,128,768]{3,2,1,0:T(8,128)(2,1)}, f32[16,256]{1,0:T(8,128)S(1)}, f32[1024,256]{1,0:T(8,128)S(1)}) custom-call(f32[8,2,128,256]{3,2,1,0:T(8,128)} %bitcast.178, f32[8,2,128,768]{3,2,1,0:T(8,128)} %bitcast.149, f32[8,2,128,768]{3,2,1,0:T(8,128)} %bitcast.150, ...), custom_call_target="tpu_custom_call", output_to_operand_aliasing={{0}: (11, {})} | custom-call | flops 3221225472 | bytes 20971520 | tf_op jit(solution)/shard_map/mixer_backward/pallas_call | solution.py:331
  473.7 10.7 %convolution_convert_fusion.2 = bf16[2048,768]{1,0:T(8,128)(2,1)S(1)} fusion(bf16[2048,2048]{1,0:T(8,128)(2,1)} %bitcast.164, bf16[2048,768]{1,0:T(8,128)(2,1)} %bitcast.191), kind=kOutput, calls=%fused_computation.2 | convolution fusion | flops 6444023808 | bytes 14680064 | tf_op jit(solution)/shard_map/dot_general | solution.py:31
  488.6 9.1 %convolution_convert_fusion = bf16[2048,2048]{1,0:T(8,128)(2,1)} fusion(bf16[2048,768]{1,0:T(8,128)(2,1)S(1)} %bitcast.192, bf16[2048,768]{0,1:T(8,128)(2,1)S(1)} %bitcast.190), kind=kOutput, calls=%fused_computation | convolution fusion | flops 6446645248 | bytes 14680064 | tf_op jit(solution)/shard_map/dot_general | solution.py:35
  503.0 2.8 collective-permute-start.64
  506.0 3.1 collective-permute-start.62
  511.9 5.6 collective-permute-start.73
  517.6 3.0 collective-permute-start.71
  523.7 3.2 collective-permute-start.70
  532.4 3.1 collective-permute-start.68
  544.2 4.6 collective-permute-start.79
  549.6 6.4 pole_gradients.1
  556.0 3.4 collective-permute-start.77
  562.9 3.5 collective-permute-start.86
  571.8 4.7 collective-permute-done.78.right_ref
  583.2 4.5 collective-permute-done.86.right_ref.refs_0_
  602.5 3.6 collective-permute-start.83
  610.5 6.4 collective-permute-done.83.right_ref
  628.3 5.2 finish.7
  633.6 5.7 finish.6
  639.3 5.2 finish.5
  644.5 2.9 bitcast_convert_fusion.grad_ref
  647.4 4.2 token_grad.1
  654.6 5.9 finish.9
  (496 shorter events, 226.5 us)
Async XLA Ops:
  7.2 333.4 %reduce-scatter.4.cloned.1.call-start = ((), (), s32[]{:S(2)}) async-start(), calls=%async_computation.3 | async-start | bytes 9437184 | tf_op jit(solution)/shard_map/reduce_scatter | solution.py:542
  11.3 22.3 %collective-permute-start.2 = (bf16[2,128,2048]{2,1,0:T(8,128)(2,1)}, bf16[2,128,2048]{2,1,0:T(8,128)(2,1)}, u32[]{:S(2)}, u32[]{:S(2)}) collective-permute-start(bf16[2,128,2048]{2,1,0:T(8,128)(2,1)} %fusion.10.refs_0_), channel_id=1, source_target_pairs={{0,1},{1,0},{2,3},{3,2},{4,5},{5,4},{6,7},{7,6},{8,9},{9,8},{10,11... | collective-permute-start | bytes 3145736 | tf_op jit(solution)/shard_map/ppermute | solution.py:685
  11.3 28.1 %collective-permute-start = (bf16[2,128,2048]{2,1,0:T(8,128)(2,1)}, bf16[2,128,2048]{2,1,0:T(8,128)(2,1)S(1)}, u32[]{:S(2)}, u32[]{:S(2)}) collective-permute-start(bf16[2,128,2048]{2,1,0:T(8,128)(2,1)} %fusion.10.refs_0_), channel_id=1, source_target_pairs={{0,2},{1,3},{2,0},{3,1},{4,6},{5,7},{6,4},{7,5},{8,10},{9,11},{10,... | collective-permute-start | bytes 3145736 | tf_op jit(solution)/shard_map/ppermute | solution.py:685
  12.8 26.6 %collective-permute-start.1 = (bf16[2,128,2048]{2,1,0:T(8,128)(2,1)}, bf16[2,128,2048]{2,1,0:T(8,128)(2,1)}, u32[]{:S(2)}, u32[]{:S(2)}) collective-permute-start(bf16[2,128,2048]{2,1,0:T(8,128)(2,1)} %fusion.10.refs_0_), channel_id=1, source_target_pairs={{0,4},{1,5},{2,6},{3,7},{4,0},{5,1},{6,2},{7,3},{8,12},{9,13},{10,... | collective-permute-start | bytes 3145736 | tf_op jit(solution)/shard_map/ppermute | solution.py:685
  55.8 25.3 %collective-permute-start.7 = (bf16[2,128,2048]{2,1,0:T(8,128)(2,1)}, bf16[2,128,2048]{2,1,0:T(8,128)(2,1)S(1)}, u32[]{:S(2)}, u32[]{:S(2)}) collective-permute-start(bf16[2,128,2048]{2,1,0:T(8,128)(2,1)} %fusion.15.refs_0_), channel_id=1, source_target_pairs={{0,2},{1,3},{2,0},{3,1},{4,6},{5,7},{6,4},{7,5},{8,10},{9,11},{10,... | collective-permute-start | bytes 3145736 | tf_op jit(solution)/shard_map/ppermute | solution.py:685
  56.4 25.1 %collective-permute-start.8 = (bf16[2,128,2048]{2,1,0:T(8,128)(2,1)}, bf16[2,128,2048]{2,1,0:T(8,128)(2,1)}, u32[]{:S(2)}, u32[]{:S(2)}) collective-permute-start(bf16[2,128,2048]{2,1,0:T(8,128)(2,1)} %fusion.15.refs_0_), channel_id=1, source_target_pairs={{0,4},{1,5},{2,6},{3,7},{4,0},{5,1},{6,2},{7,3},{8,12},{9,13},{10,... | collective-permute-start | bytes 3145736 | tf_op jit(solution)/shard_map/ppermute | solution.py:685
  90.5 21.0 %collective-permute-start.21 = (bf16[1,128,2048]{2,1,0:T(8,128)(2,1)S(1)}, bf16[1,128,2048]{2,1,0:T(8,128)(2,1)S(1)}, u32[]{:S(2)}, u32[]{:S(2)}) collective-permute-start(bf16[1,128,2048]{2,1,0:T(8,128)(2,1)S(1)} %get-tuple-element.281), channel_id=1, source_target_pairs={{0,4},{1,5},{2,6},{3,7},{4,0},{5,1},{6,2},{7,3},{8,12},{9,13},{10,... | collective-permute-start | bytes 1572872 | tf_op jit(solution)/shard_map/ppermute | solution.py:685
  91.1 23.0 %collective-permute-start.18 = (bf16[1,128,2048]{2,1,0:T(8,128)(2,1)S(1)}, bf16[1,128,2048]{2,1,0:T(8,128)(2,1)S(1)}, u32[]{:S(2)}, u32[]{:S(2)}) collective-permute-start(bf16[1,128,2048]{2,1,0:T(8,128)(2,1)S(1)} %get-tuple-element.280), channel_id=1, source_target_pairs={{0,2},{1,3},{2,0},{3,1},{4,6},{5,7},{6,4},{7,5},{8,10},{9,11},{10,... | collective-permute-start | bytes 1572872 | tf_op jit(solution)/shard_map/ppermute | solution.py:685
  91.7 23.8 %collective-permute-start.12 = (bf16[2,128,2048]{2,1,0:T(8,128)(2,1)S(1)}, bf16[2,128,2048]{2,1,0:T(8,128)(2,1)S(1)}, u32[]{:S(2)}, u32[]{:S(2)}) collective-permute-start(bf16[2,128,2048]{2,1,0:T(8,128)(2,1)S(1)} %slice_bitcast_fusion.8), channel_id=1, source_target_pairs={{0,1},{1,0},{2,3},{3,2},{4,5},{5,4},{6,7},{7,6},{8,9},{9,8},{10,11... | collective-permute-start | bytes 3145736 | tf_op jit(solution)/shard_map/ppermute | solution.py:685
  101.1 38.4 %collective-permute-start.23 = (bf16[2,128,2048]{2,1,0:T(8,128)(2,1)}, bf16[2,128,2048]{2,1,0:T(8,128)(2,1)S(1)}, u32[]{:S(2)}, u32[]{:S(2)}) collective-permute-start(bf16[2,128,2048]{2,1,0:T(8,128)(2,1)} %fusion.15.refs_0_), channel_id=1, source_target_pairs={{0,1},{1,0},{2,3},{3,2},{4,5},{5,4},{6,7},{7,6},{8,9},{9,8},{10,11... | collective-permute-start | bytes 3145736 | tf_op jit(solution)/shard_map/ppermute | solution.py:685
  113.2 23.2 %collective-permute-start.17 = (bf16[1,128,2048]{2,1,0:T(8,128)(2,1)S(1)}, bf16[1,128,2048]{2,1,0:T(8,128)(2,1)S(1)}, u32[]{:S(2)}, u32[]{:S(2)}) collective-permute-start(bf16[1,128,2048]{2,1,0:T(8,128)(2,1)S(1)} %slice.292), channel_id=1, source_target_pairs={{0,2},{1,3},{2,0},{3,1},{4,6},{5,7},{6,4},{7,5},{8,10},{9,11},{10,... | collective-permute-start | bytes 1572872 | tf_op jit(solution)/shard_map/ppermute | solution.py:685
  114.2 22.2 %collective-permute-start.19 = (bf16[1,128,2048]{2,1,0:T(8,128)(2,1)S(1)}, bf16[1,128,2048]{2,1,0:T(8,128)(2,1)S(1)}, u32[]{:S(2)}, u32[]{:S(2)}) collective-permute-start(bf16[1,128,2048]{2,1,0:T(8,128)(2,1)S(1)} %add_convert_fusion.1), channel_id=1, source_target_pairs={{0,4},{1,5},{2,6},{3,7},{4,0},{5,1},{6,2},{7,3},{8,12},{9,13},{10,... | collective-permute-start | bytes 1572872 | tf_op jit(solution)/shard_map/ppermute | solution.py:685
  115.5 22.6 %collective-permute-start.20 = (bf16[1,128,2048]{2,1,0:T(8,128)(2,1)S(1)}, bf16[1,128,2048]{2,1,0:T(8,128)(2,1)S(1)}, u32[]{:S(2)}, u32[]{:S(2)}) collective-permute-start(bf16[1,128,2048]{2,1,0:T(8,128)(2,1)S(1)} %slice.291), channel_id=1, source_target_pairs={{0,4},{1,5},{2,6},{3,7},{4,0},{5,1},{6,2},{7,3},{8,12},{9,13},{10,... | collective-permute-start | bytes 1572872 | tf_op jit(solution)/shard_map/ppermute | solution.py:685
  140.7 25.6 %collective-permute-start.24 = (bf16[2,128,2048]{2,1,0:T(8,128)(2,1)S(1)}, bf16[2,128,2048]{2,1,0:T(8,128)(2,1)S(1)}, u32[]{:S(2)}, u32[]{:S(2)}) collective-permute-start(bf16[2,128,2048]{2,1,0:T(8,128)(2,1)S(1)} %multiply_convert_fusion.1.refs_0_), channel_id=1, source_target_pairs={{0,2},{1,3},{2,0},{3,1},{4,6},{5,7},{6,4},{7,5},{8,10},{9,11},{10,... | collective-permute-start | bytes 3145736 | tf_op jit(solution)/shard_map/ppermute | solution.py:685
  142.2 25.3 %collective-permute-start.25 = (bf16[2,128,2048]{2,1,0:T(8,128)(2,1)S(1)}, bf16[2,128,2048]{2,1,0:T(8,128)(2,1)S(1)}, u32[]{:S(2)}, u32[]{:S(2)}) collective-permute-start(bf16[2,128,2048]{2,1,0:T(8,128)(2,1)S(1)} %multiply_convert_fusion.1.refs_0_), channel_id=1, source_target_pairs={{0,4},{1,5},{2,6},{3,7},{4,0},{5,1},{6,2},{7,3},{8,12},{9,13},{10,... | collective-permute-start | bytes 3145736 | tf_op jit(solution)/shard_map/ppermute | solution.py:685
  150.1 19.8 %collective-permute-start.34 = (bf16[2,128,2048]{2,1,0:T(8,128)(2,1)S(1)}, bf16[2,128,2048]{2,1,0:T(8,128)(2,1)S(1)}, u32[]{:S(2)}, u32[]{:S(2)}) collective-permute-start(bf16[2,128,2048]{2,1,0:T(8,128)(2,1)S(1)} %multiply_convert_fusion.1.refs_0_), channel_id=1, source_target_pairs={{0,1},{1,0},{2,3},{3,2},{4,5},{5,4},{6,7},{7,6},{8,9},{9,8},{10,11... | collective-permute-start | bytes 3145736 | tf_op jit(solution)/shard_map/ppermute | solution.py:685
  168.1 25.6 %collective-permute-start.30 = (bf16[1,128,2048]{2,1,0:T(8,128)(2,1)S(1)}, bf16[1,128,2048]{2,1,0:T(8,128)(2,1)S(1)}, u32[]{:S(2)}, u32[]{:S(2)}) collective-permute-start(bf16[1,128,2048]{2,1,0:T(8,128)(2,1)S(1)} %slice.209), channel_id=1, source_target_pairs={{0,4},{1,5},{2,6},{3,7},{4,0},{5,1},{6,2},{7,3},{8,12},{9,13},{10,... | collective-permute-start | bytes 1572872 | tf_op jit(solution)/shard_map/ppermute | solution.py:685
  169.4 24.3 %collective-permute-start.31 = (bf16[1,128,2048]{2,1,0:T(8,128)(2,1)S(1)}, bf16[1,128,2048]{2,1,0:T(8,128)(2,1)S(1)}, u32[]{:S(2)}, u32[]{:S(2)}) collective-permute-start(bf16[1,128,2048]{2,1,0:T(8,128)(2,1)S(1)} %slice.210), channel_id=1, source_target_pairs={{0,2},{1,3},{2,0},{3,1},{4,6},{5,7},{6,4},{7,5},{8,10},{9,11},{10,... | collective-permute-start | bytes 1572872 | tf_op jit(solution)/shard_map/ppermute | solution.py:685
  212.3 20.9 %collective-permute-start.37 = (bf16[176,2048]{1,0:T(8,128)(2,1)S(1)}, bf16[176,2048]{1,0:T(8,128)(2,1)S(1)}, u32[]{:S(2)}, u32[]{:S(2)}) collective-permute-start(bf16[176,2048]{1,0:T(8,128)(2,1)S(1)} %get-tuple-element.562.left_ref), channel_id=1, source_target_pairs={{0,8},{24,16},{1,9},{25,17},{2,10},{26,18},{3,11},{27,19},{4,12},{... | collective-permute-start | bytes 2162696 | tf_op jit(solution)/shard_map/ppermute | solution.py:730
  213.6 38.4 %collective-permute-start.40 = (bf16[176,2048]{1,0:T(8,128)(2,1)S(1)}, bf16[176,2048]{1,0:T(8,128)(2,1)S(1)}, u32[]{:S(2)}, u32[]{:S(2)}) collective-permute-start(bf16[176,2048]{1,0:T(8,128)(2,1)S(1)} %get-tuple-element.561.left_ref), channel_id=1, source_target_pairs={{0,8},{24,16},{1,9},{25,17},{2,10},{26,18},{3,11},{27,19},{4,12},{... | collective-permute-start | bytes 2162696 | tf_op jit(solution)/shard_map/ppermute | solution.py:730
  252.9 148.7 %all-gather.3.cloned.1.call-start = ((), (), s32[]{:S(2)}) async-start(), calls=%async_computation.6 | async-start | bytes 9437184 | tf_op jit(solution)/shard_map/all_gather | solution.py:538
  255.1 21.3 %collective-permute-start.38 = (bf16[176,2048]{1,0:T(8,128)(2,1)}, bf16[176,2048]{1,0:T(8,128)(2,1)}, u32[]{:S(2)}, u32[]{:S(2)}) collective-permute-start(bf16[176,2048]{1,0:T(8,128)(2,1)} %add.182.left_ref), channel_id=1, source_target_pairs={{8,16},{16,8},{9,17},{17,9},{10,18},{18,10},{11,19},{19,11},{12,20... | collective-permute-start | bytes 2162696 | tf_op jit(solution)/shard_map/ppermute | solution.py:735
  259.5 21.3 %collective-permute-start.39 = (bf16[176,2048]{1,0:T(8,128)(2,1)}, bf16[176,2048]{1,0:T(8,128)(2,1)}, u32[]{:S(2)}, u32[]{:S(2)}) collective-permute-start(bf16[176,2048]{1,0:T(8,128)(2,1)} %get-tuple-element.560.left_ref), channel_id=1, source_target_pairs={{0,8},{24,16},{1,9},{25,17},{2,10},{26,18},{3,11},{27,19},{4,12},{... | collective-permute-start | bytes 2162696 | tf_op jit(solution)/shard_map/ppermute | solution.py:730
  263.4 30.0 %collective-permute-start.43 = (bf16[176,2048]{1,0:T(8,128)(2,1)S(1)}, bf16[176,2048]{1,0:T(8,128)(2,1)S(1)}, u32[]{:S(2)}, u32[]{:S(2)}) collective-permute-start(bf16[176,2048]{1,0:T(8,128)(2,1)S(1)} %add.184.left_ref), channel_id=1, source_target_pairs={{8,16},{16,8},{9,17},{17,9},{10,18},{18,10},{11,19},{19,11},{12,20... | collective-permute-start | bytes 2162696 | tf_op jit(solution)/shard_map/ppermute | solution.py:735
  265.8 30.3 %collective-permute-start.44 = (bf16[176,2048]{1,0:T(8,128)(2,1)S(1)}, bf16[176,2048]{1,0:T(8,128)(2,1)S(1)}, u32[]{:S(2)}, u32[]{:S(2)}) collective-permute-start(bf16[176,2048]{1,0:T(8,128)(2,1)S(1)} %get-tuple-element.559.left_ref), channel_id=1, source_target_pairs={{0,8},{24,16},{1,9},{25,17},{2,10},{26,18},{3,11},{27,19},{4,12},{... | collective-permute-start | bytes 2162696 | tf_op jit(solution)/shard_map/ppermute | solution.py:730
  282.6 29.0 %collective-permute-start.42 = (bf16[176,2048]{1,0:T(8,128)(2,1)S(1)}, bf16[176,2048]{1,0:T(8,128)(2,1)S(1)}, u32[]{:S(2)}, u32[]{:S(2)}) collective-permute-start(bf16[176,2048]{1,0:T(8,128)(2,1)S(1)} %merge.10.refs_1_), channel_id=1, source_target_pairs={{0,8},{24,16},{8,0},{16,24},{1,9},{25,17},{9,1},{17,25},{2,10},{26... | collective-permute-start | bytes 2162696 | tf_op jit(solution)/shard_map/ppermute | solution.py:727
  284.3 27.3 %collective-permute-start.41 = (bf16[176,2048]{1,0:T(8,128)(2,1)S(1)}, bf16[176,2048]{1,0:T(8,128)(2,1)}, u32[]{:S(2)}, u32[]{:S(2)}) collective-permute-start(bf16[176,2048]{1,0:T(8,128)(2,1)S(1)} %add.183.left_ref), channel_id=1, source_target_pairs={{8,16},{16,8},{9,17},{17,9},{10,18},{18,10},{11,19},{19,11},{12,20... | collective-permute-start | bytes 2162696 | tf_op jit(solution)/shard_map/ppermute | solution.py:735
  298.0 29.0 %collective-permute-start.48 = (bf16[176,2048]{1,0:T(8,128)(2,1)S(1)}, bf16[176,2048]{1,0:T(8,128)(2,1)S(1)}, u32[]{:S(2)}, u32[]{:S(2)}) collective-permute-start(bf16[176,2048]{1,0:T(8,128)(2,1)S(1)} %merge.12.refs_3_), channel_id=1, source_target_pairs={{0,8},{24,16},{8,0},{16,24},{1,9},{25,17},{9,1},{17,25},{2,10},{26... | collective-permute-start | bytes 2162696 | tf_op jit(solution)/shard_map/ppermute | solution.py:727
  299.6 27.5 %collective-permute-start.47 = (bf16[176,2048]{1,0:T(8,128)(2,1)S(1)}, bf16[176,2048]{1,0:T(8,128)(2,1)}, u32[]{:S(2)}, u32[]{:S(2)}) collective-permute-start(bf16[176,2048]{1,0:T(8,128)(2,1)S(1)} %add.186.left_ref), channel_id=1, source_target_pairs={{8,16},{16,8},{9,17},{17,9},{10,18},{18,10},{11,19},{19,11},{12,20... | collective-permute-start | bytes 2162696 | tf_op jit(solution)/shard_map/ppermute | solution.py:735
  313.5 26.3 %collective-permute-start.46 = (bf16[176,2048]{1,0:T(8,128)(2,1)S(1)}, bf16[176,2048]{1,0:T(8,128)(2,1)S(1)}, u32[]{:S(2)}, u32[]{:S(2)}) collective-permute-start(bf16[176,2048]{1,0:T(8,128)(2,1)S(1)} %merge.11.refs_5_), channel_id=1, source_target_pairs={{0,8},{24,16},{8,0},{16,24},{1,9},{25,17},{9,1},{17,25},{2,10},{26... | collective-permute-start | bytes 2162696 | tf_op jit(solution)/shard_map/ppermute | solution.py:727
  315.0 25.6 %collective-permute-start.45 = (bf16[176,2048]{1,0:T(8,128)(2,1)S(1)}, bf16[176,2048]{1,0:T(8,128)(2,1)}, u32[]{:S(2)}, u32[]{:S(2)}) collective-permute-start(bf16[176,2048]{1,0:T(8,128)(2,1)S(1)} %add.185.left_ref), channel_id=1, source_target_pairs={{8,16},{16,8},{9,17},{17,9},{10,18},{18,10},{11,19},{19,11},{12,20... | collective-permute-start | bytes 2162696 | tf_op jit(solution)/shard_map/ppermute | solution.py:735
  347.2 258.9 %reduce-scatter.6.cloned.1.call-start = ((), (), s32[]{:S(2)}) async-start(), calls=%async_computation.4 | async-start | bytes 9437184 | tf_op jit(solution)/shard_map/reduce_scatter | solution.py:542
  349.0 25.1 %collective-permute-start.52 = (bf16[176,2048]{1,0:T(8,128)(2,1)S(1)}, bf16[176,2048]{1,0:T(8,128)(2,1)S(1)}, u32[]{:S(2)}, u32[]{:S(2)}) collective-permute-start(bf16[176,2048]{1,0:T(8,128)(2,1)S(1)} %merge.14.refs_7_), channel_id=1, source_target_pairs={{0,8},{24,16},{8,0},{16,24},{1,9},{25,17},{9,1},{17,25},{2,10},{26... | collective-permute-start | bytes 2162696 | tf_op jit(solution)/shard_map/ppermute | solution.py:727
  350.5 23.5 %collective-permute-start.51 = (bf16[176,2048]{1,0:T(8,128)(2,1)S(1)}, bf16[176,2048]{1,0:T(8,128)(2,1)S(1)}, u32[]{:S(2)}, u32[]{:S(2)}) collective-permute-start(bf16[176,2048]{1,0:T(8,128)(2,1)S(1)} %add.188.left_ref), channel_id=1, source_target_pairs={{8,16},{16,8},{9,17},{17,9},{10,18},{18,10},{11,19},{19,11},{12,20... | collective-permute-start | bytes 2162696 | tf_op jit(solution)/shard_map/ppermute | solution.py:735
  356.5 26.4 %collective-permute-start.50 = (bf16[176,2048]{1,0:T(8,128)(2,1)}, bf16[176,2048]{1,0:T(8,128)(2,1)}, u32[]{:S(2)}, u32[]{:S(2)}) collective-permute-start(bf16[176,2048]{1,0:T(8,128)(2,1)} %merge.13.refs_1_), channel_id=1, source_target_pairs={{0,8},{24,16},{8,0},{16,24},{1,9},{25,17},{9,1},{17,25},{2,10},{26... | collective-permute-start | bytes 2162696 | tf_op jit(solution)/shard_map/ppermute | solution.py:727
  358.9 27.1 %collective-permute-start.49 = (bf16[176,2048]{1,0:T(8,128)(2,1)}, bf16[176,2048]{1,0:T(8,128)(2,1)S(1)}, u32[]{:S(2)}, u32[]{:S(2)}) collective-permute-start(bf16[176,2048]{1,0:T(8,128)(2,1)} %add.187.left_ref), channel_id=1, source_target_pairs={{8,16},{16,8},{9,17},{17,9},{10,18},{18,10},{11,19},{19,11},{12,20... | collective-permute-start | bytes 2162696 | tf_op jit(solution)/shard_map/ppermute | solution.py:735
  377.5 20.7 %collective-permute-start.56 = (bf16[176,2048]{1,0:T(8,128)(2,1)S(1)}, bf16[176,2048]{1,0:T(8,128)(2,1)S(1)}, u32[]{:S(2)}, u32[]{:S(2)}) collective-permute-start(bf16[176,2048]{1,0:T(8,128)(2,1)S(1)} %merge.16.refs_3_), channel_id=1, source_target_pairs={{0,8},{24,16},{8,0},{16,24},{1,9},{25,17},{9,1},{17,25},{2,10},{26... | collective-permute-start | bytes 2162696 | tf_op jit(solution)/shard_map/ppermute | solution.py:727
  379.1 22.5 %collective-permute-start.55 = (bf16[176,2048]{1,0:T(8,128)(2,1)S(1)}, bf16[176,2048]{1,0:T(8,128)(2,1)}, u32[]{:S(2)}, u32[]{:S(2)}) collective-permute-start(bf16[176,2048]{1,0:T(8,128)(2,1)S(1)} %add.190.left_ref), channel_id=1, source_target_pairs={{8,16},{16,8},{9,17},{17,9},{10,18},{18,10},{11,19},{19,11},{12,20... | collective-permute-start | bytes 2162696 | tf_op jit(solution)/shard_map/ppermute | solution.py:735
  389.5 24.7 %collective-permute-start.54 = (bf16[176,2048]{1,0:T(8,128)(2,1)}, bf16[176,2048]{1,0:T(8,128)(2,1)}, u32[]{:S(2)}, u32[]{:S(2)}) collective-permute-start(bf16[176,2048]{1,0:T(8,128)(2,1)} %merge.15.refs_5_), channel_id=1, source_target_pairs={{0,8},{24,16},{8,0},{16,24},{1,9},{25,17},{9,1},{17,25},{2,10},{26... | collective-permute-start | bytes 2162696 | tf_op jit(solution)/shard_map/ppermute | solution.py:727
  391.7 22.6 %collective-permute-start.53 = (bf16[176,2048]{1,0:T(8,128)(2,1)}, bf16[176,2048]{1,0:T(8,128)(2,1)}, u32[]{:S(2)}, u32[]{:S(2)}) collective-permute-start(bf16[176,2048]{1,0:T(8,128)(2,1)} %add.189.left_ref), channel_id=1, source_target_pairs={{8,16},{16,8},{9,17},{17,9},{10,18},{18,10},{11,19},{19,11},{12,20... | collective-permute-start | bytes 2162696 | tf_op jit(solution)/shard_map/ppermute | solution.py:735
  414.3 230.2 %reduce-scatter.8.cloned.1.call-start = ((), (), s32[]{:S(2)}) async-start(), calls=%async_computation.5 | async-start | bytes 9437184 | tf_op jit(solution)/shard_map/reduce_scatter | solution.py:542
  416.3 24.7 %collective-permute-start.61 = (bf16[176,2048]{1,0:T(8,128)(2,1)S(1)}, bf16[176,2048]{1,0:T(8,128)(2,1)S(1)}, u32[]{:S(2)}, u32[]{:S(2)}) collective-permute-start(bf16[176,2048]{1,0:T(8,128)(2,1)S(1)} %merge.17.refs_7_), channel_id=1, source_target_pairs={{0,8},{24,16},{8,0},{16,24},{1,9},{25,17},{9,1},{17,25},{2,10},{26... | collective-permute-start | bytes 2162696 | tf_op jit(solution)/shard_map/ppermute | solution.py:727
  417.9 23.2 %collective-permute-start.60 = (bf16[176,2048]{1,0:T(8,128)(2,1)S(1)}, bf16[176,2048]{1,0:T(8,128)(2,1)S(1)}, u32[]{:S(2)}, u32[]{:S(2)}) collective-permute-start(bf16[176,2048]{1,0:T(8,128)(2,1)S(1)} %add.193.left_ref), channel_id=1, source_target_pairs={{8,16},{16,8},{9,17},{17,9},{10,18},{18,10},{11,19},{19,11},{12,20... | collective-permute-start | bytes 2162696 | tf_op jit(solution)/shard_map/ppermute | solution.py:735
  441.1 46.9 %collective-permute-start.59 = (bf16[176,2048]{1,0:T(8,128)(2,1)S(1)}, bf16[176,2048]{1,0:T(8,128)(2,1)S(1)}, u32[]{:S(2)}, u32[]{:S(2)}) collective-permute-start(bf16[176,2048]{1,0:T(8,128)(2,1)S(1)} %add.192.refs_1_), channel_id=1, source_target_pairs={{8,0},{16,24},{9,1},{17,25},{10,2},{18,26},{11,3},{19,27},{12,4},{... | collective-permute-start | bytes 2162696 | tf_op jit(solution)/shard_map/ppermute | solution.py:733
  442.9 43.3 %collective-permute-start.58 = (bf16[128,2048]{1,0:T(8,128)(2,1)S(1)}, bf16[128,2048]{1,0:T(8,128)(2,1)S(1)}, u32[]{:S(2)}, u32[]{:S(2)}) collective-permute-start(bf16[128,2048]{1,0:T(8,128)(2,1)S(1)} %get-tuple-element.570.left_ref), channel_id=1, source_target_pairs={{0,8},{24,16},{1,9},{25,17},{2,10},{26,18},{3,11},{27,19},{4,12},{... | collective-permute-start | bytes 1572872 | tf_op jit(solution)/shard_map/ppermute | solution.py:730
  445.6 42.4 %collective-permute-start.57 = (bf16[176,2048]{1,0:T(8,128)(2,1)S(1)}, bf16[176,2048]{1,0:T(8,128)(2,1)S(1)}, u32[]{:S(2)}, u32[]{:S(2)}) collective-permute-start(bf16[176,2048]{1,0:T(8,128)(2,1)S(1)} %add.191.left_ref), channel_id=1, source_target_pairs={{8,16},{16,8},{9,17},{17,9},{10,18},{18,10},{11,19},{19,11},{12,20... | collective-permute-start | bytes 2162696 | tf_op jit(solution)/shard_map/ppermute | solution.py:735
  450.1 50.6 %collective-permute-start.67 = (bf16[176,2048]{1,0:T(8,128)(2,1)S(1)}, bf16[176,2048]{1,0:T(8,128)(2,1)}, u32[]{:S(2)}, u32[]{:S(2)}) collective-permute-start(bf16[176,2048]{1,0:T(8,128)(2,1)S(1)} %add.197.refs_3_), channel_id=1, source_target_pairs={{8,0},{16,24},{9,1},{17,25},{10,2},{18,26},{11,3},{19,27},{12,4},{... | collective-permute-start | bytes 2162696 | tf_op jit(solution)/shard_map/ppermute | solution.py:733
  454.3 46.4 %collective-permute-start.65 = (bf16[176,2048]{1,0:T(8,128)(2,1)S(1)}, bf16[176,2048]{1,0:T(8,128)(2,1)S(1)}, u32[]{:S(2)}, u32[]{:S(2)}) collective-permute-start(bf16[176,2048]{1,0:T(8,128)(2,1)S(1)} %add.196.left_ref), channel_id=1, source_target_pairs={{8,16},{16,8},{9,17},{17,9},{10,18},{18,10},{11,19},{19,11},{12,20... | collective-permute-start | bytes 2162696 | tf_op jit(solution)/shard_map/ppermute | solution.py:735
  503.0 20.5 %collective-permute-start.64 = (bf16[176,2048]{1,0:T(8,128)(2,1)S(1)}, bf16[176,2048]{1,0:T(8,128)(2,1)}, u32[]{:S(2)}, u32[]{:S(2)}) collective-permute-start(bf16[176,2048]{1,0:T(8,128)(2,1)S(1)} %add.195.refs_5_), channel_id=1, source_target_pairs={{8,0},{16,24},{9,1},{17,25},{10,2},{18,26},{11,3},{19,27},{12,4},{... | collective-permute-start | bytes 2162696 | tf_op jit(solution)/shard_map/ppermute | solution.py:733
  511.9 25.5 %collective-permute-start.73 = (bf16[176,2048]{1,0:T(8,128)(2,1)S(1)}, bf16[176,2048]{1,0:T(8,128)(2,1)}, u32[]{:S(2)}, u32[]{:S(2)}) collective-permute-start(bf16[176,2048]{1,0:T(8,128)(2,1)S(1)} %add.201.refs_7_), channel_id=1, source_target_pairs={{8,0},{16,24},{9,1},{17,25},{10,2},{18,26},{11,3},{19,27},{12,4},{... | collective-permute-start | bytes 2162696 | tf_op jit(solution)/shard_map/ppermute | solution.py:733
  520.6 16.8 %collective-permute-start.72 = (bf16[1024,256]{1,0:T(8,128)(2,1)S(1)}, bf16[1024,256]{1,0:T(8,128)(2,1)S(1)}, u32[]{:S(2)}, u32[]{:S(2)}) collective-permute-start(bf16[1024,256]{1,0:T(8,128)(2,1)S(1)} %get-tuple-element.567.left_ref), channel_id=1, source_target_pairs={{0,8},{24,16},{1,9},{25,17},{2,10},{26,18},{3,11},{27,19},{4,12},{... | collective-permute-start | bytes 1572872 | tf_op jit(solution)/shard_map/ppermute | solution.py:730
  523.7 35.8 %collective-permute-start.70 = (bf16[128,2048]{1,0:T(8,128)(2,1)S(1)}, bf16[128,2048]{1,0:T(8,128)(2,1)S(1)}, u32[]{:S(2)}, u32[]{:S(2)}) collective-permute-start(bf16[128,2048]{1,0:T(8,128)(2,1)S(1)} %add.199.refs_1_), channel_id=1, source_target_pairs={{8,0},{16,24},{9,1},{17,25},{10,2},{18,26},{11,3},{19,27},{12,4},{... | collective-permute-start | bytes 1572872 | tf_op jit(solution)/shard_map/ppermute | solution.py:733
  528.9 31.8 %collective-permute-start.69 = (bf16[1024,256]{1,0:T(8,128)(2,1)S(1)}, bf16[1024,256]{1,0:T(8,128)(2,1)S(1)}, u32[]{:S(2)}, u32[]{:S(2)}) collective-permute-start(bf16[1024,256]{1,0:T(8,128)(2,1)S(1)} %get-tuple-element.566.left_ref), channel_id=1, source_target_pairs={{0,8},{24,16},{1,9},{25,17},{2,10},{26,18},{3,11},{27,19},{4,12},{... | collective-permute-start | bytes 1572872 | tf_op jit(solution)/shard_map/ppermute | solution.py:730
  532.4 28.4 %collective-permute-start.68 = (bf16[1024,256]{1,0:T(8,128)(2,1)S(1)}, bf16[1024,256]{1,0:T(8,128)(2,1)S(1)}, u32[]{:S(2)}, u32[]{:S(2)}) collective-permute-start(bf16[1024,256]{1,0:T(8,128)(2,1)S(1)} %add.198.left_ref), channel_id=1, source_target_pairs={{8,16},{16,8},{9,17},{17,9},{10,18},{18,10},{11,19},{19,11},{12,20... | collective-permute-start | bytes 1572872 | tf_op jit(solution)/shard_map/ppermute | solution.py:735
  544.2 25.5 %collective-permute-start.79 = (bf16[128,2048]{1,0:T(8,128)(2,1)S(1)}, bf16[128,2048]{1,0:T(8,128)(2,1)}, u32[]{:S(2)}, u32[]{:S(2)}) collective-permute-start(bf16[128,2048]{1,0:T(8,128)(2,1)S(1)} %add.203.refs_3_), channel_id=1, source_target_pairs={{8,0},{16,24},{9,1},{17,25},{10,2},{18,26},{11,3},{19,27},{12,4},{... | collective-permute-start | bytes 1572872 | tf_op jit(solution)/shard_map/ppermute | solution.py:733
  559.5 17.1 %collective-permute-start.78 = (bf16[1024,256]{1,0:T(8,128)(2,1)}, bf16[1024,256]{1,0:T(8,128)(2,1)}, u32[]{:S(2)}, u32[]{:S(2)}) collective-permute-start(bf16[1024,256]{1,0:T(8,128)(2,1)} %get-tuple-element.565.left_ref), channel_id=1, source_target_pairs={{0,8},{24,16},{1,9},{25,17},{2,10},{26,18},{3,11},{27,19},{4,12},{... | collective-permute-start | bytes 1572872 | tf_op jit(solution)/shard_map/ppermute | solution.py:730
  562.9 24.8 %collective-permute-start.86 = (bf16[1024,256]{1,0:T(8,128)(2,1)S(1)}, bf16[1024,256]{1,0:T(8,128)(2,1)S(1)}, u32[]{:S(2)}, u32[]{:S(2)}) collective-permute-start(bf16[1024,256]{1,0:T(8,128)(2,1)S(1)} %merge.19.refs_1_), channel_id=1, source_target_pairs={{0,8},{24,16},{8,0},{16,24},{1,9},{25,17},{9,1},{17,25},{2,10},{26... | collective-permute-start | bytes 1572872 | tf_op jit(solution)/shard_map/ppermute | solution.py:727
  567.2 20.5 %collective-permute-start.85 = (bf16[1024,256]{1,0:T(8,128)(2,1)}, bf16[1024,256]{1,0:T(8,128)(2,1)}, u32[]{:S(2)}, u32[]{:S(2)}) collective-permute-start(bf16[1024,256]{1,0:T(8,128)(2,1)} %add.207.left_ref), channel_id=1, source_target_pairs={{8,16},{16,8},{9,17},{17,9},{10,18},{18,10},{11,19},{19,11},{12,20... | collective-permute-start | bytes 1572872 | tf_op jit(solution)/shard_map/ppermute | solution.py:735
  577.9 19.6 %collective-permute-start.81 = (bf16[1024,256]{1,0:T(8,128)(2,1)S(1)}, bf16[1024,256]{1,0:T(8,128)(2,1)S(1)}, u32[]{:S(2)}, u32[]{:S(2)}) collective-permute-start(bf16[1024,256]{1,0:T(8,128)(2,1)S(1)} %merge.18.refs_3_), channel_id=1, source_target_pairs={{0,8},{24,16},{8,0},{16,24},{1,9},{25,17},{9,1},{17,25},{2,10},{26... | collective-permute-start | bytes 1572872 | tf_op jit(solution)/shard_map/ppermute | solution.py:727
  579.4 18.1 %collective-permute-start.80 = (bf16[1024,256]{1,0:T(8,128)(2,1)S(1)}, bf16[1024,256]{1,0:T(8,128)(2,1)S(1)}, u32[]{:S(2)}, u32[]{:S(2)}) collective-permute-start(bf16[1024,256]{1,0:T(8,128)(2,1)S(1)} %add.204.left_ref), channel_id=1, source_target_pairs={{8,16},{16,8},{9,17},{17,9},{10,18},{18,10},{11,19},{19,11},{12,20... | collective-permute-start | bytes 1572872 | tf_op jit(solution)/shard_map/ppermute | solution.py:735
  589.6 18.1 %collective-permute-start.88 = (bf16[1024,256]{1,0:T(8,128)(2,1)}, bf16[1024,256]{1,0:T(8,128)(2,1)}, u32[]{:S(2)}, u32[]{:S(2)}) collective-permute-start(bf16[1024,256]{1,0:T(8,128)(2,1)} %add.209.refs_5_), channel_id=1, source_target_pairs={{8,0},{16,24},{9,1},{17,25},{10,2},{18,26},{11,3},{19,27},{12,4},{... | collective-permute-start | bytes 1572872 | tf_op jit(solution)/shard_map/ppermute | solution.py:733
  618.1 26.4 %collective-permute-start.91 = (bf16[1024,256]{1,0:T(8,128)(2,1)S(1)}, bf16[1024,256]{1,0:T(8,128)(2,1)}, u32[]{:S(2)}, u32[]{:S(2)}) collective-permute-start(bf16[1024,256]{1,0:T(8,128)(2,1)S(1)} %add.213.refs_11_), channel_id=1, source_target_pairs={{8,0},{16,24},{9,1},{17,25},{10,2},{18,26},{11,3},{19,27},{12,4},{... | collective-permute-start | bytes 1572872 | tf_op jit(solution)/shard_map/ppermute | solution.py:733
  620.2 24.3 %collective-permute-start.92 = (bf16[96,256]{1,0:T(8,128)(2,1)S(1)}, bf16[96,256]{1,0:T(8,128)(2,1)S(1)}, u32[]{:S(2)}, u32[]{:S(2)}) collective-permute-start(bf16[96,256]{1,0:T(8,128)(2,1)S(1)} %add.212), channel_id=1, source_target_pairs={{8,0},{16,24},{9,1},{17,25},{10,2},{18,26},{11,3},{19,27},{12,4},{... | collective-permute-start | bytes 147464 | tf_op jit(solution)/shard_map/ppermute | solution.py:815
  623.5 28.1 %collective-permute-start.90 = (bf16[1024,256]{1,0:T(8,128)(2,1)}, bf16[1024,256]{1,0:T(8,128)(2,1)}, u32[]{:S(2)}, u32[]{:S(2)}) collective-permute-start(bf16[1024,256]{1,0:T(8,128)(2,1)} %add.211.refs_9_), channel_id=1, source_target_pairs={{8,0},{16,24},{9,1},{17,25},{10,2},{18,26},{11,3},{19,27},{12,4},{... | collective-permute-start | bytes 1572872 | tf_op jit(solution)/shard_map/ppermute | solution.py:733
  (137 other events, 1083.3 us)
Sparse Core Ops, SparseCore 0:
  253.0 70.9 reduce-scatter.3
  347.3 52.6 all-gather.2
  414.4 69.7 reduce-scatter.5
  501.7 70.9 reduce-scatter.7

commit v5 on v4

--- a/solution.py
+++ b/solution.py
@@ -14,6 +14,7 @@
 f32 = jnp.float32
 STEP = 32
 VMEM_LIMIT = 52 * 1024 * 1024
+SMALL_LIMIT = 30 * 1024 * 1024
 
 
 def dft_matrix(length):
@@ -234,8 +235,8 @@
     return pl.CostEstimate(flops=flops, bytes_accessed=nbytes, transcendentals=0)
 
 
-def params():
-    return pltpu.CompilerParams(vmem_limit_bytes=VMEM_LIMIT)
+def params(limit=VMEM_LIMIT):
+    return pltpu.CompilerParams(vmem_limit_bytes=limit)
 
 
 def make_filter(tables, residue_t, dft):
@@ -452,7 +453,7 @@
         ),
         out_shape=[out_type(*output) for output in outputs],
         input_output_aliases={first + i: i for i in range(len(filled))},
-        compiler_params=params(),
+        compiler_params=params(VMEM_LIMIT if kernel is project_kernel else SMALL_LIMIT),
         cost_estimate=cost(len(group) * rows * work, sum(op.size * 2 for op in fixed)),
         name=kernel.__name__.removesuffix("_kernel"),
     )(*operands)
@@ -481,7 +482,7 @@
             in_specs=[left_spec] * len(lefts) + [whole(right.shape) for right in rights],
             out_specs=pl.BlockSpec((1, rows, width), lambda i: (i, 0, 0)),
             out_shape=jax.ShapeDtypeStruct((blocks, rows, width), dtype),
-            compiler_params=params(),
+            compiler_params=params(SMALL_LIMIT),
             cost_estimate=cost(sum(2 * left.size * width for left in lefts), 2 * blocks * rows * width),
             name="sum_products",
         )(*lefts, *rights)
@@ -505,7 +506,7 @@
         in_specs=[part, part, part, whole((1, width))],
         out_specs=pl.BlockSpec((1, rows, 1, width), lambda i: (i, 0, 0, 0)),
         out_shape=jax.ShapeDtypeStruct((seqs, rows, 1, width), f32),
-        compiler_params=params(),
+        compiler_params=params(SMALL_LIMIT),
         cost_estimate=cost(1000, 1000),
         name="token_grad",
     )(grad_normed, rows_in, grad_second, gain.reshape(1, width))
@@ -528,7 +529,7 @@
         ],
         out_specs=pl.BlockSpec((height, tile), lambda j: (0, j)),
         out_shape=jax.ShapeDtypeStruct((height, width), bf16),
-        compiler_params=params(),
+        compiler_params=params(SMALL_LIMIT),
         cost_estimate=cost(2 * height * depth * width, 2 * depth * width),
         name="weight_gradient",
     )(left, right)
@@ -565,7 +566,7 @@
             out_specs=pl.BlockSpec((height, width), lambda i, e: (i, 0)),
         ),
         out_shape=jax.ShapeDtypeStruct((height * len(pairs), width), f32),
-        compiler_params=params(),
+        compiler_params=params(SMALL_LIMIT),
         cost_estimate=cost(1000, 1000),
         name="finish",
     )(end, *operands)
@@ -585,7 +586,7 @@
         in_specs=[piece, piece],
         out_specs=piece,
         out_shape=jax.ShapeDtypeStruct(left.shape, bf16),
-        compiler_params=params(),
+        compiler_params=params(SMALL_LIMIT),
         cost_estimate=cost(1000, 1000),
         name="add",
     )(left, right)
@@ -604,7 +605,7 @@
             num_scalar_prefetch=1, grid=(1,), in_specs=[piece] * 3, out_specs=piece
         ),
         out_shape=jax.ShapeDtypeStruct(left.shape, bf16),
-        compiler_params=params(),
+        compiler_params=params(SMALL_LIMIT),
         cost_estimate=cost(1000, 1000),
         name="merge",
     )(end, part, left, right)
@@ -651,8 +652,8 @@
     def gather(self, block):
         return WholeGather(block)
 
-    def scatter(self, array, product, coming):
-        return scatter_whole(product(array))
+    def scatter(self, array, product, coming, compute):
+        return scatter_whole(product(array)), compute()
 
     def sum_mp(self, part):
         return lax.psum(part, "mp")
@@ -749,7 +750,7 @@
     def gather(self, block):
         return SquareGather(block)
 
-    def scatter(self, array, product, coming):
+    def scatter(self, array, product, coming, compute):
         def both(mine, other):
             return mine.astype(f32) + swap(other, 1).astype(f32)
 
@@ -761,17 +762,21 @@
         from_far_low, from_far_high = swap(far_low, 2), swap(far_high, 4)
         x_sum = both(side[0], side[1])
         y_sum = both(side[2], side[3])
-        x_sum, y_sum = coming.tie(["far"], x_sum, y_sum)
+        own = both(near[0], near[1])
+        own, x_sum, y_sum = coming.tie(["near", "side"], own, x_sum, y_sum)
         own_low_x = swap(x_sum[:half].astype(bf16), 2)
         own_high_y = swap(y_sum[half:].astype(bf16), 4)
-        own = both(near[0], near[1])
+        beside = compute()
+        from_far_low, from_far_high, own_low_x, own_high_y, beside = together(
+            from_far_low, from_far_high, own_low_x, own_high_y, beside
+        )
         y_low = (y_sum[:half] + from_far_low.astype(f32)).astype(bf16)
         x_high = (x_sum[half:] + from_far_high.astype(f32)).astype(bf16)
         own_low_y = swap(y_low, 4)
         own_high_x = swap(x_high, 2)
         low = own[:half] + own_low_x.astype(f32) + own_low_y.astype(f32)
         high = own[half:] + own_high_y.astype(f32) + own_high_x.astype(f32)
-        return jnp.concatenate([low, high], axis=0)
+        return jnp.concatenate([low, high], axis=0), beside
 
     def sum_mp(self, part):
         for bit in (1, 2, 4):
@@ -901,22 +906,22 @@
     def hidden_backed(group, number, filled):
         return arrive(hidden_back_kernel, group, number, (down_proj,), (), ((hidden_units, f32, True), (width, bf16, False)), filled)
 
-    second = rows_in + links.scatter(gated, mixed_out, grad_coming)
+    def beside_scatter():
+        return hidden_backed(grad_coming.side(), 1, hidden_backed(grad_coming.near(), 0, ()))
+
+    mixed_sum, filled = links.scatter(gated, mixed_out, grad_coming, beside_scatter)
+    second = rows_in + mixed_sum
     scale_second = row_scale(second)
     mlp_normed = (second * scale_second * mlp_gain).astype(bf16)
-    mlp_normed, grad_coming.here = together(mlp_normed, grad_coming.here)
     coming = links.gather(mlp_normed)
-    filled = hidden_backed(grad_coming.near(), 0, ())
-    filled = hidden_backed(grad_coming.side(), 1, filled)
     grad_hidden, grad_final_all = hidden_backed(grad_coming.far(), 2, filled)
-    (grad_hidden,) = coming.tie(["side"], grad_hidden)
 
     def fed(group, number, filled):
         outputs = ((hidden_units, bf16, True),) * 3 + ((width, bf16, False),)
         return arrive(feed_kernel, group, number, (gate_t, up_t), (grad_hidden,), outputs, filled)
 
+    (filled,) = coming.tie(["side"], fed(coming.near(), 0, ()))
     coming.reach()
-    filled = fed(coming.near(), 0, ())
     filled = fed(coming.side(), 1, filled)
     (filled,) = coming.tie(["far"], filled)
     hidden, grad_gate, grad_up, mlp_all = fed(coming.far(), 2, filled)

time: 680 us -> 670 us (0.985)
  the two profiles are of different devices: /device:TPU:8 before, /device:TPU:0 now
where the time goes in v5:
time: 670 us; the launch traced here: 657 us
  Pallas kernels  224 us (33%)
  starting transfers between devices  149 us (22%)
  waiting for transfers between devices  123 us (18%)
  local copies, waits for them, and re-layouts  87.7 us (13%)
  other arithmetic  28.4 us (4%)
  matrix products  27.5 us (4%)
  between operations  16.6 us (2%)
    unnamed x332, local copies, waits for them, and re-layouts  76.2 us
    ppermute x40, waiting for transfers between devices, swap(): return lax.ppermute(block, 'mp', [(i, i ^ bit) for i in range(8)])  58.3 us
    ppermute x10, starting transfers between devices, advance(): started['in'] = lax.ppermute(self.part, 'dp', [(0, 1), (3, 2)])  52.5 us
    pallas_call x9, Pallas kernels, on_arrival(): pl.pallas_call(partial(kernel, [len(block) for block in group], len(fille...  49.6 us
    pallas_call x2, Pallas kernels, mixer_back(): pl.pallas_call(partial(mixer_back_kernel, first, last), grid=(1,), in_spe...  34.8 us
    ppermute x40, starting transfers between devices, swap(): return lax.ppermute(block, 'mp', [(i, i ^ bit) for i in range(8)])  28.9 us
    pallas_call x3, Pallas kernels, call(): pl.pallas_call(kernel, grid=(blocks,), in_specs=[left_spec] * len(lefts)...  27.7 us
    ppermute x10, starting transfers between devices, advance(): lax.ppermute(self.total, 'dp', [(0, 1), (3, 2), (1, 0), (2, 3)])  27 us
  transfers between devices with their start and end apart: 97, of which 48 were waited for; matrix products, arithmetic and copies ran while one was open for 9% of the time, Pallas kernels for 32%

profile of v5, /device:TPU:0, one launch (start us, length us, event | category | flops | bytes accessed | tf_op | source)
XLA Modules:
  0.0 656.6 jit_solution(530152393786165677)
XLA Ops:
  20.6 5.0 copy.56
  25.7 8.0 %modal_filter.1.filt_ref.refs_8_ = f32[2048,256]{1,0:T(8,128)} custom-call(f32[32,16,256]{2,1,0:T(8,128)S(1)} %get-tuple-element.591.hre_ref, f32[32,16,256]{2,1,0:T(8,128)S(1)} %get-tuple-element.590.him_ref, f32[16,32,256]{2,1,0:T(8,128)S(1)} %get-tuple-element.589.lre_ref, f32[16,32,256]{2,1,0:T(8,128)} %get-tuple-element.588.lim_ref, ...), custom_call_target="tpu_custom_call" | custom-call | tf_op jit(solution)/shard_map/modal_filter/pallas_call | solution.py:247
  35.0 5.8 project.3
  46.2 8.5 %project.4 = (f32[8,256,768]{2,1,0:T(8,128)}, bf16[8,256,2048]{2,1,0:T(8,128)(2,1)}) custom-call(s32[1]{0:T(128)} %bitcast.me_ref, bf16[2,128,2048]{2,1,0:T(8,128)(2,1)S(1)} %collective-permute-done.refs_0_, bf16[2,128,2048]{2,1,0:T(8,128)(2,1)} %copy-done.157, ...), custom_call_target="tpu_custom_call", output_to_operand_aliasing={{0}: (6, {}), {1}: (7, {})} | custom-call | flops 3221225472 | bytes 3145728 | tf_op jit(solution)/shard_map/project/pallas_call | solution.py:444
  59.9 5.5 project.5
  65.3 17.0 %mixer_forward.1 = (bf16[8,2,128,256]{3,2,1,0:T(8,128)(2,1)S(1)}, bf16[8,2,128,256]{3,2,1,0:T(8,128)(2,1)}, f32[2,1024,256]{2,1,0:T(8,128)}, f32[2,2048,256]{2,1,0:T(8,128)}) custom-call(s32[1]{0:T(128)} %bitcast.me_ref, f32[8,2,128,768]{3,2,1,0:T(8,128)} %bitcast.163, f32[8,2,128,768]{3,2,1,0:T(8,128)} %bitcast.164, f32[8,2,128,768]{3,2,1,0:T(8,128)} %bitcast.165, ...), custom_call_target="tpu_custom_call" | custom-call | flops 4294967296 | bytes 20971520 | tf_op jit(solution)/shard_map/mixer_forward/pallas_call | solution.py:290
  101.0 3.3 hidden_back.3
  104.4 4.7 hidden_back.4
  113.2 8.8 %collective-permute-done.18 = bf16[1,128,2048]{2,1,0:T(8,128)(2,1)S(1)} collective-permute-done((bf16[1,128,2048]{2,1,0:T(8,128)(2,1)S(1)}, bf16[1,128,2048]{2,1,0:T(8,128)(2,1)S(1)}, u32[]{:S(2)}, u32[]{:S(2)}) %collective-permute-start.18) | collective-permute-done | bytes 524320 | tf_op jit(solution)/shard_map/ppermute | solution.py:686
  127.9 10.5 %collective-permute-done.23 = bf16[1,128,2048]{2,1,0:T(8,128)(2,1)S(1)} collective-permute-done((bf16[1,128,2048]{2,1,0:T(8,128)(2,1)S(1)}, bf16[1,128,2048]{2,1,0:T(8,128)(2,1)S(1)}, u32[]{:S(2)}, u32[]{:S(2)}) %collective-permute-start.23) | collective-permute-done | bytes 524320 | tf_op jit(solution)/shard_map/ppermute | solution.py:686
  153.4 3.3 copy-done.4
  156.7 5.1 feed.3
  161.8 8.2 %collective-permute-done.24.refs_0_ = bf16[2,128,2048]{2,1,0:T(8,128)(2,1)S(1)} collective-permute-done((bf16[2,128,2048]{2,1,0:T(8,128)(2,1)S(1)}, bf16[2,128,2048]{2,1,0:T(8,128)(2,1)S(1)}, u32[]{:S(2)}, u32[]{:S(2)}) %collective-permute-start.24) | collective-permute-done | bytes 1048608 | tf_op jit(solution)/shard_map/ppermute | solution.py:686
  174.7 9.5 %feed.4 = (bf16[704,2048]{1,0:T(8,128)(2,1)S(1)}, bf16[704,2048]{1,0:T(8,128)(2,1)S(1)}, bf16[704,2048]{1,0:T(8,128)(2,1)S(1)}, bf16[8,256,2048]{2,1,0:T(8,128)(2,1)}) custom-call(s32[1]{0:T(128)} %bitcast.me_ref, ...), custom_call_target="tpu_custom_call", output_to_operand_aliasing={{0}: (8, {}), {1}: (9, {}), {2}: (10, {}), {3}: (11, {})} | custom-call | flops 5905580032 | bytes 5767168 | tf_op jit(solution)/shard_map/feed/pallas_call | solution.py:444
  189.0 5.1 feed.5
  197.2 3.4 copy-done.5
  200.6 4.4 weight_gradient.6
  205.2 3.5 collective-permute-start.37
  210.5 4.4 weight_gradient.7
  214.9 10.2 %collective-permute-done.37.right_ref = bf16[176,2048]{1,0:T(8,128)(2,1)S(1)} collective-permute-done((bf16[176,2048]{1,0:T(8,128)(2,1)S(1)}, bf16[176,2048]{1,0:T(8,128)(2,1)S(1)}, u32[]{:S(2)}, u32[]{:S(2)}) %collective-permute-start.37) | collective-permute-done | bytes 720928 | tf_op jit(solution)/shard_map/ppermute | solution.py:731
  225.2 15.4 %sum_products.3 = bf16[8,256,2048]{2,1,0:T(8,128)(2,1)S(1)} custom-call(bf16[704,2048]{1,0:T(8,128)(2,1)S(1)} %copy-done.7, bf16[704,2048]{1,0:T(8,128)(2,1)S(1)} %copy-done.11, bf16[704,2048]{1,0:T(8,128)(2,1)S(1)} %bitcast.148, bf16[704,2048]{1,0:T(8,128)(2,1)S(1)} %bitcast.152), custom_call_target="tpu_custom_call" | custom-call | flops 11811160064 | bytes 8388608 | tf_op jit(solution)/shard_map/sum_products/pallas_call | solution.py:479
  240.6 3.3 copy-done.27
  250.9 7.2 %collective-permute-start.39 = (bf16[176,2048]{1,0:T(8,128)(2,1)}, bf16[176,2048]{1,0:T(8,128)(2,1)}, u32[]{:S(2)}, u32[]{:S(2)}) collective-permute-start(bf16[176,2048]{1,0:T(8,128)(2,1)} %get-tuple-element.570.left_ref), channel_id=1, source_target_pairs={{0,8},{24,16},{1,9},{25,17},{2,10},{26,18},{3,11},{27,19},{4,12},{... | collective-permute-start | bytes 2162696 | tf_op jit(solution)/shard_map/ppermute | solution.py:731
  264.0 3.4 copy-done
  269.2 4.4 weight_gradient.8
  281.3 3.6 copy-done.1
  284.9 4.4 weight_gradient.9
  293.2 3.5 copy-done.2
  296.7 4.4 weight_gradient.10
  301.1 3.8 collective-permute-done.42.right_ref.refs_0_
  310.5 3.4 copy-done.3
  314.0 4.4 weight_gradient.11
  322.1 10.9 %collective-permute-done.46.right_ref.refs_4_ = bf16[176,2048]{1,0:T(8,128)(2,1)S(1)} collective-permute-done((bf16[176,2048]{1,0:T(8,128)(2,1)S(1)}, bf16[176,2048]{1,0:T(8,128)(2,1)S(1)}, u32[]{:S(2)}, u32[]{:S(2)}) %collective-permute-start.46) | collective-permute-done | bytes 720928 | tf_op jit(solution)/shard_map/ppermute | solution.py:728
  337.5 4.1 fusion.30
  357.0 8.5 %sum_products.4 = bf16[8,256,2048]{2,1,0:T(8,128)(2,1)S(1)} custom-call(bf16[704,2048]{1,0:T(8,128)(2,1)S(1)} %get-tuple-element.356.left_ref.refs_0_, bf16[704,2048]{1,0:T(8,128)(2,1)S(1)} %copy-done.25), custom_call_target="tpu_custom_call" | custom-call | flops 5905580032 | bytes 8388608 | tf_op jit(solution)/shard_map/sum_products/pallas_call | solution.py:479
  365.5 3.3 copy-done.26
  382.6 4.8 collective-permute-start.54
  390.6 4.6 collective-permute-done.56.right_ref.refs_2_
  397.0 3.4 copy-done.13
  400.4 3.8 sum_products.5
  404.2 3.3 fusion
  410.6 4.8 collective-permute-start.61
  417.6 18.7 %mixer_backward.2 = (bf16[8,2,128,768]{3,2,1,0:T(8,128)(2,1)}, f32[16,256]{1,0:T(8,128)S(1)}, f32[2048,256]{1,0:T(8,128)}) custom-call(f32[8,2,128,256]{3,2,1,0:T(8,128)} %bitcast.153, f32[8,2,128,768]{3,2,1,0:T(8,128)} %bitcast.166, f32[8,2,128,768]{3,2,1,0:T(8,128)} %bitcast.167, f32[8,2,128,768]{3,2,1,0:T(8,128)} %bitcast.168, ...), custom_call_target="tpu_custom_call" | custom-call | flops 3221225472 | bytes 20971520 | tf_op jit(solution)/shard_map/mixer_backward/pallas_call | solution.py:332
  437.8 4.6 collective-permute-start.58
  447.0 16.1 %mixer_backward.3 = (bf16[8,2,128,768]{3,2,1,0:T(8,128)(2,1)}, f32[16,256]{1,0:T(8,128)S(1)}, f32[1024,256]{1,0:T(8,128)S(1)}) custom-call(f32[8,2,128,256]{3,2,1,0:T(8,128)} %bitcast.154, f32[8,2,128,768]{3,2,1,0:T(8,128)} %bitcast.169, f32[8,2,128,768]{3,2,1,0:T(8,128)} %bitcast.170, ...), custom_call_target="tpu_custom_call", output_to_operand_aliasing={{0}: (11, {})} | custom-call | flops 3221225472 | bytes 20971520 | tf_op jit(solution)/shard_map/mixer_backward/pallas_call | solution.py:332
  463.0 11.2 %convolution_convert_fusion.2 = bf16[2048,768]{1,0:T(8,128)(2,1)S(1)} fusion(bf16[2048,2048]{1,0:T(8,128)(2,1)} %bitcast.178, bf16[2048,768]{1,0:T(8,128)(2,1)} %bitcast.191), kind=kOutput, calls=%fused_computation.2 | convolution fusion | flops 6444023808 | bytes 14680064 | tf_op jit(solution)/shard_map/dot_general | solution.py:32
  476.0 6.6 %collective-permute-start.66 = (bf16[128,2048]{1,0:T(8,128)(2,1)S(1)}, bf16[128,2048]{1,0:T(8,128)(2,1)S(1)}, u32[]{:S(2)}, u32[]{:S(2)}) collective-permute-start(bf16[128,2048]{1,0:T(8,128)(2,1)S(1)} %get-tuple-element.579.left_ref), channel_id=1, source_target_pairs={{0,8},{24,16},{1,9},{25,17},{2,10},{26,18},{3,11},{27,19},{4,12},{... | collective-permute-start | bytes 1572872 | tf_op jit(solution)/shard_map/ppermute | solution.py:731
  482.7 9.2 %convolution_convert_fusion = bf16[2048,2048]{1,0:T(8,128)(2,1)} fusion(bf16[2048,768]{1,0:T(8,128)(2,1)S(1)} %bitcast.192, bf16[2048,768]{0,1:T(8,128)(2,1)S(1)} %bitcast.190), kind=kOutput, calls=%fused_computation | convolution fusion | flops 6446645248 | bytes 14680064 | tf_op jit(solution)/shard_map/dot_general | solution.py:36
  498.3 6.9 %collective-permute-start.63 = (bf16[1024,256]{1,0:T(8,128)(2,1)S(1)}, bf16[1024,256]{1,0:T(8,128)(2,1)S(1)}, u32[]{:S(2)}, u32[]{:S(2)}) collective-permute-start(bf16[1024,256]{1,0:T(8,128)(2,1)S(1)} %get-tuple-element.578.left_ref), channel_id=1, source_target_pairs={{0,8},{24,16},{1,9},{25,17},{2,10},{26,18},{3,11},{27,19},{4,12},{... | collective-permute-start | bytes 1572872 | tf_op jit(solution)/shard_map/ppermute | solution.py:731
  507.8 7.5 %collective-permute-start.72 = (bf16[1024,256]{1,0:T(8,128)(2,1)S(1)}, bf16[1024,256]{1,0:T(8,128)(2,1)S(1)}, u32[]{:S(2)}, u32[]{:S(2)}) collective-permute-start(bf16[1024,256]{1,0:T(8,128)(2,1)S(1)} %get-tuple-element.577.left_ref), channel_id=1, source_target_pairs={{0,8},{24,16},{1,9},{25,17},{2,10},{26,18},{3,11},{27,19},{4,12},{... | collective-permute-start | bytes 1572872 | tf_op jit(solution)/shard_map/ppermute | solution.py:731
  519.2 4.6 collective-permute-start.69
  527.7 4.6 collective-permute-done.73.refs_6_
  541.8 6.4 pole_gradients.1
  549.8 7.7 %collective-permute-start.78 = (bf16[1024,256]{1,0:T(8,128)(2,1)}, bf16[1024,256]{1,0:T(8,128)(2,1)}, u32[]{:S(2)}, u32[]{:S(2)}) collective-permute-start(bf16[1024,256]{1,0:T(8,128)(2,1)} %get-tuple-element.575.left_ref), channel_id=1, source_target_pairs={{0,8},{24,16},{1,9},{25,17},{2,10},{26,18},{3,11},{27,19},{4,12},{... | collective-permute-start | bytes 1572872 | tf_op jit(solution)/shard_map/ppermute | solution.py:731
  561.0 8.3 %collective-permute-done.78.right_ref = bf16[1024,256]{1,0:T(8,128)(2,1)} collective-permute-done((bf16[1024,256]{1,0:T(8,128)(2,1)}, bf16[1024,256]{1,0:T(8,128)(2,1)}, u32[]{:S(2)}, u32[]{:S(2)}) %collective-permute-start.78) | collective-permute-done | bytes 524320 | tf_op jit(solution)/shard_map/ppermute | solution.py:731
  575.2 4.2 collective-permute-start.82
  587.1 3.2 collective-permute-done.82.right_ref
  596.5 2.9 multiply_convert_fusion
  599.5 7.2 %collective-permute-done.84.refs_6_ = bf16[1024,256]{1,0:T(8,128)(2,1)} collective-permute-done((bf16[1024,256]{1,0:T(8,128)(2,1)S(1)}, bf16[1024,256]{1,0:T(8,128)(2,1)}, u32[]{:S(2)}, u32[]{:S(2)}) %collective-permute-start.84) | collective-permute-done | bytes 524320 | tf_op jit(solution)/shard_map/ppermute | solution.py:734
  618.5 3.0 finish.7
  621.8 5.0 finish.6
  626.9 3.0 finish.5
  634.7 2.9 collective-permute-done.90.refs_8_
  643.7 5.9 finish.9
  (616 shorter events, 243.5 us)
Async XLA Ops:
  7.2 327.6 %reduce-scatter.4.cloned.1.call-start = ((), (), s32[]{:S(2)}) async-start(), calls=%async_computation.3 | async-start | bytes 9437184 | tf_op jit(solution)/shard_map/reduce_scatter | solution.py:543
  11.3 23.7 %collective-permute-start.2 = (bf16[2,128,2048]{2,1,0:T(8,128)(2,1)}, bf16[2,128,2048]{2,1,0:T(8,128)(2,1)}, u32[]{:S(2)}, u32[]{:S(2)}) collective-permute-start(bf16[2,128,2048]{2,1,0:T(8,128)(2,1)} %fusion.10.refs_0_), channel_id=1, source_target_pairs={{0,1},{1,0},{2,3},{3,2},{4,5},{5,4},{6,7},{7,6},{8,9},{9,8},{10,11... | collective-permute-start | bytes 3145736 | tf_op jit(solution)/shard_map/ppermute | solution.py:686
  11.7 29.1 %collective-permute-start = (bf16[2,128,2048]{2,1,0:T(8,128)(2,1)}, bf16[2,128,2048]{2,1,0:T(8,128)(2,1)S(1)}, u32[]{:S(2)}, u32[]{:S(2)}) collective-permute-start(bf16[2,128,2048]{2,1,0:T(8,128)(2,1)} %fusion.10.refs_0_), channel_id=1, source_target_pairs={{0,2},{1,3},{2,0},{3,1},{4,6},{5,7},{6,4},{7,5},{8,10},{9,11},{10,... | collective-permute-start | bytes 3145736 | tf_op jit(solution)/shard_map/ppermute | solution.py:686
  14.2 26.6 %collective-permute-start.1 = (bf16[2,128,2048]{2,1,0:T(8,128)(2,1)}, bf16[2,128,2048]{2,1,0:T(8,128)(2,1)}, u32[]{:S(2)}, u32[]{:S(2)}) collective-permute-start(bf16[2,128,2048]{2,1,0:T(8,128)(2,1)} %fusion.10.refs_0_), channel_id=1, source_target_pairs={{0,4},{1,5},{2,6},{3,7},{4,0},{5,1},{6,2},{7,3},{8,12},{9,13},{10,... | collective-permute-start | bytes 3145736 | tf_op jit(solution)/shard_map/ppermute | solution.py:686
  57.4 25.3 %collective-permute-start.8 = (bf16[2,128,2048]{2,1,0:T(8,128)(2,1)}, bf16[2,128,2048]{2,1,0:T(8,128)(2,1)S(1)}, u32[]{:S(2)}, u32[]{:S(2)}) collective-permute-start(bf16[2,128,2048]{2,1,0:T(8,128)(2,1)} %fusion.15.refs_0_), channel_id=1, source_target_pairs={{0,2},{1,3},{2,0},{3,1},{4,6},{5,7},{6,4},{7,5},{8,10},{9,11},{10,... | collective-permute-start | bytes 3145736 | tf_op jit(solution)/shard_map/ppermute | solution.py:686
  57.8 25.0 %collective-permute-start.9 = (bf16[2,128,2048]{2,1,0:T(8,128)(2,1)}, bf16[2,128,2048]{2,1,0:T(8,128)(2,1)S(1)}, u32[]{:S(2)}, u32[]{:S(2)}) collective-permute-start(bf16[2,128,2048]{2,1,0:T(8,128)(2,1)} %fusion.15.refs_0_), channel_id=1, source_target_pairs={{0,4},{1,5},{2,6},{3,7},{4,0},{5,1},{6,2},{7,3},{8,12},{9,13},{10,... | collective-permute-start | bytes 3145736 | tf_op jit(solution)/shard_map/ppermute | solution.py:686
  96.6 15.0 %collective-permute-start.16 = (bf16[1,128,2048]{2,1,0:T(8,128)(2,1)}, bf16[1,128,2048]{2,1,0:T(8,128)(2,1)S(1)}, u32[]{:S(2)}, u32[]{:S(2)}) collective-permute-start(bf16[1,128,2048]{2,1,0:T(8,128)(2,1)} %get-tuple-element.284), channel_id=1, source_target_pairs={{0,2},{1,3},{2,0},{3,1},{4,6},{5,7},{6,4},{7,5},{8,10},{9,11},{10,... | collective-permute-start | bytes 1572872 | tf_op jit(solution)/shard_map/ppermute | solution.py:686
  98.2 15.0 %collective-permute-start.17 = (bf16[1,128,2048]{2,1,0:T(8,128)(2,1)}, bf16[1,128,2048]{2,1,0:T(8,128)(2,1)S(1)}, u32[]{:S(2)}, u32[]{:S(2)}) collective-permute-start(bf16[1,128,2048]{2,1,0:T(8,128)(2,1)} %get-tuple-element.285), channel_id=1, source_target_pairs={{0,4},{1,5},{2,6},{3,7},{4,0},{5,1},{6,2},{7,3},{8,12},{9,13},{10,... | collective-permute-start | bytes 1572872 | tf_op jit(solution)/shard_map/ppermute | solution.py:686
  99.8 22.3 %collective-permute-start.18 = (bf16[1,128,2048]{2,1,0:T(8,128)(2,1)S(1)}, bf16[1,128,2048]{2,1,0:T(8,128)(2,1)S(1)}, u32[]{:S(2)}, u32[]{:S(2)}) collective-permute-start(bf16[1,128,2048]{2,1,0:T(8,128)(2,1)S(1)} %slice.286), channel_id=1, source_target_pairs={{0,2},{1,3},{2,0},{3,1},{4,6},{5,7},{6,4},{7,5},{8,10},{9,11},{10,... | collective-permute-start | bytes 1572872 | tf_op jit(solution)/shard_map/ppermute | solution.py:686
  100.6 22.8 %collective-permute-start.19 = (bf16[1,128,2048]{2,1,0:T(8,128)(2,1)S(1)}, bf16[1,128,2048]{2,1,0:T(8,128)(2,1)S(1)}, u32[]{:S(2)}, u32[]{:S(2)}) collective-permute-start(bf16[1,128,2048]{2,1,0:T(8,128)(2,1)S(1)} %slice.285), channel_id=1, source_target_pairs={{0,4},{1,5},{2,6},{3,7},{4,0},{5,1},{6,2},{7,3},{8,12},{9,13},{10,... | collective-permute-start | bytes 1572872 | tf_op jit(solution)/shard_map/ppermute | solution.py:686
  125.9 22.7 %collective-permute-start.27 = (bf16[1,128,2048]{2,1,0:T(8,128)(2,1)S(1)}, bf16[1,128,2048]{2,1,0:T(8,128)(2,1)S(1)}, u32[]{:S(2)}, u32[]{:S(2)}) collective-permute-start(bf16[1,128,2048]{2,1,0:T(8,128)(2,1)S(1)} %slice.207), channel_id=1, source_target_pairs={{0,4},{1,5},{2,6},{3,7},{4,0},{5,1},{6,2},{7,3},{8,12},{9,13},{10,... | collective-permute-start | bytes 1572872 | tf_op jit(solution)/shard_map/ppermute | solution.py:686
  126.4 22.6 %collective-permute-start.28 = (bf16[1,128,2048]{2,1,0:T(8,128)(2,1)S(1)}, bf16[1,128,2048]{2,1,0:T(8,128)(2,1)S(1)}, u32[]{:S(2)}, u32[]{:S(2)}) collective-permute-start(bf16[1,128,2048]{2,1,0:T(8,128)(2,1)S(1)} %slice.208), channel_id=1, source_target_pairs={{0,2},{1,3},{2,0},{3,1},{4,6},{5,7},{6,4},{7,5},{8,10},{9,11},{10,... | collective-permute-start | bytes 1572872 | tf_op jit(solution)/shard_map/ppermute | solution.py:686
  143.1 27.0 %collective-permute-start.24 = (bf16[2,128,2048]{2,1,0:T(8,128)(2,1)S(1)}, bf16[2,128,2048]{2,1,0:T(8,128)(2,1)S(1)}, u32[]{:S(2)}, u32[]{:S(2)}) collective-permute-start(bf16[2,128,2048]{2,1,0:T(8,128)(2,1)S(1)} %multiply_convert_fusion.1.refs_0_), channel_id=1, source_target_pairs={{0,2},{1,3},{2,0},{3,1},{4,6},{5,7},{6,4},{7,5},{8,10},{9,11},{10,... | collective-permute-start | bytes 3145736 | tf_op jit(solution)/shard_map/ppermute | solution.py:686
  144.7 25.9 %collective-permute-start.25 = (bf16[2,128,2048]{2,1,0:T(8,128)(2,1)S(1)}, bf16[2,128,2048]{2,1,0:T(8,128)(2,1)S(1)}, u32[]{:S(2)}, u32[]{:S(2)}) collective-permute-start(bf16[2,128,2048]{2,1,0:T(8,128)(2,1)S(1)} %multiply_convert_fusion.1.refs_0_), channel_id=1, source_target_pairs={{0,4},{1,5},{2,6},{3,7},{4,0},{5,1},{6,2},{7,3},{8,12},{9,13},{10,... | collective-permute-start | bytes 3145736 | tf_op jit(solution)/shard_map/ppermute | solution.py:686
  205.2 20.0 %collective-permute-start.37 = (bf16[176,2048]{1,0:T(8,128)(2,1)S(1)}, bf16[176,2048]{1,0:T(8,128)(2,1)S(1)}, u32[]{:S(2)}, u32[]{:S(2)}) collective-permute-start(bf16[176,2048]{1,0:T(8,128)(2,1)S(1)} %get-tuple-element.572.left_ref), channel_id=1, source_target_pairs={{0,8},{24,16},{1,9},{25,17},{2,10},{26,18},{3,11},{27,19},{4,12},{... | collective-permute-start | bytes 2162696 | tf_op jit(solution)/shard_map/ppermute | solution.py:731
  208.8 35.1 %collective-permute-start.40 = (bf16[176,2048]{1,0:T(8,128)(2,1)S(1)}, bf16[176,2048]{1,0:T(8,128)(2,1)S(1)}, u32[]{:S(2)}, u32[]{:S(2)}) collective-permute-start(bf16[176,2048]{1,0:T(8,128)(2,1)S(1)} %get-tuple-element.571.left_ref), channel_id=1, source_target_pairs={{0,8},{24,16},{1,9},{25,17},{2,10},{26,18},{3,11},{27,19},{4,12},{... | collective-permute-start | bytes 2162696 | tf_op jit(solution)/shard_map/ppermute | solution.py:731
  244.8 152.2 %all-gather.3.cloned.1.call-start = ((), (), s32[]{:S(2)}) async-start(), calls=%async_computation.6 | async-start | bytes 9437184 | tf_op jit(solution)/shard_map/all_gather | solution.py:539
  248.1 25.6 %collective-permute-start.38 = (bf16[176,2048]{1,0:T(8,128)(2,1)}, bf16[176,2048]{1,0:T(8,128)(2,1)}, u32[]{:S(2)}, u32[]{:S(2)}) collective-permute-start(bf16[176,2048]{1,0:T(8,128)(2,1)} %add.178.left_ref), channel_id=1, source_target_pairs={{8,16},{16,8},{9,17},{17,9},{10,18},{18,10},{11,19},{19,11},{12,20... | collective-permute-start | bytes 2162696 | tf_op jit(solution)/shard_map/ppermute | solution.py:736
  250.9 23.3 %collective-permute-start.39 = (bf16[176,2048]{1,0:T(8,128)(2,1)}, bf16[176,2048]{1,0:T(8,128)(2,1)}, u32[]{:S(2)}, u32[]{:S(2)}) collective-permute-start(bf16[176,2048]{1,0:T(8,128)(2,1)} %get-tuple-element.570.left_ref), channel_id=1, source_target_pairs={{0,8},{24,16},{1,9},{25,17},{2,10},{26,18},{3,11},{27,19},{4,12},{... | collective-permute-start | bytes 2162696 | tf_op jit(solution)/shard_map/ppermute | solution.py:731
  260.9 28.5 %collective-permute-start.43 = (bf16[176,2048]{1,0:T(8,128)(2,1)S(1)}, bf16[176,2048]{1,0:T(8,128)(2,1)S(1)}, u32[]{:S(2)}, u32[]{:S(2)}) collective-permute-start(bf16[176,2048]{1,0:T(8,128)(2,1)S(1)} %add.180.left_ref), channel_id=1, source_target_pairs={{8,16},{16,8},{9,17},{17,9},{10,18},{18,10},{11,19},{19,11},{12,20... | collective-permute-start | bytes 2162696 | tf_op jit(solution)/shard_map/ppermute | solution.py:736
  261.8 27.6 %collective-permute-start.44 = (bf16[176,2048]{1,0:T(8,128)(2,1)S(1)}, bf16[176,2048]{1,0:T(8,128)(2,1)S(1)}, u32[]{:S(2)}, u32[]{:S(2)}) collective-permute-start(bf16[176,2048]{1,0:T(8,128)(2,1)S(1)} %copy-done.69), channel_id=1, source_target_pairs={{0,8},{24,16},{1,9},{25,17},{2,10},{26,18},{3,11},{27,19},{4,12},{... | collective-permute-start | bytes 2162696 | tf_op jit(solution)/shard_map/ppermute | solution.py:731
  276.2 28.7 %collective-permute-start.42 = (bf16[176,2048]{1,0:T(8,128)(2,1)S(1)}, bf16[176,2048]{1,0:T(8,128)(2,1)S(1)}, u32[]{:S(2)}, u32[]{:S(2)}) collective-permute-start(bf16[176,2048]{1,0:T(8,128)(2,1)S(1)} %merge.10.refs_1_), channel_id=1, source_target_pairs={{0,8},{24,16},{8,0},{16,24},{1,9},{25,17},{9,1},{17,25},{2,10},{26... | collective-permute-start | bytes 2162696 | tf_op jit(solution)/shard_map/ppermute | solution.py:728
  280.6 24.4 %collective-permute-start.41 = (bf16[176,2048]{1,0:T(8,128)(2,1)S(1)}, bf16[176,2048]{1,0:T(8,128)(2,1)S(1)}, u32[]{:S(2)}, u32[]{:S(2)}) collective-permute-start(bf16[176,2048]{1,0:T(8,128)(2,1)S(1)} %add.179.left_ref), channel_id=1, source_target_pairs={{8,16},{16,8},{9,17},{17,9},{10,18},{18,10},{11,19},{19,11},{12,20... | collective-permute-start | bytes 2162696 | tf_op jit(solution)/shard_map/ppermute | solution.py:736
  289.8 30.6 %collective-permute-start.48 = (bf16[176,2048]{1,0:T(8,128)(2,1)S(1)}, bf16[176,2048]{1,0:T(8,128)(2,1)S(1)}, u32[]{:S(2)}, u32[]{:S(2)}) collective-permute-start(bf16[176,2048]{1,0:T(8,128)(2,1)S(1)} %merge.12.refs_3_), channel_id=1, source_target_pairs={{0,8},{24,16},{8,0},{16,24},{1,9},{25,17},{9,1},{17,25},{2,10},{26... | collective-permute-start | bytes 2162696 | tf_op jit(solution)/shard_map/ppermute | solution.py:728
  292.5 28.8 %collective-permute-start.47 = (bf16[176,2048]{1,0:T(8,128)(2,1)S(1)}, bf16[176,2048]{1,0:T(8,128)(2,1)S(1)}, u32[]{:S(2)}, u32[]{:S(2)}) collective-permute-start(bf16[176,2048]{1,0:T(8,128)(2,1)S(1)} %add.182.left_ref), channel_id=1, source_target_pairs={{8,16},{16,8},{9,17},{17,9},{10,18},{18,10},{11,19},{19,11},{12,20... | collective-permute-start | bytes 2162696 | tf_op jit(solution)/shard_map/ppermute | solution.py:736
  307.1 25.9 %collective-permute-start.46 = (bf16[176,2048]{1,0:T(8,128)(2,1)S(1)}, bf16[176,2048]{1,0:T(8,128)(2,1)S(1)}, u32[]{:S(2)}, u32[]{:S(2)}) collective-permute-start(bf16[176,2048]{1,0:T(8,128)(2,1)S(1)} %merge.11.refs_5_), channel_id=1, source_target_pairs={{0,8},{24,16},{8,0},{16,24},{1,9},{25,17},{9,1},{17,25},{2,10},{26... | collective-permute-start | bytes 2162696 | tf_op jit(solution)/shard_map/ppermute | solution.py:728
  309.8 24.1 %collective-permute-start.45 = (bf16[176,2048]{1,0:T(8,128)(2,1)S(1)}, bf16[176,2048]{1,0:T(8,128)(2,1)S(1)}, u32[]{:S(2)}, u32[]{:S(2)}) collective-permute-start(bf16[176,2048]{1,0:T(8,128)(2,1)S(1)} %add.181.left_ref), channel_id=1, source_target_pairs={{8,16},{16,8},{9,17},{17,9},{10,18},{18,10},{11,19},{19,11},{12,20... | collective-permute-start | bytes 2162696 | tf_op jit(solution)/shard_map/ppermute | solution.py:736
  341.5 253.5 %reduce-scatter.6.cloned.1.call-start = ((), (), s32[]{:S(2)}) async-start(), calls=%async_computation.4 | async-start | bytes 9437184 | tf_op jit(solution)/shard_map/reduce_scatter | solution.py:543
  345.3 23.5 %collective-permute-start.52 = (bf16[176,2048]{1,0:T(8,128)(2,1)S(1)}, bf16[176,2048]{1,0:T(8,128)(2,1)S(1)}, u32[]{:S(2)}, u32[]{:S(2)}) collective-permute-start(bf16[176,2048]{1,0:T(8,128)(2,1)S(1)} %merge.14.refs_7_), channel_id=1, source_target_pairs={{0,8},{24,16},{8,0},{16,24},{1,9},{25,17},{9,1},{17,25},{2,10},{26... | collective-permute-start | bytes 2162696 | tf_op jit(solution)/shard_map/ppermute | solution.py:728
  348.0 21.6 %collective-permute-start.51 = (bf16[176,2048]{1,0:T(8,128)(2,1)S(1)}, bf16[176,2048]{1,0:T(8,128)(2,1)S(1)}, u32[]{:S(2)}, u32[]{:S(2)}) collective-permute-start(bf16[176,2048]{1,0:T(8,128)(2,1)S(1)} %add.184.left_ref), channel_id=1, source_target_pairs={{8,16},{16,8},{9,17},{17,9},{10,18},{18,10},{11,19},{19,11},{12,20... | collective-permute-start | bytes 2162696 | tf_op jit(solution)/shard_map/ppermute | solution.py:736
  351.9 28.0 %collective-permute-start.50 = (bf16[176,2048]{1,0:T(8,128)(2,1)}, bf16[176,2048]{1,0:T(8,128)(2,1)}, u32[]{:S(2)}, u32[]{:S(2)}) collective-permute-start(bf16[176,2048]{1,0:T(8,128)(2,1)} %merge.13.refs_1_), channel_id=1, source_target_pairs={{0,8},{24,16},{8,0},{16,24},{1,9},{25,17},{9,1},{17,25},{2,10},{26... | collective-permute-start | bytes 2162696 | tf_op jit(solution)/shard_map/ppermute | solution.py:728
  355.4 24.4 %collective-permute-start.49 = (bf16[176,2048]{1,0:T(8,128)(2,1)}, bf16[176,2048]{1,0:T(8,128)(2,1)}, u32[]{:S(2)}, u32[]{:S(2)}) collective-permute-start(bf16[176,2048]{1,0:T(8,128)(2,1)} %add.183.left_ref), channel_id=1, source_target_pairs={{8,16},{16,8},{9,17},{17,9},{10,18},{18,10},{11,19},{19,11},{12,20... | collective-permute-start | bytes 2162696 | tf_op jit(solution)/shard_map/ppermute | solution.py:736
  374.1 21.1 %collective-permute-start.56 = (bf16[176,2048]{1,0:T(8,128)(2,1)S(1)}, bf16[176,2048]{1,0:T(8,128)(2,1)S(1)}, u32[]{:S(2)}, u32[]{:S(2)}) collective-permute-start(bf16[176,2048]{1,0:T(8,128)(2,1)S(1)} %merge.16.refs_3_), channel_id=1, source_target_pairs={{0,8},{24,16},{8,0},{16,24},{1,9},{25,17},{9,1},{17,25},{2,10},{26... | collective-permute-start | bytes 2162696 | tf_op jit(solution)/shard_map/ppermute | solution.py:728
  376.5 19.6 %collective-permute-start.55 = (bf16[176,2048]{1,0:T(8,128)(2,1)S(1)}, bf16[176,2048]{1,0:T(8,128)(2,1)S(1)}, u32[]{:S(2)}, u32[]{:S(2)}) collective-permute-start(bf16[176,2048]{1,0:T(8,128)(2,1)S(1)} %add.186.left_ref), channel_id=1, source_target_pairs={{8,16},{16,8},{9,17},{17,9},{10,18},{18,10},{11,19},{19,11},{12,20... | collective-permute-start | bytes 2162696 | tf_op jit(solution)/shard_map/ppermute | solution.py:736
  382.6 25.3 %collective-permute-start.54 = (bf16[176,2048]{1,0:T(8,128)(2,1)}, bf16[176,2048]{1,0:T(8,128)(2,1)}, u32[]{:S(2)}, u32[]{:S(2)}) collective-permute-start(bf16[176,2048]{1,0:T(8,128)(2,1)} %merge.15.refs_5_), channel_id=1, source_target_pairs={{0,8},{24,16},{8,0},{16,24},{1,9},{25,17},{9,1},{17,25},{2,10},{26... | collective-permute-start | bytes 2162696 | tf_op jit(solution)/shard_map/ppermute | solution.py:728
  388.7 19.3 %collective-permute-start.53 = (bf16[176,2048]{1,0:T(8,128)(2,1)S(1)}, bf16[176,2048]{1,0:T(8,128)(2,1)}, u32[]{:S(2)}, u32[]{:S(2)}) collective-permute-start(bf16[176,2048]{1,0:T(8,128)(2,1)S(1)} %add.185.left_ref), channel_id=1, source_target_pairs={{8,16},{16,8},{9,17},{17,9},{10,18},{18,10},{11,19},{19,11},{12,20... | collective-permute-start | bytes 2162696 | tf_op jit(solution)/shard_map/ppermute | solution.py:736
  408.0 222.1 %reduce-scatter.8.cloned.1.call-start = ((), (), s32[]{:S(2)}) async-start(), calls=%async_computation.5 | async-start | bytes 9437184 | tf_op jit(solution)/shard_map/reduce_scatter | solution.py:543
  410.6 25.7 %collective-permute-start.61 = (bf16[176,2048]{1,0:T(8,128)(2,1)S(1)}, bf16[176,2048]{1,0:T(8,128)(2,1)S(1)}, u32[]{:S(2)}, u32[]{:S(2)}) collective-permute-start(bf16[176,2048]{1,0:T(8,128)(2,1)S(1)} %merge.17.refs_7_), channel_id=1, source_target_pairs={{0,8},{24,16},{8,0},{16,24},{1,9},{25,17},{9,1},{17,25},{2,10},{26... | collective-permute-start | bytes 2162696 | tf_op jit(solution)/shard_map/ppermute | solution.py:728
  415.5 20.8 %collective-permute-start.60 = (bf16[176,2048]{1,0:T(8,128)(2,1)S(1)}, bf16[176,2048]{1,0:T(8,128)(2,1)S(1)}, u32[]{:S(2)}, u32[]{:S(2)}) collective-permute-start(bf16[176,2048]{1,0:T(8,128)(2,1)S(1)} %add.189.left_ref), channel_id=1, source_target_pairs={{8,16},{16,8},{9,17},{17,9},{10,18},{18,10},{11,19},{19,11},{12,20... | collective-permute-start | bytes 2162696 | tf_op jit(solution)/shard_map/ppermute | solution.py:736
  436.4 46.3 %collective-permute-start.59 = (bf16[176,2048]{1,0:T(8,128)(2,1)S(1)}, bf16[176,2048]{1,0:T(8,128)(2,1)S(1)}, u32[]{:S(2)}, u32[]{:S(2)}) collective-permute-start(bf16[176,2048]{1,0:T(8,128)(2,1)S(1)} %add.188.refs_1_), channel_id=1, source_target_pairs={{8,0},{16,24},{9,1},{17,25},{10,2},{18,26},{11,3},{19,27},{12,4},{... | collective-permute-start | bytes 2162696 | tf_op jit(solution)/shard_map/ppermute | solution.py:734
  437.8 38.2 %collective-permute-start.58 = (bf16[128,2048]{1,0:T(8,128)(2,1)S(1)}, bf16[128,2048]{1,0:T(8,128)(2,1)S(1)}, u32[]{:S(2)}, u32[]{:S(2)}) collective-permute-start(bf16[128,2048]{1,0:T(8,128)(2,1)S(1)} %get-tuple-element.580.left_ref), channel_id=1, source_target_pairs={{0,8},{24,16},{1,9},{25,17},{2,10},{26,18},{3,11},{27,19},{4,12},{... | collective-permute-start | bytes 1572872 | tf_op jit(solution)/shard_map/ppermute | solution.py:731
  443.7 39.0 %collective-permute-start.57 = (bf16[176,2048]{1,0:T(8,128)(2,1)S(1)}, bf16[176,2048]{1,0:T(8,128)(2,1)S(1)}, u32[]{:S(2)}, u32[]{:S(2)}) collective-permute-start(bf16[176,2048]{1,0:T(8,128)(2,1)S(1)} %add.187.left_ref), channel_id=1, source_target_pairs={{8,16},{16,8},{9,17},{17,9},{10,18},{18,10},{11,19},{19,11},{12,20... | collective-permute-start | bytes 2162696 | tf_op jit(solution)/shard_map/ppermute | solution.py:736
  444.6 48.2 %collective-permute-start.67 = (bf16[176,2048]{1,0:T(8,128)(2,1)S(1)}, bf16[176,2048]{1,0:T(8,128)(2,1)S(1)}, u32[]{:S(2)}, u32[]{:S(2)}) collective-permute-start(bf16[176,2048]{1,0:T(8,128)(2,1)S(1)} %add.193.refs_3_), channel_id=1, source_target_pairs={{8,0},{16,24},{9,1},{17,25},{10,2},{18,26},{11,3},{19,27},{12,4},{... | collective-permute-start | bytes 2162696 | tf_op jit(solution)/shard_map/ppermute | solution.py:734
  446.1 47.5 %collective-permute-start.65 = (bf16[176,2048]{1,0:T(8,128)(2,1)S(1)}, bf16[176,2048]{1,0:T(8,128)(2,1)S(1)}, u32[]{:S(2)}, u32[]{:S(2)}) collective-permute-start(bf16[176,2048]{1,0:T(8,128)(2,1)S(1)} %add.192.left_ref), channel_id=1, source_target_pairs={{8,16},{16,8},{9,17},{17,9},{10,18},{18,10},{11,19},{19,11},{12,20... | collective-permute-start | bytes 2162696 | tf_op jit(solution)/shard_map/ppermute | solution.py:736
  476.0 15.9 %collective-permute-start.66 = (bf16[128,2048]{1,0:T(8,128)(2,1)S(1)}, bf16[128,2048]{1,0:T(8,128)(2,1)S(1)}, u32[]{:S(2)}, u32[]{:S(2)}) collective-permute-start(bf16[128,2048]{1,0:T(8,128)(2,1)S(1)} %get-tuple-element.579.left_ref), channel_id=1, source_target_pairs={{0,8},{24,16},{1,9},{25,17},{2,10},{26,18},{3,11},{27,19},{4,12},{... | collective-permute-start | bytes 1572872 | tf_op jit(solution)/shard_map/ppermute | solution.py:731
  495.8 21.1 %collective-permute-start.64 = (bf16[176,2048]{1,0:T(8,128)(2,1)S(1)}, bf16[176,2048]{1,0:T(8,128)(2,1)S(1)}, u32[]{:S(2)}, u32[]{:S(2)}) collective-permute-start(bf16[176,2048]{1,0:T(8,128)(2,1)S(1)} %add.191.refs_5_), channel_id=1, source_target_pairs={{8,0},{16,24},{9,1},{17,25},{10,2},{18,26},{11,3},{19,27},{12,4},{... | collective-permute-start | bytes 2162696 | tf_op jit(solution)/shard_map/ppermute | solution.py:734
  498.3 17.0 %collective-permute-start.63 = (bf16[1024,256]{1,0:T(8,128)(2,1)S(1)}, bf16[1024,256]{1,0:T(8,128)(2,1)S(1)}, u32[]{:S(2)}, u32[]{:S(2)}) collective-permute-start(bf16[1024,256]{1,0:T(8,128)(2,1)S(1)} %get-tuple-element.578.left_ref), channel_id=1, source_target_pairs={{0,8},{24,16},{1,9},{25,17},{2,10},{26,18},{3,11},{27,19},{4,12},{... | collective-permute-start | bytes 1572872 | tf_op jit(solution)/shard_map/ppermute | solution.py:731
  505.4 26.9 %collective-permute-start.73 = (bf16[176,2048]{1,0:T(8,128)(2,1)S(1)}, bf16[176,2048]{1,0:T(8,128)(2,1)S(1)}, u32[]{:S(2)}, u32[]{:S(2)}) collective-permute-start(bf16[176,2048]{1,0:T(8,128)(2,1)S(1)} %add.197.refs_7_), channel_id=1, source_target_pairs={{8,0},{16,24},{9,1},{17,25},{10,2},{18,26},{11,3},{19,27},{12,4},{... | collective-permute-start | bytes 2162696 | tf_op jit(solution)/shard_map/ppermute | solution.py:734
  507.0 17.8 %collective-permute-start.71 = (bf16[128,2048]{1,0:T(8,128)(2,1)S(1)}, bf16[128,2048]{1,0:T(8,128)(2,1)S(1)}, u32[]{:S(2)}, u32[]{:S(2)}) collective-permute-start(bf16[128,2048]{1,0:T(8,128)(2,1)S(1)} %add.196.left_ref), channel_id=1, source_target_pairs={{8,16},{16,8},{9,17},{17,9},{10,18},{18,10},{11,19},{19,11},{12,20... | collective-permute-start | bytes 1572872 | tf_op jit(solution)/shard_map/ppermute | solution.py:736
  507.8 19.8 %collective-permute-start.72 = (bf16[1024,256]{1,0:T(8,128)(2,1)S(1)}, bf16[1024,256]{1,0:T(8,128)(2,1)S(1)}, u32[]{:S(2)}, u32[]{:S(2)}) collective-permute-start(bf16[1024,256]{1,0:T(8,128)(2,1)S(1)} %get-tuple-element.577.left_ref), channel_id=1, source_target_pairs={{0,8},{24,16},{1,9},{25,17},{2,10},{26,18},{3,11},{27,19},{4,12},{... | collective-permute-start | bytes 1572872 | tf_op jit(solution)/shard_map/ppermute | solution.py:731
  517.0 32.7 %collective-permute-start.70 = (bf16[128,2048]{1,0:T(8,128)(2,1)S(1)}, bf16[128,2048]{1,0:T(8,128)(2,1)S(1)}, u32[]{:S(2)}, u32[]{:S(2)}) collective-permute-start(bf16[128,2048]{1,0:T(8,128)(2,1)S(1)} %add.195.refs_1_), channel_id=1, source_target_pairs={{8,0},{16,24},{9,1},{17,25},{10,2},{18,26},{11,3},{19,27},{12,4},{... | collective-permute-start | bytes 1572872 | tf_op jit(solution)/shard_map/ppermute | solution.py:734
  519.2 38.2 %collective-permute-start.69 = (bf16[1024,256]{1,0:T(8,128)(2,1)S(1)}, bf16[1024,256]{1,0:T(8,128)(2,1)S(1)}, u32[]{:S(2)}, u32[]{:S(2)}) collective-permute-start(bf16[1024,256]{1,0:T(8,128)(2,1)S(1)} %get-tuple-element.576.left_ref), channel_id=1, source_target_pairs={{0,8},{24,16},{1,9},{25,17},{2,10},{26,18},{3,11},{27,19},{4,12},{... | collective-permute-start | bytes 1572872 | tf_op jit(solution)/shard_map/ppermute | solution.py:731
  524.8 32.6 %collective-permute-start.68 = (bf16[1024,256]{1,0:T(8,128)(2,1)S(1)}, bf16[1024,256]{1,0:T(8,128)(2,1)S(1)}, u32[]{:S(2)}, u32[]{:S(2)}) collective-permute-start(bf16[1024,256]{1,0:T(8,128)(2,1)S(1)} %add.194.left_ref), channel_id=1, source_target_pairs={{8,16},{16,8},{9,17},{17,9},{10,18},{18,10},{11,19},{19,11},{12,20... | collective-permute-start | bytes 1572872 | tf_op jit(solution)/shard_map/ppermute | solution.py:736
  539.5 21.5 %collective-permute-start.79 = (bf16[128,2048]{1,0:T(8,128)(2,1)}, bf16[128,2048]{1,0:T(8,128)(2,1)}, u32[]{:S(2)}, u32[]{:S(2)}) collective-permute-start(bf16[128,2048]{1,0:T(8,128)(2,1)} %add.199.refs_3_), channel_id=1, source_target_pairs={{8,0},{16,24},{9,1},{17,25},{10,2},{18,26},{11,3},{19,27},{12,4},{... | collective-permute-start | bytes 1572872 | tf_op jit(solution)/shard_map/ppermute | solution.py:734
  549.8 19.5 %collective-permute-start.78 = (bf16[1024,256]{1,0:T(8,128)(2,1)}, bf16[1024,256]{1,0:T(8,128)(2,1)}, u32[]{:S(2)}, u32[]{:S(2)}) collective-permute-start(bf16[1024,256]{1,0:T(8,128)(2,1)} %get-tuple-element.575.left_ref), channel_id=1, source_target_pairs={{0,8},{24,16},{1,9},{25,17},{2,10},{26,18},{3,11},{27,19},{4,12},{... | collective-permute-start | bytes 1572872 | tf_op jit(solution)/shard_map/ppermute | solution.py:731
  558.5 22.0 %collective-permute-start.86 = (bf16[1024,256]{1,0:T(8,128)(2,1)}, bf16[1024,256]{1,0:T(8,128)(2,1)}, u32[]{:S(2)}, u32[]{:S(2)}) collective-permute-start(bf16[1024,256]{1,0:T(8,128)(2,1)} %merge.19.refs_1_), channel_id=1, source_target_pairs={{0,8},{24,16},{8,0},{16,24},{1,9},{25,17},{9,1},{17,25},{2,10},{26... | collective-permute-start | bytes 1572872 | tf_op jit(solution)/shard_map/ppermute | solution.py:728
  559.4 21.1 %collective-permute-start.85 = (bf16[1024,256]{1,0:T(8,128)(2,1)}, bf16[1024,256]{1,0:T(8,128)(2,1)}, u32[]{:S(2)}, u32[]{:S(2)}) collective-permute-start(bf16[1024,256]{1,0:T(8,128)(2,1)} %add.203.left_ref), channel_id=1, source_target_pairs={{8,16},{16,8},{9,17},{17,9},{10,18},{18,10},{11,19},{19,11},{12,20... | collective-permute-start | bytes 1572872 | tf_op jit(solution)/shard_map/ppermute | solution.py:736
  570.7 19.6 %collective-permute-start.81 = (bf16[1024,256]{1,0:T(8,128)(2,1)S(1)}, bf16[1024,256]{1,0:T(8,128)(2,1)S(1)}, u32[]{:S(2)}, u32[]{:S(2)}) collective-permute-start(bf16[1024,256]{1,0:T(8,128)(2,1)S(1)} %merge.18.refs_3_), channel_id=1, source_target_pairs={{0,8},{24,16},{8,0},{16,24},{1,9},{25,17},{9,1},{17,25},{2,10},{26... | collective-permute-start | bytes 1572872 | tf_op jit(solution)/shard_map/ppermute | solution.py:728
  574.5 15.8 %collective-permute-start.80 = (bf16[1024,256]{1,0:T(8,128)(2,1)S(1)}, bf16[1024,256]{1,0:T(8,128)(2,1)S(1)}, u32[]{:S(2)}, u32[]{:S(2)}) collective-permute-start(bf16[1024,256]{1,0:T(8,128)(2,1)S(1)} %add.200.left_ref), channel_id=1, source_target_pairs={{8,16},{16,8},{9,17},{17,9},{10,18},{18,10},{11,19},{19,11},{12,20... | collective-permute-start | bytes 1572872 | tf_op jit(solution)/shard_map/ppermute | solution.py:736
  575.2 15.0 %collective-permute-start.82 = (bf16[96,256]{1,0:T(8,128)(2,1)S(1)}, bf16[96,256]{1,0:T(8,128)(2,1)S(1)}, u32[]{:S(2)}, u32[]{:S(2)}) collective-permute-start(bf16[96,256]{1,0:T(8,128)(2,1)S(1)} %pad.5.left_ref), channel_id=1, source_target_pairs={{0,8},{24,16},{1,9},{25,17},{2,10},{26,18},{3,11},{27,19},{4,12},{... | collective-permute-start | bytes 147464 | tf_op jit(solution)/shard_map/ppermute | solution.py:812
  591.2 15.5 %collective-permute-start.84 = (bf16[1024,256]{1,0:T(8,128)(2,1)S(1)}, bf16[1024,256]{1,0:T(8,128)(2,1)}, u32[]{:S(2)}, u32[]{:S(2)}) collective-permute-start(bf16[1024,256]{1,0:T(8,128)(2,1)S(1)} %add.202.refs_7_), channel_id=1, source_target_pairs={{8,0},{16,24},{9,1},{17,25},{10,2},{18,26},{11,3},{19,27},{12,4},{... | collective-permute-start | bytes 1572872 | tf_op jit(solution)/shard_map/ppermute | solution.py:734
  608.6 21.4 %collective-permute-start.91 = (bf16[1024,256]{1,0:T(8,128)(2,1)}, bf16[1024,256]{1,0:T(8,128)(2,1)}, u32[]{:S(2)}, u32[]{:S(2)}) collective-permute-start(bf16[1024,256]{1,0:T(8,128)(2,1)} %add.209.refs_11_), channel_id=1, source_target_pairs={{8,0},{16,24},{9,1},{17,25},{10,2},{18,26},{11,3},{19,27},{12,4},{... | collective-permute-start | bytes 1572872 | tf_op jit(solution)/shard_map/ppermute | solution.py:734
  609.9 20.1 %collective-permute-start.92 = (bf16[96,256]{1,0:T(8,128)(2,1)S(1)}, bf16[96,256]{1,0:T(8,128)(2,1)S(1)}, u32[]{:S(2)}, u32[]{:S(2)}) collective-permute-start(bf16[96,256]{1,0:T(8,128)(2,1)S(1)} %add.208), channel_id=1, source_target_pairs={{8,0},{16,24},{9,1},{17,25},{10,2},{18,26},{11,3},{19,27},{12,4},{... | collective-permute-start | bytes 147464 | tf_op jit(solution)/shard_map/ppermute | solution.py:820
  613.2 24.3 %collective-permute-start.90 = (bf16[1024,256]{1,0:T(8,128)(2,1)}, bf16[1024,256]{1,0:T(8,128)(2,1)}, u32[]{:S(2)}, u32[]{:S(2)}) collective-permute-start(bf16[1024,256]{1,0:T(8,128)(2,1)} %add.207.refs_9_), channel_id=1, source_target_pairs={{8,0},{16,24},{9,1},{17,25},{10,2},{18,26},{11,3},{19,27},{12,4},{... | collective-permute-start | bytes 1572872 | tf_op jit(solution)/shard_map/ppermute | solution.py:734
  (197 other events, 1330.2 us)
Sparse Core Ops, SparseCore 0:
  244.9 71.3 reduce-scatter.3
  341.7 53.4 all-gather.2
  408.1 72.6 reduce-scatter.5
  494.6 71.0 reduce-scatter.7

commit v6 on v5

--- a/solution.py
+++ b/solution.py
@@ -529,7 +529,7 @@
         ],
         out_specs=pl.BlockSpec((height, tile), lambda j: (0, j)),
         out_shape=jax.ShapeDtypeStruct((height, width), bf16),
-        compiler_params=params(SMALL_LIMIT),
+        compiler_params=params(),
         cost_estimate=cost(2 * height * depth * width, 2 * depth * width),
         name="weight_gradient",
     )(left, right)

time: 670 us -> 672 us (level)
  Pallas kernels: 224 us -> 241 us
  local copies, waits for them, and re-layouts: 87.7 us -> 73.6 us
    unnamed x332 -> x316, local copies, waits for them, and re-layouts: 76.2 us -> 60.6 us
    pallas_call x6, Pallas kernels: 26.5 us -> 40.4 us  [outer(): pl.pallas_call(outer_kernel, grid=(width // tile,), in_specs=[pl.BlockSpe...]
  transfers between devices with their start and end apart: 97 -> 97, of which waited for: 48 -> 45; matrix products, arithmetic and copies ran while one was open for 9% -> 9% of each run, Pallas kernels for 32% -> 34%
where the time goes in v6:
time: 672 us; the launch traced here: 659 us
  Pallas kernels  241 us (36%)
  starting transfers between devices  154 us (23%)
  waiting for transfers between devices  118 us (18%)
  local copies, waits for them, and re-layouts  73.6 us (11%)
  other arithmetic  27.9 us (4%)
  matrix products  27.5 us (4%)
  between operations  16.5 us (2%)
    unnamed x316, local copies, waits for them, and re-layouts  60.6 us
    ppermute x40, waiting for transfers between devices, swap(): return lax.ppermute(block, 'mp', [(i, i ^ bit) for i in range(8)])  58.4 us
    ppermute x10, starting transfers between devices, advance(): started['in'] = lax.ppermute(self.part, 'dp', [(0, 1), (3, 2)])  56 us
    pallas_call x9, Pallas kernels, on_arrival(): pl.pallas_call(partial(kernel, [len(block) for block in group], len(fille...  49.5 us
    pallas_call x6, Pallas kernels, outer(): pl.pallas_call(outer_kernel, grid=(width // tile,), in_specs=[pl.BlockSpe...  40.4 us
    pallas_call x2, Pallas kernels, mixer_back(): pl.pallas_call(partial(mixer_back_kernel, first, last), grid=(1,), in_spe...  34.3 us
    ppermute x40, starting transfers between devices, swap(): return lax.ppermute(block, 'mp', [(i, i ^ bit) for i in range(8)])  29.1 us
    ppermute x10, starting transfers between devices, advance(): lax.ppermute(self.total, 'dp', [(0, 1), (3, 2), (1, 0), (2, 3)])  28.4 us
  transfers between devices with their start and end apart: 97, of which 45 were waited for; matrix products, arithmetic and copies ran while one was open for 9% of the time, Pallas kernels for 34%

profile of v6, /device:TPU:0, one launch (start us, length us, event | category | flops | bytes accessed | tf_op | source)
XLA Modules:
  0.0 658.9 jit_solution(15500983907862800821)
XLA Ops:
  15.8 2.8 fusion.23
  20.6 5.0 copy.56
  25.7 8.0 %modal_filter.1.filt_ref.refs_8_ = f32[2048,256]{1,0:T(8,128)} custom-call(f32[32,16,256]{2,1,0:T(8,128)S(1)} %get-tuple-element.591.hre_ref, f32[32,16,256]{2,1,0:T(8,128)S(1)} %get-tuple-element.590.him_ref, f32[16,32,256]{2,1,0:T(8,128)S(1)} %get-tuple-element.589.lre_ref, f32[16,32,256]{2,1,0:T(8,128)} %get-tuple-element.588.lim_ref, ...), custom_call_target="tpu_custom_call" | custom-call | tf_op jit(solution)/shard_map/modal_filter/pallas_call | solution.py:247
  35.0 5.8 project.3
  46.2 8.4 %project.4 = (f32[8,256,768]{2,1,0:T(8,128)}, bf16[8,256,2048]{2,1,0:T(8,128)(2,1)}) custom-call(s32[1]{0:T(128)} %bitcast.me_ref, bf16[2,128,2048]{2,1,0:T(8,128)(2,1)S(1)} %collective-permute-done.refs_0_, bf16[2,128,2048]{2,1,0:T(8,128)(2,1)} %copy-done.149, ...), custom_call_target="tpu_custom_call", output_to_operand_aliasing={{0}: (6, {}), {1}: (7, {})} | custom-call | flops 3221225472 | bytes 3145728 | tf_op jit(solution)/shard_map/project/pallas_call | solution.py:444
  59.9 5.4 project.5
  65.3 17.0 %mixer_forward.1 = (bf16[8,2,128,256]{3,2,1,0:T(8,128)(2,1)S(1)}, bf16[8,2,128,256]{3,2,1,0:T(8,128)(2,1)}, f32[2,1024,256]{2,1,0:T(8,128)}, f32[2,2048,256]{2,1,0:T(8,128)}) custom-call(s32[1]{0:T(128)} %bitcast.me_ref, f32[8,2,128,768]{3,2,1,0:T(8,128)} %bitcast.159, f32[8,2,128,768]{3,2,1,0:T(8,128)} %bitcast.160, f32[8,2,128,768]{3,2,1,0:T(8,128)} %bitcast.161, ...), custom_call_target="tpu_custom_call" | custom-call | flops 4294967296 | bytes 20971520 | tf_op jit(solution)/shard_map/mixer_forward/pallas_call | solution.py:290
  90.8 2.7 collective-permute-done.14
  100.7 3.4 hidden_back.3
  104.1 4.7 hidden_back.4
  112.8 9.0 %collective-permute-done.18 = bf16[1,128,2048]{2,1,0:T(8,128)(2,1)S(1)} collective-permute-done((bf16[1,128,2048]{2,1,0:T(8,128)(2,1)S(1)}, bf16[1,128,2048]{2,1,0:T(8,128)(2,1)S(1)}, u32[]{:S(2)}, u32[]{:S(2)}) %collective-permute-start.18) | collective-permute-done | bytes 524320 | tf_op jit(solution)/shard_map/ppermute | solution.py:686
  127.4 10.5 %collective-permute-done.23 = bf16[1,128,2048]{2,1,0:T(8,128)(2,1)S(1)} collective-permute-done((bf16[1,128,2048]{2,1,0:T(8,128)(2,1)S(1)}, bf16[1,128,2048]{2,1,0:T(8,128)(2,1)S(1)}, u32[]{:S(2)}, u32[]{:S(2)}) %collective-permute-start.23) | collective-permute-done | bytes 524320 | tf_op jit(solution)/shard_map/ppermute | solution.py:686
  145.7 2.9 collective-permute-done.27.refs_0_
  153.4 3.3 copy-done
  156.7 5.2 feed.3
  161.9 7.7 %collective-permute-done.24.refs_0_ = bf16[2,128,2048]{2,1,0:T(8,128)(2,1)S(1)} collective-permute-done((bf16[2,128,2048]{2,1,0:T(8,128)(2,1)S(1)}, bf16[2,128,2048]{2,1,0:T(8,128)(2,1)S(1)}, u32[]{:S(2)}, u32[]{:S(2)}) %collective-permute-start.24) | collective-permute-done | bytes 1048608 | tf_op jit(solution)/shard_map/ppermute | solution.py:686
  174.4 9.5 %feed.4 = (bf16[704,2048]{1,0:T(8,128)(2,1)S(1)}, bf16[704,2048]{1,0:T(8,128)(2,1)S(1)}, bf16[704,2048]{1,0:T(8,128)(2,1)S(1)}, bf16[8,256,2048]{2,1,0:T(8,128)(2,1)}) custom-call(s32[1]{0:T(128)} %bitcast.me_ref, ...), custom_call_target="tpu_custom_call", output_to_operand_aliasing={{0}: (8, {}), {1}: (9, {}), {2}: (10, {}), {3}: (11, {})} | custom-call | flops 5905580032 | bytes 5767168 | tf_op jit(solution)/shard_map/feed/pallas_call | solution.py:444
  188.7 5.2 feed.5
  198.7 6.6 weight_gradient.6
  205.4 4.4 collective-permute-start.37
  212.3 6.9 %weight_gradient.7 = bf16[352,2048]{1,0:T(8,128)(2,1)S(1)} custom-call(bf16[704,2048]{1,0:T(8,128)(2,1)} %copy-done.1, bf16[2048,2048]{1,0:T(8,128)(2,1)} %bitcast.138), custom_call_target="tpu_custom_call" | custom-call | flops 2952790016 | bytes 8388608 | tf_op jit(solution)/shard_map/weight_gradient/pallas_call | solution.py:523
  219.2 6.2 collective-permute-done.37.right_ref
  227.2 15.4 %sum_products.3 = bf16[8,256,2048]{2,1,0:T(8,128)(2,1)S(1)} custom-call(bf16[704,2048]{1,0:T(8,128)(2,1)S(1)} %copy-done.4, bf16[704,2048]{1,0:T(8,128)(2,1)S(1)} %copy-done.6, bf16[704,2048]{1,0:T(8,128)(2,1)S(1)} %bitcast.144, bf16[704,2048]{1,0:T(8,128)(2,1)S(1)} %bitcast.148), custom_call_target="tpu_custom_call" | custom-call | flops 11811160064 | bytes 8388608 | tf_op jit(solution)/shard_map/sum_products/pallas_call | solution.py:479
  242.6 3.3 copy-done.21
  250.8 6.5 collective-permute-start.39
  259.3 3.1 collective-permute-start.44
  262.4 6.9 %weight_gradient.8 = bf16[352,2048]{1,0:T(8,128)(2,1)S(1)} custom-call(bf16[704,2048]{1,0:T(8,128)(2,1)} %copy-done.3, bf16[2048,2048]{1,0:T(8,128)(2,1)} %bitcast.168), custom_call_target="tpu_custom_call" | custom-call | flops 2952790016 | bytes 8388608 | tf_op jit(solution)/shard_map/weight_gradient/pallas_call | solution.py:523
  269.3 4.8 collective-permute-done.39.right_ref
  281.3 6.8 %weight_gradient.9 = bf16[352,2048]{1,0:T(8,128)(2,1)S(1)} custom-call(bf16[704,2048]{1,0:T(8,128)(2,1)} %copy-done.3, bf16[2048,2048]{1,0:T(8,128)(2,1)} %bitcast.169), custom_call_target="tpu_custom_call" | custom-call | flops 2952790016 | bytes 8388608 | tf_op jit(solution)/shard_map/weight_gradient/pallas_call | solution.py:523
  293.1 6.7 %weight_gradient.10 = bf16[352,2048]{1,0:T(8,128)(2,1)S(1)} custom-call(bf16[704,2048]{1,0:T(8,128)(2,1)} %copy-done.5, bf16[2048,2048]{1,0:T(8,128)(2,1)} %bitcast.170), custom_call_target="tpu_custom_call" | custom-call | flops 2952790016 | bytes 8388608 | tf_op jit(solution)/shard_map/weight_gradient/pallas_call | solution.py:523
  299.8 5.0 collective-permute-done.42.right_ref.refs_0_
  310.5 6.7 %weight_gradient.11 = bf16[352,2048]{1,0:T(8,128)(2,1)S(1)} custom-call(bf16[704,2048]{1,0:T(8,128)(2,1)} %copy-done.5, bf16[2048,2048]{1,0:T(8,128)(2,1)} %bitcast.171), custom_call_target="tpu_custom_call" | custom-call | flops 2952790016 | bytes 8388608 | tf_op jit(solution)/shard_map/weight_gradient/pallas_call | solution.py:523
  322.1 10.8 %collective-permute-done.46.right_ref.refs_4_ = bf16[176,2048]{1,0:T(8,128)(2,1)S(1)} collective-permute-done((bf16[176,2048]{1,0:T(8,128)(2,1)S(1)}, bf16[176,2048]{1,0:T(8,128)(2,1)S(1)}, u32[]{:S(2)}, u32[]{:S(2)}) %collective-permute-start.46) | collective-permute-done | bytes 720928 | tf_op jit(solution)/shard_map/ppermute | solution.py:728
  337.2 3.7 fusion.30
  356.9 8.5 %sum_products.4 = bf16[8,256,2048]{2,1,0:T(8,128)(2,1)S(1)} custom-call(bf16[704,2048]{1,0:T(8,128)(2,1)S(1)} %copy-done.2, bf16[704,2048]{1,0:T(8,128)(2,1)S(1)} %copy-done.19), custom_call_target="tpu_custom_call" | custom-call | flops 5905580032 | bytes 8388608 | tf_op jit(solution)/shard_map/sum_products/pallas_call | solution.py:479
  365.5 4.1 copy-done.20
  379.2 2.6 merge.15.refs_5_
  382.7 6.2 collective-permute-start.54
  396.0 3.4 copy-done.7
  399.4 4.2 sum_products.5
  403.6 3.3 fusion
  410.9 5.5 collective-permute-start.61
  419.1 18.2 %mixer_backward.2 = (bf16[8,2,128,768]{3,2,1,0:T(8,128)(2,1)}, f32[16,256]{1,0:T(8,128)S(1)}, f32[2048,256]{1,0:T(8,128)}) custom-call(f32[8,2,128,256]{3,2,1,0:T(8,128)} %bitcast.149, f32[8,2,128,768]{3,2,1,0:T(8,128)} %bitcast.162, f32[8,2,128,768]{3,2,1,0:T(8,128)} %bitcast.163, f32[8,2,128,768]{3,2,1,0:T(8,128)} %bitcast.164, ...), custom_call_target="tpu_custom_call" | custom-call | flops 3221225472 | bytes 20971520 | tf_op jit(solution)/shard_map/mixer_backward/pallas_call | solution.py:332
  438.9 4.8 collective-permute-start.58
  448.3 16.1 %mixer_backward.3 = (bf16[8,2,128,768]{3,2,1,0:T(8,128)(2,1)}, f32[16,256]{1,0:T(8,128)S(1)}, f32[1024,256]{1,0:T(8,128)S(1)}) custom-call(f32[8,2,128,256]{3,2,1,0:T(8,128)} %bitcast.150, f32[8,2,128,768]{3,2,1,0:T(8,128)} %bitcast.165, f32[8,2,128,768]{3,2,1,0:T(8,128)} %bitcast.166, ...), custom_call_target="tpu_custom_call", output_to_operand_aliasing={{0}: (11, {})} | custom-call | flops 3221225472 | bytes 20971520 | tf_op jit(solution)/shard_map/mixer_backward/pallas_call | solution.py:332
  464.4 11.2 %convolution_convert_fusion.2 = bf16[2048,768]{1,0:T(8,128)(2,1)S(1)} fusion(bf16[2048,2048]{1,0:T(8,128)(2,1)} %bitcast.178, bf16[2048,768]{1,0:T(8,128)(2,1)} %bitcast.191), kind=kOutput, calls=%fused_computation.2 | convolution fusion | flops 6444023808 | bytes 14680064 | tf_op jit(solution)/shard_map/dot_general | solution.py:32
  477.4 6.6 collective-permute-start.66
  484.0 9.2 %convolution_convert_fusion = bf16[2048,2048]{1,0:T(8,128)(2,1)} fusion(bf16[2048,768]{1,0:T(8,128)(2,1)S(1)} %bitcast.192, bf16[2048,768]{0,1:T(8,128)(2,1)S(1)} %bitcast.190), kind=kOutput, calls=%fused_computation | convolution fusion | flops 6446645248 | bytes 14680064 | tf_op jit(solution)/shard_map/dot_general | solution.py:36
  500.8 6.8 %collective-permute-start.63 = (bf16[1024,256]{1,0:T(8,128)(2,1)S(1)}, bf16[1024,256]{1,0:T(8,128)(2,1)S(1)}, u32[]{:S(2)}, u32[]{:S(2)}) collective-permute-start(bf16[1024,256]{1,0:T(8,128)(2,1)S(1)} %get-tuple-element.578.left_ref), channel_id=1, source_target_pairs={{0,8},{24,16},{1,9},{25,17},{2,10},{26,18},{3,11},{27,19},{4,12},{... | collective-permute-start | bytes 1572872 | tf_op jit(solution)/shard_map/ppermute | solution.py:731
  510.3 9.6 %collective-permute-start.72 = (bf16[1024,256]{1,0:T(8,128)(2,1)S(1)}, bf16[1024,256]{1,0:T(8,128)(2,1)S(1)}, u32[]{:S(2)}, u32[]{:S(2)}) collective-permute-start(bf16[1024,256]{1,0:T(8,128)(2,1)S(1)} %get-tuple-element.577.left_ref), channel_id=1, source_target_pairs={{0,8},{24,16},{1,9},{25,17},{2,10},{26,18},{3,11},{27,19},{4,12},{... | collective-permute-start | bytes 1572872 | tf_op jit(solution)/shard_map/ppermute | solution.py:731
  522.3 4.6 collective-permute-start.69
  529.0 3.2 collective-permute-done.72.right_ref
  544.5 6.4 pole_gradients.1
  552.4 7.3 %collective-permute-start.78 = (bf16[1024,256]{1,0:T(8,128)(2,1)}, bf16[1024,256]{1,0:T(8,128)(2,1)}, u32[]{:S(2)}, u32[]{:S(2)}) collective-permute-start(bf16[1024,256]{1,0:T(8,128)(2,1)} %get-tuple-element.575.left_ref), channel_id=1, source_target_pairs={{0,8},{24,16},{1,9},{25,17},{2,10},{26,18},{3,11},{27,19},{4,12},{... | collective-permute-start | bytes 1572872 | tf_op jit(solution)/shard_map/ppermute | solution.py:731
  564.4 7.2 %collective-permute-done.78.right_ref = bf16[1024,256]{1,0:T(8,128)(2,1)} collective-permute-done((bf16[1024,256]{1,0:T(8,128)(2,1)}, bf16[1024,256]{1,0:T(8,128)(2,1)}, u32[]{:S(2)}, u32[]{:S(2)}) %collective-permute-start.78) | collective-permute-done | bytes 524320 | tf_op jit(solution)/shard_map/ppermute | solution.py:731
  577.5 4.5 collective-permute-start.82
  589.3 3.2 collective-permute-done.82.right_ref
  598.8 2.9 multiply_convert_fusion
  601.7 7.5 %collective-permute-done.84.refs_6_ = bf16[1024,256]{1,0:T(8,128)(2,1)} collective-permute-done((bf16[1024,256]{1,0:T(8,128)(2,1)S(1)}, bf16[1024,256]{1,0:T(8,128)(2,1)}, u32[]{:S(2)}, u32[]{:S(2)}) %collective-permute-start.84) | collective-permute-done | bytes 524320 | tf_op jit(solution)/shard_map/ppermute | solution.py:734
  621.4 3.0 finish.7
  624.7 5.0 finish.6
  629.7 3.0 finish.5
  636.9 2.9 collective-permute-done.90.refs_8_
  646.0 5.9 finish.9
  (600 shorter events, 235.6 us)
Async XLA Ops:
  7.2 327.5 %reduce-scatter.4.cloned.1.call-start = ((), (), s32[]{:S(2)}) async-start(), calls=%async_computation.3 | async-start | bytes 9437184 | tf_op jit(solution)/shard_map/reduce_scatter | solution.py:543
  11.3 23.7 %collective-permute-start.2 = (bf16[2,128,2048]{2,1,0:T(8,128)(2,1)}, bf16[2,128,2048]{2,1,0:T(8,128)(2,1)}, u32[]{:S(2)}, u32[]{:S(2)}) collective-permute-start(bf16[2,128,2048]{2,1,0:T(8,128)(2,1)} %fusion.10.refs_0_), channel_id=1, source_target_pairs={{0,1},{1,0},{2,3},{3,2},{4,5},{5,4},{6,7},{7,6},{8,9},{9,8},{10,11... | collective-permute-start | bytes 3145736 | tf_op jit(solution)/shard_map/ppermute | solution.py:686
  11.7 29.1 %collective-permute-start = (bf16[2,128,2048]{2,1,0:T(8,128)(2,1)}, bf16[2,128,2048]{2,1,0:T(8,128)(2,1)S(1)}, u32[]{:S(2)}, u32[]{:S(2)}) collective-permute-start(bf16[2,128,2048]{2,1,0:T(8,128)(2,1)} %fusion.10.refs_0_), channel_id=1, source_target_pairs={{0,2},{1,3},{2,0},{3,1},{4,6},{5,7},{6,4},{7,5},{8,10},{9,11},{10,... | collective-permute-start | bytes 3145736 | tf_op jit(solution)/shard_map/ppermute | solution.py:686
  14.2 26.6 %collective-permute-start.1 = (bf16[2,128,2048]{2,1,0:T(8,128)(2,1)}, bf16[2,128,2048]{2,1,0:T(8,128)(2,1)}, u32[]{:S(2)}, u32[]{:S(2)}) collective-permute-start(bf16[2,128,2048]{2,1,0:T(8,128)(2,1)} %fusion.10.refs_0_), channel_id=1, source_target_pairs={{0,4},{1,5},{2,6},{3,7},{4,0},{5,1},{6,2},{7,3},{8,12},{9,13},{10,... | collective-permute-start | bytes 3145736 | tf_op jit(solution)/shard_map/ppermute | solution.py:686
  57.4 25.3 %collective-permute-start.8 = (bf16[2,128,2048]{2,1,0:T(8,128)(2,1)}, bf16[2,128,2048]{2,1,0:T(8,128)(2,1)S(1)}, u32[]{:S(2)}, u32[]{:S(2)}) collective-permute-start(bf16[2,128,2048]{2,1,0:T(8,128)(2,1)} %fusion.15.refs_0_), channel_id=1, source_target_pairs={{0,2},{1,3},{2,0},{3,1},{4,6},{5,7},{6,4},{7,5},{8,10},{9,11},{10,... | collective-permute-start | bytes 3145736 | tf_op jit(solution)/shard_map/ppermute | solution.py:686
  57.8 25.0 %collective-permute-start.9 = (bf16[2,128,2048]{2,1,0:T(8,128)(2,1)}, bf16[2,128,2048]{2,1,0:T(8,128)(2,1)S(1)}, u32[]{:S(2)}, u32[]{:S(2)}) collective-permute-start(bf16[2,128,2048]{2,1,0:T(8,128)(2,1)} %fusion.15.refs_0_), channel_id=1, source_target_pairs={{0,4},{1,5},{2,6},{3,7},{4,0},{5,1},{6,2},{7,3},{8,12},{9,13},{10,... | collective-permute-start | bytes 3145736 | tf_op jit(solution)/shard_map/ppermute | solution.py:686
  96.3 15.0 %collective-permute-start.16 = (bf16[1,128,2048]{2,1,0:T(8,128)(2,1)}, bf16[1,128,2048]{2,1,0:T(8,128)(2,1)S(1)}, u32[]{:S(2)}, u32[]{:S(2)}) collective-permute-start(bf16[1,128,2048]{2,1,0:T(8,128)(2,1)} %get-tuple-element.284), channel_id=1, source_target_pairs={{0,2},{1,3},{2,0},{3,1},{4,6},{5,7},{6,4},{7,5},{8,10},{9,11},{10,... | collective-permute-start | bytes 1572872 | tf_op jit(solution)/shard_map/ppermute | solution.py:686
  99.5 22.2 %collective-permute-start.18 = (bf16[1,128,2048]{2,1,0:T(8,128)(2,1)S(1)}, bf16[1,128,2048]{2,1,0:T(8,128)(2,1)S(1)}, u32[]{:S(2)}, u32[]{:S(2)}) collective-permute-start(bf16[1,128,2048]{2,1,0:T(8,128)(2,1)S(1)} %slice.286), channel_id=1, source_target_pairs={{0,2},{1,3},{2,0},{3,1},{4,6},{5,7},{6,4},{7,5},{8,10},{9,11},{10,... | collective-permute-start | bytes 1572872 | tf_op jit(solution)/shard_map/ppermute | solution.py:686
  100.2 22.6 %collective-permute-start.19 = (bf16[1,128,2048]{2,1,0:T(8,128)(2,1)S(1)}, bf16[1,128,2048]{2,1,0:T(8,128)(2,1)S(1)}, u32[]{:S(2)}, u32[]{:S(2)}) collective-permute-start(bf16[1,128,2048]{2,1,0:T(8,128)(2,1)S(1)} %slice.285), channel_id=1, source_target_pairs={{0,4},{1,5},{2,6},{3,7},{4,0},{5,1},{6,2},{7,3},{8,12},{9,13},{10,... | collective-permute-start | bytes 1572872 | tf_op jit(solution)/shard_map/ppermute | solution.py:686
  123.0 14.9 %collective-permute-start.23 = (bf16[1,128,2048]{2,1,0:T(8,128)(2,1)S(1)}, bf16[1,128,2048]{2,1,0:T(8,128)(2,1)S(1)}, u32[]{:S(2)}, u32[]{:S(2)}) collective-permute-start(bf16[1,128,2048]{2,1,0:T(8,128)(2,1)S(1)} %add_convert_fusion), channel_id=1, source_target_pairs={{0,2},{1,3},{2,0},{3,1},{4,6},{5,7},{6,4},{7,5},{8,10},{9,11},{10,... | collective-permute-start | bytes 1572872 | tf_op jit(solution)/shard_map/ppermute | solution.py:686
  125.4 23.2 %collective-permute-start.27 = (bf16[1,128,2048]{2,1,0:T(8,128)(2,1)S(1)}, bf16[1,128,2048]{2,1,0:T(8,128)(2,1)S(1)}, u32[]{:S(2)}, u32[]{:S(2)}) collective-permute-start(bf16[1,128,2048]{2,1,0:T(8,128)(2,1)S(1)} %slice.207), channel_id=1, source_target_pairs={{0,4},{1,5},{2,6},{3,7},{4,0},{5,1},{6,2},{7,3},{8,12},{9,13},{10,... | collective-permute-start | bytes 1572872 | tf_op jit(solution)/shard_map/ppermute | solution.py:686
  125.9 22.7 %collective-permute-start.28 = (bf16[1,128,2048]{2,1,0:T(8,128)(2,1)S(1)}, bf16[1,128,2048]{2,1,0:T(8,128)(2,1)S(1)}, u32[]{:S(2)}, u32[]{:S(2)}) collective-permute-start(bf16[1,128,2048]{2,1,0:T(8,128)(2,1)S(1)} %slice.208), channel_id=1, source_target_pairs={{0,2},{1,3},{2,0},{3,1},{4,6},{5,7},{6,4},{7,5},{8,10},{9,11},{10,... | collective-permute-start | bytes 1572872 | tf_op jit(solution)/shard_map/ppermute | solution.py:686
  142.6 27.0 %collective-permute-start.24 = (bf16[2,128,2048]{2,1,0:T(8,128)(2,1)S(1)}, bf16[2,128,2048]{2,1,0:T(8,128)(2,1)S(1)}, u32[]{:S(2)}, u32[]{:S(2)}) collective-permute-start(bf16[2,128,2048]{2,1,0:T(8,128)(2,1)S(1)} %multiply_convert_fusion.1.refs_0_), channel_id=1, source_target_pairs={{0,2},{1,3},{2,0},{3,1},{4,6},{5,7},{6,4},{7,5},{8,10},{9,11},{10,... | collective-permute-start | bytes 3145736 | tf_op jit(solution)/shard_map/ppermute | solution.py:686
  144.2 26.1 %collective-permute-start.25 = (bf16[2,128,2048]{2,1,0:T(8,128)(2,1)S(1)}, bf16[2,128,2048]{2,1,0:T(8,128)(2,1)S(1)}, u32[]{:S(2)}, u32[]{:S(2)}) collective-permute-start(bf16[2,128,2048]{2,1,0:T(8,128)(2,1)S(1)} %multiply_convert_fusion.1.refs_0_), channel_id=1, source_target_pairs={{0,4},{1,5},{2,6},{3,7},{4,0},{5,1},{6,2},{7,3},{8,12},{9,13},{10,... | collective-permute-start | bytes 3145736 | tf_op jit(solution)/shard_map/ppermute | solution.py:686
  205.4 20.0 %collective-permute-start.37 = (bf16[176,2048]{1,0:T(8,128)(2,1)S(1)}, bf16[176,2048]{1,0:T(8,128)(2,1)}, u32[]{:S(2)}, u32[]{:S(2)}) collective-permute-start(bf16[176,2048]{1,0:T(8,128)(2,1)S(1)} %get-tuple-element.572.left_ref), channel_id=1, source_target_pairs={{0,8},{24,16},{1,9},{25,17},{2,10},{26,18},{3,11},{27,19},{4,12},{... | collective-permute-start | bytes 2162696 | tf_op jit(solution)/shard_map/ppermute | solution.py:731
  209.8 36.2 %collective-permute-start.40 = (bf16[176,2048]{1,0:T(8,128)(2,1)S(1)}, bf16[176,2048]{1,0:T(8,128)(2,1)}, u32[]{:S(2)}, u32[]{:S(2)}) collective-permute-start(bf16[176,2048]{1,0:T(8,128)(2,1)S(1)} %get-tuple-element.571.left_ref), channel_id=1, source_target_pairs={{0,8},{24,16},{1,9},{25,17},{2,10},{26,18},{3,11},{27,19},{4,12},{... | collective-permute-start | bytes 2162696 | tf_op jit(solution)/shard_map/ppermute | solution.py:731
  246.0 150.0 %all-gather.3.cloned.1.call-start = ((), (), s32[]{:S(2)}) async-start(), calls=%async_computation.6 | async-start | bytes 9437184 | tf_op jit(solution)/shard_map/all_gather | solution.py:539
  248.2 21.1 %collective-permute-start.38 = (bf16[176,2048]{1,0:T(8,128)(2,1)}, bf16[176,2048]{1,0:T(8,128)(2,1)}, u32[]{:S(2)}, u32[]{:S(2)}) collective-permute-start(bf16[176,2048]{1,0:T(8,128)(2,1)} %add.178.left_ref), channel_id=1, source_target_pairs={{8,16},{16,8},{9,17},{17,9},{10,18},{18,10},{11,19},{19,11},{12,20... | collective-permute-start | bytes 2162696 | tf_op jit(solution)/shard_map/ppermute | solution.py:736
  250.8 23.3 %collective-permute-start.39 = (bf16[176,2048]{1,0:T(8,128)(2,1)}, bf16[176,2048]{1,0:T(8,128)(2,1)S(1)}, u32[]{:S(2)}, u32[]{:S(2)}) collective-permute-start(bf16[176,2048]{1,0:T(8,128)(2,1)} %get-tuple-element.570.left_ref), channel_id=1, source_target_pairs={{0,8},{24,16},{1,9},{25,17},{2,10},{26,18},{3,11},{27,19},{4,12},{... | collective-permute-start | bytes 2162696 | tf_op jit(solution)/shard_map/ppermute | solution.py:731
  258.6 29.4 %collective-permute-start.43 = (bf16[176,2048]{1,0:T(8,128)(2,1)S(1)}, bf16[176,2048]{1,0:T(8,128)(2,1)S(1)}, u32[]{:S(2)}, u32[]{:S(2)}) collective-permute-start(bf16[176,2048]{1,0:T(8,128)(2,1)S(1)} %add.180.left_ref), channel_id=1, source_target_pairs={{8,16},{16,8},{9,17},{17,9},{10,18},{18,10},{11,19},{19,11},{12,20... | collective-permute-start | bytes 2162696 | tf_op jit(solution)/shard_map/ppermute | solution.py:736
  259.3 30.1 %collective-permute-start.44 = (bf16[176,2048]{1,0:T(8,128)(2,1)S(1)}, bf16[176,2048]{1,0:T(8,128)(2,1)S(1)}, u32[]{:S(2)}, u32[]{:S(2)}) collective-permute-start(bf16[176,2048]{1,0:T(8,128)(2,1)S(1)} %get-tuple-element.569.left_ref), channel_id=1, source_target_pairs={{0,8},{24,16},{1,9},{25,17},{2,10},{26,18},{3,11},{27,19},{4,12},{... | collective-permute-start | bytes 2162696 | tf_op jit(solution)/shard_map/ppermute | solution.py:731
  276.8 28.1 %collective-permute-start.42 = (bf16[176,2048]{1,0:T(8,128)(2,1)S(1)}, bf16[176,2048]{1,0:T(8,128)(2,1)S(1)}, u32[]{:S(2)}, u32[]{:S(2)}) collective-permute-start(bf16[176,2048]{1,0:T(8,128)(2,1)S(1)} %merge.10.refs_1_), channel_id=1, source_target_pairs={{0,8},{24,16},{8,0},{16,24},{1,9},{25,17},{9,1},{17,25},{2,10},{26... | collective-permute-start | bytes 2162696 | tf_op jit(solution)/shard_map/ppermute | solution.py:728
  280.5 24.3 %collective-permute-start.41 = (bf16[176,2048]{1,0:T(8,128)(2,1)S(1)}, bf16[176,2048]{1,0:T(8,128)(2,1)S(1)}, u32[]{:S(2)}, u32[]{:S(2)}) collective-permute-start(bf16[176,2048]{1,0:T(8,128)(2,1)S(1)} %add.179.left_ref), channel_id=1, source_target_pairs={{8,16},{16,8},{9,17},{17,9},{10,18},{18,10},{11,19},{19,11},{12,20... | collective-permute-start | bytes 2162696 | tf_op jit(solution)/shard_map/ppermute | solution.py:736
  289.7 30.6 %collective-permute-start.48 = (bf16[176,2048]{1,0:T(8,128)(2,1)S(1)}, bf16[176,2048]{1,0:T(8,128)(2,1)S(1)}, u32[]{:S(2)}, u32[]{:S(2)}) collective-permute-start(bf16[176,2048]{1,0:T(8,128)(2,1)S(1)} %merge.12.refs_3_), channel_id=1, source_target_pairs={{0,8},{24,16},{8,0},{16,24},{1,9},{25,17},{9,1},{17,25},{2,10},{26... | collective-permute-start | bytes 2162696 | tf_op jit(solution)/shard_map/ppermute | solution.py:728
  292.4 28.8 %collective-permute-start.47 = (bf16[176,2048]{1,0:T(8,128)(2,1)S(1)}, bf16[176,2048]{1,0:T(8,128)(2,1)S(1)}, u32[]{:S(2)}, u32[]{:S(2)}) collective-permute-start(bf16[176,2048]{1,0:T(8,128)(2,1)S(1)} %add.182.left_ref), channel_id=1, source_target_pairs={{8,16},{16,8},{9,17},{17,9},{10,18},{18,10},{11,19},{19,11},{12,20... | collective-permute-start | bytes 2162696 | tf_op jit(solution)/shard_map/ppermute | solution.py:736
  307.1 25.8 %collective-permute-start.46 = (bf16[176,2048]{1,0:T(8,128)(2,1)S(1)}, bf16[176,2048]{1,0:T(8,128)(2,1)S(1)}, u32[]{:S(2)}, u32[]{:S(2)}) collective-permute-start(bf16[176,2048]{1,0:T(8,128)(2,1)S(1)} %merge.11.refs_5_), channel_id=1, source_target_pairs={{0,8},{24,16},{8,0},{16,24},{1,9},{25,17},{9,1},{17,25},{2,10},{26... | collective-permute-start | bytes 2162696 | tf_op jit(solution)/shard_map/ppermute | solution.py:728
  309.8 24.0 %collective-permute-start.45 = (bf16[176,2048]{1,0:T(8,128)(2,1)S(1)}, bf16[176,2048]{1,0:T(8,128)(2,1)S(1)}, u32[]{:S(2)}, u32[]{:S(2)}) collective-permute-start(bf16[176,2048]{1,0:T(8,128)(2,1)S(1)} %add.181.left_ref), channel_id=1, source_target_pairs={{8,16},{16,8},{9,17},{17,9},{10,18},{18,10},{11,19},{19,11},{12,20... | collective-permute-start | bytes 2162696 | tf_op jit(solution)/shard_map/ppermute | solution.py:736
  340.9 256.4 %reduce-scatter.6.cloned.1.call-start = ((), (), s32[]{:S(2)}) async-start(), calls=%async_computation.4 | async-start | bytes 9437184 | tf_op jit(solution)/shard_map/reduce_scatter | solution.py:543
  344.6 25.0 %collective-permute-start.52 = (bf16[176,2048]{1,0:T(8,128)(2,1)S(1)}, bf16[176,2048]{1,0:T(8,128)(2,1)S(1)}, u32[]{:S(2)}, u32[]{:S(2)}) collective-permute-start(bf16[176,2048]{1,0:T(8,128)(2,1)S(1)} %merge.14.refs_7_), channel_id=1, source_target_pairs={{0,8},{24,16},{8,0},{16,24},{1,9},{25,17},{9,1},{17,25},{2,10},{26... | collective-permute-start | bytes 2162696 | tf_op jit(solution)/shard_map/ppermute | solution.py:728
  348.5 21.9 %collective-permute-start.51 = (bf16[176,2048]{1,0:T(8,128)(2,1)S(1)}, bf16[176,2048]{1,0:T(8,128)(2,1)S(1)}, u32[]{:S(2)}, u32[]{:S(2)}) collective-permute-start(bf16[176,2048]{1,0:T(8,128)(2,1)S(1)} %add.184.left_ref), channel_id=1, source_target_pairs={{8,16},{16,8},{9,17},{17,9},{10,18},{18,10},{11,19},{19,11},{12,20... | collective-permute-start | bytes 2162696 | tf_op jit(solution)/shard_map/ppermute | solution.py:736
  352.5 25.7 %collective-permute-start.50 = (bf16[176,2048]{1,0:T(8,128)(2,1)}, bf16[176,2048]{1,0:T(8,128)(2,1)}, u32[]{:S(2)}, u32[]{:S(2)}) collective-permute-start(bf16[176,2048]{1,0:T(8,128)(2,1)} %merge.13.refs_1_), channel_id=1, source_target_pairs={{0,8},{24,16},{8,0},{16,24},{1,9},{25,17},{9,1},{17,25},{2,10},{26... | collective-permute-start | bytes 2162696 | tf_op jit(solution)/shard_map/ppermute | solution.py:728
  355.4 22.8 %collective-permute-start.49 = (bf16[176,2048]{1,0:T(8,128)(2,1)}, bf16[176,2048]{1,0:T(8,128)(2,1)}, u32[]{:S(2)}, u32[]{:S(2)}) collective-permute-start(bf16[176,2048]{1,0:T(8,128)(2,1)} %add.183.left_ref), channel_id=1, source_target_pairs={{8,16},{16,8},{9,17},{17,9},{10,18},{18,10},{11,19},{19,11},{12,20... | collective-permute-start | bytes 2162696 | tf_op jit(solution)/shard_map/ppermute | solution.py:736
  374.9 19.3 %collective-permute-start.56 = (bf16[176,2048]{1,0:T(8,128)(2,1)S(1)}, bf16[176,2048]{1,0:T(8,128)(2,1)S(1)}, u32[]{:S(2)}, u32[]{:S(2)}) collective-permute-start(bf16[176,2048]{1,0:T(8,128)(2,1)S(1)} %merge.16.refs_3_), channel_id=1, source_target_pairs={{0,8},{24,16},{8,0},{16,24},{1,9},{25,17},{9,1},{17,25},{2,10},{26... | collective-permute-start | bytes 2162696 | tf_op jit(solution)/shard_map/ppermute | solution.py:728
  377.4 17.7 %collective-permute-start.55 = (bf16[176,2048]{1,0:T(8,128)(2,1)S(1)}, bf16[176,2048]{1,0:T(8,128)(2,1)S(1)}, u32[]{:S(2)}, u32[]{:S(2)}) collective-permute-start(bf16[176,2048]{1,0:T(8,128)(2,1)S(1)} %add.186.left_ref), channel_id=1, source_target_pairs={{8,16},{16,8},{9,17},{17,9},{10,18},{18,10},{11,19},{19,11},{12,20... | collective-permute-start | bytes 2162696 | tf_op jit(solution)/shard_map/ppermute | solution.py:736
  382.7 24.4 %collective-permute-start.54 = (bf16[176,2048]{1,0:T(8,128)(2,1)}, bf16[176,2048]{1,0:T(8,128)(2,1)}, u32[]{:S(2)}, u32[]{:S(2)}) collective-permute-start(bf16[176,2048]{1,0:T(8,128)(2,1)} %merge.15.refs_5_), channel_id=1, source_target_pairs={{0,8},{24,16},{8,0},{16,24},{1,9},{25,17},{9,1},{17,25},{2,10},{26... | collective-permute-start | bytes 2162696 | tf_op jit(solution)/shard_map/ppermute | solution.py:728
  391.1 16.0 %collective-permute-start.53 = (bf16[176,2048]{1,0:T(8,128)(2,1)}, bf16[176,2048]{1,0:T(8,128)(2,1)}, u32[]{:S(2)}, u32[]{:S(2)}) collective-permute-start(bf16[176,2048]{1,0:T(8,128)(2,1)} %add.185.left_ref), channel_id=1, source_target_pairs={{8,16},{16,8},{9,17},{17,9},{10,18},{18,10},{11,19},{19,11},{12,20... | collective-permute-start | bytes 2162696 | tf_op jit(solution)/shard_map/ppermute | solution.py:736
  407.1 225.6 %reduce-scatter.8.cloned.1.call-start = ((), (), s32[]{:S(2)}) async-start(), calls=%async_computation.5 | async-start | bytes 9437184 | tf_op jit(solution)/shard_map/reduce_scatter | solution.py:543
  410.9 26.4 %collective-permute-start.61 = (bf16[176,2048]{1,0:T(8,128)(2,1)S(1)}, bf16[176,2048]{1,0:T(8,128)(2,1)S(1)}, u32[]{:S(2)}, u32[]{:S(2)}) collective-permute-start(bf16[176,2048]{1,0:T(8,128)(2,1)S(1)} %merge.17.refs_7_), channel_id=1, source_target_pairs={{0,8},{24,16},{8,0},{16,24},{1,9},{25,17},{9,1},{17,25},{2,10},{26... | collective-permute-start | bytes 2162696 | tf_op jit(solution)/shard_map/ppermute | solution.py:728
  416.5 20.7 %collective-permute-start.60 = (bf16[176,2048]{1,0:T(8,128)(2,1)S(1)}, bf16[176,2048]{1,0:T(8,128)(2,1)S(1)}, u32[]{:S(2)}, u32[]{:S(2)}) collective-permute-start(bf16[176,2048]{1,0:T(8,128)(2,1)S(1)} %add.189.left_ref), channel_id=1, source_target_pairs={{8,16},{16,8},{9,17},{17,9},{10,18},{18,10},{11,19},{19,11},{12,20... | collective-permute-start | bytes 2162696 | tf_op jit(solution)/shard_map/ppermute | solution.py:736
  437.3 46.6 %collective-permute-start.59 = (bf16[176,2048]{1,0:T(8,128)(2,1)S(1)}, bf16[176,2048]{1,0:T(8,128)(2,1)S(1)}, u32[]{:S(2)}, u32[]{:S(2)}) collective-permute-start(bf16[176,2048]{1,0:T(8,128)(2,1)S(1)} %add.188.refs_1_), channel_id=1, source_target_pairs={{8,0},{16,24},{9,1},{17,25},{10,2},{18,26},{11,3},{19,27},{12,4},{... | collective-permute-start | bytes 2162696 | tf_op jit(solution)/shard_map/ppermute | solution.py:734
  438.9 38.5 %collective-permute-start.58 = (bf16[128,2048]{1,0:T(8,128)(2,1)S(1)}, bf16[128,2048]{1,0:T(8,128)(2,1)S(1)}, u32[]{:S(2)}, u32[]{:S(2)}) collective-permute-start(bf16[128,2048]{1,0:T(8,128)(2,1)S(1)} %get-tuple-element.580.left_ref), channel_id=1, source_target_pairs={{0,8},{24,16},{1,9},{25,17},{2,10},{26,18},{3,11},{27,19},{4,12},{... | collective-permute-start | bytes 1572872 | tf_op jit(solution)/shard_map/ppermute | solution.py:731
  444.9 39.0 %collective-permute-start.57 = (bf16[176,2048]{1,0:T(8,128)(2,1)S(1)}, bf16[176,2048]{1,0:T(8,128)(2,1)S(1)}, u32[]{:S(2)}, u32[]{:S(2)}) collective-permute-start(bf16[176,2048]{1,0:T(8,128)(2,1)S(1)} %add.187.left_ref), channel_id=1, source_target_pairs={{8,16},{16,8},{9,17},{17,9},{10,18},{18,10},{11,19},{19,11},{12,20... | collective-permute-start | bytes 2162696 | tf_op jit(solution)/shard_map/ppermute | solution.py:736
  445.9 48.2 %collective-permute-start.67 = (bf16[176,2048]{1,0:T(8,128)(2,1)S(1)}, bf16[176,2048]{1,0:T(8,128)(2,1)S(1)}, u32[]{:S(2)}, u32[]{:S(2)}) collective-permute-start(bf16[176,2048]{1,0:T(8,128)(2,1)S(1)} %add.193.refs_3_), channel_id=1, source_target_pairs={{8,0},{16,24},{9,1},{17,25},{10,2},{18,26},{11,3},{19,27},{12,4},{... | collective-permute-start | bytes 2162696 | tf_op jit(solution)/shard_map/ppermute | solution.py:734
  447.4 47.5 %collective-permute-start.65 = (bf16[176,2048]{1,0:T(8,128)(2,1)S(1)}, bf16[176,2048]{1,0:T(8,128)(2,1)S(1)}, u32[]{:S(2)}, u32[]{:S(2)}) collective-permute-start(bf16[176,2048]{1,0:T(8,128)(2,1)S(1)} %add.192.left_ref), channel_id=1, source_target_pairs={{8,16},{16,8},{9,17},{17,9},{10,18},{18,10},{11,19},{19,11},{12,20... | collective-permute-start | bytes 2162696 | tf_op jit(solution)/shard_map/ppermute | solution.py:736
  477.4 15.9 %collective-permute-start.66 = (bf16[128,2048]{1,0:T(8,128)(2,1)S(1)}, bf16[128,2048]{1,0:T(8,128)(2,1)S(1)}, u32[]{:S(2)}, u32[]{:S(2)}) collective-permute-start(bf16[128,2048]{1,0:T(8,128)(2,1)S(1)} %get-tuple-element.579.left_ref), channel_id=1, source_target_pairs={{0,8},{24,16},{1,9},{25,17},{2,10},{26,18},{3,11},{27,19},{4,12},{... | collective-permute-start | bytes 1572872 | tf_op jit(solution)/shard_map/ppermute | solution.py:731
  498.2 21.7 %collective-permute-start.64 = (bf16[176,2048]{1,0:T(8,128)(2,1)S(1)}, bf16[176,2048]{1,0:T(8,128)(2,1)S(1)}, u32[]{:S(2)}, u32[]{:S(2)}) collective-permute-start(bf16[176,2048]{1,0:T(8,128)(2,1)S(1)} %add.191.refs_5_), channel_id=1, source_target_pairs={{8,0},{16,24},{9,1},{17,25},{10,2},{18,26},{11,3},{19,27},{12,4},{... | collective-permute-start | bytes 2162696 | tf_op jit(solution)/shard_map/ppermute | solution.py:734
  500.8 19.1 %collective-permute-start.63 = (bf16[1024,256]{1,0:T(8,128)(2,1)S(1)}, bf16[1024,256]{1,0:T(8,128)(2,1)S(1)}, u32[]{:S(2)}, u32[]{:S(2)}) collective-permute-start(bf16[1024,256]{1,0:T(8,128)(2,1)S(1)} %get-tuple-element.578.left_ref), channel_id=1, source_target_pairs={{0,8},{24,16},{1,9},{25,17},{2,10},{26,18},{3,11},{27,19},{4,12},{... | collective-permute-start | bytes 1572872 | tf_op jit(solution)/shard_map/ppermute | solution.py:731
  507.9 27.0 %collective-permute-start.73 = (bf16[176,2048]{1,0:T(8,128)(2,1)S(1)}, bf16[176,2048]{1,0:T(8,128)(2,1)S(1)}, u32[]{:S(2)}, u32[]{:S(2)}) collective-permute-start(bf16[176,2048]{1,0:T(8,128)(2,1)S(1)} %add.197.refs_7_), channel_id=1, source_target_pairs={{8,0},{16,24},{9,1},{17,25},{10,2},{18,26},{11,3},{19,27},{12,4},{... | collective-permute-start | bytes 2162696 | tf_op jit(solution)/shard_map/ppermute | solution.py:734
  509.5 18.4 %collective-permute-start.71 = (bf16[128,2048]{1,0:T(8,128)(2,1)S(1)}, bf16[128,2048]{1,0:T(8,128)(2,1)S(1)}, u32[]{:S(2)}, u32[]{:S(2)}) collective-permute-start(bf16[128,2048]{1,0:T(8,128)(2,1)S(1)} %add.196.left_ref), channel_id=1, source_target_pairs={{8,16},{16,8},{9,17},{17,9},{10,18},{18,10},{11,19},{19,11},{12,20... | collective-permute-start | bytes 1572872 | tf_op jit(solution)/shard_map/ppermute | solution.py:736
  510.3 21.9 %collective-permute-start.72 = (bf16[1024,256]{1,0:T(8,128)(2,1)S(1)}, bf16[1024,256]{1,0:T(8,128)(2,1)S(1)}, u32[]{:S(2)}, u32[]{:S(2)}) collective-permute-start(bf16[1024,256]{1,0:T(8,128)(2,1)S(1)} %get-tuple-element.577.left_ref), channel_id=1, source_target_pairs={{0,8},{24,16},{1,9},{25,17},{2,10},{26,18},{3,11},{27,19},{4,12},{... | collective-permute-start | bytes 1572872 | tf_op jit(solution)/shard_map/ppermute | solution.py:731
  520.1 32.3 %collective-permute-start.70 = (bf16[128,2048]{1,0:T(8,128)(2,1)S(1)}, bf16[128,2048]{1,0:T(8,128)(2,1)S(1)}, u32[]{:S(2)}, u32[]{:S(2)}) collective-permute-start(bf16[128,2048]{1,0:T(8,128)(2,1)S(1)} %add.195.refs_1_), channel_id=1, source_target_pairs={{8,0},{16,24},{9,1},{17,25},{10,2},{18,26},{11,3},{19,27},{12,4},{... | collective-permute-start | bytes 1572872 | tf_op jit(solution)/shard_map/ppermute | solution.py:734
  522.3 37.4 %collective-permute-start.69 = (bf16[1024,256]{1,0:T(8,128)(2,1)S(1)}, bf16[1024,256]{1,0:T(8,128)(2,1)S(1)}, u32[]{:S(2)}, u32[]{:S(2)}) collective-permute-start(bf16[1024,256]{1,0:T(8,128)(2,1)S(1)} %get-tuple-element.576.left_ref), channel_id=1, source_target_pairs={{0,8},{24,16},{1,9},{25,17},{2,10},{26,18},{3,11},{27,19},{4,12},{... | collective-permute-start | bytes 1572872 | tf_op jit(solution)/shard_map/ppermute | solution.py:731
  527.9 31.8 %collective-permute-start.68 = (bf16[1024,256]{1,0:T(8,128)(2,1)S(1)}, bf16[1024,256]{1,0:T(8,128)(2,1)S(1)}, u32[]{:S(2)}, u32[]{:S(2)}) collective-permute-start(bf16[1024,256]{1,0:T(8,128)(2,1)S(1)} %add.194.left_ref), channel_id=1, source_target_pairs={{8,16},{16,8},{9,17},{17,9},{10,18},{18,10},{11,19},{19,11},{12,20... | collective-permute-start | bytes 1572872 | tf_op jit(solution)/shard_map/ppermute | solution.py:736
  542.3 22.1 %collective-permute-start.79 = (bf16[128,2048]{1,0:T(8,128)(2,1)}, bf16[128,2048]{1,0:T(8,128)(2,1)}, u32[]{:S(2)}, u32[]{:S(2)}) collective-permute-start(bf16[128,2048]{1,0:T(8,128)(2,1)} %add.199.refs_3_), channel_id=1, source_target_pairs={{8,0},{16,24},{9,1},{17,25},{10,2},{18,26},{11,3},{19,27},{12,4},{... | collective-permute-start | bytes 1572872 | tf_op jit(solution)/shard_map/ppermute | solution.py:734
  552.4 19.2 %collective-permute-start.78 = (bf16[1024,256]{1,0:T(8,128)(2,1)}, bf16[1024,256]{1,0:T(8,128)(2,1)}, u32[]{:S(2)}, u32[]{:S(2)}) collective-permute-start(bf16[1024,256]{1,0:T(8,128)(2,1)} %get-tuple-element.575.left_ref), channel_id=1, source_target_pairs={{0,8},{24,16},{1,9},{25,17},{2,10},{26,18},{3,11},{27,19},{4,12},{... | collective-permute-start | bytes 1572872 | tf_op jit(solution)/shard_map/ppermute | solution.py:731
  562.0 20.8 %collective-permute-start.86 = (bf16[1024,256]{1,0:T(8,128)(2,1)}, bf16[1024,256]{1,0:T(8,128)(2,1)}, u32[]{:S(2)}, u32[]{:S(2)}) collective-permute-start(bf16[1024,256]{1,0:T(8,128)(2,1)} %merge.19.refs_1_), channel_id=1, source_target_pairs={{0,8},{24,16},{8,0},{16,24},{1,9},{25,17},{9,1},{17,25},{2,10},{26... | collective-permute-start | bytes 1572872 | tf_op jit(solution)/shard_map/ppermute | solution.py:728
  562.9 19.9 %collective-permute-start.85 = (bf16[1024,256]{1,0:T(8,128)(2,1)}, bf16[1024,256]{1,0:T(8,128)(2,1)}, u32[]{:S(2)}, u32[]{:S(2)}) collective-permute-start(bf16[1024,256]{1,0:T(8,128)(2,1)} %add.203.left_ref), channel_id=1, source_target_pairs={{8,16},{16,8},{9,17},{17,9},{10,18},{18,10},{11,19},{19,11},{12,20... | collective-permute-start | bytes 1572872 | tf_op jit(solution)/shard_map/ppermute | solution.py:736
  573.0 19.5 %collective-permute-start.81 = (bf16[1024,256]{1,0:T(8,128)(2,1)S(1)}, bf16[1024,256]{1,0:T(8,128)(2,1)S(1)}, u32[]{:S(2)}, u32[]{:S(2)}) collective-permute-start(bf16[1024,256]{1,0:T(8,128)(2,1)S(1)} %merge.18.refs_3_), channel_id=1, source_target_pairs={{0,8},{24,16},{8,0},{16,24},{1,9},{25,17},{9,1},{17,25},{2,10},{26... | collective-permute-start | bytes 1572872 | tf_op jit(solution)/shard_map/ppermute | solution.py:728
  576.8 15.7 %collective-permute-start.80 = (bf16[1024,256]{1,0:T(8,128)(2,1)S(1)}, bf16[1024,256]{1,0:T(8,128)(2,1)S(1)}, u32[]{:S(2)}, u32[]{:S(2)}) collective-permute-start(bf16[1024,256]{1,0:T(8,128)(2,1)S(1)} %add.200.left_ref), channel_id=1, source_target_pairs={{8,16},{16,8},{9,17},{17,9},{10,18},{18,10},{11,19},{19,11},{12,20... | collective-permute-start | bytes 1572872 | tf_op jit(solution)/shard_map/ppermute | solution.py:736
  577.5 15.0 %collective-permute-start.82 = (bf16[96,256]{1,0:T(8,128)(2,1)S(1)}, bf16[96,256]{1,0:T(8,128)(2,1)S(1)}, u32[]{:S(2)}, u32[]{:S(2)}) collective-permute-start(bf16[96,256]{1,0:T(8,128)(2,1)S(1)} %pad.5.left_ref), channel_id=1, source_target_pairs={{0,8},{24,16},{1,9},{25,17},{2,10},{26,18},{3,11},{27,19},{4,12},{... | collective-permute-start | bytes 147464 | tf_op jit(solution)/shard_map/ppermute | solution.py:812
  593.4 15.9 %collective-permute-start.84 = (bf16[1024,256]{1,0:T(8,128)(2,1)S(1)}, bf16[1024,256]{1,0:T(8,128)(2,1)}, u32[]{:S(2)}, u32[]{:S(2)}) collective-permute-start(bf16[1024,256]{1,0:T(8,128)(2,1)S(1)} %add.202.refs_7_), channel_id=1, source_target_pairs={{8,0},{16,24},{9,1},{17,25},{10,2},{18,26},{11,3},{19,27},{12,4},{... | collective-permute-start | bytes 1572872 | tf_op jit(solution)/shard_map/ppermute | solution.py:734
  611.2 21.5 %collective-permute-start.91 = (bf16[1024,256]{1,0:T(8,128)(2,1)}, bf16[1024,256]{1,0:T(8,128)(2,1)}, u32[]{:S(2)}, u32[]{:S(2)}) collective-permute-start(bf16[1024,256]{1,0:T(8,128)(2,1)} %add.209.refs_11_), channel_id=1, source_target_pairs={{8,0},{16,24},{9,1},{17,25},{10,2},{18,26},{11,3},{19,27},{12,4},{... | collective-permute-start | bytes 1572872 | tf_op jit(solution)/shard_map/ppermute | solution.py:734
  612.6 20.2 %collective-permute-start.92 = (bf16[96,256]{1,0:T(8,128)(2,1)S(1)}, bf16[96,256]{1,0:T(8,128)(2,1)S(1)}, u32[]{:S(2)}, u32[]{:S(2)}) collective-permute-start(bf16[96,256]{1,0:T(8,128)(2,1)S(1)} %add.208), channel_id=1, source_target_pairs={{8,0},{16,24},{9,1},{17,25},{10,2},{18,26},{11,3},{19,27},{12,4},{... | collective-permute-start | bytes 147464 | tf_op jit(solution)/shard_map/ppermute | solution.py:820
  616.0 23.8 %collective-permute-start.90 = (bf16[1024,256]{1,0:T(8,128)(2,1)}, bf16[1024,256]{1,0:T(8,128)(2,1)}, u32[]{:S(2)}, u32[]{:S(2)}) collective-permute-start(bf16[1024,256]{1,0:T(8,128)(2,1)} %add.207.refs_9_), channel_id=1, source_target_pairs={{8,0},{16,24},{9,1},{17,25},{10,2},{18,26},{11,3},{19,27},{12,4},{... | collective-permute-start | bytes 1572872 | tf_op jit(solution)/shard_map/ppermute | solution.py:734
  (189 other events, 1260.1 us)
Sparse Core Ops, SparseCore 0:
  246.1 71.2 reduce-scatter.3
  341.0 53.2 all-gather.2
  407.3 73.1 reduce-scatter.5
  495.9 70.7 reduce-scatter.7
